TPU v7x, 32 devices: a whole 2x2x4 slice. The times are simulated.
32 devices in a mesh: ctx: 16 (over z, y, core), tp: 2 (over x).
Axes of the slice: x: 2, y: 2, z: 4, core: 2. Of those that a mesh axis runs over, the one named last changes fastest.
Arguments:
- queries: bfloat16 [8192, 4096], P('ctx', 'tp'), may hold values from -5 to 5
- keys: bfloat16 [8192, 4096], P('ctx', 'tp'), may hold values from -5 to 5
- values: bfloat16 [8192, 4096], P('ctx', 'tp'), may hold values from -21 to 21
- log_decay: float32 [32, 8192], P('tp', 'ctx'), may hold values from -0.7 to 0
- gate: bfloat16 [8192, 4096], P('ctx', 'tp'), may hold values from -6 to 6
- gain: float32 [4096], P('tp'), may hold values from 0.5 to 1.5
- grad_out: bfloat16 [8192, 4096], P(('ctx', 'tp')), may hold values from -20 to 20
Outputs:
- query_grad: bfloat16 [8192, 4096], P('ctx', 'tp')
- key_grad: bfloat16 [8192, 4096], P('ctx', 'tp')
- value_grad: bfloat16 [8192, 4096], P('ctx', 'tp')
- gate_grad: bfloat16 [8192, 4096], P('ctx', 'tp')
- gain_grad: float32 [4096], P('tp')
All inputs are finite; a program needn't handle non-finite values.
Results may differ from a plain program's by a relative error of at most 0.005.
Values may be sent and summed in bfloat16 or wider, within the bound.
No kernel may reach another device: no remote copies, remote signals or barrier semaphores. Data moves between devices by JAX's collectives and lax.ppermute only.
A program may use at most 128 MiB of HBM per device.

v0:
```python
import jax
import jax.numpy as jnp
from jax import lax
from jax.sharding import PartitionSpec as P

HEAD = 128
BLOCK = 512


HIGH_PRECISION = lax.Precision.HIGHEST
EPSILON = 1e-06


def carried_in(part, axis, combine, identity, reverse):
    count = lax.axis_size(axis)
    place = lax.axis_index(axis)
    ahead = count - 1 - place if reverse else place
    gathered = jax.tree.map(lambda a: lax.all_gather(a, axis), part)
    state = jax.tree.map(lambda a, e: jnp.zeros_like(a) + jnp.asarray(e, a.dtype), part, identity)

    def one(lap, state):
        source = count - 1 - lap if reverse else lap
        return combine(
            state, jax.tree.map(lambda a: lax.dynamic_index_in_dim(a, source, 0, False), gathered)
        )

    return lax.fori_loop(0, ahead, one, state)


def state_sweep(block_decay_rates, partial_terms, reverse_order):

    def step_forward_fn(carried_state, element):
        rate_row, addend = element
        return (jnp.exp(rate_row)[:, None, None] * carried_state + addend, carried_state)

    final, before = lax.scan(
        step_forward_fn,
        jnp.zeros_like(partial_terms[0]),
        (block_decay_rates, partial_terms),
        reverse=reverse_order,
    )
    return (before, final)


def link_states(earlier, later):
    return (earlier[0] * later[0], later[0][:, None, None] * earlier[1] + later[1])


def local(queries, keys, values, log_decay, gate, gain, grad_out):
    rows_here, cols_here = queries.shape
    heads_here = cols_here // HEAD
    count = rows_here // BLOCK
    channels = cols_here * lax.axis_size("tp")
    grad_rows = lax.all_to_all(grad_out, "tp", split_axis=1, concat_axis=0, tiled=True)
    shape4 = (count, BLOCK, heads_here, HEAD)
    query_blocks = queries.reshape(shape4)
    key_blocks = keys.reshape(shape4)
    value_blocks = values.reshape(shape4)
    decay_sum = jnp.cumsum(log_decay.reshape(heads_here, count, BLOCK), axis=2)
    by_head = jnp.transpose(decay_sum, (1, 0, 2))
    decay_sum = jnp.transpose(decay_sum, (1, 2, 0))
    block_decay_rate = decay_sum[:, -1, :]
    causal = jnp.tril(jnp.ones((BLOCK, BLOCK), dtype=bool))
    spread = by_head[:, :, :, None] - by_head[:, :, None, :]
    table = jnp.where(causal[None, None], jnp.exp(jnp.minimum(spread, 0.0)), 0.0)
    attention_scores = jnp.einsum(
        "blhd,bmhd->bhlm", query_blocks, key_blocks, preferred_element_type=jnp.float32
    )
    probs = (attention_scores * table).astype(jnp.bfloat16)
    intra = jnp.einsum("bhlm,bmhe->blhe", probs, value_blocks, preferred_element_type=jnp.float32)
    growth = jnp.exp(decay_sum)[..., None]
    decay_shrink = jnp.exp(block_decay_rate[:, None, :] - decay_sum)[..., None]
    full_value_rows = value_blocks.astype(jnp.float32)
    query_decayed = query_blocks.astype(jnp.float32) * growth
    key_with_decay = key_blocks.astype(jnp.float32) * decay_shrink
    partial_terms = jnp.einsum(
        "zoas,zoai->zasi", key_with_decay, full_value_rows, precision=HIGH_PRECISION
    )
    state_before_block, block_local_state = state_sweep(block_decay_rate, partial_terms, False)
    totals = jnp.cumsum(block_decay_rate, axis=0)
    device_decay = jnp.exp(totals[-1])
    incoming = carried_in(
        (device_decay, block_local_state),
        "ctx",
        link_states,
        (jnp.ones_like(device_decay), jnp.zeros_like(block_local_state)),
        False,
    )[1]
    entering = jnp.exp(totals - block_decay_rate)
    prev_states = state_before_block + entering[:, :, None, None] * incoming[None]
    attention = intra + jnp.einsum(
        "blhd,bhde->blhe", query_decayed, prev_states, precision=HIGH_PRECISION
    )
    gain_heads = gain.reshape(heads_here, HEAD)
    grad_blocks = grad_rows.reshape(shape4).astype(jnp.float32)
    opened = jax.nn.sigmoid(gate.reshape(shape4).astype(jnp.float32))
    dnorm = grad_blocks * opened
    dscaled = dnorm * gain_heads
    squares = jnp.sum(attention * attention, axis=(2, 3))
    inner = jnp.sum(attention * dscaled, axis=(2, 3))
    squares, inner = lax.psum((squares, inner), "tp")
    rscale = lax.rsqrt(squares / channels + EPSILON)[:, :, None, None]
    normed = attention * rscale * gain_heads
    gate_grad = (
        (grad_blocks * normed * opened * (1.0 - opened))
        .astype(jnp.bfloat16)
        .reshape(rows_here, cols_here)
    )
    gain_part = jnp.sum(dnorm * attention * rscale, axis=(0, 1)).reshape(cols_here)
    gain_grad = lax.psum(gain_part, "ctx")
    dattn = (
        dscaled * rscale - attention * (inner[:, :, None, None] * rscale**3 / channels)
    ).astype(jnp.bfloat16)
    dprobs = jnp.einsum("blhe,bmhe->bhlm", dattn, value_blocks, preferred_element_type=jnp.float32)
    scores_gradient = (dprobs * table).astype(jnp.bfloat16)
    wide_dattn = dattn.astype(jnp.float32)
    query_grad = jnp.einsum(
        "bhlm,bmhd->blhd", scores_gradient, key_blocks, preferred_element_type=jnp.float32
    )
    query_grad = query_grad + jnp.einsum(
        "blhe,bhde->blhd", wide_dattn * growth, prev_states, precision=HIGH_PRECISION
    )
    backterms = jnp.einsum("zoas,zoai->zasi", query_decayed, wide_dattn, precision=HIGH_PRECISION)
    after_local, local_grad = state_sweep(block_decay_rate, backterms, True)
    outgoing = carried_in(
        (device_decay, local_grad),
        "ctx",
        link_states,
        (jnp.ones_like(device_decay), jnp.zeros_like(local_grad)),
        True,
    )[1]
    leaving = jnp.exp(totals[-1][None, :] - totals)
    after_states = after_local + leaving[:, :, None, None] * outgoing[None]
    key_grad = jnp.einsum(
        "bhlm,blhd->bmhd", scores_gradient, query_blocks, preferred_element_type=jnp.float32
    )
    key_grad = key_grad + jnp.einsum(
        "bmhe,bhde->bmhd", full_value_rows * decay_shrink, after_states, precision=HIGH_PRECISION
    )
    value_grad = jnp.einsum("bhlm,blhe->bmhe", probs, dattn, preferred_element_type=jnp.float32)
    value_grad = value_grad + jnp.einsum(
        "bmhd,bhde->bmhe", key_with_decay, after_states, precision=HIGH_PRECISION
    )
    flat = (rows_here, cols_here)
    return (
        query_grad.astype(jnp.bfloat16).reshape(flat),
        key_grad.astype(jnp.bfloat16).reshape(flat),
        value_grad.astype(jnp.bfloat16).reshape(flat),
        gate_grad,
        gain_grad,
    )


def solution(mesh):
    return jax.shard_map(
        local,
        mesh=mesh,
        in_specs=(
            P("ctx", "tp"),
            P("ctx", "tp"),
            P("ctx", "tp"),
            P("tp", "ctx"),
            P("ctx", "tp"),
            P("tp"),
            P(("ctx", "tp"), None),
        ),
        out_specs=(P("ctx", "tp"), P("ctx", "tp"), P("ctx", "tp"), P("ctx", "tp"), P("tp")),
        check_vma=False,
    )
```

profile of v0, /device:TPU:0, one launch (start us, length us, event | category | flops | bytes accessed | tf_op | source)
XLA Modules:
  0.0 395.4 jit_solution(5468108753447658006)
XLA Ops:
  9.9 7.0 %fusion.42 = f32[16,128,128]{2,1,0:T(8,128)} fusion(f32[512,16]{0,1:T(8,128)S(1)} %copy.138, f32[16]{0:T(128)S(1)} %get-tuple-element.226, bf16[512,2048]{1,0:T(8,128)(2,1)S(1)} %copy-done, bf16[512,2048]{1,0:T(8,128)(2,1)} %param.12), kind=kOutput, calls=%fused_computation.62 | convolution fusion | flops 1612972032 | bytes 5275712 | tf_op jit(solution)/shard_map/zoas,zoai->zasi/dot_general | solution.py:76
  21.1 4.8 %all-to-all-start = ((bf16[256,2,2048]{0,2,1:T(8,128)(2,1)}), bf16[256,2,2048]{0,2,1:T(8,128)(2,1)}, u32[]{:S(2)}, u32[]{:S(2)}) async-start(bf16[256,2,2048]{0,2,1:T(8,128)(2,1)} %bitcast.203), calls=%async_computation | async-start | bytes 4194304 | tf_op jit(solution)/shard_map/all_to_all | solution.py:54
  30.3 9.6 %multiply_convert_fusion.1 = bf16[16,512,512]{2,1,0:T(8,128)(2,1)} fusion(bf16[512,16,128]{0,2,1:T(8,128)(2,1)} %bitcast.198, f32[16,512]{1,0:T(8,128)S(1)} %bitcast_add_fusion.6, pred[512,512]{1,0:T(8,128)(4,1)S(1)} %iota_compare_fusion, bf16[512,2048]{1,0:T(8,128)(2,1)} %param.12), kind=kOutput, calls=%fused_computation.5 | convolution fusion | flops 1094713344 | bytes 12877824 | tf_op jit(solution)/shard_map/blhd,bmhd->bhlm/dot_general | solution.py:66
  43.0 5.4 %copy.128 = f32[512,2048]{0,1:T(8,128)} copy(f32[512,2048]{1,0:T(8,128)} %add_divide_fusion) | data formatting | bytes 8388608 | tf_op jit(solution)/shard_map/div | solution.py:96
  48.3 23.3 %all-gather = f32[16,1,16]{2,1,0:T(1,128)S(1)} all-gather(f32[1,1,16]{2,1,0:T(1,128)S(1)} %get-tuple-element.228), channel_id=2, replica_groups=mesh['ctx'=16,'tp'=2] {'ctx'}, dimensions={0}, use_global_device_ids=true | all-gather | bytes 1088 | tf_op jit(solution)/shard_map/all_gather | solution.py:18
  71.7 8.9 %fusion.24 = f32[16,512,128]{1,2,0:T(8,128)} fusion(bf16[16,512,512]{2,1,0:T(8,128)(2,1)} %multiply_convert_fusion.1, bf16[512,2048]{1,0:T(8,128)(2,1)S(1)} %copy-done), kind=kOutput, calls=%fused_computation.44 | convolution fusion | flops 1073741824 | bytes 14680064 | tf_op jit(solution)/shard_map/bhlm,bmhe->blhe/dot_general | solution.py:70
  82.5 12.2 %copy.127 = f32[2,256,2048]{1,0,2:T(2,128)} copy(f32[2,256,2048]{1,2,0:T(8,128)S(1)} %convert_bitcast_fusion) | data formatting | bytes 8388608 | tf_op jit(solution)/shard_map/convert_element_type | solution.py:95
  94.7 6.5 %reshape.414 = f32[1,512,16,128]{1,3,2,0:T(8,128)} reshape(f32[2,256,2048]{1,0,2:T(2,128)} %copy.127) | data formatting | bytes 8388608 | tf_op jit(solution)/shard_map/convert_element_type | solution.py:95
  101.2 45.5 %all-gather.6.cloned.1.call-done = f32[256,128,128]{2,1,0:T(8,128)} async-done(((f32[16,128,128]{2,1,0:T(8,128)}), f32[256,128,128]{2,1,0:T(8,128)}) %all-gather.6.cloned.1.call-update) | async-done | bytes 16777232 | tf_op jit(solution)/shard_map/all_gather | solution.py:18
  146.9 9.2 %fusion.4 = (f32[512]{0:T(512)S(1)}, f32[16,128,512]{2,1,0:T(8,128)}) fusion(bf16[512,16,128]{0,2,1:T(8,128)(2,1)} %bitcast.199, f32[512,16]{0,1:T(8,128)S(1)} %copy.142, f32[16,128,128]{2,1,0:T(8,128)S(1)} %get-tuple-element.163, f32[16]{0:T(128)S(1)} %get-tuple-element.225, f32[16,512,128]{1,2,0:T(8,128)} %fusion.24), kind=kOutput, calls=%fused_computation.18 | convolution fusion | flops 1616117248 | bytes 11569216 | tf_op jit(solution)/shard_map/blhd,bhde->blhe/dot_general | solution.py:91
  156.0 4.9 %psum.21 = f32[1,512]{1,0:T(1,128)S(1)} all-reduce(f32[1,512]{1,0:T(1,128)S(1)} %bitcast.220), channel_id=1, replica_groups=mesh['ctx'=16,'tp'=2] {'tp'}, use_global_device_ids=true, to_apply=%region_5.6 | all-reduce | flops 512 | bytes 4096 | tf_op jit(solution)/shard_map/psum | solution.py:101
  161.0 9.2 %fusion.14 = (f32[16,128]{1,0:T(8,128)S(1)}, f32[512]{0:T(512)S(1)}, bf16[1,512,16,128]{1,3,2,0:T(8,128)(2,1)}) fusion(f32[16,128,512]{2,1,0:T(8,128)} %get-tuple-element.230, f32[512]{0:T(512)S(1)} %bitcast.217, f32[1,512,16,128]{1,3,2,0:T(8,128)} %reshape.414, f32[1,512,16,128]{1,3,2,0:T(8,128)} %bitcast.197, f32[16,128]{1,0:T(8,128)S(1)} %bitcast.214, ...), kind=kLoop, calls=%fused_computation.28 | loop fusion | flops 15726080 | bytes 18894848 | tf_op jit(solution)/shard_map/reduce_sum | solution.py:109
  170.2 5.1 %psum.22 = f32[512]{0:T(512)S(1)} all-reduce(f32[512]{0:T(512)S(1)} %get-tuple-element.201), channel_id=1, replica_groups=mesh['ctx'=16,'tp'=2] {'tp'}, use_global_device_ids=true, to_apply=%region_7.8 | all-reduce | flops 512 | bytes 4096 | tf_op jit(solution)/shard_map/psum | solution.py:101
  175.3 5.3 %fusion.7 = bf16[1,512,16,128]{1,3,2,0:T(8,128)(2,1)S(1)} fusion(f32[16,128,512]{2,1,0:T(8,128)} %get-tuple-element.230, f32[512]{0:T(512)S(1)} %fusion.66, f32[512]{0:T(512)S(1)} %bitcast.219, f32[16,128]{1,0:T(8,128)S(1)} %bitcast.215, f32[1,512,16,128]{1,3,2,0:T(8,128)} %reshape.414, f32[512,2048]{0,1:T(8,128)} %copy.128), kind=kLoop, calls=%fused_computation.21 | loop fusion | flops 6291456 | bytes 14692352 | tf_op jit(solution)/shard_map/convert_element_type | solution.py:113
  189.0 7.6 %fusion.1 = f32[16,128,512]{2,1,0:T(8,128)} fusion(bf16[1,512,16,128]{1,3,2,0:T(8,128)(2,1)} %copy-done.2, f32[512,16]{0,1:T(8,128)S(1)} %copy.142, f32[16,128,128]{2,1,0:T(8,128)S(1)} %get-tuple-element.163, f32[16]{0:T(128)S(1)} %get-tuple-element.225), kind=kOutput, calls=%fused_computation.9 | convolution fusion | flops 1612972032 | bytes 7372864 | tf_op jit(solution)/shard_map/blhe,bhde->blhd/dot_general | solution.py:120
  196.6 7.1 %multiply_convert_fusion = bf16[16,512,512]{2,1,0:T(8,128)(2,1)} fusion(f32[16,512]{1,0:T(8,128)S(1)} %bitcast_add_fusion.6, pred[512,512]{1,0:T(8,128)(4,1)S(1)} %iota_compare_fusion, bf16[1,512,16,128]{1,3,2,0:T(8,128)(2,1)S(1)} %copy-done.3, bf16[512,2048]{1,0:T(8,128)(2,1)S(1)} %copy-done), kind=kOutput, calls=%fused_computation.4 | convolution fusion | flops 1094713344 | bytes 12877824 | tf_op jit(solution)/shard_map/blhe,bmhe->bhlm/dot_general | solution.py:114
  203.7 8.2 %fusion.3 = bf16[16,128,512]{2,1,0:T(8,128)(2,1)} fusion(f32[16,128,512]{2,1,0:T(8,128)S(1)} %copy-done.5, bf16[16,512,512]{2,1,0:T(8,128)(2,1)} %multiply_convert_fusion, bf16[512,2048]{1,0:T(8,128)(2,1)} %param.12), kind=kOutput, calls=%fused_computation.12 | convolution fusion | flops 1075838976 | bytes 16777216 | tf_op jit(solution)/shard_map/bhlm,bmhd->blhd/dot_general | solution.py:117
  216.0 53.0 %psum.23 = f32[2048]{0:T(1024)} all-reduce(f32[2048]{0:T(1024)S(1)} %bitcast.216), channel_id=1, replica_groups=mesh['ctx'=16,'tp'=2] {'ctx'}, use_global_device_ids=true, to_apply=%region_11.12 | all-reduce | flops 2048 | bytes 16384 | tf_op jit(solution)/shard_map/psum | solution.py:110
  269.0 62.5 %all-gather.8.cloned.1.call-done = f32[256,128,128]{2,1,0:T(8,128)} async-done(((f32[16,128,128]{2,1,0:T(8,128)}), f32[256,128,128]{2,1,0:T(8,128)}) %all-gather.8.cloned.1.call-update) | async-done | bytes 16777232 | tf_op jit(solution)/shard_map/all_gather | solution.py:18
  331.6 22.7 %while.17 = (s32[]{:T(128)}, f32[16,128,128]{2,1,0:T(8,128)S(1)}, s32[]{:T(128)}, f32[16,16]{1,0:T(8,128)S(1)}, f32[16,16,128,128]{3,2,1,0:T(8,128)}, /*index=5*/s32[]{:T(128)}, s32[]{:T(128)}, s32[]{:T(128)}, s32[]{:T(128)}) while((s32[]{:T(128)}, f32[16,128,128]{2,1,0:T(8,128)S(1)}, s32[]{:T(128)}, f32[16,16]{1,0:T(8,128)S(1)}, ...), condition=%wide.region_9.10_spmd, body=%wide.region_8.9_spmd.sunk | while | flops 524294 | bytes 3146075 | solution.py:27
  354.3 6.1 %fusion.15 = f32[16,128,512]{2,1,0:T(8,128)} fusion(f32[512,16]{0,1:T(8,128)S(1)} %copy.138, f32[16,128,128]{2,1,0:T(8,128)S(1)} %get-tuple-element.164, f32[16]{0:T(128)S(1)} %get-tuple-element.225, bf16[512,2048]{1,0:T(8,128)(2,1)S(1)} %copy-done), kind=kOutput, calls=%fused_computation.32 | convolution fusion | flops 1612972032 | bytes 7372864 | tf_op jit(solution)/shard_map/bmhe,bhde->bmhd/dot_general | solution.py:137
  360.4 6.0 %fusion.22 = f32[16,128,512]{2,1,0:T(8,128)S(1)} fusion(f32[512,16]{0,1:T(8,128)S(1)} %copy.138, f32[16,128,128]{2,1,0:T(8,128)S(1)} %get-tuple-element.164, f32[16]{0:T(128)S(1)} %get-tuple-element.225, bf16[512,2048]{1,0:T(8,128)(2,1)S(1)} %copy-done.6), kind=kOutput, calls=%fused_computation.41 | convolution fusion | flops 1612972032 | bytes 7372864 | tf_op jit(solution)/shard_map/bmhd,bhde->bmhe/dot_general | solution.py:141
  366.4 6.2 %add_convert_fusion = bf16[16,128,512]{2,1,0:T(8,128)(2,1)} fusion(f32[16,128,512]{2,1,0:T(8,128)S(1)} %fusion.22, bf16[16,512,512]{2,1,0:T(8,128)(2,1)} %multiply_convert_fusion.1, bf16[1,512,16,128]{1,3,2,0:T(8,128)(2,1)S(1)} %copy-done.4), kind=kOutput, calls=%fused_computation.31 | convolution fusion | flops 1075838976 | bytes 16777216 | tf_op jit(solution)/shard_map/bhlm,blhe->bmhe/dot_general | solution.py:140
  376.5 7.8 %fusion = bf16[16,128,512]{2,1,0:T(8,128)(2,1)} fusion(f32[16,128,512]{2,1,0:T(8,128)} %fusion.15, bf16[512,16,128]{0,2,1:T(8,128)(2,1)} %bitcast.200, bf16[16,512,512]{2,1,0:T(8,128)(2,1)} %multiply_convert_fusion), kind=kOutput, calls=%fused_computation.8 | convolution fusion | flops 1075838976 | bytes 16777216 | tf_op jit(solution)/shard_map/bhlm,blhd->bmhd/dot_general | solution.py:134
  (86 shorter events, 58.7 us)
Async XLA Ops:
  7.2 2.8 copy-start
  7.2 139.5 %all-gather.6.cloned.1.call-start = ((), (), s32[]{:S(2)}) async-start(), calls=%async_computation.1 | async-start | bytes 17825792 | tf_op jit(solution)/shard_map/all_gather | solution.py:18
  21.1 59.5 %all-to-all-start = ((bf16[256,2,2048]{0,2,1:T(8,128)(2,1)}), bf16[256,2,2048]{0,2,1:T(8,128)(2,1)}, u32[]{:S(2)}, u32[]{:S(2)}) async-start(bf16[256,2,2048]{0,2,1:T(8,128)(2,1)} %bitcast.203), calls=%async_computation | async-start | bytes 4194304 | tf_op jit(solution)/shard_map/all_to_all | solution.py:54
  25.9 305.6 %all-gather.8.cloned.1.call-start = ((), (), s32[]{:S(2)}) async-start(), calls=%async_computation.2 | async-start | bytes 17825792 | tf_op jit(solution)/shard_map/all_gather | solution.py:18
  30.3 9.6 %copy-start.7 = (bf16[512,2048]{1,0:T(8,128)(2,1)S(1)}, bf16[512,2048]{1,0:T(8,128)(2,1)}, u32[]{:S(2)}) copy-start(bf16[512,2048]{1,0:T(8,128)(2,1)} %param.15) | copy-start | bytes 6291460
  146.8 14.1 %copy-start.8 = (f32[2048]{0:T(1024)S(1)}, f32[2048]{0:T(1024)}, u32[]{:S(2)}) copy-start(f32[2048]{0:T(1024)} %param.16) | copy-start | bytes 24580
  175.3 6.6 %copy-start.1 = (bf16[512,2048]{0,1:T(8,128)(2,1)S(1)}, bf16[512,2048]{0,1:T(8,128)(2,1)}, u32[]{:S(2)}) copy-start(bf16[512,2048]{0,1:T(8,128)(2,1)} %copy.166) | copy-start | bytes 6291460
  180.6 1.3 copy-start.2
  189.0 7.6 %copy-start.3 = (bf16[1,512,16,128]{1,3,2,0:T(8,128)(2,1)S(1)}, bf16[1,512,16,128]{1,3,2,0:T(8,128)(2,1)}, u32[]{:S(2)}) copy-start(bf16[1,512,16,128]{1,3,2,0:T(8,128)(2,1)} %copy-done.2) | copy-start | bytes 6291460
  196.6 7.1 %copy-start.5 = (f32[16,128,512]{2,1,0:T(8,128)S(1)}, f32[16,128,512]{2,1,0:T(8,128)}, u32[]{:S(2)}) copy-start(f32[16,128,512]{2,1,0:T(8,128)} %fusion.1) | copy-start | bytes 12582916
  354.3 6.1 %copy-start.6 = (bf16[512,2048]{1,0:T(8,128)(2,1)S(1)}, bf16[512,2048]{1,0:T(8,128)(2,1)}, u32[]{:S(2)}) copy-start(bf16[512,2048]{1,0:T(8,128)(2,1)} %param.12) | copy-start | bytes 6291460
  360.4 6.0 %copy-start.4 = (bf16[1,512,16,128]{1,3,2,0:T(8,128)(2,1)S(1)}, bf16[1,512,16,128]{1,3,2,0:T(8,128)(2,1)}, u32[]{:S(2)}) copy-start(bf16[1,512,16,128]{1,3,2,0:T(8,128)(2,1)} %copy-done.2) | copy-start | bytes 6291460
Sparse Core Ops, SparseCore 0:
  17.1 129.5 all-gather.5
  185.2 146.2 all-gather.7
where the time goes:
time: 403 us; the launch traced here: 395 us
  waiting for transfers between devices  108 us (27%)
  matrix products  86.7 us (22%)
  blocking collectives  86.3 us (21%)
  local copies, waits for them, and re-layouts  51.3 us (13%)
  other arithmetic  42.6 us (11%)
  between operations  14.7 us (4%)
  starting transfers between devices  4.9 us (1%)
    all_gather x2, waiting for transfers between devices, carried_in(): gathered = jax.tree.map(lambda a: lax.all_gather(a, axis), part)  108 us
    psum x1, blocking collectives, local(): gain_grad = lax.psum(gain_part, 'ctx')  53 us
    all_gather x1, blocking collectives, carried_in(): gathered = jax.tree.map(lambda a: lax.all_gather(a, axis), part)  23.3 us
    add x15, other arithmetic, link_states(): later[0][:, None, None] * earlier[1] + later[1]  21.7 us
    unnamed x23, local copies, waits for them, and re-layouts  21.2 us
    convert_element_type x2, local copies, waits for them, and re-layouts, local(): grad_blocks = grad_rows.reshape(shape4).astype(jnp.float32)  18.7 us
    psum x2, blocking collectives, local(): squares, inner = lax.psum((squares, inner), 'tp')  10 us
    dot_general x1, matrix products, local(): jnp.einsum('blhd,bmhd->bhlm', query_blocks, key_blocks, preferred_element...  9.59 us
  transfers between devices with their start and end apart: 3, of which 2 were waited for; matrix products, arithmetic and copies ran while one was open for 22% of the time, Pallas kernels for 0%

commit v1 on v0

v1 whole, which is shorter than its diff:
```python
import functools

import jax
import jax.numpy as jnp
from jax import lax
from jax.experimental import pallas as pl
from jax.experimental.pallas import tpu as pltpu
from jax.sharding import PartitionSpec as P

HEAD = 128
BLOCK = 512
TEAM = 4
EPSILON = 1e-06
F32 = jnp.float32
BF16 = jnp.bfloat16
VMEM_LIMIT = 48 * 1024 * 1024


def dot(a, b, ca, cb, precision=None):
    return lax.dot_general(
        a, b, (((ca,), (cb,)), ((), ())), preferred_element_type=F32, precision=precision
    )


def head_cols(j):
    return slice(j * HEAD, (j + 1) * HEAD)


def call(body, grid, info, inputs, in_specs, out_shape, out_specs, scratch, flops, name):
    nbytes = sum(x.size * x.dtype.itemsize for x in inputs)
    nbytes += sum(x.size * x.dtype.itemsize for x in out_shape)
    return pl.pallas_call(
        body,
        grid_spec=pltpu.PrefetchScalarGridSpec(
            num_scalar_prefetch=1,
            grid=grid,
            in_specs=in_specs,
            out_specs=out_specs,
            scratch_shapes=scratch,
        ),
        out_shape=out_shape,
        compiler_params=pltpu.CompilerParams(vmem_limit_bytes=VMEM_LIMIT),
        cost_estimate=pl.CostEstimate(flops=flops, bytes_accessed=nbytes, transcendentals=0),
        name=name,
    )(info, *inputs)


def ahead(d, s):
    return lax.rem(s[0] + d, TEAM)


def behind(d, s):
    return lax.rem(s[0] + TEAM - d, TEAM)


def cols_spec(rows, width, quarter):
    return pl.BlockSpec((rows, width), lambda d, s: (0, quarter(d, s)))


def row_spec(quarter):
    return pl.BlockSpec((1, 8, BLOCK), lambda d, s: (quarter(d, s), 0, 0))


def col_spec(quarter):
    return pl.BlockSpec((1, BLOCK, HEAD), lambda d, s: (quarter(d, s), 0, 0))


def whole(shape):
    return pl.BlockSpec(shape, lambda d, s: (0,) * len(shape))


def local_states_body(hq, s, k, v, ld, l0, l1, l2, l3, row, col):
    d = pl.program_id(0)
    outs = (l0, l1, l2, l3)
    rows = ld.shape[0]
    offset = lax.rem(ahead(d, s) * hq, rows)
    x = ld[0:hq, :]
    for c in range(hq, rows, hq):
        x = jnp.where(offset == c, ld[c : c + hq, :], x)
    x = jnp.concatenate([x, jnp.zeros((8 - hq, BLOCK), F32)], axis=0)
    lane = lax.broadcasted_iota(jnp.int32, (8, BLOCK), 1)
    step = 1
    while step < BLOCK:
        x = x + jnp.where(lane >= step, pltpu.roll(x, step, 1), 0.0)
        step *= 2
    row[0] = x
    spread = jnp.concatenate([x, jnp.zeros((HEAD - 8, BLOCK), F32)], axis=0).T
    col[0] = spread
    shrink = jnp.exp(spread[BLOCK - 1 : BLOCK, :] - spread)
    for j in range(hq):
        kd = (k[:, head_cols(j)].astype(F32) * shrink[:, j : j + 1]).astype(BF16)
        part = dot(kd, v[:, head_cols(j)], 0, 0).astype(BF16)
        for i in range(TEAM):

            @pl.when(d == i)
            def _():
                outs[i][j] = part


def table_block(col, row, j, i, half):
    t = jnp.exp(col[0, i * half : (i + 1) * half, j : j + 1] - row[0, j : j + 1, 0 : (i + 1) * half])
    shape = (half, (i + 1) * half)
    at = lax.broadcasted_iota(jnp.int32, shape, 0) + i * half
    other = lax.broadcasted_iota(jnp.int32, shape, 1)
    return jnp.where(at >= other, t, 0.0)


def intra_body(hq, s, q, k, v, row, col, intra):
    half = BLOCK // 2
    for j in range(hq):
        c = head_cols(j)
        for i in range(2):
            mine = slice(i * half, (i + 1) * half)
            upto = slice(0, (i + 1) * half)
            scores = dot(q[mine, c], k[upto, c], 1, 1)
            probs = (scores * table_block(col, row, j, i, half)).astype(BF16)
            intra[mine, c] = dot(probs, v[upto, c], 1, 0)


def attention_body(hq, s, q, intra, gate, own, got, gain, col, s0, s1, s2, s3, att, sums, state, sq, inn):
    d = pl.program_id(0)
    for i, ref in enumerate((s0, s1, s2, s3)):

        @pl.when(d == i)
        def _():
            state[...] = ref[...]

    @pl.when(d == 0)
    def _():
        sq[...] = jnp.zeros_like(sq)
        inn[...] = jnp.zeros_like(inn)

    part = own.shape[0]
    for j in range(hq):
        c = head_cols(j)
        a = intra[:, c] + dot(q[:, c], state[j], 1, 0) * jnp.exp(col[0, :, j : j + 1])
        att[:, c] = a
        sq[...] += a * a
    for where, ref in ((s[1], own), (1 - s[1], got)):
        rows = pl.ds(pl.multiple_of(where * part, part), part)
        for j in range(hq):
            c = head_cols(j)
            opened = jax.nn.sigmoid(gate[rows, c].astype(F32))
            inn[rows, :] += att[rows, c] * (ref[:, c].astype(F32) * opened * gain[:, c])

    @pl.when(d == TEAM - 1)
    def _():
        ones = jnp.ones((8, HEAD), F32)
        a = dot(ones, sq[...], 1, 1, lax.Precision.HIGHEST)
        b = dot(ones, inn[...], 1, 1, lax.Precision.HIGHEST)
        sums[...] = jnp.where(lax.broadcasted_iota(jnp.int32, (8, BLOCK), 0) == 0, a, b)


def dattn_body(hq, channels, s, att, q, gate, own, got, gain, col, sum_a, sum_b, dattn, gate_grad, gain_part,
               b0, b1, b2, b3, scale):
    d = pl.program_id(0)
    outs = (b0, b1, b2, b3)

    @pl.when(d == 0)
    def _():
        total = sum_a[...] + sum_b[...]
        rs = lax.rsqrt(total[0:1, :] / channels + EPSILON)
        coef = total[1:2, :] * (rs * rs * rs) / channels
        both = jnp.concatenate([rs, coef, jnp.zeros((HEAD - 2, BLOCK), F32)], axis=0)
        scale[...] = both.T

    part = own.shape[0]
    gain_part[...] = jnp.zeros_like(gain_part)
    for where, ref in ((s[1], own), (1 - s[1], got)):
        rows = pl.ds(pl.multiple_of(where * part, part), part)
        rs = scale[rows, 0:1]
        coef = scale[rows, 1:2]
        for j in range(hq):
            c = head_cols(j)
            a = att[rows, c]
            opened = jax.nn.sigmoid(gate[rows, c].astype(F32))
            dnorm = ref[:, c].astype(F32) * opened
            scaled = a * rs
            dscaled = dnorm * gain[:, c]
            gain_part[:, c] += jnp.sum(dnorm * scaled, axis=0, keepdims=True)
            gate_grad[rows, c] = (dscaled * scaled * (1.0 - opened)).astype(BF16)
            dattn[rows, c] = (dscaled * rs - a * coef).astype(BF16)
    for j in range(hq):
        c = head_cols(j)
        qd = (q[:, c].astype(F32) * jnp.exp(col[0, :, j : j + 1])).astype(BF16)
        back = dot(qd, dattn[:, c], 0, 0).astype(BF16)
        for i in range(TEAM):

            @pl.when(d == i)
            def _():
                outs[i][j] = back


def local_grads_body(hq, s, q, k, v, dattn, row, col, s0, s1, s2, s3, query_grad, dk, dv, state):
    d = pl.program_id(0)
    for i, ref in enumerate((s0, s1, s2, s3)):

        @pl.when(d == i)
        def _():
            state[...] = ref[...]

    half = BLOCK // 2
    for j in range(hq):
        c = head_cols(j)
        for i in (1, 0):
            mine = slice(i * half, (i + 1) * half)
            upto = slice(0, (i + 1) * half)
            table = table_block(col, row, j, i, half)
            probs = (dot(q[mine, c], k[upto, c], 1, 1) * table).astype(BF16)
            dscores = (dot(dattn[mine, c], v[upto, c], 1, 1) * table).astype(BF16)
            inter = dot(dattn[mine, c], state[j], 1, 1) * jnp.exp(col[0, mine, j : j + 1])
            query_grad[mine, c] = (dot(dscores, k[upto, c], 1, 0) + inter).astype(BF16)
            dkey = dot(dscores, q[mine, c], 0, 0)
            dvalue = dot(probs, dattn[mine, c], 0, 0)
            if i == 1:
                dk[:, c] = dkey
                dv[:, c] = dvalue
            else:
                dk[upto, c] += dkey
                dv[upto, c] += dvalue


def final_body(hq, s, k, v, dk, dv, col, r0, r1, r2, r3, key_grad, value_grad, state):
    d = pl.program_id(0)
    for i, ref in enumerate((r0, r1, r2, r3)):

        @pl.when(d == i)
        def _():
            state[...] = ref[...]

    for j in range(hq):
        c = head_cols(j)
        shrink = jnp.exp(col[0, BLOCK - 1 : BLOCK, j : j + 1] - col[0, :, j : j + 1])
        key_grad[:, c] = (dk[:, c] + dot(v[:, c], state[j], 1, 1) * shrink).astype(BF16)
        value_grad[:, c] = (dv[:, c] + dot(k[:, c], state[j], 1, 0) * shrink).astype(BF16)


def group_total_body(hq, base, w, a0, a1, a2, a3, out):
    for j in range(hq):
        total = a0[j].astype(F32) * w[base, j]
        for d, ref in ((1, a1), (2, a2), (3, a3)):
            total = total + ref[j].astype(F32) * w[base + d, j]
        out[j] = total.astype(BF16)


def entering_body(hq, base, groups, w, *refs):
    parts = refs[:TEAM]
    far = refs[TEAM : TEAM + groups - 1]
    outs = refs[TEAM + groups - 1 :]
    b_far = base + TEAM
    b_in = b_far + groups - 1
    b_mix = b_in + TEAM
    for j in range(hq):
        incoming = jnp.zeros((HEAD, HEAD), F32)
        for k in range(groups - 1):
            incoming = incoming + far[k][j].astype(F32) * w[b_far + k, j]
        for d in range(TEAM):
            total = incoming * w[b_in + d, j]
            for i in range(TEAM):
                total = total + parts[i][j].astype(F32) * w[b_mix + d * TEAM + i, j]
            outs[d][j] = total.astype(BF16)


def scan_weights(edges, place, team, groups, hq):
    r = lax.rem(place, team)
    p = place // team
    low, high, valid = [], [], []

    def add(a, b, ok=True):
        low.append(a)
        high.append(b)
        valid.append(jnp.asarray(ok))

    first = team * p
    for reverse in (False, True):
        source = [lax.rem(r + team - d, team) for d in range(team)]
        target = [lax.rem(r + d, team) for d in range(team)]
        for d in range(team):
            if reverse:
                add(first, first + source[d])
            else:
                add(first + source[d] + 1, first + team)
        for k in range(1, groups):
            if reverse:
                add(first + team, first + team * k)
            else:
                add(first - team * (k - 1), first)
        for d in range(team):
            if reverse:
                add(first + target[d] + 1, first + team)
            else:
                add(first, first + target[d])
        for d in range(team):
            for i in range(team):
                if reverse:
                    add(first + target[d] + 1, first + source[i], source[i] > target[d])
                else:
                    add(first + source[i] + 1, first + target[d], source[i] < target[d])
    low = jnp.stack(low)[:, None]
    high = jnp.stack(high)[:, None]
    valid = jnp.stack(valid)[:, None]
    at = jnp.arange(team * groups, dtype=jnp.int32)[None, :]
    inside = ((at >= low) & (at < high)).astype(F32)
    mine = lax.dynamic_slice_in_dim(edges, r * hq, hq, 1)
    total = jnp.sum(inside[:, :, None] * mine[None], axis=1)
    return jnp.where(valid, jnp.exp(total), 0.0)


def scan_states(parts, weights, base, groups, hq, reverse):
    n = TEAM * groups
    shape = jax.ShapeDtypeStruct((hq, HEAD, HEAD), BF16)
    vmem = pl.BlockSpec(memory_space=pltpu.VMEM)
    smem = pl.BlockSpec(memory_space=pltpu.SMEM)

    def around(d):
        return [(i, i - i % TEAM + (i + d) % TEAM) for i in range(n)]

    terms = [parts[0]] + [lax.ppermute(parts[d], "ctx", around(d)) for d in range(1, TEAM)]
    total = pl.pallas_call(
        functools.partial(group_total_body, hq, base),
        in_specs=[smem] + [vmem] * TEAM,
        out_specs=vmem,
        out_shape=shape,
        name="group_total",
    )(weights, *terms)
    far = []
    for k in range(1, groups):
        move = -TEAM * k if reverse else TEAM * k
        pairs = [(i, i + move) for i in range(n) if 0 <= i + move < n]
        far.append(lax.ppermute(total, "ctx", pairs))
    entering = pl.pallas_call(
        functools.partial(entering_body, hq, base, groups),
        in_specs=[smem] + [vmem] * (TEAM + groups - 1),
        out_specs=[vmem] * TEAM,
        out_shape=[shape] * TEAM,
        name="entering",
    )(weights, *terms, *far)
    return [entering[0]] + [lax.ppermute(entering[d], "ctx", around(d)) for d in range(1, TEAM)]


def local(queries, keys, values, log_decay, gate, gain, grad_out):
    rows, width = queries.shape
    heads = width // HEAD
    hq = heads // TEAM
    tp = lax.axis_size("tp")
    groups = lax.axis_size("ctx") // TEAM
    channels = width * tp
    place = lax.axis_index("ctx")
    mine = lax.axis_index("tp")
    w = hq * HEAD
    part = grad_out.shape[0]
    bf = lambda *shape: jax.ShapeDtypeStruct(shape, BF16)
    f32 = lambda *shape: jax.ShapeDtypeStruct(shape, F32)

    if tp == 2:
        away = lax.dynamic_slice_in_dim(grad_out, (1 - mine) * width, width, 1)
        got = lax.ppermute(away, "tp", [(0, 1), (1, 0)])
        own, own_base = grad_out, mine * TEAM
        half = mine
        part = grad_out.shape[0]
    else:
        every = lax.all_to_all(grad_out, "tp", split_axis=1, concat_axis=0, tiled=True)
        own, got = every[: rows // 2], every[rows // 2 :]
        own_base = jnp.int32(0)
        half = jnp.int32(0)
        part = rows // 2
    info = jnp.stack([lax.rem(place, TEAM), half, own_base]).astype(jnp.int32)

    edges = lax.all_gather(jnp.sum(log_decay, axis=1), "ctx")
    weights = scan_weights(edges, place, TEAM, groups, hq)
    reverse_base = weights.shape[0] // 2

    state_shape = [bf(hq, HEAD, HEAD)] * TEAM
    state_specs = [whole((hq, HEAD, HEAD))] * TEAM
    state_scratch = pltpu.VMEM((hq, HEAD, HEAD), BF16)
    decay_rows = 8 if heads % 8 == 0 else heads
    per = decay_rows // hq
    small = 2 * heads * rows * HEAD * HEAD
    large = 2 * heads * rows * rows * HEAD

    *parts, row, col = call(
        functools.partial(local_states_body, hq),
        (TEAM,),
        info,
        [keys, values, log_decay],
        [
            cols_spec(rows, w, ahead),
            cols_spec(rows, w, ahead),
            pl.BlockSpec((decay_rows, rows), lambda d, s: (ahead(d, s) // per, 0)),
        ],
        state_shape + [f32(TEAM, 8, rows), f32(TEAM, rows, HEAD)],
        state_specs + [row_spec(ahead), col_spec(ahead)],
        [],
        small,
        "local_states",
    )
    entering = scan_states(parts, weights, 0, groups, hq, False)

    own_spec = pl.BlockSpec((part, w), lambda d, s: (0, s[2] + behind(d, s)))
    own_spec_ahead = pl.BlockSpec((part, w), lambda d, s: (0, s[2] + ahead(d, s)))
    b_cols = cols_spec(rows, w, behind)
    a_cols = cols_spec(rows, w, ahead)
    (intra,) = call(
        functools.partial(intra_body, hq),
        (TEAM,),
        info,
        [queries, keys, values, row, col],
        [b_cols, b_cols, b_cols, row_spec(behind), col_spec(behind)],
        [f32(rows, width)],
        [b_cols],
        [],
        2 * large,
        "intra",
    )
    gain_row = gain.reshape(1, width)
    att, sums = call(
        functools.partial(attention_body, hq),
        (TEAM,),
        info,
        [queries, intra, gate, own, got, gain_row, col, *entering],
        [b_cols, b_cols, b_cols, own_spec, cols_spec(part, w, behind), cols_spec(1, w, behind), col_spec(behind)]
        + state_specs,
        [f32(rows, width), f32(8, rows)],
        [b_cols, whole((8, rows))],
        [state_scratch, pltpu.VMEM((rows, HEAD), F32), pltpu.VMEM((rows, HEAD), F32)],
        small,
        "attention",
    )
    if tp == 2:
        others = lax.ppermute(sums, "tp", [(0, 1), (1, 0)])
    else:
        others = lax.psum(sums, "tp") - sums
    dattn, gate_grad, gain_part, *parts = call(
        functools.partial(dattn_body, hq, channels),
        (TEAM,),
        info,
        [att, queries, gate, own, got, gain_row, col, sums, others],
        [a_cols, a_cols, a_cols, own_spec_ahead, cols_spec(part, w, ahead), cols_spec(1, w, ahead), col_spec(ahead)]
        + [whole((8, rows))] * 2,
        [bf(rows, width), bf(rows, width), f32(1, width)] + state_shape,
        [a_cols, a_cols, cols_spec(1, w, ahead)] + state_specs,
        [pltpu.VMEM((rows, HEAD), F32)],
        small,
        "dattn",
    )
    leaving = scan_states(parts, weights, reverse_base, groups, hq, True)
    gain_grad = lax.psum(gain_part.reshape(width), "ctx")
    query_grad, dk, dv = call(
        functools.partial(local_grads_body, hq),
        (TEAM,),
        info,
        [queries, keys, values, dattn, row, col, *entering],
        [b_cols] * 4 + [row_spec(behind), col_spec(behind)] + state_specs,
        [bf(rows, width), f32(rows, width), f32(rows, width)],
        [b_cols] * 3,
        [state_scratch],
        5 * large,
        "local_grads",
    )
    key_grad, value_grad = call(
        functools.partial(final_body, hq),
        (TEAM,),
        info,
        [keys, values, dk, dv, col, *leaving],
        [b_cols] * 4 + [col_spec(behind)] + state_specs,
        [bf(rows, width), bf(rows, width)],
        [b_cols] * 2,
        [state_scratch],
        2 * small,
        "final",
    )
    return query_grad, key_grad, value_grad, gate_grad, gain_grad


def solution(mesh):
    return jax.shard_map(
        local,
        mesh=mesh,
        in_specs=(
            P("ctx", "tp"),
            P("ctx", "tp"),
            P("ctx", "tp"),
            P("tp", "ctx"),
            P("ctx", "tp"),
            P("tp"),
            P(("ctx", "tp"), None),
        ),
        out_specs=(P("ctx", "tp"), P("ctx", "tp"), P("ctx", "tp"), P("ctx", "tp"), P("tp")),
        check_vma=False,
    )
```

time: 403 us -> 204 us (0.51); the launches traced: 395 us -> 204 us
  matrix products: 86.7 us -> 0 us
  waiting for transfers between devices: 108 us -> 23.9 us
  Pallas kernels: 0 us -> 72.7 us
  other arithmetic: 42.6 us -> 0.98 us
  local copies, waits for them, and re-layouts: 51.3 us -> 18.5 us
  blocking collectives: 86.3 us -> 63.6 us
  starting transfers between devices: 4.9 us -> 22.4 us
  between operations: 14.7 us -> 1.5 us
    all_gather x2 -> x0, waiting for transfers between devices: 108 us -> none  [carried_in(): gathered = jax.tree.map(lambda a: lax.all_gather(a, axis), part)]
    dot_general x12 -> x0, matrix products: 86.7 us -> none  [the longest x1 9.59 us: local(): jnp.einsum('blhd,bmhd->bhlm', query_blocks, key_blocks, preferred_element...]
    pallas_call x0 -> x10, Pallas kernels: none -> 72.7 us  [the longest x6 63.6 us: call(): pl.pallas_call(body, grid_spec=pltpu.PrefetchScalarGridSpec(num_scalar_pr...]
    unnamed x0 -> x1, blocking collectives: none -> 33 us
    psum x3 -> x1, blocking collectives: 63 us -> 30.6 us  [local(): gain_grad = lax.psum(gain_part.reshape(width), 'ctx')]
    ppermute x0 -> x20, waiting for transfers between devices: none -> 23.9 us  [the longest x6 16 us: scan_states(): far.append(lax.ppermute(total, 'ctx', pairs))]
    all_gather x1 -> x0, blocking collectives: 23.3 us -> none  [carried_in(): gathered = jax.tree.map(lambda a: lax.all_gather(a, axis), part)]
    ppermute x0 -> x20, starting transfers between devices: none -> 22.4 us  [the longest x6 7.74 us: scan_states(): far.append(lax.ppermute(total, 'ctx', pairs))]
  transfers between devices with their start and end apart: 3 -> 20, of which waited for: 2 -> 9; matrix products, arithmetic and copies ran while one was open for 22% -> 1% of each run, Pallas kernels for 0% -> 20%
where the time goes in v1:
time: 204 us
  Pallas kernels  72.7 us (36%)
  blocking collectives  63.6 us (31%)
  waiting for transfers between devices  23.9 us (12%)
  starting transfers between devices  22.4 us (11%)
  local copies, waits for them, and re-layouts  18.5 us (9%)
    pallas_call x6, Pallas kernels, call(): pl.pallas_call(body, grid_spec=pltpu.PrefetchScalarGridSpec(num_scalar_pr...  63.6 us
    unnamed x1, blocking collectives  33 us
    psum x1, blocking collectives, local(): gain_grad = lax.psum(gain_part.reshape(width), 'ctx')  30.6 us
    ppermute x6, waiting for transfers between devices, scan_states(): far.append(lax.ppermute(total, 'ctx', pairs))  16 us
    unnamed x53, local copies, waits for them, and re-layouts  15.3 us
    ppermute x6, starting transfers between devices, scan_states(): far.append(lax.ppermute(total, 'ctx', pairs))  7.74 us
    ppermute x6, starting transfers between devices, scan_states(): lax.ppermute(parts[d], 'ctx', around(d))  5.89 us
    ppermute x6, starting transfers between devices, scan_states(): lax.ppermute(entering[d], 'ctx', around(d))  5.32 us
  transfers between devices with their start and end apart: 20, of which 9 were waited for; matrix products, arithmetic and copies ran while one was open for 1% of the time, Pallas kernels for 20%

profile of v1, /device:TPU:0, one launch (start us, length us, event | category | flops | bytes accessed | tf_op | source)
XLA Modules:
  0.0 203.5 jit_solution(3735748215473401440)
XLA Ops:
  0.7 2.5 %constant_dynamic-slice_fusion.1 = bf16[256,2048]{1,0:T(8,128)(2,1)} fusion(bf16[256,4096]{1,0:T(8,128)(2,1)} %own.3, s32[]{:T(128)S(6)} %select_n.15), kind=kLoop, calls=%fused_computation.8 | loop fusion | bytes 2097156 | tf_op jit(solution)/shard_map/dynamic_slice | solution.py:356
  3.1 2.9 %collective-permute-start = (bf16[256,2048]{1,0:T(8,128)(2,1)}, bf16[256,2048]{1,0:T(8,128)(2,1)}, u32[]{:S(2)}, u32[]{:S(2)}) collective-permute-start(bf16[256,2048]{1,0:T(8,128)(2,1)} %constant_dynamic-slice_fusion.1), channel_id=1, source_target_pairs={{0,1},{1,0},{2,3},{3,2},{4,5},{5,4},{6,7},{7,6},{8,9},{9,8},{10,11... | collective-permute-start | bytes 3145736 | tf_op jit(solution)/shard_map/ppermute | solution.py:357
  6.1 1.6 copy-done.1
  7.7 10.0 %local_states.1 = (bf16[4,128,128]{2,1,0:T(8,128)(2,1)S(1)}, bf16[4,128,128]{2,1,0:T(8,128)(2,1)}, bf16[4,128,128]{2,1,0:T(8,128)(2,1)S(1)}, bf16[4,128,128]{2,1...) custom-call(s32[3]{0:T(128)S(1)} %pad_add_fusion.s, bf16[512,2048]{1,0:T(8,128)(2,1)S(1)} %copy-done, ...), custom_call_target="tpu_custom_call" | custom-call | flops 268435456 | bytes 5865472 | tf_op jit(solution)/shard_map/local_states/pallas_call | solution.py:32
  19.0 1.5 collective-permute-start.2
  23.7 33.0 %all-reduce.1 = f32[16,16]{1,0:T(8,128)S(1)} all-reduce(f32[16,16]{1,0:T(8,128)S(1)} %reshape.64), channel_id=2, replica_groups=mesh['ctx'=16,'tp'=2] {'ctx'}, use_global_device_ids=true, to_apply=%add | all-reduce | flops 256 | bytes 2048
  58.2 2.0 group_total.2
  68.3 2.5 %entering.2 = (bf16[4,128,128]{2,1,0:T(8,128)(2,1)}, bf16[4,128,128]{2,1,0:T(8,128)(2,1)}, bf16[4,128,128]{2,1,0:T(8,128)(2,1)}, bf16[4,128,128]{2,1,0:T(8,128)(2,1)}) custom-call(f32[54,4]{1,0:T(8,128)} %broadcast_select_fusion.w, bf16[4,128,128]{2,1,0:T(8,128)(2,1)} %copy-done.6, bf16[4,128,128]{2,1,0:T(8,128)(2,1)} %collective-permute-done.1.a1.refs_1_, ...), custom_call_target="tpu_custom_call" | custom-call | tf_op jit(solution)/shard_map/entering/pallas_call | solution.py:331
  70.8 2.1 %collective-permute-start.8 = (bf16[4,128,128]{2,1,0:T(8,128)(2,1)}, bf16[4,128,128]{2,1,0:T(8,128)(2,1)S(1)}, u32[]{:S(2)}, u32[]{:S(2)}) collective-permute-start(bf16[4,128,128]{2,1,0:T(8,128)(2,1)} %get-tuple-element.41), channel_id=1, source_target_pairs={{0,4},{2,6},{4,0},{6,2},{8,12},{10,14},{12,8},{14,10},{16,20},{18,... | collective-permute-start | bytes 393224 | tf_op jit(solution)/shard_map/ppermute | solution.py:338
  72.9 1.6 copy-done.3
  75.3 8.8 %intra.1 = f32[512,2048]{1,0:T(8,128)} custom-call(s32[3]{0:T(128)S(1)} %pad_add_fusion.s, bf16[512,2048]{1,0:T(8,128)(2,1)S(1)} %copy-done.3, bf16[512,2048]{1,0:T(8,128)(2,1)S(1)} %copy-done, bf16[512,2048]{1,0:T(8,128)(2,1)} %v.7, f32[4,8,512]{2,1,0:T(8,128)S(1)} %copy-done.14, f32[4,512,128]{2,1,0:T(8,128)S(1)} %get-tuple-element.34.col), custom_call_target="tpu_custom_call" | custom-call | flops 2147483648 | bytes 11599872 | tf_op jit(solution)/shard_map/intra/pallas_call | solution.py:32
  84.2 8.6 %attention.1 = (f32[512,2048]{1,0:T(8,128)}, f32[8,512]{1,0:T(8,128)S(1)}) custom-call(s32[3]{0:T(128)S(1)} %pad_add_fusion.s, bf16[512,2048]{1,0:T(8,128)(2,1)S(1)} %copy-done.4, f32[512,2048]{1,0:T(8,128)} %intra.1, bf16[512,2048]{1,0:T(8,128)(2,1)} %gate.3, bf16[256,4096]{1,0:T(8,128)(2,1)} %own.3, bf16[256,2048]{1,0:T(8,128)(2,1)} %collective-permute-done.got, ...), custom_call_target="tpu_custom_call" | custom-call | flops 268435456 | bytes 17326080 | tf_op jit(solution)/shard_map/attention/pallas_call | solution.py:32
  93.4 3.2 %collective-permute-done.10.sum_b = f32[8,512]{1,0:T(8,128)S(1)} collective-permute-done((f32[8,512]{1,0:T(8,128)S(1)}, f32[8,512]{1,0:T(8,128)S(1)}, u32[]{:S(2)}, u32[]{:S(2)}) %collective-permute-start.10) | collective-permute-done | bytes 16416 | tf_op jit(solution)/shard_map/ppermute | solution.py:430
  96.6 11.8 %dattn.1 = (bf16[512,2048]{1,0:T(8,128)(2,1)S(1)}, bf16[512,2048]{1,0:T(8,128)(2,1)}, f32[1,2048]{1,0:T(1,128)S(1)}, bf16[4,128,128]{2,1,0:T(8,128)(2,1)S(1)}, b...) custom-call(s32[3]{0:T(128)S(1)} %pad_add_fusion.s, ...), custom_call_target="tpu_custom_call" | custom-call | flops 268435456 | bytes 17350656 | tf_op jit(solution)/shard_map/dattn/pallas_call | solution.py:32
  113.3 2.3 %collective-permute-done.11.a1.refs_1_ = bf16[4,128,128]{2,1,0:T(8,128)(2,1)S(1)} collective-permute-done((bf16[4,128,128]{2,1,0:T(8,128)(2,1)S(1)}, bf16[4,128,128]{2,1,0:T(8,128)(2,1)S(1)}, u32[]{:S(2)}, u32[]{:S(2)}) %collective-permute-start.11) | collective-permute-done | bytes 131104 | tf_op jit(solution)/shard_map/ppermute | solution.py:318
  118.6 2.0 group_total.3
  124.6 6.7 %collective-permute-done.16.refs_6_ = bf16[4,128,128]{2,1,0:T(8,128)(2,1)} collective-permute-done((bf16[4,128,128]{2,1,0:T(8,128)(2,1)}, bf16[4,128,128]{2,1,0:T(8,128)(2,1)}, u32[]{:S(2)}, u32[]{:S(2)}) %collective-permute-start.16) | collective-permute-done | bytes 131104 | tf_op jit(solution)/shard_map/ppermute | solution.py:330
  131.3 5.9 %collective-permute-done.15.refs_5_ = bf16[4,128,128]{2,1,0:T(8,128)(2,1)} collective-permute-done((bf16[4,128,128]{2,1,0:T(8,128)(2,1)}, bf16[4,128,128]{2,1,0:T(8,128)(2,1)}, u32[]{:S(2)}, u32[]{:S(2)}) %collective-permute-start.15) | collective-permute-done | bytes 131104 | tf_op jit(solution)/shard_map/ppermute | solution.py:330
  137.1 2.5 %entering.3 = (bf16[4,128,128]{2,1,0:T(8,128)(2,1)}, bf16[4,128,128]{2,1,0:T(8,128)(2,1)}, bf16[4,128,128]{2,1,0:T(8,128)(2,1)}, bf16[4,128,128]{2,1,0:T(8,128)(2,1)}) custom-call(f32[54,4]{1,0:T(8,128)} %broadcast_select_fusion.w, bf16[4,128,128]{2,1,0:T(8,128)(2,1)} %copy-done.7, bf16[4,128,128]{2,1,0:T(8,128)(2,1)} %copy-done.18, ...), custom_call_target="tpu_custom_call" | custom-call | tf_op jit(solution)/shard_map/entering/pallas_call | solution.py:331
  142.8 1.6 copy-done.5
  146.2 16.9 %local_grads.1 = (bf16[512,2048]{1,0:T(8,128)(2,1)}, f32[512,2048]{1,0:T(8,128)}, f32[512,2048]{1,0:T(8,128)}) custom-call(s32[3]{0:T(128)S(1)} %pad_add_fusion.s, bf16[512,2048]{1,0:T(8,128)(2,1)S(1)} %copy-done.5, bf16[512,2048]{1,0:T(8,128)(2,1)S(1)} %copy-done, bf16[512,2048]{1,0:T(8,128)(2,1)} %v.7, bf16[512,2048]{1,0:T(8,128)(2,1)} %copy-done.17, ...), custom_call_target="tpu_custom_call" | custom-call | flops 5368709120 | bytes 20512768 | tf_op jit(solution)/shard_map/local_grads/pallas_call | solution.py:32
  163.1 30.6 %psum.7 = f32[2048]{0:T(1024)} all-reduce(f32[2048]{0:T(1024)S(1)} %bitcast.50), channel_id=1, replica_groups=mesh['ctx'=16,'tp'=2] {'ctx'}, use_global_device_ids=true, to_apply=%region_2.3 | all-reduce | flops 2048 | bytes 16384 | tf_op jit(solution)/shard_map/psum | solution.py:447
  193.7 1.6 copy-done.2
  196.2 7.3 %final.1 = (bf16[512,2048]{1,0:T(8,128)(2,1)}, bf16[512,2048]{1,0:T(8,128)(2,1)}) custom-call(s32[3]{0:T(128)S(1)} %pad_add_fusion.s, bf16[512,2048]{1,0:T(8,128)(2,1)S(1)} %copy-done, bf16[512,2048]{1,0:T(8,128)(2,1)S(1)} %copy-done.2, f32[512,2048]{1,0:T(8,128)} %get-tuple-element.47.dk, f32[512,2048]{1,0:T(8,128)} %get-tuple-element.48.dv, ...), custom_call_target="tpu_custom_call" | custom-call | flops 536870912 | bytes 18350080 | tf_op jit(solution)/shard_map/final/pallas_call | solution.py:32
  (97 shorter events, 32.3 us)
Async XLA Ops:
  3.1 81.1 %collective-permute-start = (bf16[256,2048]{1,0:T(8,128)(2,1)}, bf16[256,2048]{1,0:T(8,128)(2,1)}, u32[]{:S(2)}, u32[]{:S(2)}) collective-permute-start(bf16[256,2048]{1,0:T(8,128)(2,1)} %constant_dynamic-slice_fusion.1), channel_id=1, source_target_pairs={{0,1},{1,0},{2,3},{3,2},{4,5},{5,4},{6,7},{7,6},{8,9},{9,8},{10,11... | collective-permute-start | bytes 3145736 | tf_op jit(solution)/shard_map/ppermute | solution.py:357
  7.7 14.4 %copy-start.24 = (u32[32]{0:T(128)S(1)}, u32[32]{0:T(128)}, u32[]{:S(2)}) copy-start(u32[32]{0:T(128)} %constant.87) | copy-start | bytes 388
  19.0 39.2 %collective-permute-start.1 = (bf16[4,128,128]{2,1,0:T(8,128)(2,1)}, bf16[4,128,128]{2,1,0:T(8,128)(2,1)}, u32[]{:S(2)}, u32[]{:S(2)}) collective-permute-start(bf16[4,128,128]{2,1,0:T(8,128)(2,1)} %get-tuple-element.36), channel_id=1, source_target_pairs={{0,2},{2,4},{4,6},{6,0},{8,10},{10,12},{12,14},{14,8},{16,18},{18,... | collective-permute-start | bytes 393224 | tf_op jit(solution)/shard_map/ppermute | solution.py:318
  19.0 39.2 %collective-permute-start.2 = (bf16[4,128,128]{2,1,0:T(8,128)(2,1)S(1)}, bf16[4,128,128]{2,1,0:T(8,128)(2,1)}, u32[]{:S(2)}, u32[]{:S(2)}) collective-permute-start(bf16[4,128,128]{2,1,0:T(8,128)(2,1)S(1)} %get-tuple-element.37), channel_id=1, source_target_pairs={{0,4},{2,6},{4,0},{6,2},{8,12},{10,14},{12,8},{14,10},{16,20},{18,... | collective-permute-start | bytes 393224 | tf_op jit(solution)/shard_map/ppermute | solution.py:318
  20.6 37.7 %collective-permute-start.3 = (bf16[4,128,128]{2,1,0:T(8,128)(2,1)S(1)}, bf16[4,128,128]{2,1,0:T(8,128)(2,1)}, u32[]{:S(2)}, u32[]{:S(2)}) collective-permute-start(bf16[4,128,128]{2,1,0:T(8,128)(2,1)S(1)} %get-tuple-element.38), channel_id=1, source_target_pairs={{0,6},{2,0},{4,2},{6,4},{8,14},{10,8},{12,10},{14,12},{16,22},{18,... | collective-permute-start | bytes 393224 | tf_op jit(solution)/shard_map/ppermute | solution.py:318
  60.3 4.5 %collective-permute-start.6 = (bf16[4,128,128]{2,1,0:T(8,128)(2,1)}, bf16[4,128,128]{2,1,0:T(8,128)(2,1)S(1)}, u32[]{:S(2)}, u32[]{:S(2)}) collective-permute-start(bf16[4,128,128]{2,1,0:T(8,128)(2,1)} %group_total.2), channel_id=1, source_target_pairs={{0,24},{2,26},{4,28},{6,30},{1,25},{3,27},{5,29},{7,31}} | collective-permute-start | bytes 393224 | tf_op jit(solution)/shard_map/ppermute | solution.py:330
  61.6 4.6 %collective-permute-start.5 = (bf16[4,128,128]{2,1,0:T(8,128)(2,1)}, bf16[4,128,128]{2,1,0:T(8,128)(2,1)S(1)}, u32[]{:S(2)}, u32[]{:S(2)}) collective-permute-start(bf16[4,128,128]{2,1,0:T(8,128)(2,1)} %group_total.2), channel_id=1, source_target_pairs={{0,16},{2,18},{4,20},{6,22},{8,24},{10,26},{12,28},{14,30},{1,17},... | collective-permute-start | bytes 393224 | tf_op jit(solution)/shard_map/ppermute | solution.py:330
  62.9 4.7 %collective-permute-start.4 = (bf16[4,128,128]{2,1,0:T(8,128)(2,1)}, bf16[4,128,128]{2,1,0:T(8,128)(2,1)S(1)}, u32[]{:S(2)}, u32[]{:S(2)}) collective-permute-start(bf16[4,128,128]{2,1,0:T(8,128)(2,1)} %group_total.2), channel_id=1, source_target_pairs={{0,8},{2,10},{4,12},{6,14},{8,16},{10,18},{12,20},{14,22},{16,24},... | collective-permute-start | bytes 393224 | tf_op jit(solution)/shard_map/ppermute | solution.py:330
  70.8 13.4 %collective-permute-start.7 = (bf16[4,128,128]{2,1,0:T(8,128)(2,1)}, bf16[4,128,128]{2,1,0:T(8,128)(2,1)S(1)}, u32[]{:S(2)}, u32[]{:S(2)}) collective-permute-start(bf16[4,128,128]{2,1,0:T(8,128)(2,1)} %get-tuple-element.40), channel_id=1, source_target_pairs={{0,2},{2,4},{4,6},{6,0},{8,10},{10,12},{12,14},{14,8},{16,18},{18,... | collective-permute-start | bytes 393224 | tf_op jit(solution)/shard_map/ppermute | solution.py:338
  70.8 13.4 %collective-permute-start.8 = (bf16[4,128,128]{2,1,0:T(8,128)(2,1)}, bf16[4,128,128]{2,1,0:T(8,128)(2,1)S(1)}, u32[]{:S(2)}, u32[]{:S(2)}) collective-permute-start(bf16[4,128,128]{2,1,0:T(8,128)(2,1)} %get-tuple-element.41), channel_id=1, source_target_pairs={{0,4},{2,6},{4,0},{6,2},{8,12},{10,14},{12,8},{14,10},{16,20},{18,... | collective-permute-start | bytes 393224 | tf_op jit(solution)/shard_map/ppermute | solution.py:338
  72.9 11.3 %collective-permute-start.9 = (bf16[4,128,128]{2,1,0:T(8,128)(2,1)}, bf16[4,128,128]{2,1,0:T(8,128)(2,1)S(1)}, u32[]{:S(2)}, u32[]{:S(2)}) collective-permute-start(bf16[4,128,128]{2,1,0:T(8,128)(2,1)} %get-tuple-element.42), channel_id=1, source_target_pairs={{0,6},{2,0},{4,2},{6,4},{8,14},{10,8},{12,10},{14,12},{16,22},{18,... | collective-permute-start | bytes 393224 | tf_op jit(solution)/shard_map/ppermute | solution.py:338
  75.3 8.9 %copy-start.4 = (bf16[512,2048]{1,0:T(8,128)(2,1)S(1)}, bf16[512,2048]{1,0:T(8,128)(2,1)}, u32[]{:S(2)}) copy-start(bf16[512,2048]{1,0:T(8,128)(2,1)} %q.7) | copy-start | bytes 6291460
  75.3 8.9 %copy-start.8 = (bf16[4,128,128]{2,1,0:T(8,128)(2,1)S(1)}, bf16[4,128,128]{2,1,0:T(8,128)(2,1)}, u32[]{:S(2)}) copy-start(bf16[4,128,128]{2,1,0:T(8,128)(2,1)} %get-tuple-element.39.s0) | copy-start | bytes 393220
  75.3 8.9 %copy-start.16 = (f32[2048]{0:T(1024)S(1)}, f32[2048]{0:T(1024)}, u32[]{:S(2)}) copy-start(f32[2048]{0:T(1024)} %param.12) | copy-start | bytes 24580
  92.9 3.7 %collective-permute-start.10 = (f32[8,512]{1,0:T(8,128)S(1)}, f32[8,512]{1,0:T(8,128)S(1)}, u32[]{:S(2)}, u32[]{:S(2)}) collective-permute-start(f32[8,512]{1,0:T(8,128)S(1)} %get-tuple-element.44.sum_a), channel_id=1, source_target_pairs={{0,1},{1,0},{2,3},{3,2},{4,5},{5,4},{6,7},{7,6},{8,9},{9,8},{10,11... | collective-permute-start | bytes 49160 | tf_op jit(solution)/shard_map/ppermute | solution.py:430
  110.4 5.2 %collective-permute-start.11 = (bf16[4,128,128]{2,1,0:T(8,128)(2,1)S(1)}, bf16[4,128,128]{2,1,0:T(8,128)(2,1)S(1)}, u32[]{:S(2)}, u32[]{:S(2)}) collective-permute-start(bf16[4,128,128]{2,1,0:T(8,128)(2,1)S(1)} %get-tuple-element.50), channel_id=1, source_target_pairs={{0,2},{2,4},{4,6},{6,0},{8,10},{10,12},{12,14},{14,8},{16,18},{18,... | collective-permute-start | bytes 393224 | tf_op jit(solution)/shard_map/ppermute | solution.py:318
  110.4 6.3 %collective-permute-start.12 = (bf16[4,128,128]{2,1,0:T(8,128)(2,1)S(1)}, bf16[4,128,128]{2,1,0:T(8,128)(2,1)S(1)}, u32[]{:S(2)}, u32[]{:S(2)}) collective-permute-start(bf16[4,128,128]{2,1,0:T(8,128)(2,1)S(1)} %get-tuple-element.51), channel_id=1, source_target_pairs={{0,4},{2,6},{4,0},{6,2},{8,12},{10,14},{12,8},{14,10},{16,20},{18,... | collective-permute-start | bytes 393224 | tf_op jit(solution)/shard_map/ppermute | solution.py:318
  111.9 6.1 %collective-permute-start.13 = (bf16[4,128,128]{2,1,0:T(8,128)(2,1)S(1)}, bf16[4,128,128]{2,1,0:T(8,128)(2,1)S(1)}, u32[]{:S(2)}, u32[]{:S(2)}) collective-permute-start(bf16[4,128,128]{2,1,0:T(8,128)(2,1)S(1)} %get-tuple-element.52), channel_id=1, source_target_pairs={{0,6},{2,0},{4,2},{6,4},{8,14},{10,8},{12,10},{14,12},{16,22},{18,... | collective-permute-start | bytes 393224 | tf_op jit(solution)/shard_map/ppermute | solution.py:318
  120.7 10.6 %collective-permute-start.16 = (bf16[4,128,128]{2,1,0:T(8,128)(2,1)}, bf16[4,128,128]{2,1,0:T(8,128)(2,1)}, u32[]{:S(2)}, u32[]{:S(2)}) collective-permute-start(bf16[4,128,128]{2,1,0:T(8,128)(2,1)} %group_total.3), channel_id=1, source_target_pairs={{24,0},{26,2},{28,4},{30,6},{25,1},{27,3},{29,5},{31,7}} | collective-permute-start | bytes 393224 | tf_op jit(solution)/shard_map/ppermute | solution.py:330
  122.0 15.2 %collective-permute-start.15 = (bf16[4,128,128]{2,1,0:T(8,128)(2,1)}, bf16[4,128,128]{2,1,0:T(8,128)(2,1)}, u32[]{:S(2)}, u32[]{:S(2)}) collective-permute-start(bf16[4,128,128]{2,1,0:T(8,128)(2,1)} %group_total.3), channel_id=1, source_target_pairs={{16,0},{18,2},{20,4},{22,6},{24,8},{26,10},{28,12},{30,14},{17,1},... | collective-permute-start | bytes 393224 | tf_op jit(solution)/shard_map/ppermute | solution.py:330
  123.3 13.9 %collective-permute-start.14 = (bf16[4,128,128]{2,1,0:T(8,128)(2,1)}, bf16[4,128,128]{2,1,0:T(8,128)(2,1)}, u32[]{:S(2)}, u32[]{:S(2)}) collective-permute-start(bf16[4,128,128]{2,1,0:T(8,128)(2,1)} %group_total.3), channel_id=1, source_target_pairs={{8,0},{10,2},{12,4},{14,6},{16,8},{18,10},{20,12},{22,14},{24,16},... | collective-permute-start | bytes 393224 | tf_op jit(solution)/shard_map/ppermute | solution.py:330
  139.7 54.0 %collective-permute-start.17 = (bf16[4,128,128]{2,1,0:T(8,128)(2,1)}, bf16[4,128,128]{2,1,0:T(8,128)(2,1)}, u32[]{:S(2)}, u32[]{:S(2)}) collective-permute-start(bf16[4,128,128]{2,1,0:T(8,128)(2,1)} %get-tuple-element.54), channel_id=1, source_target_pairs={{0,2},{2,4},{4,6},{6,0},{8,10},{10,12},{12,14},{14,8},{16,18},{18,... | collective-permute-start | bytes 393224 | tf_op jit(solution)/shard_map/ppermute | solution.py:338
  140.6 53.1 %collective-permute-start.18 = (bf16[4,128,128]{2,1,0:T(8,128)(2,1)}, bf16[4,128,128]{2,1,0:T(8,128)(2,1)}, u32[]{:S(2)}, u32[]{:S(2)}) collective-permute-start(bf16[4,128,128]{2,1,0:T(8,128)(2,1)} %get-tuple-element.55), channel_id=1, source_target_pairs={{0,4},{2,6},{4,0},{6,2},{8,12},{10,14},{12,8},{14,10},{16,20},{18,... | collective-permute-start | bytes 393224 | tf_op jit(solution)/shard_map/ppermute | solution.py:338
  141.5 52.2 %collective-permute-start.19 = (bf16[4,128,128]{2,1,0:T(8,128)(2,1)}, bf16[4,128,128]{2,1,0:T(8,128)(2,1)}, u32[]{:S(2)}, u32[]{:S(2)}) collective-permute-start(bf16[4,128,128]{2,1,0:T(8,128)(2,1)} %get-tuple-element.56), channel_id=1, source_target_pairs={{0,6},{2,0},{4,2},{6,4},{8,14},{10,8},{12,10},{14,12},{16,22},{18,... | collective-permute-start | bytes 393224 | tf_op jit(solution)/shard_map/ppermute | solution.py:338
  (21 other events, 41.8 us)

commit v2 on v0

v2 whole, which is shorter than its diff:
```python
import functools

import jax
import jax.numpy as jnp
from jax import lax
from jax.experimental import pallas as pl
from jax.experimental.pallas import tpu as pltpu
from jax.sharding import PartitionSpec as P

HEAD = 128
BLOCK = 512
HALF = BLOCK // 2
EXTRA = 16
EPSILON = 1e-06
F32 = jnp.float32
BF16 = jnp.bfloat16
VMEM_LIMIT = 60 * 1024 * 1024


def nt(a, b, precision=None):
    return lax.dot_general(a, b, (((1,), (1,)), ((), ())), preferred_element_type=F32, precision=precision)


def nn(a, b):
    return lax.dot_general(a, b, (((1,), (0,)), ((), ())), preferred_element_type=F32)


def head_cols(j):
    return slice(j * HEAD, (j + 1) * HEAD)


def piece(i):
    return slice(i * HALF, (i + 1) * HALF)


def split_terms(x, count):
    terms = []
    for _ in range(count):
        term = x.astype(BF16)
        terms.append(term)
        x = x - term.astype(F32)
    return terms


def call(body, grid, info, inputs, in_specs, out_shape, out_specs, scratch, flops, name):
    nbytes = sum(x.size * x.dtype.itemsize for x in inputs)
    nbytes += sum(x.size * x.dtype.itemsize for x in out_shape)
    return pl.pallas_call(
        body,
        grid_spec=pltpu.PrefetchScalarGridSpec(
            num_scalar_prefetch=1,
            grid=grid,
            in_specs=in_specs,
            out_specs=out_specs,
            scratch_shapes=scratch,
        ),
        out_shape=out_shape,
        compiler_params=pltpu.CompilerParams(vmem_limit_bytes=VMEM_LIMIT),
        cost_estimate=pl.CostEstimate(flops=flops, bytes_accessed=nbytes, transcendentals=0),
        name=name,
    )(info, *inputs)


def cols_spec(rows, width):
    return pl.BlockSpec((rows, width), lambda d, s: (0, d))


def lead_spec(*shape):
    return pl.BlockSpec(shape, lambda d, s: (d,) + (0,) * (len(shape) - 1))


def whole(shape):
    return pl.BlockSpec(shape, lambda d, s: (0,) * len(shape))


def transposed(x):
    eye = (
        lax.broadcasted_iota(jnp.int32, (HEAD, HEAD), 0) == lax.broadcasted_iota(jnp.int32, (HEAD, HEAD), 1)
    ).astype(BF16)
    return nt(eye, x)


def local_states_body(hq, sends, s, k, v, ld, *refs):
    if sends:
        grad, parts, row, col, away, tri = refs
        away[...] = grad[...]
    else:
        parts, row, col, tri = refs
    d = pl.program_id(0)

    @pl.when(d == 0)
    def _():
        at = lax.broadcasted_iota(jnp.int32, (BLOCK, BLOCK), 0)
        other = lax.broadcasted_iota(jnp.int32, (BLOCK, BLOCK), 1)
        tri[...] = (at >= other).astype(BF16)

    rows = ld.shape[0]
    offset = lax.rem(d * hq, rows)
    x = ld[0:hq, :]
    for c in range(hq, rows, hq):
        x = jnp.where(offset == c, ld[c : c + hq, :], x)
    x = jnp.concatenate([x, jnp.zeros((EXTRA - hq, BLOCK), F32)], axis=0)
    terms = split_terms(x, 3)
    sums = jnp.zeros((EXTRA, BLOCK), F32)
    down = jnp.zeros((BLOCK, EXTRA), F32)
    for term in reversed(terms):
        sums = sums + nt(term, tri[...])
        down = down + nt(tri[...], term)
    row[0] = sums[0:8]
    col[0, :, 0:EXTRA] = down
    edge = sums[:, BLOCK - 1 : BLOCK]
    shrink = jnp.exp(edge - sums)
    at = lax.broadcasted_iota(jnp.int32, (EXTRA, HEAD), 0)
    for j in range(hq):
        kd = (transposed(k[:, head_cols(j)]) * shrink[j : j + 1, :]).astype(BF16)
        parts[j, 0:HEAD, :] = nn(kd, v[:, head_cols(j)]).astype(BF16)
        e = split_terms(jnp.broadcast_to(edge[j : j + 1, :], (EXTRA, HEAD)), 3)
        out = jnp.zeros((EXTRA, HEAD), F32)
        for i in range(3):
            out = jnp.where(at == i, e[i].astype(F32), out)
        parts[j, HEAD : HEAD + EXTRA, :] = out.astype(BF16)


def forward_scan_body(got, out):
    n, tall, _ = got.shape
    tall -= EXTRA
    state = jnp.zeros((tall, HEAD), F32)
    for j in range(n):
        out[j] = state.astype(BF16)
        decay = jnp.exp(jnp.sum(got[j, tall : tall + EXTRA, :].astype(F32), axis=0, keepdims=True))
        state = state * decay + got[j, 0:tall, :].astype(F32)


def reverse_scan_body(edges, got, out):
    n, tall, _ = got.shape
    tall -= EXTRA
    state = jnp.zeros((tall, HEAD), F32)
    gain = jnp.zeros((EXTRA, HEAD), F32)
    for j in reversed(range(n)):
        out[j, 0:tall, :] = state.astype(BF16)
        decay = jnp.exp(jnp.sum(edges[j, tall : tall + EXTRA, :].astype(F32), axis=0, keepdims=True))
        state = state * decay + got[j, 0:tall, :].astype(F32)
        gain = gain + got[j, tall : tall + EXTRA, :].astype(F32)
    rows = gain_rows(jnp.sum(gain, axis=0, keepdims=True))
    for j in range(n):
        out[j, tall : tall + EXTRA, :] = rows


def gain_rows(total):
    at = lax.broadcasted_iota(jnp.int32, (EXTRA, HEAD), 0)
    high, low = split_terms(jnp.broadcast_to(total, (EXTRA, HEAD)), 2)
    return jnp.where(at == 0, high.astype(F32), jnp.where(at == 1, low.astype(F32), 0.0)).astype(BF16)


def lower_mask():
    return lax.broadcasted_iota(jnp.int32, (HALF, HALF), 0) >= lax.broadcasted_iota(jnp.int32, (HALF, HALF), 1)


def upper_mask():
    return lax.broadcasted_iota(jnp.int32, (HALF, HALF), 0) <= lax.broadcasted_iota(jnp.int32, (HALF, HALF), 1)


def intra_body(hq, s, q, k, v, row, col, intra):
    mask = lower_mask()
    for j in range(hq):
        c = head_cols(j)
        for i in range(2):
            total = None
            for m in range(i + 1):
                table = jnp.exp(col[0, piece(i), j : j + 1] - row[0, j : j + 1, piece(m)])
                if m == i:
                    table = jnp.where(mask, table, 0.0)
                probs = (nt(q[piece(i), c], k[piece(m), c]) * table).astype(BF16)
                term = nn(probs, v[piece(m), c])
                total = term if total is None else total + term
            intra[piece(i), c] = total


def dscaled_body(hq, s, gate, own, got, gain, q, row, dscaled, turned):
    part = own.shape[0]
    for where, ref in ((s[0], own), (1 - s[0], got)):
        rows = pl.ds(pl.multiple_of(where * part, part), part)
        opened = jax.nn.sigmoid(gate[rows, :].astype(F32))
        dscaled[rows, :] = ref[...].astype(F32) * opened * gain[...]
    growth = jnp.exp(row[0])
    for j in range(hq):
        turned[j] = (transposed(q[:, head_cols(j)]) * growth[j : j + 1, :]).astype(BF16)


def attention_body(hq, s, q, intra, dscaled, col, state, att, sums, sq, inn):
    d = pl.program_id(0)

    @pl.when(d == 0)
    def _():
        sq[...] = jnp.zeros_like(sq)
        inn[...] = jnp.zeros_like(inn)

    for i in range(BLOCK // HEAD):
        r = head_cols(i)
        a_sq = sq[r, :]
        a_in = inn[r, :]
        for j in range(hq):
            c = head_cols(j)
            a = intra[r, c] + nn(q[r, c], state[j, 0:HEAD, :]) * jnp.exp(col[0, r, j : j + 1])
            att[r, c] = a
            a_sq = a_sq + a * a
            a_in = a_in + a * dscaled[r, c]
        sq[r, :] = a_sq
        inn[r, :] = a_in

    @pl.when(d == pl.num_programs(0) - 1)
    def _():
        ones = jnp.ones((8, HEAD), F32)
        a = nt(ones, sq[...], lax.Precision.HIGHEST)
        b = nt(ones, inn[...], lax.Precision.HIGHEST)
        sums[...] = jnp.where(lax.broadcasted_iota(jnp.int32, (8, BLOCK), 0) == 0, a, b)


def dattn_body(hq, channels, s, att, dscaled, turned, gain, sum_a, sum_b, dattn, parts, scale):
    d = pl.program_id(0)

    @pl.when(d == 0)
    def _():
        total = sum_a[...] + sum_b[...]
        rs = lax.rsqrt(total[0:1, :] / channels + EPSILON)
        coef = total[1:2, :] * (rs * rs * rs) / channels
        both = jnp.concatenate([rs, coef, jnp.zeros((HEAD - 2, BLOCK), F32)], axis=0)
        scale[...] = both.T

    for j in range(hq):
        c = head_cols(j)
        gsum = jnp.zeros((8, HEAD), F32)
        for i in range(BLOCK // HEAD):
            r = head_cols(i)
            a = att[r, c]
            t = dscaled[r, c] * scale[r, 0:1]
            dattn[r, c] = (t - a * scale[r, 1:2]).astype(BF16)
            gsum = gsum + jnp.sum((t * a).reshape(HEAD // 8, 8, HEAD), axis=0)
        parts[j, 0:HEAD, :] = nn(turned[j], dattn[:, c]).astype(BF16)
        total = jnp.sum(gsum, axis=0, keepdims=True) / gain[:, c]
        parts[j, HEAD : HEAD + EXTRA, :] = gain_rows(total)


def query_body(hq, s, k, v, dattn, row, col, state, gate, att, dscaled, scale, query_grad, gate_grad):
    mask = lower_mask()
    for j in range(hq):
        c = head_cols(j)
        for i in range(2):
            d = dattn[piece(i), c]
            total = nt(d, state[j, 0:HEAD, :]) * jnp.exp(col[0, piece(i), j : j + 1])
            for m in range(i + 1):
                table = jnp.exp(col[0, piece(i), j : j + 1] - row[0, j : j + 1, piece(m)])
                if m == i:
                    table = jnp.where(mask, table, 0.0)
                dscores = (nt(d, v[piece(m), c]) * table).astype(BF16)
                total = total + nn(dscores, k[piece(m), c])
            query_grad[piece(i), c] = total.astype(BF16)
        opened = jax.nn.sigmoid(gate[:, c].astype(F32))
        gate_grad[:, c] = (dscaled[:, c] * att[:, c] * scale[:, 0:1] * (1.0 - opened)).astype(BF16)


def key_value_body(hq, s, q, k, v, dattn, row, col, dk, dv):
    mask = upper_mask()
    for j in range(hq):
        c = head_cols(j)
        for i in range(2):
            dkey = dvalue = None
            for m in range(i, 2):
                table = jnp.exp(row[0, j : j + 1, piece(m)] - col[0, piece(i), j : j + 1])
                if m == i:
                    table = jnp.where(mask, table, 0.0)
                probs = (nt(k[piece(i), c], q[piece(m), c]) * table).astype(BF16)
                dscores = (nt(v[piece(i), c], dattn[piece(m), c]) * table).astype(BF16)
                a = nn(dscores, q[piece(m), c])
                b = nn(probs, dattn[piece(m), c])
                dkey, dvalue = (a, b) if dkey is None else (dkey + a, dvalue + b)
            dk[piece(i), c] = dkey
            dv[piece(i), c] = dvalue


def final_body(hq, s, k, v, dk, dv, col, state, key_grad, value_grad, gain_grad):
    for j in range(hq):
        c = head_cols(j)
        shrink = jnp.exp(col[0, BLOCK - 1 : BLOCK, j : j + 1] - col[0, :, j : j + 1])
        after = state[j, 0:HEAD, :]
        key_grad[:, c] = (dk[:, c] + nt(v[:, c], after) * shrink).astype(BF16)
        value_grad[:, c] = (dv[:, c] + nn(k[:, c], after) * shrink).astype(BF16)
        gain_grad[:, c] = jnp.sum(state[j, HEAD : HEAD + EXTRA, :].astype(F32), axis=0, keepdims=True)


def plain(body, inputs, out_shape, name):
    return pl.pallas_call(
        body,
        out_shape=out_shape,
        compiler_params=pltpu.CompilerParams(vmem_limit_bytes=VMEM_LIMIT),
        name=name,
    )(*inputs)


def local(queries, keys, values, log_decay, gate, gain, grad_out):
    rows, width = queries.shape
    heads = width // HEAD
    hq = min(4, heads)
    grid = (heads // hq,)
    tp = lax.axis_size("tp")
    n = lax.axis_size("ctx")
    channels = width * tp
    mine = lax.axis_index("tp")
    w = hq * HEAD
    bf = lambda *shape: jax.ShapeDtypeStruct(shape, BF16)
    f32 = lambda *shape: jax.ShapeDtypeStruct(shape, F32)
    tall = heads * HEAD // n
    copies = n // heads

    def spread(payload):
        if copies == 1:
            return payload
        body = payload[:, :HEAD].reshape(n, tall, HEAD)
        return jnp.concatenate([body, jnp.repeat(payload[:, HEAD:], copies, axis=0)], axis=1)

    def collect(chunks):
        if copies == 1:
            return chunks
        body = chunks[:, :tall].reshape(heads, HEAD, HEAD)
        return jnp.concatenate([body, chunks[::copies, tall:]], axis=1)

    def swap(x):
        return lax.all_to_all(x, "ctx", split_axis=0, concat_axis=0, tiled=True)

    swaps = tp == 2
    part = rows // 2
    if swaps:
        own = grad_out
        half = mine
        blocks = grid[0]
        info = jnp.stack([mine, mine * blocks, (1 - mine) * blocks]).astype(jnp.int32)
    else:
        every = lax.all_to_all(grad_out, "tp", split_axis=1, concat_axis=0, tiled=True)
        own, got = every[:part], every[part:]
        info = jnp.zeros((3,), jnp.int32)

    decay_rows = 8 if heads % 8 == 0 else heads
    per = decay_rows // hq
    small = 2 * heads * rows * HEAD * HEAD
    large = 2 * heads * rows * rows * HEAD
    cols = cols_spec(rows, w)
    row_spec = lead_spec(1, 8, BLOCK)
    col_spec = lead_spec(1, BLOCK, HEAD)
    state_spec = lead_spec(hq, HEAD + EXTRA, HEAD)
    narrow_spec = lead_spec(hq, HEAD, HEAD)
    half_spec = cols_spec(part, w)
    gain_spec = cols_spec(1, w)
    gain_row = gain.reshape(1, width)

    outs = call(
        functools.partial(local_states_body, hq, swaps),
        grid,
        info,
        [keys, values, log_decay] + [grad_out] * swaps,
        [cols, cols, pl.BlockSpec((decay_rows, rows), lambda d, s: (d // per, 0))]
        + [pl.BlockSpec((part, w), lambda d, s: (0, s[2] + d))] * swaps,
        [bf(heads, HEAD + EXTRA, HEAD), f32(grid[0], 8, rows), f32(grid[0], rows, HEAD)]
        + [bf(part, width)] * swaps,
        [state_spec, row_spec, col_spec] + [half_spec] * swaps,
        [pltpu.VMEM((BLOCK, BLOCK), BF16)],
        small,
        "local_states",
    )
    parts, row, col = outs[:3]
    received = swap(spread(parts))
    if swaps:
        got = lax.ppermute(outs[3], "tp", [(0, 1), (1, 0)])
    own_spec = pl.BlockSpec((part, w), lambda d, s: (0, s[1] + d))

    (intra,) = call(
        functools.partial(intra_body, hq),
        grid,
        info,
        [queries, keys, values, row, col],
        [cols] * 3 + [row_spec, col_spec],
        [f32(rows, width)],
        [cols],
        [],
        2 * large,
        "intra",
    )
    entering = plain(forward_scan_body, [received], bf(n, tall, HEAD), "forward_scan")
    entering = swap(entering)
    if copies > 1:
        entering = entering.reshape(heads, HEAD, HEAD)
    dscaled, turned = call(
        functools.partial(dscaled_body, hq),
        grid,
        info,
        [gate, own, got, gain_row, queries, row],
        [cols, own_spec, half_spec, gain_spec, cols, row_spec],
        [f32(rows, width), bf(heads, HEAD, rows)],
        [cols, lead_spec(hq, HEAD, rows)],
        [],
        small,
        "dscaled",
    )
    att, sums = call(
        functools.partial(attention_body, hq),
        grid,
        info,
        [queries, intra, dscaled, col, entering],
        [cols, cols, cols, col_spec, narrow_spec],
        [f32(rows, width), f32(8, rows)],
        [cols, whole((8, rows))],
        [pltpu.VMEM((rows, HEAD), F32), pltpu.VMEM((rows, HEAD), F32)],
        small,
        "attention",
    )
    if swaps:
        others = lax.ppermute(sums, "tp", [(0, 1), (1, 0)])
    else:
        others = lax.psum(sums, "tp") - sums
    dattn, parts, scale = call(
        functools.partial(dattn_body, hq, channels),
        grid,
        info,
        [att, dscaled, turned, gain_row, sums, others],
        [cols, cols, lead_spec(hq, HEAD, rows), gain_spec] + [whole((8, rows))] * 2,
        [bf(rows, width), bf(heads, HEAD + EXTRA, HEAD), f32(rows, HEAD)],
        [cols, state_spec, whole((rows, HEAD))],
        [],
        small,
        "dattn",
    )
    received_back = swap(spread(parts))
    query_grad, gate_grad = call(
        functools.partial(query_body, hq),
        grid,
        info,
        [keys, values, dattn, row, col, entering, gate, att, dscaled, scale],
        [cols] * 3 + [row_spec, col_spec, narrow_spec] + [cols] * 3 + [whole((rows, HEAD))],
        [bf(rows, width), bf(rows, width)],
        [cols] * 2,
        [],
        2 * large + small,
        "query",
    )
    leaving = plain(reverse_scan_body, [received, received_back], bf(n, tall + EXTRA, HEAD), "reverse_scan")
    leaving, late_dattn = lax.optimization_barrier((leaving, dattn))
    leaving = collect(swap(leaving))
    dk, dv = call(
        functools.partial(key_value_body, hq),
        grid,
        info,
        [queries, keys, values, late_dattn, row, col],
        [cols] * 4 + [row_spec, col_spec],
        [f32(rows, width), f32(rows, width)],
        [cols] * 2,
        [],
        4 * large,
        "key_value",
    )
    key_grad, value_grad, gain_grad = call(
        functools.partial(final_body, hq),
        grid,
        info,
        [keys, values, dk, dv, col, leaving],
        [cols] * 4 + [col_spec, state_spec],
        [bf(rows, width), bf(rows, width), f32(1, width)],
        [cols] * 2 + [gain_spec],
        [],
        2 * small,
        "final",
    )
    return query_grad, key_grad, value_grad, gate_grad, gain_grad.reshape(width)


def solution(mesh):
    return jax.shard_map(
        local,
        mesh=mesh,
        in_specs=(
            P("ctx", "tp"),
            P("ctx", "tp"),
            P("ctx", "tp"),
            P("tp", "ctx"),
            P("ctx", "tp"),
            P("tp"),
            P(("ctx", "tp"), None),
        ),
        out_specs=(P("ctx", "tp"), P("ctx", "tp"), P("ctx", "tp"), P("ctx", "tp"), P("tp")),
        check_vma=False,
    )
```

time: 403 us -> 148 us (0.37); the launches traced: 395 us -> 147 us
  waiting for transfers between devices: 108 us -> 16.5 us
  matrix products: 86.7 us -> 0 us
  Pallas kernels: 0 us -> 83.5 us
  blocking collectives: 86.3 us -> 23.4 us
  local copies, waits for them, and re-layouts: 51.3 us -> 4.06 us
  other arithmetic: 42.6 us -> 0.67 us
  between operations: 14.7 us -> 0.7 us
  starting transfers between devices: 4.9 us -> 18.4 us
    all_gather x2 -> x0, waiting for transfers between devices: 108 us -> none  [carried_in(): gathered = jax.tree.map(lambda a: lax.all_gather(a, axis), part)]
    dot_general x12 -> x0, matrix products: 86.7 us -> none  [the longest x1 9.59 us: local(): jnp.einsum('blhd,bmhd->bhlm', query_blocks, key_blocks, preferred_element...]
    pallas_call x0 -> x10, Pallas kernels: none -> 83.5 us  [the longest x8 79.2 us: call(): pl.pallas_call(body, grid_spec=pltpu.PrefetchScalarGridSpec(num_scalar_pr...]
    psum x3 -> x0, blocking collectives: 63 us -> none  [the longest x1 53 us: local(): gain_grad = lax.psum(gain_part, 'ctx')]
    all_to_all x0 -> x1, blocking collectives: none -> 23.4 us  [swap(): return lax.all_to_all(x, 'ctx', split_axis=0, concat_axis=0, tiled=True)]
    all_gather x1 -> x0, blocking collectives: 23.3 us -> none  [carried_in(): gathered = jax.tree.map(lambda a: lax.all_gather(a, axis), part)]
    add x15 -> x0, other arithmetic: 21.7 us -> none  [link_states(): later[0][:, None, None] * earlier[1] + later[1]]
    convert_element_type x2 -> x0, local copies, waits for them, and re-layouts: 18.7 us -> none  [local(): grad_blocks = grad_rows.reshape(shape4).astype(jnp.float32)]
  transfers between devices with their start and end apart: 3 -> 5, of which waited for: 2 -> 2; matrix products, arithmetic and copies ran while one was open for 22% -> 0% of each run, Pallas kernels for 0% -> 31%
where the time goes in v2:
time: 148 us; the launch traced here: 147 us
  Pallas kernels  83.5 us (56%)
  blocking collectives  23.4 us (16%)
  starting transfers between devices  18.4 us (12%)
  waiting for transfers between devices  16.5 us (11%)
  local copies, waits for them, and re-layouts  4.06 us (3%)
    pallas_call x8, Pallas kernels, call(): pl.pallas_call(body, grid_spec=pltpu.PrefetchScalarGridSpec(num_scalar_pr...  79.2 us
    all_to_all x1, blocking collectives, swap(): return lax.all_to_all(x, 'ctx', split_axis=0, concat_axis=0, tiled=True)  23.4 us
    all_to_all x3, starting transfers between devices, swap(): return lax.all_to_all(x, 'ctx', split_axis=0, concat_axis=0, tiled=True)  15.4 us
    all_to_all x3, waiting for transfers between devices, swap(): return lax.all_to_all(x, 'ctx', split_axis=0, concat_axis=0, tiled=True)  14 us
    pallas_call x2, Pallas kernels, plain(): pl.pallas_call(body, out_shape=out_shape, compiler_params=pltpu.CompilerP...  4.25 us
    unnamed x10, local copies, waits for them, and re-layouts  4.06 us
  transfers between devices with their start and end apart: 5, of which 2 were waited for; matrix products, arithmetic and copies ran while one was open for 0% of the time, Pallas kernels for 31%

profile of v2, /device:TPU:0, one launch (start us, length us, event | category | flops | bytes accessed | tf_op | source)
XLA Modules:
  0.0 147.2 jit_solution(2985034775642497886)
XLA Ops:
  0.6 0.7 pad_add_fusion.s
  1.3 9.6 %local_states.1 = (bf16[16,144,128]{2,1,0:T(8,128)(2,1)}, f32[4,8,512]{2,1,0:T(8,128)}, f32[4,512,128]{2,1,0:T(8,128)}, bf16[256,2048]{1,0:T(8,128)(2,1)}) custom-call(s32[3]{0:T(128)} %pad_add_fusion.s, bf16[512,2048]{1,0:T(8,128)(2,1)} %k.9, bf16[512,2048]{1,0:T(8,128)(2,1)} %v.9, f32[16,512]{1,0:T(8,128)} %ld.1, bf16[256,4096]{1,0:T(8,128)(2,1)} %own.1), custom_call_target="tpu_custom_call" | custom-call | flops 268435456 | bytes 9076736 | tf_op jit(solution)/shard_map/local_states/pallas_call | solution.py:48
  10.9 7.4 %all-to-all-start = ((bf16[16,144,128]{2,1,0:T(8,128)(2,1)}), bf16[16,144,128]{2,1,0:T(8,128)(2,1)S(1)}, u32[]{:S(2)}, u32[]{:S(2)}) async-start(bf16[16,144,128]{2,1,0:T(8,128)(2,1)} %get-tuple-element.29), calls=%async_computation | async-start | bytes 1179648 | tf_op jit(solution)/shard_map/all_to_all | solution.py:328
  18.3 1.6 %collective-permute-start = (bf16[256,2048]{1,0:T(8,128)(2,1)}, bf16[256,2048]{1,0:T(8,128)(2,1)S(1)}, u32[]{:S(2)}, u32[]{:S(2)}) collective-permute-start(bf16[256,2048]{1,0:T(8,128)(2,1)} %get-tuple-element.27), channel_id=1, source_target_pairs={{0,1},{1,0},{2,3},{3,2},{4,5},{5,4},{6,7},{7,6},{8,9},{9,8},{10,11... | collective-permute-start | bytes 3145736 | tf_op jit(solution)/shard_map/ppermute | solution.py:372
  19.9 14.0 %all-to-all-done.got.edges = bf16[16,144,128]{2,1,0:T(8,128)(2,1)S(1)} async-done(((bf16[16,144,128]{2,1,0:T(8,128)(2,1)}), bf16[16,144,128]{2,1,0:T(8,128)(2,1)S(1)}, u32[]{:S(2)}, u32[]{:S(2)}) %all-to-all-start) | async-done | bytes 589856 | tf_op jit(solution)/shard_map/all_to_all | solution.py:328
  33.9 0.8 copy-done
  34.7 2.0 %forward_scan.1 = bf16[16,128,128]{2,1,0:T(8,128)(2,1)} custom-call(bf16[16,144,128]{2,1,0:T(8,128)(2,1)} %copy-done), custom_call_target="tpu_custom_call" | custom-call | tf_op jit(solution)/shard_map/forward_scan/pallas_call | solution.py:292
  36.7 4.4 %all-to-all-start.1 = ((bf16[16,128,128]{2,1,0:T(8,128)(2,1)}), bf16[16,128,128]{2,1,0:T(8,128)(2,1)S(1)}, u32[]{:S(2)}, u32[]{:S(2)}) async-start(bf16[16,128,128]{2,1,0:T(8,128)(2,1)} %forward_scan.1), calls=%async_computation.1 | async-start | bytes 1048576 | tf_op jit(solution)/shard_map/all_to_all | solution.py:328
  41.1 9.9 %intra.1 = f32[512,2048]{1,0:T(8,128)} custom-call(s32[3]{0:T(128)} %pad_add_fusion.s, bf16[512,2048]{1,0:T(8,128)(2,1)} %q.7, bf16[512,2048]{1,0:T(8,128)(2,1)} %k.9, bf16[512,2048]{1,0:T(8,128)(2,1)} %v.9, f32[4,8,512]{2,1,0:T(8,128)} %get-tuple-element.25.row, f32[4,512,128]{2,1,0:T(8,128)} %get-tuple-element.26.col), custom_call_target="tpu_custom_call" | custom-call | flops 2147483648 | bytes 11599872 | tf_op jit(solution)/shard_map/intra/pallas_call | solution.py:48
  51.0 1.0 copy-done.3
  52.0 7.1 %dscaled.1 = (f32[512,2048]{1,0:T(8,128)}, bf16[16,128,512]{2,1,0:T(8,128)(2,1)}) custom-call(s32[3]{0:T(128)} %pad_add_fusion.s, bf16[512,2048]{1,0:T(8,128)(2,1)} %gate.3, bf16[256,4096]{1,0:T(8,128)(2,1)} %own.1, bf16[256,2048]{1,0:T(8,128)(2,1)} %copy-done.3, f32[1,2048]{1,0:T(1,128)} %bitcast.5, bf16[512,2048]{1,0:T(8,128)(2,1)} %q.7, ...), custom_call_target="tpu_custom_call" | custom-call | flops 268435456 | bytes 13705216 | tf_op jit(solution)/shard_map/dscaled/pallas_call | solution.py:48
  59.2 0.8 copy-done.1
  60.0 8.7 %attention.1 = (f32[512,2048]{1,0:T(8,128)}, f32[8,512]{1,0:T(8,128)}) custom-call(s32[3]{0:T(128)} %pad_add_fusion.s, bf16[512,2048]{1,0:T(8,128)(2,1)} %q.7, f32[512,2048]{1,0:T(8,128)} %intra.1, f32[512,2048]{1,0:T(8,128)} %get-tuple-element.28.dscaled, f32[4,512,128]{2,1,0:T(8,128)} %get-tuple-element.26.col, bf16[16,128,128]{2,1,0:T(8,128)(2,1)} %copy-done.1), custom_call_target="tpu_custom_call" | custom-call | flops 268435456 | bytes 16269312 | tf_op jit(solution)/shard_map/attention/pallas_call | solution.py:48
  68.6 1.5 %collective-permute-start.1 = (f32[8,512]{1,0:T(8,128)}, f32[8,512]{1,0:T(8,128)S(1)}, u32[]{:S(2)}, u32[]{:S(2)}) collective-permute-start(f32[8,512]{1,0:T(8,128)} %get-tuple-element.32.sum_a), channel_id=1, source_target_pairs={{0,1},{1,0},{2,3},{3,2},{4,5},{5,4},{6,7},{7,6},{8,9},{9,8},{10,11... | collective-permute-start | bytes 49160 | tf_op jit(solution)/shard_map/ppermute | solution.py:416
  70.1 2.5 %collective-permute-done.1.sum_b = f32[8,512]{1,0:T(8,128)S(1)} collective-permute-done((f32[8,512]{1,0:T(8,128)}, f32[8,512]{1,0:T(8,128)S(1)}, u32[]{:S(2)}, u32[]{:S(2)}) %collective-permute-start.1) | collective-permute-done | bytes 16416 | tf_op jit(solution)/shard_map/ppermute | solution.py:416
  72.6 0.6 copy-done.4
  73.2 8.6 %dattn.1 = (bf16[512,2048]{1,0:T(8,128)(2,1)}, bf16[16,144,128]{2,1,0:T(8,128)(2,1)}, f32[512,128]{1,0:T(8,128)}) custom-call(s32[3]{0:T(128)} %pad_add_fusion.s, f32[512,2048]{1,0:T(8,128)} %get-tuple-element.30.att, f32[512,2048]{1,0:T(8,128)} %get-tuple-element.28.dscaled, bf16[16,128,512]{2,1,0:T(8,128)(2,1)} %get-tuple-element.31.turned, ...), custom_call_target="tpu_custom_call" | custom-call | flops 268435456 | bytes 13475840 | tf_op jit(solution)/shard_map/dattn/pallas_call | solution.py:48
  81.8 23.4 %all_to_all.20.got = bf16[16,144,128]{2,1,0:T(8,128)(2,1)} all-to-all(bf16[16,144,128]{2,1,0:T(8,128)(2,1)} %get-tuple-element.36), channel_id=1, replica_groups=mesh['ctx'=16,'tp'=2] {'ctx'}, dimensions={0} | all-to-all | bytes 1179648 | tf_op jit(solution)/shard_map/all_to_all | solution.py:328
  105.2 2.2 %reverse_scan.1 = bf16[16,144,128]{2,1,0:T(8,128)(2,1)} custom-call(bf16[16,144,128]{2,1,0:T(8,128)(2,1)} %copy-done, bf16[16,144,128]{2,1,0:T(8,128)(2,1)} %all_to_all.20.got), custom_call_target="tpu_custom_call" | custom-call | tf_op jit(solution)/shard_map/reverse_scan/pallas_call | solution.py:292
  107.5 3.6 %all-to-all-start.3 = ((bf16[16,144,128]{2,1,0:T(8,128)(2,1)}), bf16[16,144,128]{2,1,0:T(8,128)(2,1)S(1)}, u32[]{:S(2)}, u32[]{:S(2)}) async-start(bf16[16,144,128]{2,1,0:T(8,128)(2,1)} %reverse_scan.1), calls=%async_computation.3 | async-start | bytes 1179648 | tf_op jit(solution)/shard_map/all_to_all | solution.py:328
  111.0 13.2 %query.1 = (bf16[512,2048]{1,0:T(8,128)(2,1)}, bf16[512,2048]{1,0:T(8,128)(2,1)}) custom-call(s32[3]{0:T(128)} %pad_add_fusion.s, bf16[512,2048]{1,0:T(8,128)(2,1)} %k.9, bf16[512,2048]{1,0:T(8,128)(2,1)} %v.9, bf16[512,2048]{1,0:T(8,128)(2,1)} %get-tuple-element.37.dattn, f32[4,8,512]{2,1,0:T(8,128)} %get-tuple-element.25.row, ...), custom_call_target="tpu_custom_call" | custom-call | flops 2415919104 | bytes 22872064 | tf_op jit(solution)/shard_map/query/pallas_call | solution.py:48
  124.3 13.5 %key_value.1 = (f32[512,2048]{1,0:T(8,128)}, f32[512,2048]{1,0:T(8,128)}) custom-call(s32[3]{0:T(128)} %pad_add_fusion.s, bf16[512,2048]{1,0:T(8,128)(2,1)} %q.7, bf16[512,2048]{1,0:T(8,128)(2,1)} %k.9, bf16[512,2048]{1,0:T(8,128)(2,1)} %v.9, bf16[512,2048]{1,0:T(8,128)(2,1)} %get-tuple-element.37.dattn, f32[4,8,512]{2,1,0:T(8,128)} %get-tuple-element.25.row, ...), custom_call_target="tpu_custom_call" | custom-call | flops 4294967296 | bytes 17891328 | tf_op jit(solution)/shard_map/key_value/pallas_call | solution.py:48
  137.8 0.9 copy-done.2
  138.7 8.5 %final.1 = (bf16[512,2048]{1,0:T(8,128)(2,1)}, bf16[512,2048]{1,0:T(8,128)(2,1)}, f32[1,2048]{1,0:T(1,128)}) custom-call(s32[3]{0:T(128)} %pad_add_fusion.s, bf16[512,2048]{1,0:T(8,128)(2,1)} %k.9, bf16[512,2048]{1,0:T(8,128)(2,1)} %v.9, f32[512,2048]{1,0:T(8,128)} %get-tuple-element.38.dk, f32[512,2048]{1,0:T(8,128)} %get-tuple-element.39.dv, ...), custom_call_target="tpu_custom_call" | custom-call | flops 536870912 | bytes 18423808 | tf_op jit(solution)/shard_map/final/pallas_call | solution.py:48
  (8 shorter events, 0.0 us)
Async XLA Ops:
  10.9 23.0 %all-to-all-start = ((bf16[16,144,128]{2,1,0:T(8,128)(2,1)}), bf16[16,144,128]{2,1,0:T(8,128)(2,1)S(1)}, u32[]{:S(2)}, u32[]{:S(2)}) async-start(bf16[16,144,128]{2,1,0:T(8,128)(2,1)} %get-tuple-element.29), calls=%async_computation | async-start | bytes 1179648 | tf_op jit(solution)/shard_map/all_to_all | solution.py:328
  18.3 32.7 %collective-permute-start = (bf16[256,2048]{1,0:T(8,128)(2,1)}, bf16[256,2048]{1,0:T(8,128)(2,1)S(1)}, u32[]{:S(2)}, u32[]{:S(2)}) collective-permute-start(bf16[256,2048]{1,0:T(8,128)(2,1)} %get-tuple-element.27), channel_id=1, source_target_pairs={{0,1},{1,0},{2,3},{3,2},{4,5},{5,4},{6,7},{7,6},{8,9},{9,8},{10,11... | collective-permute-start | bytes 3145736 | tf_op jit(solution)/shard_map/ppermute | solution.py:372
  33.9 0.8 copy-start
  36.7 22.5 %all-to-all-start.1 = ((bf16[16,128,128]{2,1,0:T(8,128)(2,1)}), bf16[16,128,128]{2,1,0:T(8,128)(2,1)S(1)}, u32[]{:S(2)}, u32[]{:S(2)}) async-start(bf16[16,128,128]{2,1,0:T(8,128)(2,1)} %forward_scan.1), calls=%async_computation.1 | async-start | bytes 1048576 | tf_op jit(solution)/shard_map/all_to_all | solution.py:328
  51.0 1.0 copy-start.3
  59.2 0.8 copy-start.1
  68.6 4.0 %collective-permute-start.1 = (f32[8,512]{1,0:T(8,128)}, f32[8,512]{1,0:T(8,128)S(1)}, u32[]{:S(2)}, u32[]{:S(2)}) collective-permute-start(f32[8,512]{1,0:T(8,128)} %get-tuple-element.32.sum_a), channel_id=1, source_target_pairs={{0,1},{1,0},{2,3},{3,2},{4,5},{5,4},{6,7},{7,6},{8,9},{9,8},{10,11... | collective-permute-start | bytes 49160 | tf_op jit(solution)/shard_map/ppermute | solution.py:416
  72.6 0.6 copy-start.4
  107.5 30.3 %all-to-all-start.3 = ((bf16[16,144,128]{2,1,0:T(8,128)(2,1)}), bf16[16,144,128]{2,1,0:T(8,128)(2,1)S(1)}, u32[]{:S(2)}, u32[]{:S(2)}) async-start(bf16[16,144,128]{2,1,0:T(8,128)(2,1)} %reverse_scan.1), calls=%async_computation.3 | async-start | bytes 1179648 | tf_op jit(solution)/shard_map/all_to_all | solution.py:328
  137.8 0.9 copy-start.2

commit v3 on v0

v3 whole, which is shorter than its diff:
```python
import functools

import jax
import jax.numpy as jnp
from jax import lax
from jax.experimental import pallas as pl
from jax.experimental.pallas import tpu as pltpu
from jax.sharding import PartitionSpec as P

HEAD = 128
BLOCK = 512
HALF = BLOCK // 2
EXTRA = 16
TALL = HEAD + EXTRA
TEAM = 4
EPSILON = 1e-06
F32 = jnp.float32
BF16 = jnp.bfloat16
GRANT = 12 * 1024 * 1024
VMEM = pl.BlockSpec(memory_space=pltpu.VMEM)
ANY = pl.BlockSpec(memory_space=pl.ANY)


def nt(a, b, precision=None):
    return lax.dot_general(a, b, (((1,), (1,)), ((), ())), preferred_element_type=F32, precision=precision)


def nn(a, b):
    return lax.dot_general(a, b, (((1,), (0,)), ((), ())), preferred_element_type=F32)


def piece(i):
    return slice(i * HALF, (i + 1) * HALF)


def chunk(i):
    return slice(i * HEAD, (i + 1) * HEAD)


def split_terms(x, count):
    terms = []
    for _ in range(count):
        term = x.astype(BF16)
        terms.append(term)
        x = x - term.astype(F32)
    return terms


def term_rows(x, count):
    at = lax.broadcasted_iota(jnp.int32, (EXTRA, HEAD), 0)
    out = jnp.zeros((EXTRA, HEAD), F32)
    for i, term in enumerate(split_terms(jnp.broadcast_to(x, (EXTRA, HEAD)), count)):
        out = jnp.where(at == i, term.astype(F32), out)
    return out.astype(BF16)


def row_total(ref, j):
    return jnp.sum(ref[j, HEAD:TALL, :].astype(F32), axis=0, keepdims=True)


def seat():
    return lax.rem(lax.axis_index("ctx"), TEAM)


def ahead(d):
    return lax.rem(seat() + d, TEAM)


def behind(d):
    return lax.rem(seat() + TEAM - d, TEAM)


def head_at(quarter, hq, j):
    h = quarter * hq + j
    return h, pl.ds(pl.multiple_of(h * HEAD, HEAD), HEAD)


def transposed(x):
    eye = (
        lax.broadcasted_iota(jnp.int32, (HEAD, HEAD), 0) == lax.broadcasted_iota(jnp.int32, (HEAD, HEAD), 1)
    ).astype(BF16)
    return nt(eye, x)


def call(body, inputs, out_shape, name, scratch=(), flops=0, in_specs=None, out_specs=None):
    nbytes = sum(x.size * x.dtype.itemsize for x in inputs)
    nbytes += sum(x.size * x.dtype.itemsize for x in out_shape)
    return pl.pallas_call(
        body,
        in_specs=in_specs or [VMEM] * len(inputs),
        out_specs=out_specs or [VMEM] * len(out_shape),
        out_shape=out_shape,
        scratch_shapes=list(scratch),
        compiler_params=pltpu.CompilerParams(vmem_limit_bytes=GRANT),
        cost_estimate=pl.CostEstimate(flops=flops, bytes_accessed=nbytes, transcendentals=0),
        name=name,
    )(*inputs)


def local_states_body(heads, swaps, k_hbm, v_hbm, ld, *refs):
    hq = heads // TEAM
    w = hq * HEAD
    if swaps:
        grad, p0, p1, p2, p3, row, away, own, k, v, sems, grad_sems = refs
        width = heads * HEAD
        mine = lax.axis_index("tp")
        cols = lambda t: pl.ds(pl.multiple_of(t * width, HEAD), width)
        grad_copies = [
            pltpu.make_async_copy(grad.at[:, cols(1 - mine)], away, grad_sems.at[0]),
            pltpu.make_async_copy(grad.at[:, cols(mine)], own, grad_sems.at[1]),
        ]
    else:
        p0, p1, p2, p3, row, k, v, sems = refs
        grad_copies = []
    outs = (p0, p1, p2, p3)
    order = (1, 2, 3, 0)
    copies = []
    for d in order:
        cols_d = pl.ds(pl.multiple_of(ahead(d) * w, HEAD), w)
        pair = [
            pltpu.make_async_copy(k_hbm.at[:, cols_d], k.at[d], sems.at[0, d]),
            pltpu.make_async_copy(v_hbm.at[:, cols_d], v.at[d], sems.at[1, d]),
        ]
        for c in pair:
            c.start()
        copies.append(pair)
    for c in grad_copies:
        c.start()
    at = lax.broadcasted_iota(jnp.int32, (BLOCK, BLOCK), 0)
    other = lax.broadcasted_iota(jnp.int32, (BLOCK, BLOCK), 1)
    tri = (at <= other).astype(BF16)
    x = ld[...]
    if heads < EXTRA:
        x = jnp.concatenate([x, jnp.zeros((EXTRA - heads, BLOCK), F32)], axis=0)
    a, b, c = (nn(term, tri) for term in split_terms(x, 3))
    row[...] = a + (b + c)
    for d, pair in zip(order, copies):
        for c in pair:
            c.wait()
        for j in range(hq):
            h = ahead(d) * hq + j
            sums = row[pl.ds(h, 1), :]
            edge = sums[:, BLOCK - 1 : BLOCK]
            shrink = jnp.exp(edge - sums)
            kd = (transposed(k[d, :, chunk(j)]) * shrink).astype(BF16)
            outs[d][j, 0:HEAD, :] = nn(kd, v[d, :, chunk(j)]).astype(BF16)
            outs[d][j, HEAD:TALL, :] = term_rows(jnp.broadcast_to(edge, (1, HEAD)), 3)
    for c in grad_copies:
        c.wait()


def group_total_body(reverse, hq, a0, a1, a2, a3, *refs):
    if reverse:
        edges, out = refs
    else:
        out, edges = refs
    slots = (a0, a1, a2, a3)
    src = [behind(d) for d in range(TEAM)]
    for j in range(hq):
        if reverse:
            e = [edges[j, d : d + 1, :] for d in range(TEAM)]
        else:
            e = [row_total(slots[d], j) for d in range(TEAM)]
            for d in range(TEAM):
                edges[j, d : d + 1, :] = e[d]
            edges[j, TEAM : TEAM + 1, :] = (e[0] + e[1]) + (e[2] + e[3])
            for d in range(TEAM + 1, 8):
                edges[j, d : d + 1, :] = jnp.zeros((1, HEAD), F32)
        total = jnp.zeros((HEAD, HEAD), F32)
        for d in range(TEAM):
            expo = jnp.zeros((1, HEAD), F32)
            for i in range(TEAM):
                if i != d:
                    between = src[i] < src[d] if reverse else src[i] > src[d]
                    expo = expo + jnp.where(between, e[i], 0.0)
            total = total + slots[d][j, 0:HEAD, :].astype(F32) * jnp.exp(expo)
        out[j, 0:HEAD, :] = total.astype(BF16)
        rows = term_rows((e[0] + e[1]) + (e[2] + e[3]), 3)
        if reverse:
            gains = [row_total(slots[d], j) for d in range(TEAM)]
            gain = term_rows((gains[0] + gains[1]) + (gains[2] + gains[3]), 2).astype(F32)
            at = lax.broadcasted_iota(jnp.int32, (EXTRA, HEAD), 0)
            rows = jnp.where(at < 8, rows.astype(F32), jnp.concatenate([gain[8:], gain[:8]], axis=0))
            rows = rows.astype(BF16)
        out[j, HEAD:TALL, :] = rows


def entering_body(reverse, hq, groups, *refs):
    slots = refs[:TEAM]
    total, edges = refs[TEAM : TEAM + 2]
    far = refs[TEAM + 2 : TEAM + 1 + groups]
    outs = refs[TEAM + 1 + groups :]
    src = [behind(d) for d in range(TEAM)]
    dst = [ahead(d) for d in range(TEAM)]
    group = lax.axis_index("ctx") // TEAM
    for j in range(hq):
        e = [edges[j, d : d + 1, :] for d in range(TEAM)]
        incoming = jnp.zeros((HEAD, HEAD), F32)
        gain = total[j, HEAD + 8 : TALL, :].astype(F32)
        for k in reversed(range(1, groups)):
            ref = far[k - 1]
            there = group + k < groups if reverse else group - k >= 0
            decay = jnp.exp(jnp.sum(ref[j, HEAD : HEAD + 8, :].astype(F32), axis=0, keepdims=True))
            incoming = incoming * decay + ref[j, 0:HEAD, :].astype(F32)
            incoming = jnp.where(there, incoming, 0.0)
            gain = gain + ref[j, HEAD + 8 : TALL, :].astype(F32)
        parts = [slots[i][j, 0:HEAD, :].astype(F32) for i in range(TEAM)]
        for d in range(TEAM):
            def passed(i):
                return src[i] > dst[d] if reverse else src[i] < dst[d]

            def beyond(i, m):
                return src[m] < src[i] if reverse else src[m] > src[i]

            expo = jnp.zeros((1, HEAD), F32)
            for i in range(TEAM):
                expo = expo + jnp.where(passed(i), e[i], 0.0)
            state = incoming * jnp.exp(expo)
            for i in range(TEAM):
                if (i + d) % TEAM == 0:
                    continue
                expo = jnp.zeros((1, HEAD), F32)
                for m in range(TEAM):
                    if m != i:
                        expo = expo + jnp.where(jnp.logical_and(passed(m), beyond(i, m)), e[m], 0.0)
                state = state + parts[i] * jnp.where(passed(i), jnp.exp(expo), 0.0)
            outs[d][j, 0:HEAD, :] = state.astype(BF16)
            if reverse:
                outs[d][j, HEAD:TALL, :] = term_rows(jnp.sum(gain, axis=0, keepdims=True), 2)


def masked(lower):
    at = lax.broadcasted_iota(jnp.int32, (HALF, HALF), 0)
    other = lax.broadcasted_iota(jnp.int32, (HALF, HALF), 1)
    return at >= other if lower else at <= other


def intra_body(heads, q, k, v, row, intra, col, growth, shrink):
    hq = heads // TEAM
    mask = masked(True)
    for g in range(TEAM):
        rows = row[g * hq : (g + 1) * hq, :]
        across = jnp.concatenate([rows, jnp.zeros((HEAD - hq, BLOCK), F32)], axis=0).T
        col[g] = across
        growth[g] = jnp.exp(across)
        shrink[g] = jnp.exp(across[BLOCK - 1 : BLOCK, :] - across)

    def one(g, _):
        for j in range(hq):
            h, c = head_at(g, hq, j)
            line = row[pl.ds(h, 1), :]
            for i in range(2):
                total = None
                for m in range(i + 1):
                    table = jnp.exp(col[g, piece(i), j : j + 1] - line[:, piece(m)])
                    if m == i:
                        table = jnp.where(mask, table, 0.0)
                    probs = (nt(q[piece(i), c], k[piece(m), c]) * table).astype(BF16)
                    term = nn(probs, v[piece(m), c])
                    total = term if total is None else total + term
                intra[piece(i), c] = total
        return 0

    lax.fori_loop(0, TEAM, one, 0)


def dscaled_body(heads, swaps, gate, own, got, gain, q, row, dscaled, turned):
    hq = heads // TEAM
    part = own.shape[0]
    mine = lax.axis_index("tp") if swaps else 0

    def one(g, _):
        for j in range(hq):
            h, c = head_at(g, hq, j)
            for where, ref in ((mine, own), (1 - mine, got)):
                rows = pl.ds(pl.multiple_of(where * part, part), part)
                opened = jax.nn.sigmoid(gate[rows, c].astype(F32))
                dscaled[rows, c] = ref[:, c].astype(F32) * opened * gain[:, c]
            turned[h] = (transposed(q[:, c]) * jnp.exp(row[pl.ds(h, 1), :])).astype(BF16)
        return 0

    lax.fori_loop(0, TEAM, one, 0)


def attention_body(heads, q, intra, dscaled, growth, s0, s1, s2, s3, att, sums, sq, inn):
    hq = heads // TEAM
    for i in range(BLOCK // HEAD):
        r = chunk(i)
        a_sq = jnp.zeros((HEAD, HEAD), F32)
        a_in = jnp.zeros((HEAD, HEAD), F32)
        for d, state in enumerate((s0, s1, s2, s3)):
            grow = growth[behind(d), r, :]
            for j in range(hq):
                _, c = head_at(behind(d), hq, j)
                a = intra[r, c] + nn(q[r, c], state[j, 0:HEAD, :]) * grow[:, j : j + 1]
                att[r, c] = a
                a_sq = a_sq + a * a
                a_in = a_in + a * dscaled[r, c]
        sq[r, :] = a_sq
        inn[r, :] = a_in
    ones = jnp.ones((8, HEAD), F32)
    a = nt(ones, sq[...], lax.Precision.HIGHEST)
    b = nt(ones, inn[...], lax.Precision.HIGHEST)
    sums[...] = jnp.where(lax.broadcasted_iota(jnp.int32, (8, BLOCK), 0) == 0, a, b)


def dattn_body(heads, channels, att, dscaled, turned, gain, sum_a, sum_b, dattn, scale, p0, p1, p2, p3):
    hq = heads // TEAM
    total = sum_a[...] + sum_b[...]
    rs = lax.rsqrt(total[0:1, :] / channels + EPSILON)
    coef = total[1:2, :] * (rs * rs * rs) / channels
    scale[...] = jnp.concatenate([rs, coef, jnp.zeros((HEAD - 2, BLOCK), F32)], axis=0).T
    for d, out in ((1, p1), (2, p2), (3, p3), (0, p0)):
        for j in range(hq):
            h, c = head_at(ahead(d), hq, j)
            gsum = jnp.zeros((8, HEAD), F32)
            for i in range(BLOCK // HEAD):
                r = chunk(i)
                a = att[r, c]
                t = dscaled[r, c] * scale[r, 0:1]
                dattn[r, c] = (t - a * scale[r, 1:2]).astype(BF16)
                gsum = gsum + jnp.sum((t * a).reshape(HEAD // 8, 8, HEAD), axis=0)
            out[j, 0:HEAD, :] = nn(turned[h], dattn[:, c]).astype(BF16)
            out[j, HEAD:TALL, :] = term_rows(jnp.sum(gsum, axis=0, keepdims=True) / gain[:, c], 2)


def query_body(heads, k, v, dattn, row, col, growth, s0, s1, s2, s3, gate, att, dscaled, scale, query_grad, gate_grad):
    hq = heads // TEAM
    mask = masked(True)
    for slot, state in enumerate((s0, s1, s2, s3)):
        g = behind(slot)
        for j in range(hq):
            h, c = head_at(g, hq, j)
            line = row[pl.ds(h, 1), :]
            for i in range(2):
                d = dattn[piece(i), c]
                total = nt(d, state[j, 0:HEAD, :]) * growth[g, piece(i), j : j + 1]
                for m in range(i + 1):
                    table = jnp.exp(col[g, piece(i), j : j + 1] - line[:, piece(m)])
                    if m == i:
                        table = jnp.where(mask, table, 0.0)
                    dscores = (nt(d, v[piece(m), c]) * table).astype(BF16)
                    total = total + nn(dscores, k[piece(m), c])
                query_grad[piece(i), c] = total.astype(BF16)
            opened = jax.nn.sigmoid(gate[:, c].astype(F32))
            gate_grad[:, c] = (dscaled[:, c] * att[:, c] * scale[:, 0:1] * (1.0 - opened)).astype(BF16)


def key_value_body(heads, q, k, v, dattn, row, col, dk, dv):
    hq = heads // TEAM
    mask = masked(False)

    def one(g, _):
        for n in range(hq):
            h, c = head_at(g, hq, n)
            line = row[pl.ds(h, 1), :]
            for i in range(2):
                dkey = dvalue = None
                for m in range(i, 2):
                    table = jnp.exp(line[:, piece(m)] - col[g, piece(i), n : n + 1])
                    if m == i:
                        table = jnp.where(mask, table, 0.0)
                    probs = (nt(k[piece(i), c], q[piece(m), c]) * table).astype(BF16)
                    dscores = (nt(v[piece(i), c], dattn[piece(m), c]) * table).astype(BF16)
                    a = nn(dscores, q[piece(m), c])
                    b = nn(probs, dattn[piece(m), c])
                    dkey, dvalue = (a, b) if dkey is None else (dkey + a, dvalue + b)
                dk[piece(i), c] = dkey
                dv[piece(i), c] = dvalue
        return 0

    lax.fori_loop(0, TEAM, one, 0)


def final_body(heads, k, v, dk, dv, shrink, r0, r1, r2, r3, key_grad, value_grad, gain_grad, key_out, value_out, sems):
    hq = heads // TEAM
    w = hq * HEAD
    copies = []
    for d, state in enumerate((r0, r1, r2, r3)):
        g = behind(d)
        for j in range(hq):
            _, c = head_at(g, hq, j)
            fade = shrink[g, :, j : j + 1]
            after = state[j, 0:HEAD, :]
            key_out[d, :, chunk(j)] = (dk[:, c] + nt(v[:, c], after) * fade).astype(BF16)
            value_out[d, :, chunk(j)] = (dv[:, c] + nn(k[:, c], after) * fade).astype(BF16)
            gain_grad[:, c] = row_total(state, j)
        cols = pl.ds(pl.multiple_of(g * w, HEAD), w)
        for i, (src, dst) in enumerate(((key_out, key_grad), (value_out, value_grad))):
            copy = pltpu.make_async_copy(src.at[d], dst.at[:, cols], sems.at[i, d])
            copy.start()
            copies.append(copy)
    for copy in copies:
        copy.wait()


def around(x, d):
    n = lax.axis_size("ctx")
    return lax.ppermute(x, "ctx", [(i, i - i % TEAM + (i + d) % TEAM) for i in range(n)])


def across(x, k):
    n = lax.axis_size("ctx")
    return lax.ppermute(x, "ctx", [(i, (i + TEAM * k) % n) for i in range(n)])


def local(queries, keys, values, log_decay, gate, gain, grad_out):
    rows, width = queries.shape
    heads = width // HEAD
    hq = heads // TEAM
    tp = lax.axis_size("tp")
    n = lax.axis_size("ctx")
    groups = n // TEAM
    channels = width * tp
    bf = lambda *shape: jax.ShapeDtypeStruct(shape, BF16)
    f32 = lambda *shape: jax.ShapeDtypeStruct(shape, F32)
    swaps = tp == 2
    part = rows // 2
    small = 2 * heads * rows * HEAD * HEAD
    large = 2 * heads * rows * rows * HEAD
    packed = bf(hq, TALL, HEAD)
    plain = bf(hq, HEAD, HEAD)
    table = f32(TEAM, rows, HEAD)
    gain_row = gain.reshape(1, width)

    outs = call(
        functools.partial(local_states_body, heads, swaps),
        [keys, values, log_decay] + [grad_out] * swaps,
        [packed] * TEAM + [f32(EXTRA, rows)] + [bf(part, width)] * 2 * swaps,
        "local_states",
        [pltpu.VMEM((TEAM, rows, hq * HEAD), BF16)] * 2
        + [pltpu.SemaphoreType.DMA((2, TEAM))]
        + [pltpu.SemaphoreType.DMA((2,))] * swaps,
        small,
        [ANY, ANY, VMEM] + [ANY] * swaps,
        [VMEM] * (TEAM + 1) + [ANY, VMEM] * swaps,
    )
    parts, row = outs[:TEAM], outs[TEAM]
    slots = [parts[0]] + [around(parts[d], d) for d in range(1, TEAM)]
    if swaps:
        away, own = outs[TEAM + 1 :]
        got = lax.ppermute(away, "tp", [(0, 1), (1, 0)])
    else:
        every = lax.all_to_all(grad_out, "tp", split_axis=1, concat_axis=0, tiled=True)
        own, got = every[:part], every[part:]
    intra, col, growth, shrink = call(
        functools.partial(intra_body, heads),
        [queries, keys, values, row],
        [f32(rows, width), table, table, table],
        "intra",
        flops=2 * large,
    )
    total, edges = call(
        functools.partial(group_total_body, False, hq), slots, [packed, f32(hq, 8, HEAD)], "group_total"
    )
    far = [across(total, k) for k in range(1, groups)]
    entering = call(
        functools.partial(entering_body, False, hq, groups), [*slots, total, edges, *far], [plain] * TEAM, "entering"
    )
    entering = [entering[0]] + [around(entering[d], d) for d in range(1, TEAM)]
    dscaled, turned = call(
        functools.partial(dscaled_body, heads, swaps),
        [gate, own, got, gain_row, queries, row],
        [f32(rows, width), bf(heads, HEAD, rows)],
        "dscaled",
        flops=small,
    )
    att, sums = call(
        functools.partial(attention_body, heads),
        [queries, intra, dscaled, growth, *entering],
        [f32(rows, width), f32(8, rows)],
        "attention",
        [pltpu.VMEM((rows, HEAD), F32)] * 2,
        small,
    )
    if swaps:
        others = lax.ppermute(sums, "tp", [(0, 1), (1, 0)])
    else:
        others = lax.psum(sums, "tp") - sums
    dattn, scale, *parts = call(
        functools.partial(dattn_body, heads, channels),
        [att, dscaled, turned, gain_row, sums, others],
        [bf(rows, width), f32(rows, HEAD)] + [packed] * TEAM,
        "dattn",
        flops=small,
    )
    back = [parts[0]] + [around(parts[d], d) for d in range(1, TEAM)]
    query_grad, gate_grad = call(
        functools.partial(query_body, heads),
        [keys, values, dattn, row, col, growth, *entering, gate, att, dscaled, scale],
        [bf(rows, width), bf(rows, width)],
        "query",
        flops=2 * large + small,
    )
    (total,) = call(functools.partial(group_total_body, True, hq), [*back, edges], [packed], "group_total_back")
    far = [across(total, -k) for k in range(1, groups)]
    leaving = call(
        functools.partial(entering_body, True, hq, groups), [*back, total, edges, *far], [packed] * TEAM, "leaving"
    )
    leaving = [leaving[0]] + [around(leaving[d], d) for d in range(1, TEAM)]
    dk, dv = call(
        functools.partial(key_value_body, heads),
        [queries, keys, values, dattn, row, col],
        [f32(rows, width), f32(rows, width)],
        "key_value",
        flops=4 * large,
    )
    key_grad, value_grad, gain_grad = call(
        functools.partial(final_body, heads),
        [keys, values, dk, dv, shrink, *leaving],
        [bf(rows, width), bf(rows, width), f32(1, width)],
        "final",
        [pltpu.VMEM((TEAM, rows, hq * HEAD), BF16)] * 2 + [pltpu.SemaphoreType.DMA((2, TEAM))],
        2 * small,
        out_specs=[ANY, ANY, VMEM],
    )
    return query_grad, key_grad, value_grad, gate_grad, gain_grad.reshape(width)


def solution(mesh):
    return jax.shard_map(
        local,
        mesh=mesh,
        in_specs=(
            P("ctx", "tp"),
            P("ctx", "tp"),
            P("ctx", "tp"),
            P("tp", "ctx"),
            P("ctx", "tp"),
            P("tp"),
            P(("ctx", "tp"), None),
        ),
        out_specs=(P("ctx", "tp"), P("ctx", "tp"), P("ctx", "tp"), P("ctx", "tp"), P("tp")),
        check_vma=False,
    )
```

time: 403 us -> 105 us (0.26); the launches traced: 395 us -> 105 us
  matrix products: 86.7 us -> 0 us
  blocking collectives: 86.3 us -> 0 us
  waiting for transfers between devices: 108 us -> 26.7 us
  Pallas kernels: 0 us -> 47.9 us
  local copies, waits for them, and re-layouts: 51.3 us -> 5.54 us
  other arithmetic: 42.6 us -> 0 us
  starting transfers between devices: 4.9 us -> 23.8 us
  between operations: 14.7 us -> 1 us
    all_gather x2 -> x0, waiting for transfers between devices: 108 us -> none  [carried_in(): gathered = jax.tree.map(lambda a: lax.all_gather(a, axis), part)]
    dot_general x12 -> x0, matrix products: 86.7 us -> none  [the longest x1 9.59 us: local(): jnp.einsum('blhd,bmhd->bhlm', query_blocks, key_blocks, preferred_element...]
    psum x3 -> x0, blocking collectives: 63 us -> none  [the longest x1 53 us: local(): gain_grad = lax.psum(gain_part, 'ctx')]
    pallas_call x0 -> x12, Pallas kernels: none -> 47.9 us  [call(): pl.pallas_call(body, in_specs=in_specs or [VMEM] * len(inputs), out_specs...]
    ppermute x0 -> x20, waiting for transfers between devices: none -> 26.7 us  [the longest x6 12.8 us: across(): return lax.ppermute(x, 'ctx', [(i, (i + TEAM * k) % n) for i in range(n)])]
    ppermute x0 -> x20, starting transfers between devices: none -> 23.8 us  [the longest x6 10.4 us: across(): return lax.ppermute(x, 'ctx', [(i, (i + TEAM * k) % n) for i in range(n)])]
    all_gather x1 -> x0, blocking collectives: 23.3 us -> none  [carried_in(): gathered = jax.tree.map(lambda a: lax.all_gather(a, axis), part)]
    add x15 -> x0, other arithmetic: 21.7 us -> none  [link_states(): later[0][:, None, None] * earlier[1] + later[1]]
  transfers between devices with their start and end apart: 3 -> 20, of which waited for: 2 -> 9; matrix products, arithmetic and copies ran while one was open for 22% -> 0% of each run, Pallas kernels for 0% -> 29%
where the time goes in v3:
time: 105 us
  Pallas kernels  47.9 us (46%)
  waiting for transfers between devices  26.7 us (25%)
  starting transfers between devices  23.8 us (23%)
  local copies, waits for them, and re-layouts  5.54 us (5%)
    pallas_call x12, Pallas kernels, call(): pl.pallas_call(body, in_specs=in_specs or [VMEM] * len(inputs), out_specs...  47.9 us
    ppermute x6, waiting for transfers between devices, across(): return lax.ppermute(x, 'ctx', [(i, (i + TEAM * k) % n) for i in range(n)])  12.8 us
    ppermute x12, waiting for transfers between devices, around(): lax.ppermute(x, 'ctx', [(i, i - i % TEAM + (i + d) % TEAM) for i in range...  10.7 us
    ppermute x6, starting transfers between devices, across(): return lax.ppermute(x, 'ctx', [(i, (i + TEAM * k) % n) for i in range(n)])  10.4 us
    ppermute x12, starting transfers between devices, around(): lax.ppermute(x, 'ctx', [(i, i - i % TEAM + (i + d) % TEAM) for i in range...  9.88 us
    unnamed x18, local copies, waits for them, and re-layouts  5.54 us
    ppermute x1, waiting for transfers between devices, local(): others = lax.ppermute(sums, 'tp', [(0, 1), (1, 0)])  3.2 us
    ppermute x1, starting transfers between devices, local(): got = lax.ppermute(away, 'tp', [(0, 1), (1, 0)])  3.01 us
  transfers between devices with their start and end apart: 20, of which 9 were waited for; matrix products, arithmetic and copies ran while one was open for 0% of the time, Pallas kernels for 29%

profile of v3, /device:TPU:0, one launch (start us, length us, event | category | flops | bytes accessed | tf_op | source)
XLA Modules:
  0.0 105.0 jit_solution(16413009015430482960)
XLA Ops:
  0.6 1.6 %copy-done = bf16[512,2048]{1,0:T(8,128)(2,1)S(1)} copy-done((bf16[512,2048]{1,0:T(8,128)(2,1)S(1)}, bf16[512,2048]{1,0:T(8,128)(2,1)}, u32[]{:S(2)}) %copy-start) | copy-done | bytes 2097176
  2.2 1.6 %copy-done.2 = bf16[512,2048]{1,0:T(8,128)(2,1)S(1)} copy-done((bf16[512,2048]{1,0:T(8,128)(2,1)S(1)}, bf16[512,2048]{1,0:T(8,128)(2,1)}, u32[]{:S(2)}) %copy-start.2) | copy-done | bytes 2097176
  3.8 1.6 %copy-done.6 = bf16[256,4096]{1,0:T(8,128)(2,1)S(1)} copy-done((bf16[256,4096]{1,0:T(8,128)(2,1)S(1)}, bf16[256,4096]{1,0:T(8,128)(2,1)}, u32[]{:S(2)}) %copy-start.6) | copy-done | bytes 2097176
  6.2 4.6 %local_states.1 = (bf16[4,144,128]{2,1,0:T(8,128)(2,1)S(1)}, bf16[4,144,128]{2,1,0:T(8,128)(2,1)S(1)}, bf16[4,144,128]{2,1,0:T(8,128)(2,1)S(1)}, bf16[4,144,128]...) custom-call(bf16[512,2048]{1,0:T(8,128)(2,1)S(1)} %copy-done, ...), custom_call_target="tpu_custom_call" | custom-call | flops 268435456 | bytes 9043968 | tf_op jit(solution)/shard_map/local_states/pallas_call | solution.py:88
  10.8 3.0 %collective-permute-start = (bf16[256,2048]{1,0:T(8,128)(2,1)S(1)}, bf16[256,2048]{1,0:T(8,128)(2,1)S(1)}, u32[]{:S(2)}, u32[]{:S(2)}) collective-permute-start(bf16[256,2048]{1,0:T(8,128)(2,1)S(1)} %get-tuple-element.46), channel_id=1, source_target_pairs={{0,1},{1,0},{2,3},{3,2},{4,5},{5,4},{6,7},{7,6},{8,9},{9,8},{10,11... | collective-permute-start | bytes 3145736 | tf_op jit(solution)/shard_map/ppermute | solution.py:442
  13.8 1.6 %collective-permute-start.2 = (bf16[4,144,128]{2,1,0:T(8,128)(2,1)S(1)}, bf16[4,144,128]{2,1,0:T(8,128)(2,1)S(1)}, u32[]{:S(2)}, u32[]{:S(2)}) collective-permute-start(bf16[4,144,128]{2,1,0:T(8,128)(2,1)S(1)} %get-tuple-element.51), channel_id=1, source_target_pairs={{0,4},{2,6},{4,0},{6,2},{8,12},{10,14},{12,8},{14,10},{16,20},{18,... | collective-permute-start | bytes 442376 | tf_op jit(solution)/shard_map/ppermute | solution.py:399
  16.8 2.6 %collective-permute-done.1.a1.refs_1_ = bf16[4,144,128]{2,1,0:T(8,128)(2,1)S(1)} collective-permute-done((bf16[4,144,128]{2,1,0:T(8,128)(2,1)S(1)}, bf16[4,144,128]{2,1,0:T(8,128)(2,1)S(1)}, u32[]{:S(2)}, u32[]{:S(2)}) %collective-permute-start.1) | collective-permute-done | bytes 147488 | tf_op jit(solution)/shard_map/ppermute | solution.py:399
  20.5 1.7 %collective-permute-done.3.a3.refs_3_ = bf16[4,144,128]{2,1,0:T(8,128)(2,1)S(1)} collective-permute-done((bf16[4,144,128]{2,1,0:T(8,128)(2,1)S(1)}, bf16[4,144,128]{2,1,0:T(8,128)(2,1)S(1)}, u32[]{:S(2)}, u32[]{:S(2)}) %collective-permute-start.3) | collective-permute-done | bytes 147488 | tf_op jit(solution)/shard_map/ppermute | solution.py:399
  22.3 3.7 %collective-permute-start.6 = (bf16[4,144,128]{2,1,0:T(8,128)(2,1)S(1)}, bf16[4,144,128]{2,1,0:T(8,128)(2,1)S(1)}, u32[]{:S(2)}, u32[]{:S(2)}) collective-permute-start(bf16[4,144,128]{2,1,0:T(8,128)(2,1)S(1)} %get-tuple-element.53.refs_4_), channel_id=1, source_target_pairs={{0,24},{2,26},{4,28},{6,30},{8,0},{10,2},{12,4},{14,6},{16,8},{18,... | collective-permute-start | bytes 442376 | tf_op jit(solution)/shard_map/ppermute | solution.py:404
  27.0 3.2 %collective-permute-done.6.refs_8_ = bf16[4,144,128]{2,1,0:T(8,128)(2,1)S(1)} collective-permute-done((bf16[4,144,128]{2,1,0:T(8,128)(2,1)S(1)}, bf16[4,144,128]{2,1,0:T(8,128)(2,1)S(1)}, u32[]{:S(2)}, u32[]{:S(2)}) %collective-permute-start.6) | collective-permute-done | bytes 147488 | tf_op jit(solution)/shard_map/ppermute | solution.py:404
  30.2 9.6 %collective-permute-done.5.refs_7_ = bf16[4,144,128]{2,1,0:T(8,128)(2,1)S(1)} collective-permute-done((bf16[4,144,128]{2,1,0:T(8,128)(2,1)S(1)}, bf16[4,144,128]{2,1,0:T(8,128)(2,1)S(1)}, u32[]{:S(2)}, u32[]{:S(2)}) %collective-permute-start.5) | collective-permute-done | bytes 147488 | tf_op jit(solution)/shard_map/ppermute | solution.py:404
  42.1 6.9 %intra.1 = (f32[512,2048]{1,0:T(8,128)S(1)}, f32[4,512,128]{2,1,0:T(8,128)S(1)}, f32[4,512,128]{2,1,0:T(8,128)S(1)}, f32[4,512,128]{2,1,0:T(8,128)S(1)}) custom-call(bf16[512,2048]{1,0:T(8,128)(2,1)S(1)} %copy-done.5, bf16[512,2048]{1,0:T(8,128)(2,1)S(1)} %copy-done.1, bf16[512,2048]{1,0:T(8,128)(2,1)S(1)} %copy-done.2, f32[16,512]{1,0:T(8,128)S(1)} %get-tuple-element.43.row), custom_call_target="tpu_custom_call" | custom-call | flops 2147483648 | bytes 13664256 | tf_op jit(solution)/shard_map/intra/pallas_call | solution.py:88
  49.1 2.9 %dscaled.1 = (f32[512,2048]{1,0:T(8,128)S(1)}, bf16[16,128,512]{2,1,0:T(8,128)(2,1)S(1)}) custom-call(bf16[512,2048]{1,0:T(8,128)(2,1)S(1)} %copy-done.4, bf16[256,2048]{1,0:T(8,128)(2,1)S(1)} %get-tuple-element.45.own, bf16[256,2048]{1,0:T(8,128)(2,1)S(1)} %collective-permute-done.got, f32[1,2048]{1,0:T(1,128)S(1)} %bitcast.2, ...), custom_call_target="tpu_custom_call" | custom-call | flops 268435456 | bytes 12623872 | tf_op jit(solution)/shard_map/dscaled/pallas_call | solution.py:88
  52.0 3.0 %attention.1 = (f32[512,2048]{1,0:T(8,128)S(1)}, f32[8,512]{1,0:T(8,128)S(1)}) custom-call(bf16[512,2048]{1,0:T(8,128)(2,1)S(1)} %copy-done.5, f32[512,2048]{1,0:T(8,128)S(1)} %get-tuple-element.44.intra, f32[512,2048]{1,0:T(8,128)S(1)} %get-tuple-element.47.dscaled, f32[4,512,128]{2,1,0:T(8,128)S(1)} %get-tuple-element.48.growth, ...), custom_call_target="tpu_custom_call" | custom-call | flops 268435456 | bytes 16269312 | tf_op jit(solution)/shard_map/attention/pallas_call | solution.py:88
  55.6 3.2 %collective-permute-done.10.sum_b = f32[8,512]{1,0:T(8,128)S(1)} collective-permute-done((f32[8,512]{1,0:T(8,128)S(1)}, f32[8,512]{1,0:T(8,128)S(1)}, u32[]{:S(2)}, u32[]{:S(2)}) %collective-permute-start.10) | collective-permute-done | bytes 16416 | tf_op jit(solution)/shard_map/ppermute | solution.py:477
  58.8 4.1 %dattn.1 = (bf16[512,2048]{1,0:T(8,128)(2,1)S(1)}, f32[512,128]{1,0:T(8,128)S(1)}, bf16[4,144,128]{2,1,0:T(8,128)(2,1)S(1)}, bf16[4,144,128]{2,1,0:T(8,128)(2,1)...) custom-call(f32[512,2048]{1,0:T(8,128)S(1)} %get-tuple-element.59.att, ...), custom_call_target="tpu_custom_call" | custom-call | flops 268435456 | bytes 13475840 | tf_op jit(solution)/shard_map/dattn/pallas_call | solution.py:88
  62.9 1.8 %collective-permute-start.12 = (bf16[4,144,128]{2,1,0:T(8,128)(2,1)S(1)}, bf16[4,144,128]{2,1,0:T(8,128)(2,1)S(1)}, u32[]{:S(2)}, u32[]{:S(2)}) collective-permute-start(bf16[4,144,128]{2,1,0:T(8,128)(2,1)S(1)} %get-tuple-element.71), channel_id=1, source_target_pairs={{0,4},{2,6},{4,0},{6,2},{8,12},{10,14},{12,8},{14,10},{16,20},{18,... | collective-permute-start | bytes 442376 | tf_op jit(solution)/shard_map/ppermute | solution.py:399
  66.1 2.4 %collective-permute-done.11.a1.refs_1_ = bf16[4,144,128]{2,1,0:T(8,128)(2,1)S(1)} collective-permute-done((bf16[4,144,128]{2,1,0:T(8,128)(2,1)S(1)}, bf16[4,144,128]{2,1,0:T(8,128)(2,1)S(1)}, u32[]{:S(2)}, u32[]{:S(2)}) %collective-permute-start.11) | collective-permute-done | bytes 147488 | tf_op jit(solution)/shard_map/ppermute | solution.py:399
  69.7 1.8 %collective-permute-done.13.a3.refs_3_ = bf16[4,144,128]{2,1,0:T(8,128)(2,1)S(1)} collective-permute-done((bf16[4,144,128]{2,1,0:T(8,128)(2,1)S(1)}, bf16[4,144,128]{2,1,0:T(8,128)(2,1)S(1)}, u32[]{:S(2)}, u32[]{:S(2)}) %collective-permute-start.13) | collective-permute-done | bytes 147488 | tf_op jit(solution)/shard_map/ppermute | solution.py:399
  72.5 2.0 %collective-permute-start.15 = (bf16[4,144,128]{2,1,0:T(8,128)(2,1)S(1)}, bf16[4,144,128]{2,1,0:T(8,128)(2,1)S(1)}, u32[]{:S(2)}, u32[]{:S(2)}) collective-permute-start(bf16[4,144,128]{2,1,0:T(8,128)(2,1)S(1)} %group_total_back.1.refs_4_), channel_id=1, source_target_pairs={{0,16},{2,18},{4,20},{6,22},{8,24},{10,26},{12,28},{14,30},{16,0},... | collective-permute-start | bytes 442376 | tf_op jit(solution)/shard_map/ppermute | solution.py:404
  74.5 2.8 %collective-permute-start.14 = (bf16[4,144,128]{2,1,0:T(8,128)(2,1)S(1)}, bf16[4,144,128]{2,1,0:T(8,128)(2,1)S(1)}, u32[]{:S(2)}, u32[]{:S(2)}) collective-permute-start(bf16[4,144,128]{2,1,0:T(8,128)(2,1)S(1)} %group_total_back.1.refs_4_), channel_id=1, source_target_pairs={{0,24},{2,26},{4,28},{6,30},{8,0},{10,2},{12,4},{14,6},{16,8},{18,... | collective-permute-start | bytes 442376 | tf_op jit(solution)/shard_map/ppermute | solution.py:404
  77.4 10.0 %key_value.1 = (f32[512,2048]{1,0:T(8,128)S(1)}, f32[512,2048]{1,0:T(8,128)S(1)}) custom-call(bf16[512,2048]{1,0:T(8,128)(2,1)S(1)} %copy-done.5, bf16[512,2048]{1,0:T(8,128)(2,1)S(1)} %copy-done.1, bf16[512,2048]{1,0:T(8,128)(2,1)S(1)} %copy-done.3, bf16[512,2048]{1,0:T(8,128)(2,1)S(1)} %get-tuple-element.62.dattn, f32[16,512]{1,0:T(8,128)S(1)} %get-tuple-element.43.row, ...), custom_call_target="tpu_custom_call" | custom-call | flops 4294967296 | bytes 17858560 | tf_op jit(solution)/shard_map/key_value/pallas_call | solution.py:88
  89.8 10.1 %query.1 = (bf16[512,2048]{1,0:T(8,128)(2,1)}, bf16[512,2048]{1,0:T(8,128)(2,1)}) custom-call(bf16[512,2048]{1,0:T(8,128)(2,1)S(1)} %copy-done.1, bf16[512,2048]{1,0:T(8,128)(2,1)S(1)} %copy-done.3, bf16[512,2048]{1,0:T(8,128)(2,1)S(1)} %get-tuple-element.62.dattn, f32[16,512]{1,0:T(8,128)S(1)} %get-tuple-element.43.row, ...), custom_call_target="tpu_custom_call" | custom-call | flops 2415919104 | bytes 23887872 | tf_op jit(solution)/shard_map/query/pallas_call | solution.py:88
  100.0 4.8 %final.1 = (bf16[512,2048]{1,0:T(8,128)(2,1)}, bf16[512,2048]{1,0:T(8,128)(2,1)}, f32[1,2048]{1,0:T(1,128)}) custom-call(bf16[512,2048]{1,0:T(8,128)(2,1)S(1)} %copy-done.1, bf16[512,2048]{1,0:T(8,128)(2,1)S(1)} %copy-done.3, f32[512,2048]{1,0:T(8,128)S(1)} %get-tuple-element.66.dk, f32[512,2048]{1,0:T(8,128)S(1)} %get-tuple-element.67.dv, ...), custom_call_target="tpu_custom_call" | custom-call | flops 536870912 | bytes 18423808 | tf_op jit(solution)/shard_map/final/pallas_call | solution.py:88
  (46 shorter events, 13.5 us)
Async XLA Ops:
  6.2 35.9 %copy-start.1 = (bf16[512,2048]{1,0:T(8,128)(2,1)S(1)}, bf16[512,2048]{1,0:T(8,128)(2,1)}, u32[]{:S(2)}) copy-start(bf16[512,2048]{1,0:T(8,128)(2,1)} %k.7) | copy-start | bytes 6291460
  6.2 35.9 %copy-start.5 = (bf16[512,2048]{1,0:T(8,128)(2,1)S(1)}, bf16[512,2048]{1,0:T(8,128)(2,1)}, u32[]{:S(2)}) copy-start(bf16[512,2048]{1,0:T(8,128)(2,1)} %q.7) | copy-start | bytes 6291460
  10.8 38.2 %collective-permute-start = (bf16[256,2048]{1,0:T(8,128)(2,1)S(1)}, bf16[256,2048]{1,0:T(8,128)(2,1)S(1)}, u32[]{:S(2)}, u32[]{:S(2)}) collective-permute-start(bf16[256,2048]{1,0:T(8,128)(2,1)S(1)} %get-tuple-element.46), channel_id=1, source_target_pairs={{0,1},{1,0},{2,3},{3,2},{4,5},{5,4},{6,7},{7,6},{8,9},{9,8},{10,11... | collective-permute-start | bytes 3145736 | tf_op jit(solution)/shard_map/ppermute | solution.py:442
  13.8 5.6 %collective-permute-start.1 = (bf16[4,144,128]{2,1,0:T(8,128)(2,1)S(1)}, bf16[4,144,128]{2,1,0:T(8,128)(2,1)S(1)}, u32[]{:S(2)}, u32[]{:S(2)}) collective-permute-start(bf16[4,144,128]{2,1,0:T(8,128)(2,1)S(1)} %get-tuple-element.50), channel_id=1, source_target_pairs={{0,2},{2,4},{4,6},{6,0},{8,10},{10,12},{12,14},{14,8},{16,18},{18,... | collective-permute-start | bytes 442376 | tf_op jit(solution)/shard_map/ppermute | solution.py:399
  13.8 6.7 %collective-permute-start.2 = (bf16[4,144,128]{2,1,0:T(8,128)(2,1)S(1)}, bf16[4,144,128]{2,1,0:T(8,128)(2,1)S(1)}, u32[]{:S(2)}, u32[]{:S(2)}) collective-permute-start(bf16[4,144,128]{2,1,0:T(8,128)(2,1)S(1)} %get-tuple-element.51), channel_id=1, source_target_pairs={{0,4},{2,6},{4,0},{6,2},{8,12},{10,14},{12,8},{14,10},{16,20},{18,... | collective-permute-start | bytes 442376 | tf_op jit(solution)/shard_map/ppermute | solution.py:399
  15.3 6.8 %collective-permute-start.3 = (bf16[4,144,128]{2,1,0:T(8,128)(2,1)S(1)}, bf16[4,144,128]{2,1,0:T(8,128)(2,1)S(1)}, u32[]{:S(2)}, u32[]{:S(2)}) collective-permute-start(bf16[4,144,128]{2,1,0:T(8,128)(2,1)S(1)} %get-tuple-element.52), channel_id=1, source_target_pairs={{0,6},{2,0},{4,2},{6,4},{8,14},{10,8},{12,10},{14,12},{16,22},{18,... | collective-permute-start | bytes 442376 | tf_op jit(solution)/shard_map/ppermute | solution.py:399
  22.3 7.9 %collective-permute-start.6 = (bf16[4,144,128]{2,1,0:T(8,128)(2,1)S(1)}, bf16[4,144,128]{2,1,0:T(8,128)(2,1)S(1)}, u32[]{:S(2)}, u32[]{:S(2)}) collective-permute-start(bf16[4,144,128]{2,1,0:T(8,128)(2,1)S(1)} %get-tuple-element.53.refs_4_), channel_id=1, source_target_pairs={{0,24},{2,26},{4,28},{6,30},{8,0},{10,2},{12,4},{14,6},{16,8},{18,... | collective-permute-start | bytes 442376 | tf_op jit(solution)/shard_map/ppermute | solution.py:404
  26.0 13.8 %collective-permute-start.5 = (bf16[4,144,128]{2,1,0:T(8,128)(2,1)S(1)}, bf16[4,144,128]{2,1,0:T(8,128)(2,1)S(1)}, u32[]{:S(2)}, u32[]{:S(2)}) collective-permute-start(bf16[4,144,128]{2,1,0:T(8,128)(2,1)S(1)} %get-tuple-element.53.refs_4_), channel_id=1, source_target_pairs={{0,16},{2,18},{4,20},{6,22},{8,24},{10,26},{12,28},{14,30},{16,0},... | collective-permute-start | bytes 442376 | tf_op jit(solution)/shard_map/ppermute | solution.py:404
  26.0 13.8 %collective-permute-start.4 = (bf16[4,144,128]{2,1,0:T(8,128)(2,1)S(1)}, bf16[4,144,128]{2,1,0:T(8,128)(2,1)S(1)}, u32[]{:S(2)}, u32[]{:S(2)}) collective-permute-start(bf16[4,144,128]{2,1,0:T(8,128)(2,1)S(1)} %get-tuple-element.53.refs_4_), channel_id=1, source_target_pairs={{0,8},{2,10},{4,12},{6,14},{8,16},{10,18},{12,20},{14,22},{16,24},... | collective-permute-start | bytes 442376 | tf_op jit(solution)/shard_map/ppermute | solution.py:404
  40.3 11.7 %collective-permute-start.7 = (bf16[4,128,128]{2,1,0:T(8,128)(2,1)S(1)}, bf16[4,128,128]{2,1,0:T(8,128)(2,1)S(1)}, u32[]{:S(2)}, u32[]{:S(2)}) collective-permute-start(bf16[4,128,128]{2,1,0:T(8,128)(2,1)S(1)} %get-tuple-element.56), channel_id=1, source_target_pairs={{0,2},{2,4},{4,6},{6,0},{8,10},{10,12},{12,14},{14,8},{16,18},{18,... | collective-permute-start | bytes 393224 | tf_op jit(solution)/shard_map/ppermute | solution.py:399
  40.3 11.6 %collective-permute-start.8 = (bf16[4,128,128]{2,1,0:T(8,128)(2,1)S(1)}, bf16[4,128,128]{2,1,0:T(8,128)(2,1)S(1)}, u32[]{:S(2)}, u32[]{:S(2)}) collective-permute-start(bf16[4,128,128]{2,1,0:T(8,128)(2,1)S(1)} %get-tuple-element.57), channel_id=1, source_target_pairs={{0,4},{2,6},{4,0},{6,2},{8,12},{10,14},{12,8},{14,10},{16,20},{18,... | collective-permute-start | bytes 393224 | tf_op jit(solution)/shard_map/ppermute | solution.py:399
  40.6 11.4 %collective-permute-start.9 = (bf16[4,128,128]{2,1,0:T(8,128)(2,1)S(1)}, bf16[4,128,128]{2,1,0:T(8,128)(2,1)S(1)}, u32[]{:S(2)}, u32[]{:S(2)}) collective-permute-start(bf16[4,128,128]{2,1,0:T(8,128)(2,1)S(1)} %get-tuple-element.58), channel_id=1, source_target_pairs={{0,6},{2,0},{4,2},{6,4},{8,14},{10,8},{12,10},{14,12},{16,22},{18,... | collective-permute-start | bytes 393224 | tf_op jit(solution)/shard_map/ppermute | solution.py:399
  42.1 6.9 %copy-start.8 = (f32[2048]{0:T(1024)S(1)}, f32[2048]{0:T(1024)}, u32[]{:S(2)}) copy-start(f32[2048]{0:T(1024)} %param.12) | copy-start | bytes 24580
  55.0 3.8 %collective-permute-start.10 = (f32[8,512]{1,0:T(8,128)S(1)}, f32[8,512]{1,0:T(8,128)S(1)}, u32[]{:S(2)}, u32[]{:S(2)}) collective-permute-start(f32[8,512]{1,0:T(8,128)S(1)} %get-tuple-element.61.sum_a), channel_id=1, source_target_pairs={{0,1},{1,0},{2,3},{3,2},{4,5},{5,4},{6,7},{7,6},{8,9},{9,8},{10,11... | collective-permute-start | bytes 49160 | tf_op jit(solution)/shard_map/ppermute | solution.py:477
  58.8 18.6 %copy-start.3 = (bf16[512,2048]{1,0:T(8,128)(2,1)S(1)}, bf16[512,2048]{1,0:T(8,128)(2,1)}, u32[]{:S(2)}) copy-start(bf16[512,2048]{1,0:T(8,128)(2,1)} %v.7) | copy-start | bytes 6291460
  62.9 5.6 %collective-permute-start.11 = (bf16[4,144,128]{2,1,0:T(8,128)(2,1)S(1)}, bf16[4,144,128]{2,1,0:T(8,128)(2,1)S(1)}, u32[]{:S(2)}, u32[]{:S(2)}) collective-permute-start(bf16[4,144,128]{2,1,0:T(8,128)(2,1)S(1)} %get-tuple-element.70), channel_id=1, source_target_pairs={{0,2},{2,4},{4,6},{6,0},{8,10},{10,12},{12,14},{14,8},{16,18},{18,... | collective-permute-start | bytes 442376 | tf_op jit(solution)/shard_map/ppermute | solution.py:399
  62.9 6.7 %collective-permute-start.12 = (bf16[4,144,128]{2,1,0:T(8,128)(2,1)S(1)}, bf16[4,144,128]{2,1,0:T(8,128)(2,1)S(1)}, u32[]{:S(2)}, u32[]{:S(2)}) collective-permute-start(bf16[4,144,128]{2,1,0:T(8,128)(2,1)S(1)} %get-tuple-element.71), channel_id=1, source_target_pairs={{0,4},{2,6},{4,0},{6,2},{8,12},{10,14},{12,8},{14,10},{16,20},{18,... | collective-permute-start | bytes 442376 | tf_op jit(solution)/shard_map/ppermute | solution.py:399
  64.7 6.7 %collective-permute-start.13 = (bf16[4,144,128]{2,1,0:T(8,128)(2,1)S(1)}, bf16[4,144,128]{2,1,0:T(8,128)(2,1)S(1)}, u32[]{:S(2)}, u32[]{:S(2)}) collective-permute-start(bf16[4,144,128]{2,1,0:T(8,128)(2,1)S(1)} %get-tuple-element.72), channel_id=1, source_target_pairs={{0,6},{2,0},{4,2},{6,4},{8,14},{10,8},{12,10},{14,12},{16,22},{18,... | collective-permute-start | bytes 442376 | tf_op jit(solution)/shard_map/ppermute | solution.py:399
  71.6 15.8 %collective-permute-start.16 = (bf16[4,144,128]{2,1,0:T(8,128)(2,1)S(1)}, bf16[4,144,128]{2,1,0:T(8,128)(2,1)S(1)}, u32[]{:S(2)}, u32[]{:S(2)}) collective-permute-start(bf16[4,144,128]{2,1,0:T(8,128)(2,1)S(1)} %group_total_back.1.refs_4_), channel_id=1, source_target_pairs={{0,8},{2,10},{4,12},{6,14},{8,16},{10,18},{12,20},{14,22},{16,24},... | collective-permute-start | bytes 442376 | tf_op jit(solution)/shard_map/ppermute | solution.py:404
  72.5 14.9 %collective-permute-start.15 = (bf16[4,144,128]{2,1,0:T(8,128)(2,1)S(1)}, bf16[4,144,128]{2,1,0:T(8,128)(2,1)S(1)}, u32[]{:S(2)}, u32[]{:S(2)}) collective-permute-start(bf16[4,144,128]{2,1,0:T(8,128)(2,1)S(1)} %group_total_back.1.refs_4_), channel_id=1, source_target_pairs={{0,16},{2,18},{4,20},{6,22},{8,24},{10,26},{12,28},{14,30},{16,0},... | collective-permute-start | bytes 442376 | tf_op jit(solution)/shard_map/ppermute | solution.py:404
  74.5 12.9 %collective-permute-start.14 = (bf16[4,144,128]{2,1,0:T(8,128)(2,1)S(1)}, bf16[4,144,128]{2,1,0:T(8,128)(2,1)S(1)}, u32[]{:S(2)}, u32[]{:S(2)}) collective-permute-start(bf16[4,144,128]{2,1,0:T(8,128)(2,1)S(1)} %group_total_back.1.refs_4_), channel_id=1, source_target_pairs={{0,24},{2,26},{4,28},{6,30},{8,0},{10,2},{12,4},{14,6},{16,8},{18,... | collective-permute-start | bytes 442376 | tf_op jit(solution)/shard_map/ppermute | solution.py:404
  88.0 12.0 %collective-permute-start.17 = (bf16[4,144,128]{2,1,0:T(8,128)(2,1)S(1)}, bf16[4,144,128]{2,1,0:T(8,128)(2,1)S(1)}, u32[]{:S(2)}, u32[]{:S(2)}) collective-permute-start(bf16[4,144,128]{2,1,0:T(8,128)(2,1)S(1)} %get-tuple-element.74), channel_id=1, source_target_pairs={{0,2},{2,4},{4,6},{6,0},{8,10},{10,12},{12,14},{14,8},{16,18},{18,... | collective-permute-start | bytes 442376 | tf_op jit(solution)/shard_map/ppermute | solution.py:399
  88.1 11.9 %collective-permute-start.18 = (bf16[4,144,128]{2,1,0:T(8,128)(2,1)S(1)}, bf16[4,144,128]{2,1,0:T(8,128)(2,1)S(1)}, u32[]{:S(2)}, u32[]{:S(2)}) collective-permute-start(bf16[4,144,128]{2,1,0:T(8,128)(2,1)S(1)} %get-tuple-element.75), channel_id=1, source_target_pairs={{0,4},{2,6},{4,0},{6,2},{8,12},{10,14},{12,8},{14,10},{16,20},{18,... | collective-permute-start | bytes 442376 | tf_op jit(solution)/shard_map/ppermute | solution.py:399
  89.5 10.5 %collective-permute-start.19 = (bf16[4,144,128]{2,1,0:T(8,128)(2,1)S(1)}, bf16[4,144,128]{2,1,0:T(8,128)(2,1)S(1)}, u32[]{:S(2)}, u32[]{:S(2)}) collective-permute-start(bf16[4,144,128]{2,1,0:T(8,128)(2,1)S(1)} %get-tuple-element.76), channel_id=1, source_target_pairs={{0,6},{2,0},{4,2},{6,4},{8,14},{10,8},{12,10},{14,12},{16,22},{18,... | collective-permute-start | bytes 442376 | tf_op jit(solution)/shard_map/ppermute | solution.py:399
  (5 other events, 12.5 us)

commit v4 on v3

v4 whole, which is shorter than its diff:
```python
import functools

import jax
import jax.numpy as jnp
from jax import lax
from jax.experimental import pallas as pl
from jax.experimental.pallas import tpu as pltpu
from jax.sharding import PartitionSpec as P

HEAD = 128
BLOCK = 512
WIDE = 2 * HEAD
TEAM = 4
SIDE = 8
EXTRA = 16
EPSILON = 1e-06
F32 = jnp.float32
BF16 = jnp.bfloat16
GRANT = 12 * 1024 * 1024
VMEM = pl.BlockSpec(memory_space=pltpu.VMEM)
HBM = pl.BlockSpec(memory_space=pltpu.HBM)
ANY = pl.BlockSpec(memory_space=pl.ANY)


def nt(a, b, precision=None):
    return lax.dot_general(a, b, (((1,), (1,)), ((), ())), preferred_element_type=F32, precision=precision)


def nn(a, b):
    return lax.dot_general(a, b, (((1,), (0,)), ((), ())), preferred_element_type=F32)


def chunk(i):
    return slice(i * HEAD, (i + 1) * HEAD)


def split_terms(x, count):
    terms = []
    for _ in range(count):
        term = x.astype(BF16)
        terms.append(term)
        x = x - term.astype(F32)
    return terms


def read_wide(ref, hq):
    base = hq * HEAD
    return [
        (ref[chunk(j), :], ref[base + j : base + j + 1, :], ref[base + TEAM + j : base + TEAM + j + 1, :])
        for j in range(hq)
    ]


def write_wide(ref, hq, items):
    base = hq * HEAD
    at = lax.broadcasted_iota(jnp.int32, (SIDE, HEAD), 0)
    side = jnp.zeros((SIDE, HEAD), F32)
    for j, (term, edge, gain) in enumerate(items):
        ref[chunk(j), :] = term
        side = jnp.where(at == j, edge, side)
        side = jnp.where(at == TEAM + j, gain, side)
    ref[base : base + SIDE, :] = side


def read_narrow(ref, hq):
    base = hq * HEAD
    side = ref[base : base + EXTRA, :].astype(F32)
    row = lambda i: side[i : i + 1, :] + side[i + 1 : i + 2, :]
    return [(ref[chunk(j), :].astype(F32), row(2 * j), row(2 * TEAM + 2 * j)) for j in range(hq)]


def write_narrow(ref, hq, items):
    base = hq * HEAD
    at = lax.broadcasted_iota(jnp.int32, (EXTRA, HEAD), 0)
    side = jnp.zeros((EXTRA, HEAD), F32)
    for j, (term, edge, gain) in enumerate(items):
        ref[chunk(j), :] = term.astype(BF16)
        for first, value in ((2 * j, edge), (2 * TEAM + 2 * j, gain)):
            for i, part in enumerate(split_terms(value, 2)):
                side = jnp.where(at == first + i, part.astype(F32), side)
    ref[base : base + EXTRA, :] = side.astype(BF16)


def core():
    return lax.rem(lax.axis_index("ctx"), 2)


def pair():
    return lax.rem(lax.axis_index("ctx") // 2, 2)


def group():
    return lax.axis_index("ctx") // TEAM


def quarter_of(y, same):
    return 2 * y + (core() if same else 1 - core())


def head_at(quarter, hq, j):
    h = quarter * hq + j
    return h, pl.ds(pl.multiple_of(h * HEAD, HEAD), HEAD)


def transposed(x):
    eye = (
        lax.broadcasted_iota(jnp.int32, (HEAD, HEAD), 0) == lax.broadcasted_iota(jnp.int32, (HEAD, HEAD), 1)
    ).astype(BF16)
    return nt(eye, x)


def call(body, inputs, out_shape, name, scratch=(), flops=0, in_specs=None, out_specs=None, alias=None):
    nbytes = sum(x.size * x.dtype.itemsize for x in inputs)
    nbytes += sum(x.size * x.dtype.itemsize for x in out_shape)
    return pl.pallas_call(
        body,
        in_specs=in_specs or [VMEM] * len(inputs),
        out_specs=out_specs or [VMEM] * len(out_shape),
        out_shape=out_shape,
        scratch_shapes=list(scratch),
        input_output_aliases=alias or {},
        compiler_params=pltpu.CompilerParams(vmem_limit_bytes=GRANT),
        cost_estimate=pl.CostEstimate(flops=flops, bytes_accessed=nbytes, transcendentals=0),
        name=name,
    )(*inputs)


def joined(mine, other, mine_is_first, reverse):
    out = []
    for (a, ea, ga), (b, eb, gb) in zip(mine, other):
        near = mine_is_first if reverse else jnp.logical_not(mine_is_first)
        wa = jnp.where(near, 1.0, jnp.exp(eb))
        wb = jnp.where(near, jnp.exp(ea), 1.0)
        out.append((a * wa + b * wb, ea + eb, ga + gb))
    return out


def chip_total_body(reverse, hq, *refs):
    if reverse:
        keep, got, own, send = refs
    else:
        keep, got, _, own, send, _ = refs
    first = core() == 0
    here, there = pair(), 1 - pair()
    own_items = joined(read_wide(keep.at[here], hq), read_wide(got.at[here], hq), first, reverse)
    write_wide(own, hq, own_items)
    send_items = joined(read_wide(keep.at[there], hq), read_wide(got.at[there], hq), first, reverse)
    write_narrow(send, hq, send_items)


def group_total_body(reverse, hq, own, got, *refs):
    total, send = refs[-2:]
    items = joined(read_wide(own, hq), read_narrow(got, hq), pair() == 0, reverse)
    write_wide(total, hq, items)
    write_narrow(send, hq, items)


def doubled(reverse, hq, step, groups, before, got):
    there = group() + step < groups if reverse else group() - step >= 0
    out = []
    for old, (term, edge, gain) in zip(before, read_narrow(got, hq)):
        term = jnp.where(there, term, 0.0)
        edge = jnp.where(there, edge, 0.0)
        if old is None:
            out.append((term, edge, gain))
        else:
            out.append((old[0] + jnp.exp(old[1]) * term, old[1] + edge, old[2] + gain))
    return out


def doubling_body(reverse, hq, step, groups, total, *refs):
    so_far, send = refs[-2:]
    if step == 1:
        got = refs[0]
        before = [None] * hq
    else:
        got = refs[1]
        before = read_wide(refs[0], hq)
    items = doubled(reverse, hq, step, groups, before, got)
    write_wide(so_far, hq, items)
    whole = []
    for (t, e, g), (s, es, gs) in zip(read_wide(total, hq), items):
        whole.append((t + jnp.exp(e) * s, e + es, g + gs))
    write_narrow(send, hq, whole)


def into_chips_body(reverse, hq, step, groups, own, got_pair, total, so_far, got, *refs):
    keep, send = refs[-2:]
    before = read_wide(so_far, hq) if step > 1 else [None] * hq
    entering = doubled(reverse, hq, step, groups, before, got)
    mine_near = pair() == (1 if reverse else 0)
    kept, sent = [], []
    for (r, _, gr), (c, ec, _), (o, eo, _), (_, _, gt) in zip(
        entering, read_wide(own, hq), read_narrow(got_pair, hq), read_wide(total, hq)
    ):
        gain = gr + gt
        zero = jnp.zeros_like(ec)
        kept.append((jnp.where(mine_near, r, jnp.exp(eo) * r + o), zero, gain))
        sent.append((jnp.where(mine_near, jnp.exp(ec) * r + c, r), zero, gain))
    write_wide(keep, hq, kept)
    write_narrow(send, hq, sent)


def into_cores_body(reverse, hq, keep, got, own, other, *refs):
    mine, send = refs[-2:]
    mine_near = core() == (1 if reverse else 0)
    for y in range(2):
        a, b = read_wide(own, hq), read_narrow(other, hq)
        here = pair() == y
        items_mine, items_send = [], []
        for p, q, (k, ek, _), (g, eg, _) in zip(a, b, read_wide(keep.at[y], hq), read_wide(got.at[y], hq)):
            r = jnp.where(here, p[0], q[0])
            gain = jnp.where(here, p[2], q[2])
            zero = jnp.zeros_like(ek)
            items_mine.append((jnp.where(mine_near, r, jnp.exp(eg) * r + g), zero, gain))
            items_send.append((jnp.where(mine_near, jnp.exp(ek) * r + k, r), zero, gain))
        write_narrow(mine.at[y], hq, items_mine)
        write_narrow(send.at[y], hq, items_send)


def local_states_body(heads, swaps, k_hbm, v_hbm, ld, *refs):
    hq = heads // TEAM
    w = hq * HEAD
    if swaps:
        grad, keep, give, row, away, own, k, v, sems, grad_sems = refs
        width = heads * HEAD
        mine = lax.axis_index("tp")
        cols = lambda t: pl.ds(pl.multiple_of(t * width, HEAD), width)
        grad_copies = [
            pltpu.make_async_copy(grad.at[:, cols(1 - mine)], away, grad_sems.at[0]),
            pltpu.make_async_copy(grad.at[:, cols(mine)], own, grad_sems.at[1]),
        ]
    else:
        keep, give, row, k, v, sems = refs
        grad_copies = []
    order = [(give, 0, False), (give, 1, False), (keep, 0, True), (keep, 1, True)]
    copies = []
    for slot, (_, y, same) in enumerate(order):
        cols_d = pl.ds(pl.multiple_of(quarter_of(y, same) * w, HEAD), w)
        both = [
            pltpu.make_async_copy(k_hbm.at[:, cols_d], k.at[slot], sems.at[0, slot]),
            pltpu.make_async_copy(v_hbm.at[:, cols_d], v.at[slot], sems.at[1, slot]),
        ]
        for c in both:
            c.start()
        copies.append(both)
    for c in grad_copies:
        c.start()
    at = lax.broadcasted_iota(jnp.int32, (BLOCK, BLOCK), 0)
    other = lax.broadcasted_iota(jnp.int32, (BLOCK, BLOCK), 1)
    tri = (at <= other).astype(BF16)
    x = ld[...]
    if heads < EXTRA:
        x = jnp.concatenate([x, jnp.zeros((EXTRA - heads, BLOCK), F32)], axis=0)
    a, b, c = (nn(term, tri) for term in split_terms(x, 3))
    row[...] = a + (b + c)
    for slot, (out, y, same) in enumerate(order):
        for c in copies[slot]:
            c.wait()
        items = []
        for j in range(hq):
            sums = row[pl.ds(quarter_of(y, same) * hq + j, 1), :]
            edge = sums[:, BLOCK - 1 : BLOCK]
            kd = (transposed(k[slot, :, chunk(j)]) * jnp.exp(edge - sums)).astype(BF16)
            spread = jnp.broadcast_to(edge, (1, HEAD))
            items.append((nn(kd, v[slot, :, chunk(j)]), spread, jnp.zeros((1, HEAD), F32)))
        write_wide(out.at[y], hq, items)
    for c in grad_copies:
        c.wait()


def decays_body(heads, row, _, col, growth, shrink):
    hq = heads // TEAM
    for g in range(TEAM):
        rows = row[g * hq : (g + 1) * hq, :]
        across = jnp.concatenate([rows, jnp.zeros((HEAD - hq, BLOCK), F32)], axis=0).T
        col[g] = across
        growth[g] = jnp.exp(across)
        shrink[g] = jnp.exp(across[BLOCK - 1 : BLOCK, :] - across)


def lower_tiles(i):
    tiles = [(s, WIDE, False) for s in range(0, (i // 2) * WIDE, WIDE)]
    return tiles + [((i // 2) * WIDE, HEAD if i % 2 == 0 else WIDE, True)]


def upper_tiles(i):
    first = i * HEAD
    width = WIDE if i % 2 == 0 else HEAD
    return [(first, width, True)] + [(s, WIDE, False) for s in range(first + width, BLOCK, WIDE)]


def lower_table(left, line, i, start, width, cut):
    table = jnp.exp(left - line[:, start : start + width])
    if cut:
        at = lax.broadcasted_iota(jnp.int32, (HEAD, width), 0) + (i * HEAD - start)
        table = jnp.where(at >= lax.broadcasted_iota(jnp.int32, (HEAD, width), 1), table, 0.0)
    return table


def upper_table(left, line, i, start, width, cut):
    table = jnp.exp(line[:, start : start + width] - left)
    if cut:
        at = lax.broadcasted_iota(jnp.int32, (HEAD, width), 0)
        table = jnp.where(at <= lax.broadcasted_iota(jnp.int32, (HEAD, width), 1), table, 0.0)
    return table


def intra_body(heads, q, k, v, row, col, _, intra):
    hq = heads // TEAM

    def one(g, _):
        for j in range(hq):
            h, c = head_at(g, hq, j)
            line = row[pl.ds(h, 1), :]
            for i in range(BLOCK // HEAD):
                left = col[g, chunk(i), j : j + 1]
                total = None
                for start, width, cut in lower_tiles(i):
                    u = slice(start, start + width)
                    table = lower_table(left, line, i, start, width, cut)
                    probs = (nt(q[chunk(i), c], k[u, c]) * table).astype(BF16)
                    term = nn(probs, v[u, c])
                    total = term if total is None else total + term
                intra[chunk(i), c] = total
        return 0

    lax.fori_loop(0, TEAM, one, 0)


def dscaled_body(heads, swaps, gate, own, got, gain, q, row, dscaled, turned):
    hq = heads // TEAM
    part = own.shape[0]
    mine = lax.axis_index("tp") if swaps else 0

    def one(g, _):
        for j in range(hq):
            h, c = head_at(g, hq, j)
            for where, ref in ((mine, own), (1 - mine, got)):
                rows = pl.ds(pl.multiple_of(where * part, part), part)
                opened = jax.nn.sigmoid(gate[rows, c].astype(F32))
                dscaled[rows, c] = ref[:, c].astype(F32) * opened * gain[:, c]
            turned[h] = (transposed(q[:, c]) * jnp.exp(row[pl.ds(h, 1), :])).astype(BF16)
        return 0

    lax.fori_loop(0, TEAM, one, 0)


def by_quarter(mine, got):
    return [(ref.at[y], quarter_of(y, same)) for ref, same in ((mine, True), (got, False)) for y in range(2)]


def attention_body(heads, q, intra, dscaled, growth, mine, got, att, sums, sq, inn):
    hq = heads // TEAM
    for i in range(BLOCK // HEAD):
        r = chunk(i)
        a_sq = jnp.zeros((HEAD, HEAD), F32)
        a_in = jnp.zeros((HEAD, HEAD), F32)
        for state, g in by_quarter(mine, got):
            grow = growth[g, r, :]
            for j in range(hq):
                _, c = head_at(g, hq, j)
                a = intra[r, c] + nn(q[r, c], state[chunk(j), :]) * grow[:, j : j + 1]
                att[r, c] = a
                a_sq = a_sq + a * a
                a_in = a_in + a * dscaled[r, c]
        sq[r, :] = a_sq
        inn[r, :] = a_in
    ones = jnp.ones((8, HEAD), F32)
    a = nt(ones, sq[...], lax.Precision.HIGHEST)
    b = nt(ones, inn[...], lax.Precision.HIGHEST)
    sums[...] = jnp.where(lax.broadcasted_iota(jnp.int32, (8, BLOCK), 0) == 0, a, b)


def dattn_body(heads, channels, att, dscaled, turned, gain, row, sum_a, sum_b, dattn, scale, keep, give):
    hq = heads // TEAM
    total = sum_a[...] + sum_b[...]
    rs = lax.rsqrt(total[0:1, :] / channels + EPSILON)
    coef = total[1:2, :] * (rs * rs * rs) / channels
    scale[...] = jnp.concatenate([rs, coef, jnp.zeros((HEAD - 2, BLOCK), F32)], axis=0).T
    for out, y, same in ((give, 0, False), (give, 1, False), (keep, 0, True), (keep, 1, True)):
        items = []
        for j in range(hq):
            h, c = head_at(quarter_of(y, same), hq, j)
            gsum = jnp.zeros((8, HEAD), F32)
            for i in range(BLOCK // HEAD):
                r = chunk(i)
                a = att[r, c]
                t = dscaled[r, c] * scale[r, 0:1]
                dattn[r, c] = (t - a * scale[r, 1:2]).astype(BF16)
                gsum = gsum + jnp.sum((t * a).reshape(HEAD // 8, 8, HEAD), axis=0)
            edge = jnp.broadcast_to(row[pl.ds(h, 1), :][:, BLOCK - 1 : BLOCK], (1, HEAD))
            part = jnp.sum(gsum, axis=0, keepdims=True) / gain[:, c]
            items.append((nn(turned[h], dattn[:, c]), edge, part))
        write_wide(out.at[y], hq, items)


def gate_body(heads, gate, att, dscaled, scale, _, gate_grad, token):
    token[...] = jnp.zeros_like(token)

    def one(h, _):
        _, c = head_at(h, 1, 0)
        opened = jax.nn.sigmoid(gate[:, c].astype(F32))
        gate_grad[:, c] = (dscaled[:, c] * att[:, c] * scale[:, 0:1] * (1.0 - opened)).astype(BF16)
        return 0

    lax.fori_loop(0, heads, one, 0)


def query_body(heads, k, v, dattn, row, col, growth, mine, got, _, query_grad, token):
    token[...] = jnp.zeros_like(token)
    hq = heads // TEAM
    for state, g in by_quarter(mine, got):
        for j in range(hq):
            h, c = head_at(g, hq, j)
            line = row[pl.ds(h, 1), :]
            for i in range(BLOCK // HEAD):
                d = dattn[chunk(i), c]
                left = col[g, chunk(i), j : j + 1]
                total = nt(d, state[chunk(j), :]) * growth[g, chunk(i), j : j + 1]
                for start, width, cut in lower_tiles(i):
                    u = slice(start, start + width)
                    table = lower_table(left, line, i, start, width, cut)
                    dscores = (nt(d, v[u, c]) * table).astype(BF16)
                    total = total + nn(dscores, k[u, c])
                query_grad[chunk(i), c] = total.astype(BF16)


def key_value_body(heads, first, q, k, v, dattn, row, col, *refs):
    hq = heads // TEAM
    dk, dv = refs[-2:]

    def one(g, _):
        for j in range(hq):
            h, c = head_at(g, hq, j)
            line = row[pl.ds(h, 1), :]
            for i in range(BLOCK // HEAD):
                left = col[g, chunk(i), j : j + 1]
                dkey = dvalue = None
                for start, width, cut in upper_tiles(i):
                    t = slice(start, start + width)
                    table = upper_table(left, line, i, start, width, cut)
                    probs = (nt(k[chunk(i), c], q[t, c]) * table).astype(BF16)
                    dscores = (nt(v[chunk(i), c], dattn[t, c]) * table).astype(BF16)
                    a = nn(dscores, q[t, c])
                    b = nn(probs, dattn[t, c])
                    dkey, dvalue = (a, b) if dkey is None else (dkey + a, dvalue + b)
                dk[chunk(i), c] = dkey
                dv[chunk(i), c] = dvalue
        return 0

    lax.fori_loop(first, first + TEAM // 2, one, 0)


def final_body(heads, k, v, dk, dv, shrink, mine, got, key_grad, value_grad, gain_grad, key_out, value_out, sems):
    hq = heads // TEAM
    w = hq * HEAD
    copies = []
    for slot, (state, g) in enumerate(by_quarter(mine, got)):
        items = read_narrow(state, hq)
        for j in range(hq):
            _, c = head_at(g, hq, j)
            fade = shrink[g, :, j : j + 1]
            after = state[chunk(j), :]
            key_out[slot, :, chunk(j)] = (dk[:, c] + nt(v[:, c], after) * fade).astype(BF16)
            value_out[slot, :, chunk(j)] = (dv[:, c] + nn(k[:, c], after) * fade).astype(BF16)
            gain_grad[:, c] = items[j][2]
        cols = pl.ds(pl.multiple_of(g * w, HEAD), w)
        for i, (src, dst) in enumerate(((key_out, key_grad), (value_out, value_grad))):
            copy = pltpu.make_async_copy(src.at[slot], dst.at[:, cols], sems.at[i, slot])
            copy.start()
            copies.append(copy)
    for copy in copies:
        copy.wait()


def in_hbm(x):
    return pltpu.with_memory_space_constraint(x, pltpu.HBM)


def swap(x, bit):
    n = lax.axis_size("ctx")
    return lax.ppermute(x, "ctx", [(i, i ^ bit) for i in range(n)])


def across(x, k):
    n = lax.axis_size("ctx")
    return lax.ppermute(x, "ctx", [(i, (i + TEAM * k) % n) for i in range(n)])


def local(queries, keys, values, log_decay, gate, gain, grad_out):
    rows, width = queries.shape
    heads = width // HEAD
    hq = heads // TEAM
    tp = lax.axis_size("tp")
    n = lax.axis_size("ctx")
    groups = n // TEAM
    channels = width * tp
    bf = lambda *shape: jax.ShapeDtypeStruct(shape, BF16)
    f32 = lambda *shape: jax.ShapeDtypeStruct(shape, F32)
    swaps = tp == 2
    part = rows // 2
    small = 2 * heads * rows * HEAD * HEAD
    large = 2 * heads * rows * rows * HEAD
    wide = f32(hq * HEAD + SIDE, HEAD)
    wide2 = f32(2, hq * HEAD + SIDE, HEAD)
    narrow = bf(hq * HEAD + EXTRA, HEAD)
    narrow2 = bf(2, hq * HEAD + EXTRA, HEAD)
    table = f32(TEAM, rows, HEAD)
    gain_row = gain.reshape(1, width)

    def beside(work, after, name):
        return [work[name](after)] if name in work else []

    def step_call(body, reverse, inputs, unread, shapes, name, *sizes):
        return call(
            functools.partial(body, reverse, hq, *sizes),
            [*inputs, *unread],
            shapes,
            name,
            in_specs=[VMEM] * len(inputs) + [ANY] * len(unread),
        )

    def scan(reverse, keep, give, held, work):
        got = swap(give, 1)
        if held is None:
            own, send = step_call(chip_total_body, True, [keep, got], [], [wide, narrow], "chip_total_back")
        else:
            own, send, held = call(
                functools.partial(chip_total_body, False, hq),
                [keep, got, held],
                [wide, narrow, jax.ShapeDtypeStruct(held.shape, held.dtype)],
                "chip_total",
                in_specs=[VMEM, VMEM, ANY],
                out_specs=[VMEM, VMEM, ANY],
                alias={2: 2},
            )
        got_pair = swap(send, 2)
        unread = beside(work, send, "pair")
        total, send = step_call(group_total_body, reverse, [own, got_pair], unread, [wide, narrow], "group_total")
        so_far, step = total, 1
        while 2 * step < groups:
            far = across(send, -step if reverse else step)
            unread = beside(work, send, "one") if step == 1 else []
            before = [] if step == 1 else [so_far]
            so_far, send = step_call(
                doubling_body, reverse, [total, *before, far], unread, [wide, narrow], "doubling", step, groups
            )
            step *= 2
        far = across(send, -step if reverse else step)
        unread = beside(work, send, "last")
        kept, send = step_call(
            into_chips_body,
            reverse,
            [own, got_pair, total, so_far, far],
            unread,
            [wide, narrow],
            "into_chips",
            step,
            groups,
        )
        other = swap(send, 2)
        unread = beside(work, send, "pair_back")
        mine, send = step_call(
            into_cores_body, reverse, [keep, got, kept, other], unread, [narrow2, narrow2], "into_cores"
        )
        return mine, swap(send, 1), held

    outs = call(
        functools.partial(local_states_body, heads, swaps),
        [in_hbm(keys), in_hbm(values), log_decay] + [in_hbm(grad_out)] * swaps,
        [wide2, wide2, f32(EXTRA, rows)] + [bf(part, width)] * 2 * swaps,
        "local_states",
        [pltpu.VMEM((TEAM, rows, hq * HEAD), BF16)] * 2
        + [pltpu.SemaphoreType.DMA((2, TEAM))]
        + [pltpu.SemaphoreType.DMA((2,))] * swaps,
        small,
        [HBM, HBM, VMEM] + [HBM] * swaps,
        [VMEM] * 3 + [HBM, VMEM] * swaps,
    )
    keep, give, row = outs[:3]
    done = {}

    def decays_beside(after):
        done["decays"] = call(
            functools.partial(decays_body, heads),
            [row, after],
            [table] * 3,
            "decays",
            in_specs=[VMEM, ANY],
        )
        return done["decays"][0]

    def intra_beside(after):
        (done["intra"],) = call(
            functools.partial(intra_body, heads),
            [queries, keys, values, row, done["decays"][0], after],
            [f32(rows, width)],
            "intra",
            flops=2 * large,
            in_specs=[VMEM] * 5 + [ANY],
        )
        return done["intra"]

    held = outs[3] if swaps else keep
    mine, got, held = scan(False, keep, give, held, {"one": decays_beside, "last": intra_beside})
    (col, growth, shrink), intra = done["decays"], done["intra"]
    if swaps:
        own = outs[4]
        arrived = lax.ppermute(held, "tp", [(0, 1), (1, 0)])
    else:
        every = lax.all_to_all(grad_out, "tp", split_axis=1, concat_axis=0, tiled=True)
        own, arrived = every[:part], every[part:]
    dscaled, turned = call(
        functools.partial(dscaled_body, heads, swaps),
        [gate, own, arrived, gain_row, queries, row],
        [f32(rows, width), bf(heads, HEAD, rows)],
        "dscaled",
        flops=small,
    )
    att, sums = call(
        functools.partial(attention_body, heads),
        [queries, intra, dscaled, growth, mine, got],
        [f32(rows, width), f32(8, rows)],
        "attention",
        [pltpu.VMEM((rows, HEAD), F32)] * 2,
        small,
    )
    if swaps:
        others = lax.ppermute(sums, "tp", [(0, 1), (1, 0)])
    else:
        others = lax.psum(sums, "tp") - sums
    dattn, scale, keep, give = call(
        functools.partial(dattn_body, heads, channels),
        [att, dscaled, turned, gain_row, row, sums, others],
        [bf(rows, width), f32(rows, HEAD), wide2, wide2],
        "dattn",
        flops=small,
    )
    def gate_beside(after):
        done["gate"], token = call(
            functools.partial(gate_body, heads),
            [gate, att, dscaled, scale, after],
            [bf(rows, width), f32(SIDE, HEAD)],
            "gate",
            flops=small,
            in_specs=[VMEM] * 4 + [ANY],
        )
        return token

    def key_value_first(after):
        done["key_value"] = call(
            functools.partial(key_value_body, heads, 0),
            [queries, keys, values, dattn, row, col, after],
            [f32(rows, width)] * 2,
            "key_value",
            flops=2 * large,
            in_specs=[VMEM] * 6 + [ANY],
        )
        return done["key_value"][0]

    def query_beside(after):
        done["query"], token = call(
            functools.partial(query_body, heads),
            [keys, values, dattn, row, col, growth, mine, got, after],
            [bf(rows, width), f32(SIDE, HEAD)],
            "query",
            flops=2 * large + small,
            in_specs=[VMEM] * 8 + [ANY],
        )
        return token

    def key_value_last(after):
        done["key_value"] = call(
            functools.partial(key_value_body, heads, TEAM // 2),
            [queries, keys, values, dattn, row, col, after, *done["key_value"]],
            [f32(rows, width)] * 2,
            "key_value",
            flops=2 * large,
            in_specs=[VMEM] * 6 + [ANY, VMEM, VMEM],
            alias={7: 0, 8: 1},
        )
        return done["key_value"][0]

    work = {"pair": gate_beside, "one": key_value_first, "last": query_beside, "pair_back": key_value_last}
    back_mine, back_got, _ = scan(True, keep, give, None, work)
    gate_grad, query_grad, (dk, dv) = done["gate"], done["query"], done["key_value"]
    key_grad, value_grad, gain_grad = call(
        functools.partial(final_body, heads),
        [keys, values, dk, dv, shrink, back_mine, back_got],
        [bf(rows, width), bf(rows, width), f32(1, width)],
        "final",
        [pltpu.VMEM((TEAM, rows, hq * HEAD), BF16)] * 2 + [pltpu.SemaphoreType.DMA((2, TEAM))],
        2 * small,
        out_specs=[HBM, HBM, VMEM],
    )
    return query_grad, key_grad, value_grad, gate_grad, gain_grad.reshape(width)


def solution(mesh):
    return jax.shard_map(
        local,
        mesh=mesh,
        in_specs=(
            P("ctx", "tp"),
            P("ctx", "tp"),
            P("ctx", "tp"),
            P("tp", "ctx"),
            P("ctx", "tp"),
            P("tp"),
            P(("ctx", "tp"), None),
        ),
        out_specs=(P("ctx", "tp"), P("ctx", "tp"), P("ctx", "tp"), P("ctx", "tp"), P("tp")),
        check_vma=False,
    )
```

time: 105 us -> 100 us (0.952)
  Pallas kernels: 47.9 us -> 60.9 us
  starting transfers between devices: 23.8 us -> 16.6 us
  waiting for transfers between devices: 26.7 us -> 20.7 us
  local copies, waits for them, and re-layouts: 5.54 us -> 0.78 us
    pallas_call x12 -> x21, Pallas kernels: 47.9 us -> 60.9 us  [call(): pl.pallas_call(body, in_specs=in_specs or [VMEM] * len(inputs), out_specs...]
    ppermute x6 -> x4, waiting for transfers between devices: 12.8 us -> 4.84 us  [across(): return lax.ppermute(x, 'ctx', [(i, (i + TEAM * k) % n) for i in range(n)])]
    unnamed x18 -> x12, local copies, waits for them, and re-layouts: 5.54 us -> 0.78 us
    ppermute x6 -> x4, starting transfers between devices: 10.4 us -> 6.04 us  [across(): return lax.ppermute(x, 'ctx', [(i, (i + TEAM * k) % n) for i in range(n)])]
    ppermute x13 -> x9, starting transfers between devices: 12.9 us -> 9.94 us  [the longest x8 7.02 us: swap(): return lax.ppermute(x, 'ctx', [(i, i ^ bit) for i in range(n)])]
    ppermute x13 -> x9, waiting for transfers between devices: 10.7 us -> 12.7 us  [the longest x8 12.7 us: swap(): return lax.ppermute(x, 'ctx', [(i, i ^ bit) for i in range(n)])]
  transfers between devices with their start and end apart: 20 -> 14, of which waited for: 9 -> 8; matrix products, arithmetic and copies ran while one was open for 0% -> 0% of each run, Pallas kernels for 29% -> 44%
where the time goes in v4:
time: 100 us
  Pallas kernels  60.9 us (61%)
  waiting for transfers between devices  20.7 us (21%)
  starting transfers between devices  16.6 us (17%)
  between operations  1.03 us (1%)
    pallas_call x21, Pallas kernels, call(): pl.pallas_call(body, in_specs=in_specs or [VMEM] * len(inputs), out_specs...  60.9 us
    ppermute x8, waiting for transfers between devices, swap(): return lax.ppermute(x, 'ctx', [(i, i ^ bit) for i in range(n)])  12.7 us
    ppermute x8, starting transfers between devices, swap(): return lax.ppermute(x, 'ctx', [(i, i ^ bit) for i in range(n)])  7.02 us
    ppermute x4, starting transfers between devices, across(): return lax.ppermute(x, 'ctx', [(i, (i + TEAM * k) % n) for i in range(n)])  6.04 us
    ppermute x4, waiting for transfers between devices, across(): return lax.ppermute(x, 'ctx', [(i, (i + TEAM * k) % n) for i in range(n)])  4.84 us
    ppermute x1, waiting for transfers between devices, local(): others = lax.ppermute(sums, 'tp', [(0, 1), (1, 0)])  3.2 us
    ppermute x1, starting transfers between devices, local(): arrived = lax.ppermute(held, 'tp', [(0, 1), (1, 0)])  2.92 us
  transfers between devices with their start and end apart: 14, of which 8 were waited for; matrix products, arithmetic and copies ran while one was open for 0% of the time, Pallas kernels for 44%

profile of v4, /device:TPU:0, one launch (start us, length us, event | category | flops | bytes accessed | tf_op | source)
XLA Modules:
  0.0 100.0 jit_solution(5296496238891321776)
XLA Ops:
  1.4 4.8 %local_states.1 = (f32[2,520,128]{2,1,0:T(8,128)S(1)}, f32[2,520,128]{2,1,0:T(8,128)S(1)}, f32[16,512]{1,0:T(8,128)S(1)}, bf16[256,2048]{1,0:T(8,128)(2,1)S(1)}, bf16[256,2048]{1,0:T(8,128)(2,1)S(1)}) custom-call(bf16[512,2048]{1,0:T(8,128)(2,1)} %k.9, bf16[512,2048]{1,0:T(8,128)(2,1)} %v.9, f32[16,512]{1,0:T(8,128)S(1)} %copy-done.4, bf16[256,4096]{1,0:T(8,128)(2,1)} %refs_0_.1), custom_call_target="tpu_custom_call" | custom-call | flops 268435456 | bytes 9519104 | tf_op jit(solution)/shard_map/local_states/pallas_call | solution.py:115
  6.7 1.5 %collective-permute-done.refs_1_.got = f32[2,520,128]{2,1,0:T(8,128)S(1)} collective-permute-done((f32[2,520,128]{2,1,0:T(8,128)S(1)}, f32[2,520,128]{2,1,0:T(8,128)S(1)}, u32[]{:S(2)}, u32[]{:S(2)}) %collective-permute-start) | collective-permute-done | bytes 532512 | tf_op jit(solution)/shard_map/ppermute | solution.py:483
  8.4 2.9 %collective-permute-start.3 = (bf16[256,2048]{1,0:T(8,128)(2,1)S(1)}, bf16[256,2048]{1,0:T(8,128)(2,1)S(1)}, u32[]{:S(2)}, u32[]{:S(2)}) collective-permute-start(bf16[256,2048]{1,0:T(8,128)(2,1)S(1)} %get-tuple-element.64), channel_id=1, source_target_pairs={{0,1},{1,0},{2,3},{3,2},{4,5},{5,4},{6,7},{7,6},{8,9},{9,8},{10,11... | collective-permute-start | bytes 3145736 | tf_op jit(solution)/shard_map/ppermute | solution.py:610
  12.8 3.8 %collective-permute-done.1.got.got_pair = bf16[528,128]{1,0:T(8,128)(2,1)S(1)} collective-permute-done((bf16[528,128]{1,0:T(8,128)(2,1)S(1)}, bf16[528,128]{1,0:T(8,128)(2,1)S(1)}, u32[]{:S(2)}, u32[]{:S(2)}) %collective-permute-start.1) | collective-permute-done | bytes 135200 | tf_op jit(solution)/shard_map/ppermute | solution.py:483
  16.8 1.8 %collective-permute-start.2 = (bf16[528,128]{1,0:T(8,128)(2,1)S(1)}, bf16[528,128]{1,0:T(8,128)(2,1)S(1)}, u32[]{:S(2)}, u32[]{:S(2)}) collective-permute-start(bf16[528,128]{1,0:T(8,128)(2,1)S(1)} %get-tuple-element.59._), channel_id=1, source_target_pairs={{0,8},{2,10},{4,12},{6,14},{8,16},{10,18},{12,20},{14,22},{16,24},... | collective-permute-start | bytes 405512 | tf_op jit(solution)/shard_map/ppermute | solution.py:488
  19.0 4.8 %collective-permute-done.2.refs_0_ = bf16[528,128]{1,0:T(8,128)(2,1)S(1)} collective-permute-done((bf16[528,128]{1,0:T(8,128)(2,1)S(1)}, bf16[528,128]{1,0:T(8,128)(2,1)S(1)}, u32[]{:S(2)}, u32[]{:S(2)}) %collective-permute-start.2) | collective-permute-done | bytes 135200 | tf_op jit(solution)/shard_map/ppermute | solution.py:488
  24.7 9.2 %intra.1.refs_0_ = f32[512,2048]{1,0:T(8,128)S(1)} custom-call(bf16[512,2048]{1,0:T(8,128)(2,1)S(1)} %copy-done.2, bf16[512,2048]{1,0:T(8,128)(2,1)S(1)} %copy-done, bf16[512,2048]{1,0:T(8,128)(2,1)S(1)} %copy-done.1, f32[16,512]{1,0:T(8,128)S(1)} %get-tuple-element.53.row, f32[4,512,128]{2,1,0:T(8,128)S(1)} %get-tuple-element.60.refs_1_.col, ...), custom_call_target="tpu_custom_call" | custom-call | flops 2147483648 | bytes 11702272 | tf_op jit(solution)/shard_map/intra/pallas_call | solution.py:115
  34.1 1.6 %collective-permute-start.5 = (bf16[528,128]{1,0:T(8,128)(2,1)S(1)}, bf16[528,128]{1,0:T(8,128)(2,1)S(1)}, u32[]{:S(2)}, u32[]{:S(2)}) collective-permute-start(bf16[528,128]{1,0:T(8,128)(2,1)S(1)} %get-tuple-element.69), channel_id=1, source_target_pairs={{0,4},{2,6},{4,0},{6,2},{8,12},{10,14},{12,8},{14,10},{16,20},{18,... | collective-permute-start | bytes 405512 | tf_op jit(solution)/shard_map/ppermute | solution.py:483
  35.7 3.5 %collective-permute-done.5.other = bf16[528,128]{1,0:T(8,128)(2,1)S(1)} collective-permute-done((bf16[528,128]{1,0:T(8,128)(2,1)S(1)}, bf16[528,128]{1,0:T(8,128)(2,1)S(1)}, u32[]{:S(2)}, u32[]{:S(2)}) %collective-permute-start.5) | collective-permute-done | bytes 135200 | tf_op jit(solution)/shard_map/ppermute | solution.py:483
  39.5 2.8 %dscaled.1 = (f32[512,2048]{1,0:T(8,128)S(1)}, bf16[16,128,512]{2,1,0:T(8,128)(2,1)S(1)}) custom-call(bf16[512,2048]{1,0:T(8,128)(2,1)S(1)} %copy-done.3, bf16[256,2048]{1,0:T(8,128)(2,1)S(1)} %get-tuple-element.63.own, bf16[256,2048]{1,0:T(8,128)(2,1)S(1)} %collective-permute-done.3.got, f32[1,2048]{1,0:T(1,128)S(1)} %bitcast.2, ...), custom_call_target="tpu_custom_call" | custom-call | flops 268435456 | bytes 12623872 | tf_op jit(solution)/shard_map/dscaled/pallas_call | solution.py:115
  42.4 3.1 %attention.1 = (f32[512,2048]{1,0:T(8,128)S(1)}, f32[8,512]{1,0:T(8,128)S(1)}) custom-call(bf16[512,2048]{1,0:T(8,128)(2,1)S(1)} %copy-done.2, f32[512,2048]{1,0:T(8,128)S(1)} %intra.1.refs_0_, f32[512,2048]{1,0:T(8,128)S(1)} %get-tuple-element.65.dscaled, f32[4,512,128]{2,1,0:T(8,128)S(1)} %get-tuple-element.66.growth, ...), custom_call_target="tpu_custom_call" | custom-call | flops 268435456 | bytes 16285696 | tf_op jit(solution)/shard_map/attention/pallas_call | solution.py:115
  46.1 3.2 %collective-permute-done.7.sum_b = f32[8,512]{1,0:T(8,128)S(1)} collective-permute-done((f32[8,512]{1,0:T(8,128)S(1)}, f32[8,512]{1,0:T(8,128)S(1)}, u32[]{:S(2)}, u32[]{:S(2)}) %collective-permute-start.7) | collective-permute-done | bytes 16416 | tf_op jit(solution)/shard_map/ppermute | solution.py:630
  49.3 3.8 %dattn.1 = (bf16[512,2048]{1,0:T(8,128)(2,1)S(1)}, f32[512,128]{1,0:T(8,128)S(1)}, f32[2,520,128]{2,1,0:T(8,128)S(1)}, f32[2,520,128]{2,1,0:T(8,128)S(1)}) custom-call(f32[512,2048]{1,0:T(8,128)S(1)} %get-tuple-element.72.att, f32[512,2048]{1,0:T(8,128)S(1)} %get-tuple-element.65.dscaled, bf16[16,128,512]{2,1,0:T(8,128)(2,1)S(1)} %get-tuple-element.73.turned, ...), custom_call_target="tpu_custom_call" | custom-call | flops 268435456 | bytes 13983744 | tf_op jit(solution)/shard_map/dattn/pallas_call | solution.py:115
  53.1 1.9 %collective-permute-done.8.refs_1_.got = f32[2,520,128]{2,1,0:T(8,128)S(1)} collective-permute-done((f32[2,520,128]{2,1,0:T(8,128)S(1)}, f32[2,520,128]{2,1,0:T(8,128)S(1)}, u32[]{:S(2)}, u32[]{:S(2)}) %collective-permute-start.8) | collective-permute-done | bytes 532512 | tf_op jit(solution)/shard_map/ppermute | solution.py:483
  55.2 1.6 %collective-permute-start.9 = (bf16[528,128]{1,0:T(8,128)(2,1)S(1)}, bf16[528,128]{1,0:T(8,128)(2,1)S(1)}, u32[]{:S(2)}, u32[]{:S(2)}) collective-permute-start(bf16[528,128]{1,0:T(8,128)(2,1)S(1)} %get-tuple-element.79._), channel_id=1, source_target_pairs={{0,4},{2,6},{4,0},{6,2},{8,12},{10,14},{12,8},{14,10},{16,20},{18,... | collective-permute-start | bytes 405512 | tf_op jit(solution)/shard_map/ppermute | solution.py:483
  56.7 3.8 %gate.4 = (bf16[512,2048]{1,0:T(8,128)(2,1)}, f32[8,128]{1,0:T(8,128)S(1)}) custom-call(bf16[512,2048]{1,0:T(8,128)(2,1)S(1)} %copy-done.3, f32[512,2048]{1,0:T(8,128)S(1)} %get-tuple-element.72.att, f32[512,2048]{1,0:T(8,128)S(1)} %get-tuple-element.65.dscaled, f32[512,128]{1,0:T(8,128)S(1)} %get-tuple-element.80.scale, ...), custom_call_target="tpu_custom_call" | custom-call | flops 268435456 | bytes 12984320 | tf_op jit(solution)/shard_map/gate/pallas_call | solution.py:115
  60.9 1.6 %collective-permute-start.10 = (bf16[528,128]{1,0:T(8,128)(2,1)S(1)}, bf16[528,128]{1,0:T(8,128)(2,1)S(1)}, u32[]{:S(2)}, u32[]{:S(2)}) collective-permute-start(bf16[528,128]{1,0:T(8,128)(2,1)S(1)} %get-tuple-element.83.refs_0_), channel_id=1, source_target_pairs={{0,24},{2,26},{4,28},{6,30},{8,0},{10,2},{12,4},{14,6},{16,8},{18,... | collective-permute-start | bytes 405512 | tf_op jit(solution)/shard_map/ppermute | solution.py:488
  62.5 7.2 %key_value.2 = (f32[512,2048]{1,0:T(8,128)S(1)}, f32[512,2048]{1,0:T(8,128)S(1)}) custom-call(bf16[512,2048]{1,0:T(8,128)(2,1)S(1)} %copy-done.2, bf16[512,2048]{1,0:T(8,128)(2,1)S(1)} %copy-done, bf16[512,2048]{1,0:T(8,128)(2,1)S(1)} %copy-done.1, bf16[512,2048]{1,0:T(8,128)(2,1)S(1)} %get-tuple-element.75.dattn, f32[16,512]{1,0:T(8,128)S(1)} %get-tuple-element.53.row, ...), custom_call_target="tpu_custom_call" | custom-call | flops 2147483648 | bytes 17993728 | tf_op jit(solution)/shard_map/key_value/pallas_call | solution.py:115
  69.8 1.8 %collective-permute-start.11 = (bf16[528,128]{1,0:T(8,128)(2,1)S(1)}, bf16[528,128]{1,0:T(8,128)(2,1)S(1)}, u32[]{:S(2)}, u32[]{:S(2)}) collective-permute-start(bf16[528,128]{1,0:T(8,128)(2,1)S(1)} %get-tuple-element.85._), channel_id=1, source_target_pairs={{0,16},{2,18},{4,20},{6,22},{8,24},{10,26},{12,28},{14,30},{16,0},... | collective-permute-start | bytes 405512 | tf_op jit(solution)/shard_map/ppermute | solution.py:488
  71.6 12.6 %query.1 = (bf16[512,2048]{1,0:T(8,128)(2,1)}, f32[8,128]{1,0:T(8,128)S(1)}) custom-call(bf16[512,2048]{1,0:T(8,128)(2,1)S(1)} %copy-done, bf16[512,2048]{1,0:T(8,128)(2,1)S(1)} %copy-done.1, bf16[512,2048]{1,0:T(8,128)(2,1)S(1)} %get-tuple-element.75.dattn, f32[16,512]{1,0:T(8,128)S(1)} %get-tuple-element.53.row, ...), custom_call_target="tpu_custom_call" | custom-call | flops 2415919104 | bytes 11198464 | tf_op jit(solution)/shard_map/query/pallas_call | solution.py:115
  84.3 1.6 %collective-permute-start.12 = (bf16[528,128]{1,0:T(8,128)(2,1)S(1)}, bf16[528,128]{1,0:T(8,128)(2,1)S(1)}, u32[]{:S(2)}, u32[]{:S(2)}) collective-permute-start(bf16[528,128]{1,0:T(8,128)(2,1)S(1)} %get-tuple-element.89.refs_0_), channel_id=1, source_target_pairs={{0,4},{2,6},{4,0},{6,2},{8,12},{10,14},{12,8},{14,10},{16,20},{18,... | collective-permute-start | bytes 405512 | tf_op jit(solution)/shard_map/ppermute | solution.py:483
  85.9 7.2 %key_value.3 = (f32[512,2048]{1,0:T(8,128)S(1)}, f32[512,2048]{1,0:T(8,128)S(1)}) custom-call(bf16[512,2048]{1,0:T(8,128)(2,1)S(1)} %copy-done.2, bf16[512,2048]{1,0:T(8,128)(2,1)S(1)} %copy-done, bf16[512,2048]{1,0:T(8,128)(2,1)S(1)} %copy-done.1, bf16[512,2048]{1,0:T(8,128)(2,1)S(1)} %get-tuple-element.75.dattn, ...), custom_call_target="tpu_custom_call", output_to_operand_aliasing={{0}: (7, {}), {1}: (8, {})} | custom-call | flops 2147483648 | bytes 26382336 | tf_op jit(solution)/shard_map/key_value/pallas_call | solution.py:115
  93.4 1.5 %collective-permute-done.13.got = bf16[2,528,128]{2,1,0:T(8,128)(2,1)S(1)} collective-permute-done((bf16[2,528,128]{2,1,0:T(8,128)(2,1)S(1)}, bf16[2,528,128]{2,1,0:T(8,128)(2,1)S(1)}, u32[]{:S(2)}, u32[]{:S(2)}) %collective-permute-start.13) | collective-permute-done | bytes 270368 | tf_op jit(solution)/shard_map/ppermute | solution.py:483
  94.9 4.9 %final.1 = (bf16[512,2048]{1,0:T(8,128)(2,1)}, bf16[512,2048]{1,0:T(8,128)(2,1)}, f32[1,2048]{1,0:T(1,128)}) custom-call(bf16[512,2048]{1,0:T(8,128)(2,1)S(1)} %copy-done, bf16[512,2048]{1,0:T(8,128)(2,1)S(1)} %copy-done.1, f32[512,2048]{1,0:T(8,128)S(1)} %get-tuple-element.91.refs_0_.dk, f32[512,2048]{1,0:T(8,128)S(1)} %get-tuple-element.92.dv, ...), custom_call_target="tpu_custom_call" | custom-call | flops 536870912 | bytes 18374656 | tf_op jit(solution)/shard_map/final/pallas_call | solution.py:115
  (37 shorter events, 6.4 us)
Async XLA Ops:
  0.6 0.8 copy-start.4
  1.4 23.3 %copy-start.1 = (bf16[512,2048]{1,0:T(8,128)(2,1)S(1)}, bf16[512,2048]{1,0:T(8,128)(2,1)}, u32[]{:S(2)}) copy-start(bf16[512,2048]{1,0:T(8,128)(2,1)} %v.9) | copy-start | bytes 6291460
  1.4 23.3 %copy-start.2 = (bf16[512,2048]{1,0:T(8,128)(2,1)S(1)}, bf16[512,2048]{1,0:T(8,128)(2,1)}, u32[]{:S(2)}) copy-start(bf16[512,2048]{1,0:T(8,128)(2,1)} %q.9) | copy-start | bytes 6291460
  6.2 18.5 %copy-start = (bf16[512,2048]{1,0:T(8,128)(2,1)S(1)}, bf16[512,2048]{1,0:T(8,128)(2,1)}, u32[]{:S(2)}) copy-start(bf16[512,2048]{1,0:T(8,128)(2,1)} %k.9) | copy-start | bytes 6291460
  6.2 2.1 %collective-permute-start = (f32[2,520,128]{2,1,0:T(8,128)S(1)}, f32[2,520,128]{2,1,0:T(8,128)S(1)}, u32[]{:S(2)}, u32[]{:S(2)}) collective-permute-start(f32[2,520,128]{2,1,0:T(8,128)S(1)} %get-tuple-element.55), channel_id=1, source_target_pairs={{0,2},{2,0},{4,6},{6,4},{8,10},{10,8},{12,14},{14,12},{16,18},{18,... | collective-permute-start | bytes 1597448 | tf_op jit(solution)/shard_map/ppermute | solution.py:483
  8.4 31.1 %collective-permute-start.3 = (bf16[256,2048]{1,0:T(8,128)(2,1)S(1)}, bf16[256,2048]{1,0:T(8,128)(2,1)S(1)}, u32[]{:S(2)}, u32[]{:S(2)}) collective-permute-start(bf16[256,2048]{1,0:T(8,128)(2,1)S(1)} %get-tuple-element.64), channel_id=1, source_target_pairs={{0,1},{1,0},{2,3},{3,2},{4,5},{5,4},{6,7},{7,6},{8,9},{9,8},{10,11... | collective-permute-start | bytes 3145736 | tf_op jit(solution)/shard_map/ppermute | solution.py:610
  11.3 5.3 %collective-permute-start.1 = (bf16[528,128]{1,0:T(8,128)(2,1)S(1)}, bf16[528,128]{1,0:T(8,128)(2,1)S(1)}, u32[]{:S(2)}, u32[]{:S(2)}) collective-permute-start(bf16[528,128]{1,0:T(8,128)(2,1)S(1)} %get-tuple-element.58), channel_id=1, source_target_pairs={{0,4},{2,6},{4,0},{6,2},{8,12},{10,14},{12,8},{14,10},{16,20},{18,... | collective-permute-start | bytes 405512 | tf_op jit(solution)/shard_map/ppermute | solution.py:483
  16.8 7.0 %collective-permute-start.2 = (bf16[528,128]{1,0:T(8,128)(2,1)S(1)}, bf16[528,128]{1,0:T(8,128)(2,1)S(1)}, u32[]{:S(2)}, u32[]{:S(2)}) collective-permute-start(bf16[528,128]{1,0:T(8,128)(2,1)S(1)} %get-tuple-element.59._), channel_id=1, source_target_pairs={{0,8},{2,10},{4,12},{6,14},{8,16},{10,18},{12,20},{14,22},{16,24},... | collective-permute-start | bytes 405512 | tf_op jit(solution)/shard_map/ppermute | solution.py:488
  23.9 10.1 %collective-permute-start.4 = (bf16[528,128]{1,0:T(8,128)(2,1)S(1)}, bf16[528,128]{1,0:T(8,128)(2,1)S(1)}, u32[]{:S(2)}, u32[]{:S(2)}) collective-permute-start(bf16[528,128]{1,0:T(8,128)(2,1)S(1)} %get-tuple-element.62._), channel_id=1, source_target_pairs={{0,16},{2,18},{4,20},{6,22},{8,24},{10,26},{12,28},{14,30},{16,0},... | collective-permute-start | bytes 405512 | tf_op jit(solution)/shard_map/ppermute | solution.py:488
  34.0 5.5 %copy-start.3 = (bf16[512,2048]{1,0:T(8,128)(2,1)S(1)}, bf16[512,2048]{1,0:T(8,128)(2,1)}, u32[]{:S(2)}) copy-start(bf16[512,2048]{1,0:T(8,128)(2,1)} %gate.5) | copy-start | bytes 6291460
  34.0 5.5 %copy-start.5 = (f32[2048]{0:T(1024)S(1)}, f32[2048]{0:T(1024)}, u32[]{:S(2)}) copy-start(f32[2048]{0:T(1024)} %param.12) | copy-start | bytes 24580
  34.1 5.1 %collective-permute-start.5 = (bf16[528,128]{1,0:T(8,128)(2,1)S(1)}, bf16[528,128]{1,0:T(8,128)(2,1)S(1)}, u32[]{:S(2)}, u32[]{:S(2)}) collective-permute-start(bf16[528,128]{1,0:T(8,128)(2,1)S(1)} %get-tuple-element.69), channel_id=1, source_target_pairs={{0,4},{2,6},{4,0},{6,2},{8,12},{10,14},{12,8},{14,10},{16,20},{18,... | collective-permute-start | bytes 405512 | tf_op jit(solution)/shard_map/ppermute | solution.py:483
  39.4 3.0 %collective-permute-start.6 = (bf16[2,528,128]{2,1,0:T(8,128)(2,1)S(1)}, bf16[2,528,128]{2,1,0:T(8,128)(2,1)S(1)}, u32[]{:S(2)}, u32[]{:S(2)}) collective-permute-start(bf16[2,528,128]{2,1,0:T(8,128)(2,1)S(1)} %get-tuple-element.71), channel_id=1, source_target_pairs={{0,2},{2,0},{4,6},{6,4},{8,10},{10,8},{12,14},{14,12},{16,18},{18,... | collective-permute-start | bytes 811016 | tf_op jit(solution)/shard_map/ppermute | solution.py:483
  45.5 3.8 %collective-permute-start.7 = (f32[8,512]{1,0:T(8,128)S(1)}, f32[8,512]{1,0:T(8,128)S(1)}, u32[]{:S(2)}, u32[]{:S(2)}) collective-permute-start(f32[8,512]{1,0:T(8,128)S(1)} %get-tuple-element.74.sum_a), channel_id=1, source_target_pairs={{0,1},{1,0},{2,3},{3,2},{4,5},{5,4},{6,7},{7,6},{8,9},{9,8},{10,11... | collective-permute-start | bytes 49160 | tf_op jit(solution)/shard_map/ppermute | solution.py:630
  53.1 2.0 %collective-permute-start.8 = (f32[2,520,128]{2,1,0:T(8,128)S(1)}, f32[2,520,128]{2,1,0:T(8,128)S(1)}, u32[]{:S(2)}, u32[]{:S(2)}) collective-permute-start(f32[2,520,128]{2,1,0:T(8,128)S(1)} %get-tuple-element.77), channel_id=1, source_target_pairs={{0,2},{2,0},{4,6},{6,4},{8,10},{10,8},{12,14},{14,12},{16,18},{18,... | collective-permute-start | bytes 1597448 | tf_op jit(solution)/shard_map/ppermute | solution.py:483
  55.2 5.7 %collective-permute-start.9 = (bf16[528,128]{1,0:T(8,128)(2,1)S(1)}, bf16[528,128]{1,0:T(8,128)(2,1)S(1)}, u32[]{:S(2)}, u32[]{:S(2)}) collective-permute-start(bf16[528,128]{1,0:T(8,128)(2,1)S(1)} %get-tuple-element.79._), channel_id=1, source_target_pairs={{0,4},{2,6},{4,0},{6,2},{8,12},{10,14},{12,8},{14,10},{16,20},{18,... | collective-permute-start | bytes 405512 | tf_op jit(solution)/shard_map/ppermute | solution.py:483
  60.9 8.8 %collective-permute-start.10 = (bf16[528,128]{1,0:T(8,128)(2,1)S(1)}, bf16[528,128]{1,0:T(8,128)(2,1)S(1)}, u32[]{:S(2)}, u32[]{:S(2)}) collective-permute-start(bf16[528,128]{1,0:T(8,128)(2,1)S(1)} %get-tuple-element.83.refs_0_), channel_id=1, source_target_pairs={{0,24},{2,26},{4,28},{6,30},{8,0},{10,2},{12,4},{14,6},{16,8},{18,... | collective-permute-start | bytes 405512 | tf_op jit(solution)/shard_map/ppermute | solution.py:488
  69.8 14.4 %collective-permute-start.11 = (bf16[528,128]{1,0:T(8,128)(2,1)S(1)}, bf16[528,128]{1,0:T(8,128)(2,1)S(1)}, u32[]{:S(2)}, u32[]{:S(2)}) collective-permute-start(bf16[528,128]{1,0:T(8,128)(2,1)S(1)} %get-tuple-element.85._), channel_id=1, source_target_pairs={{0,16},{2,18},{4,20},{6,22},{8,24},{10,26},{12,28},{14,30},{16,0},... | collective-permute-start | bytes 405512 | tf_op jit(solution)/shard_map/ppermute | solution.py:488
  84.3 8.7 %collective-permute-start.12 = (bf16[528,128]{1,0:T(8,128)(2,1)S(1)}, bf16[528,128]{1,0:T(8,128)(2,1)S(1)}, u32[]{:S(2)}, u32[]{:S(2)}) collective-permute-start(bf16[528,128]{1,0:T(8,128)(2,1)S(1)} %get-tuple-element.89.refs_0_), channel_id=1, source_target_pairs={{0,4},{2,6},{4,0},{6,2},{8,12},{10,14},{12,8},{14,10},{16,20},{18,... | collective-permute-start | bytes 405512 | tf_op jit(solution)/shard_map/ppermute | solution.py:483
  93.3 1.6 %collective-permute-start.13 = (bf16[2,528,128]{2,1,0:T(8,128)(2,1)S(1)}, bf16[2,528,128]{2,1,0:T(8,128)(2,1)S(1)}, u32[]{:S(2)}, u32[]{:S(2)}) collective-permute-start(bf16[2,528,128]{2,1,0:T(8,128)(2,1)S(1)} %get-tuple-element.96), channel_id=1, source_target_pairs={{0,2},{2,0},{4,6},{6,4},{8,10},{10,8},{12,14},{14,12},{16,18},{18,... | collective-permute-start | bytes 811016 | tf_op jit(solution)/shard_map/ppermute | solution.py:483

commit v5 on v4

--- a/solution.py
+++ b/solution.py
@@ -9,7 +9,7 @@
 
 HEAD = 128
 BLOCK = 512
-WIDE = 2 * HEAD
+HALF = BLOCK // 2
 TEAM = 4
 SIDE = 8
 EXTRA = 16
@@ -28,6 +28,10 @@
 
 def nn(a, b):
     return lax.dot_general(a, b, (((1,), (0,)), ((), ())), preferred_element_type=F32)
+
+
+def half(i):
+    return slice(i * HALF, (i + 1) * HALF)
 
 
 def chunk(i):
@@ -135,11 +139,7 @@
     return out
 
 
-def chip_total_body(reverse, hq, *refs):
-    if reverse:
-        keep, got, own, send = refs
-    else:
-        keep, got, _, own, send, _ = refs
+def chip_total_body(reverse, hq, keep, got, own, send):
     first = core() == 0
     here, there = pair(), 1 - pair()
     own_items = joined(read_wide(keep.at[here], hq), read_wide(got.at[here], hq), first, reverse)
@@ -218,117 +218,121 @@
         write_narrow(send.at[y], hq, items_send)
 
 
-def local_states_body(heads, swaps, k_hbm, v_hbm, ld, *refs):
+def local_states_body(heads, swaps, k_hbm, v_hbm, ld_hbm, *refs):
     hq = heads // TEAM
     w = hq * HEAD
     if swaps:
-        grad, keep, give, row, away, own, k, v, sems, grad_sems = refs
+        grad, keep, give, row, k, v, away, own, ld, sems, side_sems = refs
         width = heads * HEAD
         mine = lax.axis_index("tp")
         cols = lambda t: pl.ds(pl.multiple_of(t * width, HEAD), width)
-        grad_copies = [
-            pltpu.make_async_copy(grad.at[:, cols(1 - mine)], away, grad_sems.at[0]),
-            pltpu.make_async_copy(grad.at[:, cols(mine)], own, grad_sems.at[1]),
+        side_copies = [
+            pltpu.make_async_copy(grad.at[:, cols(1 - mine)], away, side_sems.at[1]),
+            pltpu.make_async_copy(grad.at[:, cols(mine)], own, side_sems.at[2]),
         ]
     else:
-        keep, give, row, k, v, sems = refs
-        grad_copies = []
+        keep, give, row, k, v, ld, sems, side_sems = refs
+        side_copies = []
+    first = pltpu.make_async_copy(ld_hbm, ld, side_sems.at[0])
+    first.start()
     order = [(give, 0, False), (give, 1, False), (keep, 0, True), (keep, 1, True)]
     copies = []
     for slot, (_, y, same) in enumerate(order):
         cols_d = pl.ds(pl.multiple_of(quarter_of(y, same) * w, HEAD), w)
         both = [
-            pltpu.make_async_copy(k_hbm.at[:, cols_d], k.at[slot], sems.at[0, slot]),
-            pltpu.make_async_copy(v_hbm.at[:, cols_d], v.at[slot], sems.at[1, slot]),
+            pltpu.make_async_copy(k_hbm.at[:, cols_d], k.at[:, cols_d], sems.at[0, slot]),
+            pltpu.make_async_copy(v_hbm.at[:, cols_d], v.at[:, cols_d], sems.at[1, slot]),
         ]
         for c in both:
             c.start()
         copies.append(both)
-    for c in grad_copies:
+    for c in side_copies:
         c.start()
     at = lax.broadcasted_iota(jnp.int32, (BLOCK, BLOCK), 0)
     other = lax.broadcasted_iota(jnp.int32, (BLOCK, BLOCK), 1)
     tri = (at <= other).astype(BF16)
+    first.wait()
     x = ld[...]
     if heads < EXTRA:
         x = jnp.concatenate([x, jnp.zeros((EXTRA - heads, BLOCK), F32)], axis=0)
-    a, b, c = (nn(term, tri) for term in split_terms(x, 3))
-    row[...] = a + (b + c)
+    sums = nn(jnp.concatenate(split_terms(x, 3), axis=0), tri)
+    row[...] = sums[0:EXTRA] + (sums[EXTRA : 2 * EXTRA] + sums[2 * EXTRA : 3 * EXTRA])
     for slot, (out, y, same) in enumerate(order):
         for c in copies[slot]:
             c.wait()
         items = []
         for j in range(hq):
-            sums = row[pl.ds(quarter_of(y, same) * hq + j, 1), :]
+            h, c = head_at(quarter_of(y, same), hq, j)
+            sums = row[pl.ds(h, 1), :]
             edge = sums[:, BLOCK - 1 : BLOCK]
-            kd = (transposed(k[slot, :, chunk(j)]) * jnp.exp(edge - sums)).astype(BF16)
+            kd = (transposed(k[:, c]) * jnp.exp(edge - sums)).astype(BF16)
             spread = jnp.broadcast_to(edge, (1, HEAD))
-            items.append((nn(kd, v[slot, :, chunk(j)]), spread, jnp.zeros((1, HEAD), F32)))
+            items.append((nn(kd, v[:, c]), spread, jnp.zeros((1, HEAD), F32)))
         write_wide(out.at[y], hq, items)
-    for c in grad_copies:
+    for c in side_copies:
         c.wait()
 
 
-def decays_body(heads, row, _, col, growth, shrink):
-    hq = heads // TEAM
+def decays_body(heads, row, q_hbm, _, col, growth, shrink, q, sem):
+    hq = heads // TEAM
+    copy = pltpu.make_async_copy(q_hbm, q, sem)
+    copy.start()
     for g in range(TEAM):
         rows = row[g * hq : (g + 1) * hq, :]
         across = jnp.concatenate([rows, jnp.zeros((HEAD - hq, BLOCK), F32)], axis=0).T
         col[g] = across
         growth[g] = jnp.exp(across)
         shrink[g] = jnp.exp(across[BLOCK - 1 : BLOCK, :] - across)
-
-
-def lower_tiles(i):
-    tiles = [(s, WIDE, False) for s in range(0, (i // 2) * WIDE, WIDE)]
-    return tiles + [((i // 2) * WIDE, HEAD if i % 2 == 0 else WIDE, True)]
-
-
-def upper_tiles(i):
-    first = i * HEAD
-    width = WIDE if i % 2 == 0 else HEAD
-    return [(first, width, True)] + [(s, WIDE, False) for s in range(first + width, BLOCK, WIDE)]
-
-
-def lower_table(left, line, i, start, width, cut):
-    table = jnp.exp(left - line[:, start : start + width])
-    if cut:
-        at = lax.broadcasted_iota(jnp.int32, (HEAD, width), 0) + (i * HEAD - start)
-        table = jnp.where(at >= lax.broadcasted_iota(jnp.int32, (HEAD, width), 1), table, 0.0)
-    return table
-
-
-def upper_table(left, line, i, start, width, cut):
-    table = jnp.exp(line[:, start : start + width] - left)
-    if cut:
-        at = lax.broadcasted_iota(jnp.int32, (HEAD, width), 0)
-        table = jnp.where(at <= lax.broadcasted_iota(jnp.int32, (HEAD, width), 1), table, 0.0)
-    return table
-
-
-def intra_body(heads, q, k, v, row, col, _, intra):
-    hq = heads // TEAM
+    copy.wait()
+
+
+def decay_table(high, low, lower):
+    table = jnp.exp(high - low)
+    at = lax.broadcasted_iota(jnp.int32, (HALF, HALF), 0)
+    other = lax.broadcasted_iota(jnp.int32, (HALF, HALF), 1)
+    if lower:
+        cut = jnp.where(at >= other, table[:, -HALF:], 0.0)
+        return cut if table.shape[1] == HALF else jnp.concatenate([table[:, :HALF], cut], axis=1)
+    cut = jnp.where(at <= other, table[:, :HALF], 0.0)
+    return cut if table.shape[1] == HALF else jnp.concatenate([cut, table[:, HALF:]], axis=1)
+
+
+def turned_probs_body(heads, first, q, k, row, col, _, *refs):
+    hq = heads // TEAM
+    tables, probs = refs[-4:-2], refs[-2:]
 
     def one(g, _):
         for j in range(hq):
             h, c = head_at(g, hq, j)
             line = row[pl.ds(h, 1), :]
-            for i in range(BLOCK // HEAD):
-                left = col[g, chunk(i), j : j + 1]
-                total = None
-                for start, width, cut in lower_tiles(i):
-                    u = slice(start, start + width)
-                    table = lower_table(left, line, i, start, width, cut)
-                    probs = (nt(q[chunk(i), c], k[u, c]) * table).astype(BF16)
-                    term = nn(probs, v[u, c])
-                    total = term if total is None else total + term
-                intra[chunk(i), c] = total
+            for i in range(2):
+                t = slice(i * HALF, BLOCK)
+                table = decay_table(line[:, t], col[g, half(i), j : j + 1], False)
+                tables[i][h] = table
+                probs[i][h] = (nt(k[half(i), c], q[t, c]) * table).astype(BF16)
         return 0
 
+    lax.fori_loop(first, first + TEAM // 2, one, 0)
+
+
+def intra_body(heads, q, k, v, row, col, _, intra):
+    hq = heads // TEAM
+
+    def one(g, _):
+        for j in range(hq):
+            h, c = head_at(g, hq, j)
+            line = row[pl.ds(h, 1), :]
+            for i in range(2):
+                u = slice(0, (i + 1) * HALF)
+                table = decay_table(col[g, half(i), j : j + 1], line[:, u], True)
+                probs = (nt(q[half(i), c], k[u, c]) * table).astype(BF16)
+                intra[half(i), c] = nn(probs, v[u, c])
+        return 0
+
     lax.fori_loop(0, TEAM, one, 0)
 
 
-def dscaled_body(heads, swaps, gate, own, got, gain, q, row, dscaled, turned):
+def dscaled_body(heads, swaps, gate, own, got, gain, q, row, _, dscaled, turned):
     hq = heads // TEAM
     part = own.shape[0]
     mine = lax.axis_index("tp") if swaps else 0
@@ -350,34 +354,55 @@
     return [(ref.at[y], quarter_of(y, same)) for ref, same in ((mine, True), (got, False)) for y in range(2)]
 
 
-def attention_body(heads, q, intra, dscaled, growth, mine, got, att, sums, sq, inn):
-    hq = heads // TEAM
-    for i in range(BLOCK // HEAD):
-        r = chunk(i)
-        a_sq = jnp.zeros((HEAD, HEAD), F32)
-        a_in = jnp.zeros((HEAD, HEAD), F32)
-        for state, g in by_quarter(mine, got):
-            grow = growth[g, r, :]
-            for j in range(hq):
-                _, c = head_at(g, hq, j)
-                a = intra[r, c] + nn(q[r, c], state[chunk(j), :]) * grow[:, j : j + 1]
-                att[r, c] = a
-                a_sq = a_sq + a * a
-                a_in = a_in + a * dscaled[r, c]
-        sq[r, :] = a_sq
-        inn[r, :] = a_in
+def diagonal(a, b):
+    zero = jnp.zeros((HEAD, HEAD), BF16)
+    return jnp.concatenate(
+        [jnp.concatenate([a, zero], axis=1), jnp.concatenate([zero, b], axis=1)], axis=0
+    )
+
+
+def attention_body(heads, q, intra, dscaled, growth, mine, got, att, sums, sq, inn, both):
+    hq = heads // TEAM
+    sides = by_quarter(mine, got)
+    step = min(hq, 2)
+    for slot, (state, g) in enumerate(sides):
+        for j in range(0, hq, step):
+            _, c = head_at(g, hq, j)
+            if step == 2:
+                c = pl.ds(pl.multiple_of((g * hq + j) * HEAD, HEAD), 2 * HEAD)
+                both[...] = nn(q[:, c], diagonal(state[chunk(j), :], state[chunk(j + 1), :]))
+            else:
+                both[:, 0:HEAD] = nn(q[:, c], state[chunk(j), :])
+            for i in range(BLOCK // HEAD):
+                r = chunk(i)
+                a_sq = a_in = 0.0
+                for m in range(step):
+                    _, c = head_at(g, hq, j + m)
+                    a = intra[r, c] + both[r, chunk(m)] * growth[g, r, j + m : j + m + 1]
+                    att[r, c] = a
+                    a_sq = a_sq + a * a
+                    a_in = a_in + a * dscaled[r, c]
+                if slot == 0 and j == 0:
+                    sq[r, :] = a_sq
+                    inn[r, :] = a_in
+                else:
+                    sq[r, :] += a_sq
+                    inn[r, :] += a_in
     ones = jnp.ones((8, HEAD), F32)
     a = nt(ones, sq[...], lax.Precision.HIGHEST)
     b = nt(ones, inn[...], lax.Precision.HIGHEST)
     sums[...] = jnp.where(lax.broadcasted_iota(jnp.int32, (8, BLOCK), 0) == 0, a, b)
 
 
-def dattn_body(heads, channels, att, dscaled, turned, gain, row, sum_a, sum_b, dattn, scale, keep, give):
+def dattn_body(heads, channels, att, dscaled, turned, gain, row, sum_a, sum_b, dattn, scale, keep, give, rsb, coefb):
     hq = heads // TEAM
     total = sum_a[...] + sum_b[...]
     rs = lax.rsqrt(total[0:1, :] / channels + EPSILON)
     coef = total[1:2, :] * (rs * rs * rs) / channels
-    scale[...] = jnp.concatenate([rs, coef, jnp.zeros((HEAD - 2, BLOCK), F32)], axis=0).T
+    down = jnp.concatenate([rs, coef, jnp.zeros((HEAD - 2, BLOCK), F32)], axis=0).T
+    rsb[...] = jnp.broadcast_to(down[:, 0:1], (BLOCK, HEAD))
+    coefb[...] = jnp.broadcast_to(down[:, 1:2], (BLOCK, HEAD))
+    scale[...] = rsb[...]
     for out, y, same in ((give, 0, False), (give, 1, False), (keep, 0, True), (keep, 1, True)):
         items = []
         for j in range(hq):
@@ -386,8 +411,8 @@
             for i in range(BLOCK // HEAD):
                 r = chunk(i)
                 a = att[r, c]
-                t = dscaled[r, c] * scale[r, 0:1]
-                dattn[r, c] = (t - a * scale[r, 1:2]).astype(BF16)
+                t = dscaled[r, c] * rsb[r, :]
+                dattn[r, c] = (t - a * coefb[r, :]).astype(BF16)
                 gsum = gsum + jnp.sum((t * a).reshape(HEAD // 8, 8, HEAD), axis=0)
             edge = jnp.broadcast_to(row[pl.ds(h, 1), :][:, BLOCK - 1 : BLOCK], (1, HEAD))
             part = jnp.sum(gsum, axis=0, keepdims=True) / gain[:, c]
@@ -395,58 +420,59 @@
         write_wide(out.at[y], hq, items)
 
 
-def gate_body(heads, gate, att, dscaled, scale, _, gate_grad, token):
+def leave(out, ref, sems, g, w):
+    cols = pl.ds(pl.multiple_of(g * w, HEAD), w)
+    copy = pltpu.make_async_copy(out, ref.at[:, cols], sems)
+    copy.start()
+    return copy
+
+
+def gate_body(heads, gate, att, dscaled, scale, _, gate_grad, token, out, sems):
+    hq = heads // TEAM
     token[...] = jnp.zeros_like(token)
-
-    def one(h, _):
-        _, c = head_at(h, 1, 0)
-        opened = jax.nn.sigmoid(gate[:, c].astype(F32))
-        gate_grad[:, c] = (dscaled[:, c] * att[:, c] * scale[:, 0:1] * (1.0 - opened)).astype(BF16)
-        return 0
-
-    lax.fori_loop(0, heads, one, 0)
-
-
-def query_body(heads, k, v, dattn, row, col, growth, mine, got, _, query_grad, token):
+    copies = []
+    for g in range(TEAM):
+        for j in range(hq):
+            _, c = head_at(g, hq, j)
+            opened = jax.nn.sigmoid(gate[:, c].astype(F32))
+            out[g, :, chunk(j)] = (dscaled[:, c] * att[:, c] * scale[...] * (1.0 - opened)).astype(BF16)
+        copies.append(leave(out.at[g], gate_grad, sems.at[g], g, hq * HEAD))
+    for copy in copies:
+        copy.wait()
+
+
+def query_body(heads, k, v, dattn, row, col, growth, mine, got, _, query_grad, token, out, sems):
+    hq = heads // TEAM
     token[...] = jnp.zeros_like(token)
-    hq = heads // TEAM
-    for state, g in by_quarter(mine, got):
+    copies = []
+    for slot, (state, g) in enumerate(by_quarter(mine, got)):
         for j in range(hq):
             h, c = head_at(g, hq, j)
             line = row[pl.ds(h, 1), :]
-            for i in range(BLOCK // HEAD):
-                d = dattn[chunk(i), c]
-                left = col[g, chunk(i), j : j + 1]
-                total = nt(d, state[chunk(j), :]) * growth[g, chunk(i), j : j + 1]
-                for start, width, cut in lower_tiles(i):
-                    u = slice(start, start + width)
-                    table = lower_table(left, line, i, start, width, cut)
-                    dscores = (nt(d, v[u, c]) * table).astype(BF16)
-                    total = total + nn(dscores, k[u, c])
-                query_grad[chunk(i), c] = total.astype(BF16)
-
-
-def key_value_body(heads, first, q, k, v, dattn, row, col, *refs):
+            for i in range(2):
+                d = dattn[half(i), c]
+                u = slice(0, (i + 1) * HALF)
+                table = decay_table(col[g, half(i), j : j + 1], line[:, u], True)
+                dscores = (nt(d, v[u, c]) * table).astype(BF16)
+                inter = nt(d, state[chunk(j), :]) * growth[g, half(i), j : j + 1]
+                out[slot, half(i), chunk(j)] = (inter + nn(dscores, k[u, c])).astype(BF16)
+        copies.append(leave(out.at[slot], query_grad, sems.at[slot], g, hq * HEAD))
+    for copy in copies:
+        copy.wait()
+
+
+def key_value_body(heads, first, q, v, dattn, table0, table1, probs0, probs1, _, *refs):
     hq = heads // TEAM
     dk, dv = refs[-2:]
 
     def one(g, _):
         for j in range(hq):
             h, c = head_at(g, hq, j)
-            line = row[pl.ds(h, 1), :]
-            for i in range(BLOCK // HEAD):
-                left = col[g, chunk(i), j : j + 1]
-                dkey = dvalue = None
-                for start, width, cut in upper_tiles(i):
-                    t = slice(start, start + width)
-                    table = upper_table(left, line, i, start, width, cut)
-                    probs = (nt(k[chunk(i), c], q[t, c]) * table).astype(BF16)
-                    dscores = (nt(v[chunk(i), c], dattn[t, c]) * table).astype(BF16)
-                    a = nn(dscores, q[t, c])
-                    b = nn(probs, dattn[t, c])
-                    dkey, dvalue = (a, b) if dkey is None else (dkey + a, dvalue + b)
-                dk[chunk(i), c] = dkey
-                dv[chunk(i), c] = dvalue
+            for i, (table, probs) in enumerate(((table0, probs0), (table1, probs1))):
+                t = slice(i * HALF, BLOCK)
+                dscores = (nt(v[half(i), c], dattn[t, c]) * table[h]).astype(BF16)
+                dk[half(i), c] = nn(dscores, q[t, c])
+                dv[half(i), c] = nn(probs[h], dattn[t, c])
         return 0
 
     lax.fori_loop(first, first + TEAM // 2, one, 0)
@@ -462,14 +488,14 @@
             _, c = head_at(g, hq, j)
             fade = shrink[g, :, j : j + 1]
             after = state[chunk(j), :]
-            key_out[slot, :, chunk(j)] = (dk[:, c] + nt(v[:, c], after) * fade).astype(BF16)
-            value_out[slot, :, chunk(j)] = (dv[:, c] + nn(k[:, c], after) * fade).astype(BF16)
+            side = jnp.concatenate([k[:, c], v[:, c]], axis=1)
+            back = items[j][0].T.astype(BF16)
+            both = nn(side, diagonal(after, back))
+            key_out[slot, :, chunk(j)] = (dk[:, c] + both[:, HEAD:] * fade).astype(BF16)
+            value_out[slot, :, chunk(j)] = (dv[:, c] + both[:, :HEAD] * fade).astype(BF16)
             gain_grad[:, c] = items[j][2]
-        cols = pl.ds(pl.multiple_of(g * w, HEAD), w)
-        for i, (src, dst) in enumerate(((key_out, key_grad), (value_out, value_grad))):
-            copy = pltpu.make_async_copy(src.at[slot], dst.at[:, cols], sems.at[i, slot])
-            copy.start()
-            copies.append(copy)
+        copies.append(leave(key_out.at[slot], key_grad, sems.at[0, slot], g, w))
+        copies.append(leave(value_out.at[slot], value_grad, sems.at[1, slot], g, w))
     for copy in copies:
         copy.wait()
 
@@ -521,20 +547,9 @@
             in_specs=[VMEM] * len(inputs) + [ANY] * len(unread),
         )
 
-    def scan(reverse, keep, give, held, work):
+    def scan(reverse, keep, give, work):
         got = swap(give, 1)
-        if held is None:
-            own, send = step_call(chip_total_body, True, [keep, got], [], [wide, narrow], "chip_total_back")
-        else:
-            own, send, held = call(
-                functools.partial(chip_total_body, False, hq),
-                [keep, got, held],
-                [wide, narrow, jax.ShapeDtypeStruct(held.shape, held.dtype)],
-                "chip_total",
-                in_specs=[VMEM, VMEM, ANY],
-                out_specs=[VMEM, VMEM, ANY],
-                alias={2: 2},
-            )
+        own, send = step_call(chip_total_body, reverse, [keep, got], [], [wide, narrow], "chip_total")
         got_pair = swap(send, 2)
         unread = beside(work, send, "pair")
         total, send = step_call(group_total_body, reverse, [own, got_pair], unread, [wide, narrow], "group_total")
@@ -564,37 +579,57 @@
         mine, send = step_call(
             into_cores_body, reverse, [keep, got, kept, other], unread, [narrow2, narrow2], "into_cores"
         )
-        return mine, swap(send, 1), held
+        return mine, swap(send, 1)
 
     outs = call(
         functools.partial(local_states_body, heads, swaps),
-        [in_hbm(keys), in_hbm(values), log_decay] + [in_hbm(grad_out)] * swaps,
-        [wide2, wide2, f32(EXTRA, rows)] + [bf(part, width)] * 2 * swaps,
+        [in_hbm(keys), in_hbm(values), in_hbm(log_decay)] + [in_hbm(grad_out)] * swaps,
+        [wide2, wide2, f32(EXTRA, rows), bf(rows, width), bf(rows, width)] + [bf(part, width)] * 2 * swaps,
         "local_states",
-        [pltpu.VMEM((TEAM, rows, hq * HEAD), BF16)] * 2
-        + [pltpu.SemaphoreType.DMA((2, TEAM))]
-        + [pltpu.SemaphoreType.DMA((2,))] * swaps,
+        [
+            pltpu.VMEM(log_decay.shape, F32),
+            pltpu.SemaphoreType.DMA((2, TEAM)),
+            pltpu.SemaphoreType.DMA((3,)),
+        ],
         small,
-        [HBM, HBM, VMEM] + [HBM] * swaps,
-        [VMEM] * 3 + [HBM, VMEM] * swaps,
+        [HBM] * (3 + swaps),
+        [VMEM] * 5 + [HBM, VMEM] * swaps,
     )
-    keep, give, row = outs[:3]
+    keep, give, row, keys, values = outs[:5]
+    if swaps:
+        own = outs[6]
+        arrived = lax.ppermute(outs[5], "tp", [(0, 1), (1, 0)])
+    else:
+        every = lax.all_to_all(grad_out, "tp", split_axis=1, concat_axis=0, tiled=True)
+        own, arrived = every[:part], every[part:]
     done = {}
 
-    def decays_beside(after):
-        done["decays"] = call(
-            functools.partial(decays_body, heads),
-            [row, after],
-            [table] * 3,
-            "decays",
-            in_specs=[VMEM, ANY],
-        )
-        return done["decays"][0]
+    def probs_beside(after):
+        if "decays" not in done:
+            *done["decays"], done["queries"] = call(
+                functools.partial(decays_body, heads),
+                [row, in_hbm(queries), after],
+                [table] * 3 + [bf(rows, width)],
+                "decays",
+                [pltpu.SemaphoreType.DMA(())],
+                in_specs=[VMEM, HBM, ANY],
+            )
+        before = done.get("probs", [])
+        done["probs"] = call(
+            functools.partial(turned_probs_body, heads, TEAM // 2 if before else 0),
+            [done["queries"], keys, row, done["decays"][0], after, *before],
+            [f32(heads, HALF, BLOCK), f32(heads, HALF, HALF), bf(heads, HALF, BLOCK), bf(heads, HALF, HALF)],
+            "turned_probs",
+            flops=large // 2,
+            in_specs=[VMEM] * 4 + [ANY] + [VMEM] * len(before),
+            alias={5 + i: i for i in range(len(before))},
+        )
+        return done["probs"][3]
 
     def intra_beside(after):
         (done["intra"],) = call(
             functools.partial(intra_body, heads),
-            [queries, keys, values, row, done["decays"][0], after],
+            [done["queries"], keys, values, row, done["decays"][0], after],
             [f32(rows, width)],
             "intra",
             flops=2 * large,
@@ -602,28 +637,27 @@
         )
         return done["intra"]
 
-    held = outs[3] if swaps else keep
-    mine, got, held = scan(False, keep, give, held, {"one": decays_beside, "last": intra_beside})
-    (col, growth, shrink), intra = done["decays"], done["intra"]
-    if swaps:
-        own = outs[4]
-        arrived = lax.ppermute(held, "tp", [(0, 1), (1, 0)])
-    else:
-        every = lax.all_to_all(grad_out, "tp", split_axis=1, concat_axis=0, tiled=True)
-        own, arrived = every[:part], every[part:]
-    dscaled, turned = call(
-        functools.partial(dscaled_body, heads, swaps),
-        [gate, own, arrived, gain_row, queries, row],
-        [f32(rows, width), bf(heads, HEAD, rows)],
-        "dscaled",
-        flops=small,
-    )
+    def dscaled_beside(after):
+        done["dscaled"] = call(
+            functools.partial(dscaled_body, heads, swaps),
+            [gate, own, arrived, gain_row, done["queries"], row, after],
+            [f32(rows, width), bf(heads, HEAD, rows)],
+            "dscaled",
+            flops=small,
+            in_specs=[VMEM] * 6 + [ANY],
+        )
+        return done["dscaled"][0]
+
+    work = {"pair": probs_beside, "one": probs_beside, "last": intra_beside, "pair_back": dscaled_beside}
+    mine, got = scan(False, keep, give, work)
+    queries = done["queries"]
+    (col, growth, shrink), intra, (dscaled, turned) = done["decays"], done["intra"], done["dscaled"]
     att, sums = call(
         functools.partial(attention_body, heads),
         [queries, intra, dscaled, growth, mine, got],
         [f32(rows, width), f32(8, rows)],
         "attention",
-        [pltpu.VMEM((rows, HEAD), F32)] * 2,
+        [pltpu.VMEM((rows, HEAD), F32)] * 2 + [pltpu.VMEM((rows, 2 * HEAD), F32)],
         small,
     )
     if swaps:
@@ -635,27 +669,32 @@
         [att, dscaled, turned, gain_row, row, sums, others],
         [bf(rows, width), f32(rows, HEAD), wide2, wide2],
         "dattn",
-        flops=small,
+        [pltpu.VMEM((rows, HEAD), F32)] * 2,
+        small,
     )
+    out_scratch = [pltpu.VMEM((TEAM, rows, hq * HEAD), BF16), pltpu.SemaphoreType.DMA((TEAM,))]
+
     def gate_beside(after):
         done["gate"], token = call(
             functools.partial(gate_body, heads),
             [gate, att, dscaled, scale, after],
             [bf(rows, width), f32(SIDE, HEAD)],
             "gate",
-            flops=small,
-            in_specs=[VMEM] * 4 + [ANY],
+            out_scratch,
+            small,
+            [VMEM] * 4 + [ANY],
+            [HBM, VMEM],
         )
         return token
 
     def key_value_first(after):
         done["key_value"] = call(
             functools.partial(key_value_body, heads, 0),
-            [queries, keys, values, dattn, row, col, after],
+            [queries, values, dattn, *done["probs"], after],
             [f32(rows, width)] * 2,
             "key_value",
             flops=2 * large,
-            in_specs=[VMEM] * 6 + [ANY],
+            in_specs=[VMEM] * 7 + [ANY],
         )
         return done["key_value"][0]
 
@@ -665,25 +704,27 @@
             [keys, values, dattn, row, col, growth, mine, got, after],
             [bf(rows, width), f32(SIDE, HEAD)],
             "query",
-            flops=2 * large + small,
-            in_specs=[VMEM] * 8 + [ANY],
+            out_scratch,
+            2 * large + small,
+            [VMEM] * 8 + [ANY],
+            [HBM, VMEM],
         )
         return token
 
     def key_value_last(after):
         done["key_value"] = call(
             functools.partial(key_value_body, heads, TEAM // 2),
-            [queries, keys, values, dattn, row, col, after, *done["key_value"]],
+            [queries, values, dattn, *done["probs"], after, *done["key_value"]],
             [f32(rows, width)] * 2,
             "key_value",
             flops=2 * large,
-            in_specs=[VMEM] * 6 + [ANY, VMEM, VMEM],
-            alias={7: 0, 8: 1},
+            in_specs=[VMEM] * 7 + [ANY, VMEM, VMEM],
+            alias={8: 0, 9: 1},
         )
         return done["key_value"][0]
 
     work = {"pair": gate_beside, "one": key_value_first, "last": query_beside, "pair_back": key_value_last}
-    back_mine, back_got, _ = scan(True, keep, give, None, work)
+    back_mine, back_got = scan(True, keep, give, work)
     gate_grad, query_grad, (dk, dv) = done["gate"], done["query"], done["key_value"]
     key_grad, value_grad, gain_grad = call(
         functools.partial(final_body, heads),

time: 100 us -> 84.2 us (0.84)
  Pallas kernels: 60.9 us -> 48 us
  waiting for transfers between devices: 20.7 us -> 15.7 us
  starting transfers between devices: 16.6 us -> 19.2 us
    pallas_call x21 -> x23, Pallas kernels: 60.9 us -> 48 us  [call(): pl.pallas_call(body, in_specs=in_specs or [VMEM] * len(inputs), out_specs...]
    ppermute x8, waiting for transfers between devices: 12.7 us -> 7.18 us  [swap(): return lax.ppermute(x, 'ctx', [(i, i ^ bit) for i in range(n)])]
    ppermute x1, waiting for transfers between devices: 0.01 us -> 1.65 us  [local(): arrived = lax.ppermute(outs[5], 'tp', [(0, 1), (1, 0)])]
    ppermute x1, waiting for transfers between devices: 3.2 us -> 1.99 us  [local(): others = lax.ppermute(sums, 'tp', [(0, 1), (1, 0)])]
    ppermute x1, starting transfers between devices: 0.57 us -> 1.77 us  [local(): others = lax.ppermute(sums, 'tp', [(0, 1), (1, 0)])]
    ppermute x4, starting transfers between devices: 6.04 us -> 7.2 us  [across(): return lax.ppermute(x, 'ctx', [(i, (i + TEAM * k) % n) for i in range(n)])]
  transfers between devices with their start and end apart: 14 -> 14, of which waited for: 8 -> 10; matrix products, arithmetic and copies ran while one was open for 0% -> 0% of each run, Pallas kernels for 44% -> 37%
where the time goes in v5:
time: 84.2 us; the launch traced here: 84 us
  Pallas kernels  48 us (57%)
  starting transfers between devices  19.2 us (23%)
  waiting for transfers between devices  15.7 us (19%)
  between operations  1.07 us (1%)
    pallas_call x23, Pallas kernels, call(): pl.pallas_call(body, in_specs=in_specs or [VMEM] * len(inputs), out_specs...  48 us
    ppermute x8, starting transfers between devices, swap(): return lax.ppermute(x, 'ctx', [(i, i ^ bit) for i in range(n)])  7.67 us
    ppermute x4, starting transfers between devices, across(): return lax.ppermute(x, 'ctx', [(i, (i + TEAM * k) % n) for i in range(n)])  7.2 us
    ppermute x8, waiting for transfers between devices, swap(): return lax.ppermute(x, 'ctx', [(i, i ^ bit) for i in range(n)])  7.18 us
    ppermute x4, waiting for transfers between devices, across(): return lax.ppermute(x, 'ctx', [(i, (i + TEAM * k) % n) for i in range(n)])  4.92 us
    ppermute x1, starting transfers between devices, local(): arrived = lax.ppermute(outs[5], 'tp', [(0, 1), (1, 0)])  2.56 us
    ppermute x1, waiting for transfers between devices, local(): others = lax.ppermute(sums, 'tp', [(0, 1), (1, 0)])  1.99 us
    ppermute x1, starting transfers between devices, local(): others = lax.ppermute(sums, 'tp', [(0, 1), (1, 0)])  1.77 us
  transfers between devices with their start and end apart: 14, of which 10 were waited for; matrix products, arithmetic and copies ran while one was open for 0% of the time, Pallas kernels for 37%

profile of v5, /device:TPU:0, one launch (start us, length us, event | category | flops | bytes accessed | tf_op | source)
XLA Modules:
  0.0 84.0 jit_solution(17471656113035691614)
XLA Ops:
  0.6 5.0 %local_states.1 = (f32[2,520,128]{2,1,0:T(8,128)S(1)}, f32[2,520,128]{2,1,0:T(8,128)S(1)}, f32[16,512]{1,0:T(8,128)S(1)}, bf16[512,2048]{1,0:T(8,128)(2,1)S(1)},...) custom-call(bf16[512,2048]{1,0:T(8,128)(2,1)} %k_hbm.1, ...), custom_call_target="tpu_custom_call" | custom-call | flops 268435456 | bytes 13713408 | tf_op jit(solution)/shard_map/local_states/pallas_call | solution.py:119
  6.2 2.6 %collective-permute-start.3 = (bf16[256,2048]{1,0:T(8,128)(2,1)S(1)}, bf16[256,2048]{1,0:T(8,128)(2,1)S(1)}, u32[]{:S(2)}, u32[]{:S(2)}) collective-permute-start(bf16[256,2048]{1,0:T(8,128)(2,1)S(1)} %get-tuple-element.81), channel_id=1, source_target_pairs={{0,1},{1,0},{2,3},{3,2},{4,5},{5,4},{6,7},{7,6},{8,9},{9,8},{10,11... | collective-permute-start | bytes 3145736 | tf_op jit(solution)/shard_map/ppermute | solution.py:601
  8.8 1.9 %collective-permute-start.1 = (bf16[528,128]{1,0:T(8,128)(2,1)S(1)}, bf16[528,128]{1,0:T(8,128)(2,1)S(1)}, u32[]{:S(2)}, u32[]{:S(2)}) collective-permute-start(bf16[528,128]{1,0:T(8,128)(2,1)S(1)} %get-tuple-element.68._), channel_id=1, source_target_pairs={{0,4},{2,6},{4,0},{6,2},{8,12},{10,14},{12,8},{14,10},{16,20},{18,... | collective-permute-start | bytes 405512 | tf_op jit(solution)/shard_map/ppermute | solution.py:509
  10.8 1.6 %decays.1 = (f32[4,512,128]{2,1,0:T(8,128)S(1)}, f32[4,512,128]{2,1,0:T(8,128)S(1)}, f32[4,512,128]{2,1,0:T(8,128)S(1)}, bf16[512,2048]{1,0:T(8,128)(2,1)S(1)}) custom-call(f32[16,512]{1,0:T(8,128)S(1)} %get-tuple-element.65.row, bf16[512,2048]{1,0:T(8,128)(2,1)} %q_hbm.1, bf16[528,128]{1,0:T(8,128)(2,1)S(1)} %get-tuple-element.68._), custom_call_target="tpu_custom_call" | custom-call | bytes 7507968 | tf_op jit(solution)/shard_map/decays/pallas_call | solution.py:119
  12.4 1.6 %turned_probs.2 = (f32[16,256,512]{2,1,0:T(8,128)S(1)}, f32[16,256,256]{2,1,0:T(8,128)S(1)}, bf16[16,256,512]{2,1,0:T(8,128)(2,1)S(1)}, bf16[16,256,256]{2,1,0:T(8,128)(2,1)S(1)}) custom-call(bf16[512,2048]{1,0:T(8,128)(2,1)S(1)} %get-tuple-element.69.q, bf16[512,2048]{1,0:T(8,128)(2,1)S(1)} %get-tuple-element.63.k, f32[16,512]{1,0:T(8,128)S(1)} %get-tuple-element.65.row, ...), custom_call_target="tpu_custom_call" | custom-call | flops 536870912 | bytes 24285184 | tf_op jit(solution)/shard_map/turned_probs/pallas_call | solution.py:119
  14.7 2.0 %collective-permute-start.2 = (bf16[528,128]{1,0:T(8,128)(2,1)S(1)}, bf16[528,128]{1,0:T(8,128)(2,1)S(1)}, u32[]{:S(2)}, u32[]{:S(2)}) collective-permute-start(bf16[528,128]{1,0:T(8,128)(2,1)S(1)} %get-tuple-element.74._), channel_id=1, source_target_pairs={{0,8},{2,10},{4,12},{6,14},{8,16},{10,18},{12,20},{14,22},{16,24},... | collective-permute-start | bytes 405512 | tf_op jit(solution)/shard_map/ppermute | solution.py:514
  16.8 1.6 %turned_probs.3 = (f32[16,256,512]{2,1,0:T(8,128)S(1)}, f32[16,256,256]{2,1,0:T(8,128)S(1)}, bf16[16,256,512]{2,1,0:T(8,128)(2,1)S(1)}, bf16[16,256,256]{2,1,0:T(8,128)(2,1)S(1)}) custom-call(bf16[512,2048]{1,0:T(8,128)(2,1)S(1)} %get-tuple-element.69.q, ...), custom_call_target="tpu_custom_call", output_to_operand_aliasing={{0}: (5, {}), {1}: (6, {}), {2}: (7, {}), {3}: (8, {})} | custom-call | flops 536870912 | bytes 43159552 | tf_op jit(solution)/shard_map/turned_probs/pallas_call | solution.py:119
  18.4 3.4 %collective-permute-done.2.refs_0_ = bf16[528,128]{1,0:T(8,128)(2,1)S(1)} collective-permute-done((bf16[528,128]{1,0:T(8,128)(2,1)S(1)}, bf16[528,128]{1,0:T(8,128)(2,1)S(1)}, u32[]{:S(2)}, u32[]{:S(2)}) %collective-permute-start.2) | collective-permute-done | bytes 135200 | tf_op jit(solution)/shard_map/ppermute | solution.py:514
  22.9 5.8 %intra.1.refs_0_ = f32[512,2048]{1,0:T(8,128)S(1)} custom-call(bf16[512,2048]{1,0:T(8,128)(2,1)S(1)} %get-tuple-element.69.q, bf16[512,2048]{1,0:T(8,128)(2,1)S(1)} %get-tuple-element.63.k, bf16[512,2048]{1,0:T(8,128)(2,1)S(1)} %get-tuple-element.64.v, f32[16,512]{1,0:T(8,128)S(1)} %get-tuple-element.65.row, f32[4,512,128]{2,1,0:T(8,128)S(1)} %get-tuple-element.70.col, ...), custom_call_target="tpu_custom_call" | custom-call | flops 2147483648 | bytes 11702272 | tf_op jit(solution)/shard_map/intra/pallas_call | solution.py:119
  29.2 1.6 %collective-permute-start.5 = (bf16[528,128]{1,0:T(8,128)(2,1)S(1)}, bf16[528,128]{1,0:T(8,128)(2,1)S(1)}, u32[]{:S(2)}, u32[]{:S(2)}) collective-permute-start(bf16[528,128]{1,0:T(8,128)(2,1)S(1)} %get-tuple-element.83._), channel_id=1, source_target_pairs={{0,4},{2,6},{4,0},{6,2},{8,12},{10,14},{12,8},{14,10},{16,20},{18,... | collective-permute-start | bytes 405512 | tf_op jit(solution)/shard_map/ppermute | solution.py:509
  30.8 1.7 %collective-permute-done.3.got = bf16[256,2048]{1,0:T(8,128)(2,1)S(1)} collective-permute-done((bf16[256,2048]{1,0:T(8,128)(2,1)S(1)}, bf16[256,2048]{1,0:T(8,128)(2,1)S(1)}, u32[]{:S(2)}, u32[]{:S(2)}) %collective-permute-start.3) | collective-permute-done | bytes 1048608 | tf_op jit(solution)/shard_map/ppermute | solution.py:601
  32.5 2.8 %dscaled.1 = (f32[512,2048]{1,0:T(8,128)S(1)}, bf16[16,128,512]{2,1,0:T(8,128)(2,1)S(1)}) custom-call(bf16[512,2048]{1,0:T(8,128)(2,1)S(1)} %copy-done.6, bf16[256,2048]{1,0:T(8,128)(2,1)S(1)} %get-tuple-element.80.own, bf16[256,2048]{1,0:T(8,128)(2,1)S(1)} %collective-permute-done.3.got, f32[1,2048]{1,0:T(1,128)S(1)} %bitcast.2, ...), custom_call_target="tpu_custom_call" | custom-call | flops 268435456 | bytes 12759040 | tf_op jit(solution)/shard_map/dscaled/pallas_call | solution.py:119
  37.2 2.9 %attention.1 = (f32[512,2048]{1,0:T(8,128)S(1)}, f32[8,512]{1,0:T(8,128)S(1)}) custom-call(bf16[512,2048]{1,0:T(8,128)(2,1)S(1)} %get-tuple-element.69.q, f32[512,2048]{1,0:T(8,128)S(1)} %intra.1.refs_0_, f32[512,2048]{1,0:T(8,128)S(1)} %get-tuple-element.84.refs_0_.dscaled, f32[4,512,128]{2,1,0:T(8,128)S(1)} %get-tuple-element.85.growth, ...), custom_call_target="tpu_custom_call" | custom-call | flops 268435456 | bytes 16285696 | tf_op jit(solution)/shard_map/attention/pallas_call | solution.py:119
  40.0 1.8 %collective-permute-start.7 = (f32[8,512]{1,0:T(8,128)S(1)}, f32[8,512]{1,0:T(8,128)S(1)}, u32[]{:S(2)}, u32[]{:S(2)}) collective-permute-start(f32[8,512]{1,0:T(8,128)S(1)} %get-tuple-element.91.sum_a), channel_id=1, source_target_pairs={{0,1},{1,0},{2,3},{3,2},{4,5},{5,4},{6,7},{7,6},{8,9},{9,8},{10,11... | collective-permute-start | bytes 49160 | tf_op jit(solution)/shard_map/ppermute | solution.py:664
  41.8 2.0 %collective-permute-done.7.sum_b = f32[8,512]{1,0:T(8,128)S(1)} collective-permute-done((f32[8,512]{1,0:T(8,128)S(1)}, f32[8,512]{1,0:T(8,128)S(1)}, u32[]{:S(2)}, u32[]{:S(2)}) %collective-permute-start.7) | collective-permute-done | bytes 16416 | tf_op jit(solution)/shard_map/ppermute | solution.py:664
  43.8 3.5 %dattn.1 = (bf16[512,2048]{1,0:T(8,128)(2,1)S(1)}, f32[512,128]{1,0:T(8,128)S(1)}, f32[2,520,128]{2,1,0:T(8,128)S(1)}, f32[2,520,128]{2,1,0:T(8,128)S(1)}) custom-call(f32[512,2048]{1,0:T(8,128)S(1)} %get-tuple-element.89.att, f32[512,2048]{1,0:T(8,128)S(1)} %get-tuple-element.84.refs_0_.dscaled, bf16[16,128,512]{2,1,0:T(8,128)(2,1)S(1)} %get-tuple-element.90.turned, ...), custom_call_target="tpu_custom_call" | custom-call | flops 268435456 | bytes 13983744 | tf_op jit(solution)/shard_map/dattn/pallas_call | solution.py:119
  47.4 1.9 %collective-permute-done.8.got = f32[2,520,128]{2,1,0:T(8,128)S(1)} collective-permute-done((f32[2,520,128]{2,1,0:T(8,128)S(1)}, f32[2,520,128]{2,1,0:T(8,128)S(1)}, u32[]{:S(2)}, u32[]{:S(2)}) %collective-permute-start.8) | collective-permute-done | bytes 532512 | tf_op jit(solution)/shard_map/ppermute | solution.py:509
  49.4 1.8 %collective-permute-start.9 = (bf16[528,128]{1,0:T(8,128)(2,1)S(1)}, bf16[528,128]{1,0:T(8,128)(2,1)S(1)}, u32[]{:S(2)}, u32[]{:S(2)}) collective-permute-start(bf16[528,128]{1,0:T(8,128)(2,1)S(1)} %get-tuple-element.96._), channel_id=1, source_target_pairs={{0,4},{2,6},{4,0},{6,2},{8,12},{10,14},{12,8},{14,10},{16,20},{18,... | collective-permute-start | bytes 405512 | tf_op jit(solution)/shard_map/ppermute | solution.py:509
  51.3 2.3 %gate.4 = (bf16[512,2048]{1,0:T(8,128)(2,1)}, f32[8,128]{1,0:T(8,128)S(1)}) custom-call(bf16[512,2048]{1,0:T(8,128)(2,1)S(1)} %copy-done.6, f32[512,2048]{1,0:T(8,128)S(1)} %get-tuple-element.89.att, f32[512,2048]{1,0:T(8,128)S(1)} %get-tuple-element.84.refs_0_.dscaled, f32[512,128]{1,0:T(8,128)S(1)} %get-tuple-element.97.scale, ...), custom_call_target="tpu_custom_call" | custom-call | flops 268435456 | bytes 12984320 | tf_op jit(solution)/shard_map/gate/pallas_call | solution.py:119
  55.2 4.1 %collective-permute-start.10 = (bf16[528,128]{1,0:T(8,128)(2,1)S(1)}, bf16[528,128]{1,0:T(8,128)(2,1)S(1)}, u32[]{:S(2)}, u32[]{:S(2)}) collective-permute-start(bf16[528,128]{1,0:T(8,128)(2,1)S(1)} %get-tuple-element.100._), channel_id=1, source_target_pairs={{0,24},{2,26},{4,28},{6,30},{8,0},{10,2},{12,4},{14,6},{16,8},{18,... | collective-permute-start | bytes 405512 | tf_op jit(solution)/shard_map/ppermute | solution.py:514
  59.3 4.0 %key_value.2 = (f32[512,2048]{1,0:T(8,128)S(1)}, f32[512,2048]{1,0:T(8,128)S(1)}) custom-call(bf16[512,2048]{1,0:T(8,128)(2,1)S(1)} %get-tuple-element.69.q, bf16[512,2048]{1,0:T(8,128)(2,1)S(1)} %get-tuple-element.64.v, bf16[512,2048]{1,0:T(8,128)(2,1)S(1)} %get-tuple-element.92.dattn, f32[16,256,512]{2,1,0:T(8,128)S(1)} %get-tuple-element.101.table0, ...), custom_call_target="tpu_custom_call" | custom-call | flops 2147483648 | bytes 33689600 | tf_op jit(solution)/shard_map/key_value/pallas_call | solution.py:119
  63.5 6.4 %query.1 = (bf16[512,2048]{1,0:T(8,128)(2,1)}, f32[8,128]{1,0:T(8,128)S(1)}) custom-call(bf16[512,2048]{1,0:T(8,128)(2,1)S(1)} %get-tuple-element.63.k, bf16[512,2048]{1,0:T(8,128)(2,1)S(1)} %get-tuple-element.64.v, bf16[512,2048]{1,0:T(8,128)(2,1)S(1)} %get-tuple-element.92.dattn, f32[16,512]{1,0:T(8,128)S(1)} %get-tuple-element.65.row, ...), custom_call_target="tpu_custom_call" | custom-call | flops 2415919104 | bytes 11198464 | tf_op jit(solution)/shard_map/query/pallas_call | solution.py:119
  72.8 4.2 %key_value.3 = (f32[512,2048]{1,0:T(8,128)S(1)}, f32[512,2048]{1,0:T(8,128)S(1)}) custom-call(bf16[512,2048]{1,0:T(8,128)(2,1)S(1)} %get-tuple-element.69.q, bf16[512,2048]{1,0:T(8,128)(2,1)S(1)} %get-tuple-element.64.v, bf16[512,2048]{1,0:T(8,128)(2,1)S(1)} %get-tuple-element.92.dattn, ...), custom_call_target="tpu_custom_call", output_to_operand_aliasing={{0}: (8, {}), {1}: (9, {})} | custom-call | flops 2147483648 | bytes 42078208 | tf_op jit(solution)/shard_map/key_value/pallas_call | solution.py:119
  78.9 4.9 %final.1 = (bf16[512,2048]{1,0:T(8,128)(2,1)}, bf16[512,2048]{1,0:T(8,128)(2,1)}, f32[1,2048]{1,0:T(1,128)}) custom-call(bf16[512,2048]{1,0:T(8,128)(2,1)S(1)} %get-tuple-element.63.k, bf16[512,2048]{1,0:T(8,128)(2,1)S(1)} %get-tuple-element.64.v, f32[512,2048]{1,0:T(8,128)S(1)} %get-tuple-element.111.refs_0_.dk, f32[512,2048]{1,0:T(8,128)S(1)} %get-tuple-element.112.dv, ...), custom_call_target="tpu_custom_call" | custom-call | flops 536870912 | bytes 18374656 | tf_op jit(solution)/shard_map/final/pallas_call | solution.py:119
  (43 shorter events, 11.4 us)
Async XLA Ops:
  5.6 3.1 %collective-permute-start = (f32[2,520,128]{2,1,0:T(8,128)S(1)}, f32[2,520,128]{2,1,0:T(8,128)S(1)}, u32[]{:S(2)}, u32[]{:S(2)}) collective-permute-start(f32[2,520,128]{2,1,0:T(8,128)S(1)} %get-tuple-element.67), channel_id=1, source_target_pairs={{0,2},{2,0},{4,6},{6,4},{8,10},{10,8},{12,14},{14,12},{16,18},{18,... | collective-permute-start | bytes 1597448 | tf_op jit(solution)/shard_map/ppermute | solution.py:509
  6.2 26.3 %collective-permute-start.3 = (bf16[256,2048]{1,0:T(8,128)(2,1)S(1)}, bf16[256,2048]{1,0:T(8,128)(2,1)S(1)}, u32[]{:S(2)}, u32[]{:S(2)}) collective-permute-start(bf16[256,2048]{1,0:T(8,128)(2,1)S(1)} %get-tuple-element.81), channel_id=1, source_target_pairs={{0,1},{1,0},{2,3},{3,2},{4,5},{5,4},{6,7},{7,6},{8,9},{9,8},{10,11... | collective-permute-start | bytes 3145736 | tf_op jit(solution)/shard_map/ppermute | solution.py:601
  8.8 5.8 %collective-permute-start.1 = (bf16[528,128]{1,0:T(8,128)(2,1)S(1)}, bf16[528,128]{1,0:T(8,128)(2,1)S(1)}, u32[]{:S(2)}, u32[]{:S(2)}) collective-permute-start(bf16[528,128]{1,0:T(8,128)(2,1)S(1)} %get-tuple-element.68._), channel_id=1, source_target_pairs={{0,4},{2,6},{4,0},{6,2},{8,12},{10,14},{12,8},{14,10},{16,20},{18,... | collective-permute-start | bytes 405512 | tf_op jit(solution)/shard_map/ppermute | solution.py:509
  14.7 7.1 %collective-permute-start.2 = (bf16[528,128]{1,0:T(8,128)(2,1)S(1)}, bf16[528,128]{1,0:T(8,128)(2,1)S(1)}, u32[]{:S(2)}, u32[]{:S(2)}) collective-permute-start(bf16[528,128]{1,0:T(8,128)(2,1)S(1)} %get-tuple-element.74._), channel_id=1, source_target_pairs={{0,8},{2,10},{4,12},{6,14},{8,16},{10,18},{12,20},{14,22},{16,24},... | collective-permute-start | bytes 405512 | tf_op jit(solution)/shard_map/ppermute | solution.py:514
  18.4 10.4 %copy-start = (f32[16,256,256]{2,1,0:T(8,128)}, f32[16,256,256]{2,1,0:T(8,128)S(1)}, u32[]{:S(2)}) copy-start(f32[16,256,256]{2,1,0:T(8,128)S(1)} %get-tuple-element.102.table1) | copy-start | bytes 12582916
  18.4 10.4 %copy-start.3 = (bf16[16,256,512]{2,1,0:T(8,128)(2,1)}, bf16[16,256,512]{2,1,0:T(8,128)(2,1)S(1)}, u32[]{:S(2)}) copy-start(bf16[16,256,512]{2,1,0:T(8,128)(2,1)S(1)} %get-tuple-element.103.probs0) | copy-start | bytes 12582916
  21.9 7.2 %collective-permute-start.4 = (bf16[528,128]{1,0:T(8,128)(2,1)S(1)}, bf16[528,128]{1,0:T(8,128)(2,1)S(1)}, u32[]{:S(2)}, u32[]{:S(2)}) collective-permute-start(bf16[528,128]{1,0:T(8,128)(2,1)S(1)} %get-tuple-element.79._), channel_id=1, source_target_pairs={{0,16},{2,18},{4,20},{6,22},{8,24},{10,26},{12,28},{14,30},{16,0},... | collective-permute-start | bytes 405512 | tf_op jit(solution)/shard_map/ppermute | solution.py:514
  29.1 3.4 %copy-start.6 = (bf16[512,2048]{1,0:T(8,128)(2,1)S(1)}, bf16[512,2048]{1,0:T(8,128)(2,1)}, u32[]{:S(2)}) copy-start(bf16[512,2048]{1,0:T(8,128)(2,1)} %gate.5) | copy-start | bytes 6291460
  29.1 3.4 %copy-start.7 = (f32[2048]{0:T(1024)S(1)}, f32[2048]{0:T(1024)}, u32[]{:S(2)}) copy-start(f32[2048]{0:T(1024)} %param.12) | copy-start | bytes 24580
  29.2 6.1 %collective-permute-start.5 = (bf16[528,128]{1,0:T(8,128)(2,1)S(1)}, bf16[528,128]{1,0:T(8,128)(2,1)S(1)}, u32[]{:S(2)}, u32[]{:S(2)}) collective-permute-start(bf16[528,128]{1,0:T(8,128)(2,1)S(1)} %get-tuple-element.83._), channel_id=1, source_target_pairs={{0,4},{2,6},{4,0},{6,2},{8,12},{10,14},{12,8},{14,10},{16,20},{18,... | collective-permute-start | bytes 405512 | tf_op jit(solution)/shard_map/ppermute | solution.py:509
  35.6 1.6 %collective-permute-start.6 = (bf16[2,528,128]{2,1,0:T(8,128)(2,1)S(1)}, bf16[2,528,128]{2,1,0:T(8,128)(2,1)S(1)}, u32[]{:S(2)}, u32[]{:S(2)}) collective-permute-start(bf16[2,528,128]{2,1,0:T(8,128)(2,1)S(1)} %get-tuple-element.88), channel_id=1, source_target_pairs={{0,2},{2,0},{4,6},{6,4},{8,10},{10,8},{12,14},{14,12},{16,18},{18,... | collective-permute-start | bytes 811016 | tf_op jit(solution)/shard_map/ppermute | solution.py:509
  40.0 3.8 %collective-permute-start.7 = (f32[8,512]{1,0:T(8,128)S(1)}, f32[8,512]{1,0:T(8,128)S(1)}, u32[]{:S(2)}, u32[]{:S(2)}) collective-permute-start(f32[8,512]{1,0:T(8,128)S(1)} %get-tuple-element.91.sum_a), channel_id=1, source_target_pairs={{0,1},{1,0},{2,3},{3,2},{4,5},{5,4},{6,7},{7,6},{8,9},{9,8},{10,11... | collective-permute-start | bytes 49160 | tf_op jit(solution)/shard_map/ppermute | solution.py:664
  47.3 2.0 %collective-permute-start.8 = (f32[2,520,128]{2,1,0:T(8,128)S(1)}, f32[2,520,128]{2,1,0:T(8,128)S(1)}, u32[]{:S(2)}, u32[]{:S(2)}) collective-permute-start(f32[2,520,128]{2,1,0:T(8,128)S(1)} %get-tuple-element.94), channel_id=1, source_target_pairs={{0,2},{2,0},{4,6},{6,4},{8,10},{10,8},{12,14},{14,12},{16,18},{18,... | collective-permute-start | bytes 1597448 | tf_op jit(solution)/shard_map/ppermute | solution.py:509
  49.4 5.7 %collective-permute-start.9 = (bf16[528,128]{1,0:T(8,128)(2,1)S(1)}, bf16[528,128]{1,0:T(8,128)(2,1)S(1)}, u32[]{:S(2)}, u32[]{:S(2)}) collective-permute-start(bf16[528,128]{1,0:T(8,128)(2,1)S(1)} %get-tuple-element.96._), channel_id=1, source_target_pairs={{0,4},{2,6},{4,0},{6,2},{8,12},{10,14},{12,8},{14,10},{16,20},{18,... | collective-permute-start | bytes 405512 | tf_op jit(solution)/shard_map/ppermute | solution.py:509
  51.3 8.1 %copy-start.1 = (f32[16,256,256]{2,1,0:T(8,128)S(1)}, f32[16,256,256]{2,1,0:T(8,128)}, u32[]{:S(2)}) copy-start(f32[16,256,256]{2,1,0:T(8,128)} %copy-done) | copy-start | bytes 12582916
  51.3 8.1 %copy-start.4 = (bf16[16,256,512]{2,1,0:T(8,128)(2,1)S(1)}, bf16[16,256,512]{2,1,0:T(8,128)(2,1)}, u32[]{:S(2)}) copy-start(bf16[16,256,512]{2,1,0:T(8,128)(2,1)} %copy-done.3) | copy-start | bytes 12582916
  55.2 8.1 %collective-permute-start.10 = (bf16[528,128]{1,0:T(8,128)(2,1)S(1)}, bf16[528,128]{1,0:T(8,128)(2,1)S(1)}, u32[]{:S(2)}, u32[]{:S(2)}) collective-permute-start(bf16[528,128]{1,0:T(8,128)(2,1)S(1)} %get-tuple-element.100._), channel_id=1, source_target_pairs={{0,24},{2,26},{4,28},{6,30},{8,0},{10,2},{12,4},{14,6},{16,8},{18,... | collective-permute-start | bytes 405512 | tf_op jit(solution)/shard_map/ppermute | solution.py:514
  63.4 7.7 %collective-permute-start.11 = (bf16[528,128]{1,0:T(8,128)(2,1)S(1)}, bf16[528,128]{1,0:T(8,128)(2,1)S(1)}, u32[]{:S(2)}, u32[]{:S(2)}) collective-permute-start(bf16[528,128]{1,0:T(8,128)(2,1)S(1)} %get-tuple-element.105._), channel_id=1, source_target_pairs={{0,16},{2,18},{4,20},{6,22},{8,24},{10,26},{12,28},{14,30},{16,0},... | collective-permute-start | bytes 405512 | tf_op jit(solution)/shard_map/ppermute | solution.py:514
  63.5 9.3 %copy-start.2 = (f32[16,256,256]{2,1,0:T(8,128)S(1)}, f32[16,256,256]{2,1,0:T(8,128)}, u32[]{:S(2)}) copy-start(f32[16,256,256]{2,1,0:T(8,128)} %copy-done) | copy-start | bytes 12582916
  63.5 9.3 %copy-start.5 = (bf16[16,256,512]{2,1,0:T(8,128)(2,1)S(1)}, bf16[16,256,512]{2,1,0:T(8,128)(2,1)}, u32[]{:S(2)}) copy-start(bf16[16,256,512]{2,1,0:T(8,128)(2,1)} %copy-done.3) | copy-start | bytes 12582916
  71.2 5.8 %collective-permute-start.12 = (bf16[528,128]{1,0:T(8,128)(2,1)S(1)}, bf16[528,128]{1,0:T(8,128)(2,1)S(1)}, u32[]{:S(2)}, u32[]{:S(2)}) collective-permute-start(bf16[528,128]{1,0:T(8,128)(2,1)S(1)} %get-tuple-element.109._), channel_id=1, source_target_pairs={{0,4},{2,6},{4,0},{6,2},{8,12},{10,14},{12,8},{14,10},{16,20},{18,... | collective-permute-start | bytes 405512 | tf_op jit(solution)/shard_map/ppermute | solution.py:509
  77.3 1.6 %collective-permute-start.13 = (bf16[2,528,128]{2,1,0:T(8,128)(2,1)S(1)}, bf16[2,528,128]{2,1,0:T(8,128)(2,1)S(1)}, u32[]{:S(2)}, u32[]{:S(2)}) collective-permute-start(bf16[2,528,128]{2,1,0:T(8,128)(2,1)S(1)} %get-tuple-element.116), channel_id=1, source_target_pairs={{0,2},{2,0},{4,6},{6,4},{8,10},{10,8},{12,14},{14,12},{16,18},{18,... | collective-permute-start | bytes 811016 | tf_op jit(solution)/shard_map/ppermute | solution.py:509

commit v6 on v5

--- a/solution.py
+++ b/solution.py
@@ -16,7 +16,7 @@
 EPSILON = 1e-06
 F32 = jnp.float32
 BF16 = jnp.bfloat16
-GRANT = 12 * 1024 * 1024
+GRANT = 6 * 1024 * 1024
 VMEM = pl.BlockSpec(memory_space=pltpu.VMEM)
 HBM = pl.BlockSpec(memory_space=pltpu.HBM)
 ANY = pl.BlockSpec(memory_space=pl.ANY)
@@ -107,10 +107,16 @@
 
 
 def transposed(x):
-    eye = (
-        lax.broadcasted_iota(jnp.int32, (HEAD, HEAD), 0) == lax.broadcasted_iota(jnp.int32, (HEAD, HEAD), 1)
-    ).astype(BF16)
+    shape = (x.shape[1], x.shape[1])
+    eye = (lax.broadcasted_iota(jnp.int32, shape, 0) == lax.broadcasted_iota(jnp.int32, shape, 1)).astype(BF16)
     return nt(eye, x)
+
+
+def several(quarter, hq):
+    count = min(hq, 2)
+    for j in range(0, hq, count):
+        h = quarter * hq + j
+        yield j, h, count, pl.ds(pl.multiple_of(h * HEAD, HEAD), count * HEAD)
 
 
 def call(body, inputs, out_shape, name, scratch=(), flops=0, in_specs=None, out_specs=None, alias=None):
@@ -218,26 +224,35 @@
         write_narrow(send.at[y], hq, items_send)
 
 
-def local_states_body(heads, swaps, k_hbm, v_hbm, ld_hbm, *refs):
+def block_states(hq, y, same, k, v, row, out):
+    items = []
+    for j, h, count, c in several(quarter_of(y, same), hq):
+        turned = transposed(k[:, c])
+        lines = [row[pl.ds(h + m, 1), :] for m in range(count)]
+        edges = [line[:, BLOCK - 1 : BLOCK] for line in lines]
+        faded = [turned[chunk(m)] * jnp.exp(edges[m] - lines[m]) for m in range(count)]
+        both = nn(jnp.concatenate([x.astype(BF16) for x in faded], axis=0), v[:, c])
+        for m in range(count):
+            items.append((both[chunk(m), chunk(m)], jnp.broadcast_to(edges[m], (1, HEAD)), jnp.zeros((1, HEAD), F32)))
+    write_wide(out.at[y], hq, items)
+
+
+def sent_states_body(heads, swaps, k_hbm, v_hbm, ld_hbm, *refs):
     hq = heads // TEAM
     w = hq * HEAD
     if swaps:
-        grad, keep, give, row, k, v, away, own, ld, sems, side_sems = refs
+        grad, give, row, k, v, away, ld, sems, side_sems = refs
         width = heads * HEAD
-        mine = lax.axis_index("tp")
-        cols = lambda t: pl.ds(pl.multiple_of(t * width, HEAD), width)
-        side_copies = [
-            pltpu.make_async_copy(grad.at[:, cols(1 - mine)], away, side_sems.at[1]),
-            pltpu.make_async_copy(grad.at[:, cols(mine)], own, side_sems.at[2]),
-        ]
+        there = pl.ds(pl.multiple_of((1 - lax.axis_index("tp")) * width, HEAD), width)
+        side_copies = [pltpu.make_async_copy(grad.at[:, there], away, side_sems.at[1])]
     else:
-        keep, give, row, k, v, ld, sems, side_sems = refs
+        give, row, k, v, ld, sems, side_sems = refs
         side_copies = []
     first = pltpu.make_async_copy(ld_hbm, ld, side_sems.at[0])
     first.start()
-    order = [(give, 0, False), (give, 1, False), (keep, 0, True), (keep, 1, True)]
+    order = [(0, False), (1, False), (0, True), (1, True)]
     copies = []
-    for slot, (_, y, same) in enumerate(order):
+    for slot, (y, same) in enumerate(order):
         cols_d = pl.ds(pl.multiple_of(quarter_of(y, same) * w, HEAD), w)
         both = [
             pltpu.make_async_copy(k_hbm.at[:, cols_d], k.at[:, cols_d], sems.at[0, slot]),
@@ -257,20 +272,18 @@
         x = jnp.concatenate([x, jnp.zeros((EXTRA - heads, BLOCK), F32)], axis=0)
     sums = nn(jnp.concatenate(split_terms(x, 3), axis=0), tri)
     row[...] = sums[0:EXTRA] + (sums[EXTRA : 2 * EXTRA] + sums[2 * EXTRA : 3 * EXTRA])
-    for slot, (out, y, same) in enumerate(order):
+    for slot, (y, same) in enumerate(order):
         for c in copies[slot]:
             c.wait()
-        items = []
-        for j in range(hq):
-            h, c = head_at(quarter_of(y, same), hq, j)
-            sums = row[pl.ds(h, 1), :]
-            edge = sums[:, BLOCK - 1 : BLOCK]
-            kd = (transposed(k[:, c]) * jnp.exp(edge - sums)).astype(BF16)
-            spread = jnp.broadcast_to(edge, (1, HEAD))
-            items.append((nn(kd, v[:, c]), spread, jnp.zeros((1, HEAD), F32)))
-        write_wide(out.at[y], hq, items)
+        if not same:
+            block_states(hq, y, same, k, v, row, give)
     for c in side_copies:
         c.wait()
+
+
+def kept_states_body(heads, k, v, row, keep):
+    for y in range(2):
+        block_states(heads // TEAM, y, True, k, v, row, keep)
 
 
 def decays_body(heads, row, q_hbm, _, col, growth, shrink, q, sem):
@@ -332,26 +345,42 @@
     lax.fori_loop(0, TEAM, one, 0)
 
 
-def dscaled_body(heads, swaps, gate, own, got, gain, q, row, _, dscaled, turned):
-    hq = heads // TEAM
-    part = own.shape[0]
+def dscaled_rows(heads, where, gate, ref, gain, dscaled):
+    part = ref.shape[0]
+    rows = pl.ds(pl.multiple_of(where * part, part), part)
+
+    def one(g, _):
+        for j in range(heads // TEAM):
+            _, c = head_at(g, heads // TEAM, j)
+            opened = jax.nn.sigmoid(gate[rows, c].astype(F32))
+            dscaled[rows, c] = ref[:, c].astype(F32) * opened * gain[:, c]
+        return 0
+
+    lax.fori_loop(0, TEAM, one, 0)
+
+
+def own_dscaled_body(heads, swaps, gate, grad, gain, q, row, _, dscaled, turned, own, sem):
+    width = heads * HEAD
     mine = lax.axis_index("tp") if swaps else 0
+    here = pl.ds(pl.multiple_of(mine * width, HEAD), width)
+    copy = pltpu.make_async_copy(grad.at[:, here], own, sem)
+    copy.start()
 
     def one(g, _):
-        for j in range(hq):
-            h, c = head_at(g, hq, j)
-            for where, ref in ((mine, own), (1 - mine, got)):
-                rows = pl.ds(pl.multiple_of(where * part, part), part)
-                opened = jax.nn.sigmoid(gate[rows, c].astype(F32))
-                dscaled[rows, c] = ref[:, c].astype(F32) * opened * gain[:, c]
-            turned[h] = (transposed(q[:, c]) * jnp.exp(row[pl.ds(h, 1), :])).astype(BF16)
+        for j, h, count, c in several(g, heads // TEAM):
+            both = transposed(q[:, c])
+            for m in range(count):
+                rows = pl.ds(pl.multiple_of((h + m) * HEAD, HEAD), HEAD)
+                turned[rows, :] = (both[chunk(m)] * jnp.exp(row[pl.ds(h + m, 1), :])).astype(BF16)
         return 0
 
     lax.fori_loop(0, TEAM, one, 0)
-
-
-def by_quarter(mine, got):
-    return [(ref.at[y], quarter_of(y, same)) for ref, same in ((mine, True), (got, False)) for y in range(2)]
+    copy.wait()
+    dscaled_rows(heads, mine, gate, own, gain, dscaled)
+
+
+def got_dscaled_body(heads, swaps, gate, got, gain, _, dscaled):
+    dscaled_rows(heads, 1 - lax.axis_index("tp") if swaps else 1, gate, got, gain, dscaled)
 
 
 def diagonal(a, b):
@@ -361,62 +390,73 @@
     )
 
 
-def attention_body(heads, q, intra, dscaled, growth, mine, got, att, sums, sq, inn, both):
-    hq = heads // TEAM
-    sides = by_quarter(mine, got)
-    step = min(hq, 2)
-    for slot, (state, g) in enumerate(sides):
-        for j in range(0, hq, step):
-            _, c = head_at(g, hq, j)
-            if step == 2:
-                c = pl.ds(pl.multiple_of((g * hq + j) * HEAD, HEAD), 2 * HEAD)
-                both[...] = nn(q[:, c], diagonal(state[chunk(j), :], state[chunk(j + 1), :]))
+def attention_body(heads, same, q, intra, dscaled, growth, state, *refs):
+    hq = heads // TEAM
+    if same:
+        att, sq, inn, both = refs
+    else:
+        _, sq_before, inn_before, att, sums, sq, inn, both = refs
+        sq[...] = sq_before[...]
+        inn[...] = inn_before[...]
+    for y in range(2):
+        g = quarter_of(y, same)
+        for j, h, count, c in several(g, hq):
+            if count == 2:
+                both[...] = nn(q[:, c], diagonal(state[y, chunk(j), :], state[y, chunk(j + 1), :]))
             else:
-                both[:, 0:HEAD] = nn(q[:, c], state[chunk(j), :])
+                both[:, 0:HEAD] = nn(q[:, c], state[y, chunk(j), :])
             for i in range(BLOCK // HEAD):
                 r = chunk(i)
                 a_sq = a_in = 0.0
-                for m in range(step):
+                for m in range(count):
                     _, c = head_at(g, hq, j + m)
                     a = intra[r, c] + both[r, chunk(m)] * growth[g, r, j + m : j + m + 1]
                     att[r, c] = a
                     a_sq = a_sq + a * a
                     a_in = a_in + a * dscaled[r, c]
-                if slot == 0 and j == 0:
+                if same and y == 0 and j == 0:
                     sq[r, :] = a_sq
                     inn[r, :] = a_in
                 else:
                     sq[r, :] += a_sq
                     inn[r, :] += a_in
-    ones = jnp.ones((8, HEAD), F32)
-    a = nt(ones, sq[...], lax.Precision.HIGHEST)
-    b = nt(ones, inn[...], lax.Precision.HIGHEST)
-    sums[...] = jnp.where(lax.broadcasted_iota(jnp.int32, (8, BLOCK), 0) == 0, a, b)
-
-
-def dattn_body(heads, channels, att, dscaled, turned, gain, row, sum_a, sum_b, dattn, scale, keep, give, rsb, coefb):
-    hq = heads // TEAM
-    total = sum_a[...] + sum_b[...]
-    rs = lax.rsqrt(total[0:1, :] / channels + EPSILON)
-    coef = total[1:2, :] * (rs * rs * rs) / channels
-    down = jnp.concatenate([rs, coef, jnp.zeros((HEAD - 2, BLOCK), F32)], axis=0).T
-    rsb[...] = jnp.broadcast_to(down[:, 0:1], (BLOCK, HEAD))
-    coefb[...] = jnp.broadcast_to(down[:, 1:2], (BLOCK, HEAD))
-    scale[...] = rsb[...]
-    for out, y, same in ((give, 0, False), (give, 1, False), (keep, 0, True), (keep, 1, True)):
+    if not same:
+        ones = jnp.ones((8, HEAD), F32)
+        a = nt(ones, sq[...], lax.Precision.HIGHEST)
+        b = nt(ones, inn[...], lax.Precision.HIGHEST)
+        sums[...] = jnp.where(lax.broadcasted_iota(jnp.int32, (8, BLOCK), 0) == 0, a, b)
+
+
+def dattn_body(heads, channels, same, att, dscaled, turned, gain, row, *refs):
+    hq = heads // TEAM
+    if same:
+        rsb, coefb, _, dattn, out = refs
+    else:
+        sum_a, sum_b, dattn, out, rsb, coefb = refs
+        total = sum_a[...] + sum_b[...]
+        rs = lax.rsqrt(total[0:1, :] / channels + EPSILON)
+        coef = total[1:2, :] * (rs * rs * rs) / channels
+        down = jnp.concatenate([rs, coef, jnp.zeros((HEAD - 2, BLOCK), F32)], axis=0).T
+        rsb[...] = jnp.broadcast_to(down[:, 0:1], (BLOCK, HEAD))
+        coefb[...] = jnp.broadcast_to(down[:, 1:2], (BLOCK, HEAD))
+    for y in range(2):
         items = []
-        for j in range(hq):
-            h, c = head_at(quarter_of(y, same), hq, j)
-            gsum = jnp.zeros((8, HEAD), F32)
-            for i in range(BLOCK // HEAD):
-                r = chunk(i)
-                a = att[r, c]
-                t = dscaled[r, c] * rsb[r, :]
-                dattn[r, c] = (t - a * coefb[r, :]).astype(BF16)
-                gsum = gsum + jnp.sum((t * a).reshape(HEAD // 8, 8, HEAD), axis=0)
-            edge = jnp.broadcast_to(row[pl.ds(h, 1), :][:, BLOCK - 1 : BLOCK], (1, HEAD))
-            part = jnp.sum(gsum, axis=0, keepdims=True) / gain[:, c]
-            items.append((nn(turned[h], dattn[:, c]), edge, part))
+        for j, h, count, cols in several(quarter_of(y, same), hq):
+            parts = []
+            for m in range(count):
+                _, c = head_at(quarter_of(y, same), hq, j + m)
+                gsum = jnp.zeros((8, HEAD), F32)
+                for i in range(BLOCK // HEAD):
+                    r = chunk(i)
+                    a = att[r, c]
+                    t = dscaled[r, c] * rsb[r, :]
+                    dattn[r, c] = (t - a * coefb[r, :]).astype(BF16)
+                    gsum = gsum + jnp.sum((t * a).reshape(HEAD // 8, 8, HEAD), axis=0)
+                parts.append(jnp.sum(gsum, axis=0, keepdims=True) / gain[:, c])
+            both = nn(turned[pl.ds(pl.multiple_of(h * HEAD, HEAD), count * HEAD), :], dattn[:, cols])
+            for m in range(count):
+                edge = jnp.broadcast_to(row[pl.ds(h + m, 1), :][:, BLOCK - 1 : BLOCK], (1, HEAD))
+                items.append((both[chunk(m), chunk(m)], edge, parts[m]))
         write_wide(out.at[y], hq, items)
 
 
@@ -439,6 +479,10 @@
         copies.append(leave(out.at[g], gate_grad, sems.at[g], g, hq * HEAD))
     for copy in copies:
         copy.wait()
+
+
+def by_quarter(mine, got):
+    return [(ref.at[y], quarter_of(y, same)) for ref, same in ((mine, True), (got, False)) for y in range(2)]
 
 
 def query_body(heads, k, v, dattn, row, col, growth, mine, got, _, query_grad, token, out, sems):
@@ -478,24 +522,25 @@
     lax.fori_loop(first, first + TEAM // 2, one, 0)
 
 
-def final_body(heads, k, v, dk, dv, shrink, mine, got, key_grad, value_grad, gain_grad, key_out, value_out, sems):
+def final_body(heads, same, k, v, dk, dv, shrink, state, *refs):
     hq = heads // TEAM
     w = hq * HEAD
+    key_grad, value_grad, gain_grad, key_out, value_out, sems = refs[-6:]
+    if not same:
+        gain_grad[...] = refs[2][...]
     copies = []
-    for slot, (state, g) in enumerate(by_quarter(mine, got)):
-        items = read_narrow(state, hq)
+    for y in range(2):
+        g = quarter_of(y, same)
+        items = read_narrow(state.at[y], hq)
         for j in range(hq):
             _, c = head_at(g, hq, j)
             fade = shrink[g, :, j : j + 1]
-            after = state[chunk(j), :]
-            side = jnp.concatenate([k[:, c], v[:, c]], axis=1)
-            back = items[j][0].T.astype(BF16)
-            both = nn(side, diagonal(after, back))
-            key_out[slot, :, chunk(j)] = (dk[:, c] + both[:, HEAD:] * fade).astype(BF16)
-            value_out[slot, :, chunk(j)] = (dv[:, c] + both[:, :HEAD] * fade).astype(BF16)
+            after = state[y, chunk(j), :]
+            key_out[y, :, chunk(j)] = (dk[:, c] + nt(v[:, c], after) * fade).astype(BF16)
+            value_out[y, :, chunk(j)] = (dv[:, c] + nn(k[:, c], after) * fade).astype(BF16)
             gain_grad[:, c] = items[j][2]
-        copies.append(leave(key_out.at[slot], key_grad, sems.at[0, slot], g, w))
-        copies.append(leave(value_out.at[slot], value_grad, sems.at[1, slot], g, w))
+        copies.append(leave(key_out.at[y], key_grad, sems.at[0, y], g, w))
+        copies.append(leave(value_out.at[y], value_grad, sems.at[1, y], g, w))
     for copy in copies:
         copy.wait()
 
@@ -582,26 +627,29 @@
         return mine, swap(send, 1)
 
     outs = call(
-        functools.partial(local_states_body, heads, swaps),
+        functools.partial(sent_states_body, heads, swaps),
         [in_hbm(keys), in_hbm(values), in_hbm(log_decay)] + [in_hbm(grad_out)] * swaps,
-        [wide2, wide2, f32(EXTRA, rows), bf(rows, width), bf(rows, width)] + [bf(part, width)] * 2 * swaps,
-        "local_states",
+        [wide2, f32(EXTRA, rows), bf(rows, width), bf(rows, width)] + [bf(part, width)] * swaps,
+        "sent_states",
         [
             pltpu.VMEM(log_decay.shape, F32),
             pltpu.SemaphoreType.DMA((2, TEAM)),
-            pltpu.SemaphoreType.DMA((3,)),
+            pltpu.SemaphoreType.DMA((2,)),
         ],
-        small,
+        small // 2,
         [HBM] * (3 + swaps),
-        [VMEM] * 5 + [HBM, VMEM] * swaps,
-    )
-    keep, give, row, keys, values = outs[:5]
+        [VMEM] * 4 + [HBM] * swaps,
+    )
+    give, row, keys, values = outs[:4]
     if swaps:
-        own = outs[6]
-        arrived = lax.ppermute(outs[5], "tp", [(0, 1), (1, 0)])
+        arrived = lax.ppermute(outs[4], "tp", [(0, 1), (1, 0)])
+        own = grad_out
     else:
         every = lax.all_to_all(grad_out, "tp", split_axis=1, concat_axis=0, tiled=True)
         own, arrived = every[:part], every[part:]
+    (keep,) = call(
+        functools.partial(kept_states_body, heads), [keys, values, row], [wide2], "kept_states", flops=small // 2
+    )
     done = {}
 
     def probs_beside(after):
@@ -639,38 +687,64 @@
 
     def dscaled_beside(after):
         done["dscaled"] = call(
-            functools.partial(dscaled_body, heads, swaps),
-            [gate, own, arrived, gain_row, done["queries"], row, after],
-            [f32(rows, width), bf(heads, HEAD, rows)],
-            "dscaled",
-            flops=small,
-            in_specs=[VMEM] * 6 + [ANY],
-        )
-        return done["dscaled"][0]
+            functools.partial(own_dscaled_body, heads, swaps),
+            [gate, in_hbm(own), gain_row, done["queries"], row, after],
+            [f32(rows, width), bf(width, rows)],
+            "own_dscaled",
+            [pltpu.VMEM((part, width), BF16), pltpu.SemaphoreType.DMA(())],
+            small,
+            [VMEM, HBM, VMEM, VMEM, VMEM, ANY],
+        )
+        return done["dscaled"][1]
 
     work = {"pair": probs_beside, "one": probs_beside, "last": intra_beside, "pair_back": dscaled_beside}
     mine, got = scan(False, keep, give, work)
     queries = done["queries"]
     (col, growth, shrink), intra, (dscaled, turned) = done["decays"], done["intra"], done["dscaled"]
+    (dscaled,) = call(
+        functools.partial(got_dscaled_body, heads, swaps),
+        [gate, arrived, gain_row, dscaled],
+        [f32(rows, width)],
+        "got_dscaled",
+        alias={3: 0},
+    )
+    tall = f32(rows, HEAD)
+    wide_scratch = pltpu.VMEM((rows, 2 * HEAD), F32)
+    att, squares, inner = call(
+        functools.partial(attention_body, heads, True),
+        [queries, intra, dscaled, growth, mine],
+        [f32(rows, width), tall, tall],
+        "attention",
+        [wide_scratch],
+        small // 2,
+    )
     att, sums = call(
-        functools.partial(attention_body, heads),
-        [queries, intra, dscaled, growth, mine, got],
+        functools.partial(attention_body, heads, False),
+        [queries, intra, dscaled, growth, got, att, squares, inner],
         [f32(rows, width), f32(8, rows)],
         "attention",
-        [pltpu.VMEM((rows, HEAD), F32)] * 2 + [pltpu.VMEM((rows, 2 * HEAD), F32)],
-        small,
+        [pltpu.VMEM((rows, HEAD), F32)] * 2 + [wide_scratch],
+        small // 2,
+        alias={5: 0},
     )
     if swaps:
         others = lax.ppermute(sums, "tp", [(0, 1), (1, 0)])
     else:
         others = lax.psum(sums, "tp") - sums
-    dattn, scale, keep, give = call(
-        functools.partial(dattn_body, heads, channels),
+    dattn, give, scale, coef = call(
+        functools.partial(dattn_body, heads, channels, False),
         [att, dscaled, turned, gain_row, row, sums, others],
-        [bf(rows, width), f32(rows, HEAD), wide2, wide2],
-        "dattn",
-        [pltpu.VMEM((rows, HEAD), F32)] * 2,
-        small,
+        [bf(rows, width), wide2, tall, tall],
+        "sent_dattn",
+        flops=small // 2,
+    )
+    dattn, keep = call(
+        functools.partial(dattn_body, heads, channels, True),
+        [att, dscaled, turned, gain_row, row, scale, coef, dattn],
+        [bf(rows, width), wide2],
+        "kept_dattn",
+        flops=small // 2,
+        alias={7: 0},
     )
     out_scratch = [pltpu.VMEM((TEAM, rows, hq * HEAD), BF16), pltpu.SemaphoreType.DMA((TEAM,))]
 
@@ -726,15 +800,18 @@
     work = {"pair": gate_beside, "one": key_value_first, "last": query_beside, "pair_back": key_value_last}
     back_mine, back_got = scan(True, keep, give, work)
     gate_grad, query_grad, (dk, dv) = done["gate"], done["query"], done["key_value"]
-    key_grad, value_grad, gain_grad = call(
-        functools.partial(final_body, heads),
-        [keys, values, dk, dv, shrink, back_mine, back_got],
+    final = lambda same, state, *before: call(
+        functools.partial(final_body, heads, same),
+        [keys, values, dk, dv, shrink, state, *before],
         [bf(rows, width), bf(rows, width), f32(1, width)],
         "final",
-        [pltpu.VMEM((TEAM, rows, hq * HEAD), BF16)] * 2 + [pltpu.SemaphoreType.DMA((2, TEAM))],
-        2 * small,
-        out_specs=[HBM, HBM, VMEM],
-    )
+        [pltpu.VMEM((2, rows, hq * HEAD), BF16)] * 2 + [pltpu.SemaphoreType.DMA((2, 2))],
+        small,
+        [VMEM] * 6 + [HBM, HBM, VMEM][: len(before)],
+        [HBM, HBM, VMEM],
+        {6 + i: i for i in range(len(before))},
+    )
+    key_grad, value_grad, gain_grad = final(False, back_got, *final(True, back_mine))
     return query_grad, key_grad, value_grad, gate_grad, gain_grad.reshape(width)
 
 

time: 84.2 us -> 78.2 us (0.929)
  waiting for transfers between devices: 15.7 us -> 11.3 us
  starting transfers between devices: 19.2 us -> 16 us
  local copies, waits for them, and re-layouts: 0.03 us -> 1.99 us
    ppermute x8, waiting for transfers between devices: 7.18 us -> 5.02 us  [swap(): return lax.ppermute(x, 'ctx', [(i, i ^ bit) for i in range(n)])]
    unnamed x16 -> x8, local copies, waits for them, and re-layouts: 0.03 us -> 1.99 us
    ppermute x4, starting transfers between devices: 7.2 us -> 5.44 us  [across(): return lax.ppermute(x, 'ctx', [(i, (i + TEAM * k) % n) for i in range(n)])]
    ppermute x1, waiting for transfers between devices: 1.65 us -> 0.01 us  [local(): arrived = lax.ppermute(outs[4], 'tp', [(0, 1), (1, 0)])]
    ppermute x4, waiting for transfers between devices: 4.92 us -> 3.47 us  [across(): return lax.ppermute(x, 'ctx', [(i, (i + TEAM * k) % n) for i in range(n)])]
    ppermute x1, starting transfers between devices: 1.77 us -> 0.93 us  [local(): others = lax.ppermute(sums, 'tp', [(0, 1), (1, 0)])]
    ppermute x1, waiting for transfers between devices: 1.99 us -> 2.83 us  [local(): others = lax.ppermute(sums, 'tp', [(0, 1), (1, 0)])]
    pallas_call x23 -> x28, Pallas kernels: 48 us -> 47.6 us  [call(): pl.pallas_call(body, in_specs=in_specs or [VMEM] * len(inputs), out_specs...]
  transfers between devices with their start and end apart: 14 -> 14, of which waited for: 10 -> 8; matrix products, arithmetic and copies ran while one was open for 0% -> 0% of each run, Pallas kernels for 37% -> 48%
where the time goes in v6:
time: 78.2 us; the launch traced here: 78 us
  Pallas kernels  47.6 us (61%)
  starting transfers between devices  16 us (20%)
  waiting for transfers between devices  11.3 us (14%)
  local copies, waits for them, and re-layouts  1.99 us (3%)
  between operations  1.07 us (1%)
    pallas_call x28, Pallas kernels, call(): pl.pallas_call(body, in_specs=in_specs or [VMEM] * len(inputs), out_specs...  47.6 us
    ppermute x8, starting transfers between devices, swap(): return lax.ppermute(x, 'ctx', [(i, i ^ bit) for i in range(n)])  7.07 us
    ppermute x4, starting transfers between devices, across(): return lax.ppermute(x, 'ctx', [(i, (i + TEAM * k) % n) for i in range(n)])  5.44 us
    ppermute x8, waiting for transfers between devices, swap(): return lax.ppermute(x, 'ctx', [(i, i ^ bit) for i in range(n)])  5.02 us
    ppermute x4, waiting for transfers between devices, across(): return lax.ppermute(x, 'ctx', [(i, (i + TEAM * k) % n) for i in range(n)])  3.47 us
    ppermute x1, waiting for transfers between devices, local(): others = lax.ppermute(sums, 'tp', [(0, 1), (1, 0)])  2.83 us
    ppermute x1, starting transfers between devices, local(): arrived = lax.ppermute(outs[4], 'tp', [(0, 1), (1, 0)])  2.56 us
    unnamed x8, local copies, waits for them, and re-layouts  1.99 us
  transfers between devices with their start and end apart: 14, of which 8 were waited for; matrix products, arithmetic and copies ran while one was open for 0% of the time, Pallas kernels for 48%

profile of v6, /device:TPU:0, one launch (start us, length us, event | category | flops | bytes accessed | tf_op | source)
XLA Modules:
  0.0 78.0 jit_solution(17945484917874608544)
XLA Ops:
  0.6 2.8 %sent_states.1 = (f32[2,520,128]{2,1,0:T(8,128)S(1)}, f32[16,512]{1,0:T(8,128)S(1)}, bf16[512,2048]{1,0:T(8,128)(2,1)S(1)}, bf16[512,2048]{1,0:T(8,128)(2,1)S(1)}, bf16[256,2048]{1,0:T(8,128)(2,1)S(1)}) custom-call(bf16[512,2048]{1,0:T(8,128)(2,1)} %k_hbm.1, bf16[512,2048]{1,0:T(8,128)(2,1)} %v_hbm.1, f32[16,512]{1,0:T(8,128)} %ld_hbm.1, bf16[256,4096]{1,0:T(8,128)(2,1)} %grad.1), custom_call_target="tpu_custom_call" | custom-call | flops 134217728 | bytes 12132352 | tf_op jit(solution)/shard_map/sent_states/pallas_call | solution.py:125
  4.0 2.6 %collective-permute-start.3 = (bf16[256,2048]{1,0:T(8,128)(2,1)S(1)}, bf16[256,2048]{1,0:T(8,128)(2,1)S(1)}, u32[]{:S(2)}, u32[]{:S(2)}) collective-permute-start(bf16[256,2048]{1,0:T(8,128)(2,1)S(1)} %get-tuple-element.85), channel_id=1, source_target_pairs={{0,1},{1,0},{2,3},{3,2},{4,5},{5,4},{6,7},{7,6},{8,9},{9,8},{10,11... | collective-permute-start | bytes 3145736 | tf_op jit(solution)/shard_map/ppermute | solution.py:645
  7.5 1.6 %collective-permute-start.1 = (bf16[528,128]{1,0:T(8,128)(2,1)S(1)}, bf16[528,128]{1,0:T(8,128)(2,1)S(1)}, u32[]{:S(2)}, u32[]{:S(2)}) collective-permute-start(bf16[528,128]{1,0:T(8,128)(2,1)S(1)} %get-tuple-element.73._), channel_id=1, source_target_pairs={{0,4},{2,6},{4,0},{6,2},{8,12},{10,14},{12,8},{14,10},{16,20},{18,... | collective-permute-start | bytes 405512 | tf_op jit(solution)/shard_map/ppermute | solution.py:554
  9.1 1.6 %decays.1 = (f32[4,512,128]{2,1,0:T(8,128)S(1)}, f32[4,512,128]{2,1,0:T(8,128)S(1)}, f32[4,512,128]{2,1,0:T(8,128)S(1)}, bf16[512,2048]{1,0:T(8,128)(2,1)S(1)}) custom-call(f32[16,512]{1,0:T(8,128)S(1)} %get-tuple-element.71.row, bf16[512,2048]{1,0:T(8,128)(2,1)} %q_hbm.1, bf16[528,128]{1,0:T(8,128)(2,1)S(1)} %get-tuple-element.73._), custom_call_target="tpu_custom_call" | custom-call | bytes 7507968 | tf_op jit(solution)/shard_map/decays/pallas_call | solution.py:125
  10.7 1.6 %turned_probs.2 = (f32[16,256,512]{2,1,0:T(8,128)S(1)}, f32[16,256,256]{2,1,0:T(8,128)S(1)}, bf16[16,256,512]{2,1,0:T(8,128)(2,1)S(1)}, bf16[16,256,256]{2,1,0:T(8,128)(2,1)S(1)}) custom-call(bf16[512,2048]{1,0:T(8,128)(2,1)S(1)} %get-tuple-element.74.q, bf16[512,2048]{1,0:T(8,128)(2,1)S(1)} %get-tuple-element.69.k, f32[16,512]{1,0:T(8,128)S(1)} %get-tuple-element.71.row, ...), custom_call_target="tpu_custom_call" | custom-call | flops 536870912 | bytes 24285184 | tf_op jit(solution)/shard_map/turned_probs/pallas_call | solution.py:125
  13.3 1.8 %collective-permute-start.2 = (bf16[528,128]{1,0:T(8,128)(2,1)S(1)}, bf16[528,128]{1,0:T(8,128)(2,1)S(1)}, u32[]{:S(2)}, u32[]{:S(2)}) collective-permute-start(bf16[528,128]{1,0:T(8,128)(2,1)S(1)} %get-tuple-element.79._), channel_id=1, source_target_pairs={{0,8},{2,10},{4,12},{6,14},{8,16},{10,18},{12,20},{14,22},{16,24},... | collective-permute-start | bytes 405512 | tf_op jit(solution)/shard_map/ppermute | solution.py:559
  15.1 1.6 %turned_probs.3 = (f32[16,256,512]{2,1,0:T(8,128)S(1)}, f32[16,256,256]{2,1,0:T(8,128)S(1)}, bf16[16,256,512]{2,1,0:T(8,128)(2,1)S(1)}, bf16[16,256,256]{2,1,0:T(8,128)(2,1)S(1)}) custom-call(bf16[512,2048]{1,0:T(8,128)(2,1)S(1)} %get-tuple-element.74.q, ...), custom_call_target="tpu_custom_call", output_to_operand_aliasing={{0}: (5, {}), {1}: (6, {}), {2}: (7, {}), {3}: (8, {})} | custom-call | flops 536870912 | bytes 43159552 | tf_op jit(solution)/shard_map/turned_probs/pallas_call | solution.py:125
  16.8 2.0 %copy-done = bf16[16,256,512]{2,1,0:T(8,128)(2,1)} copy-done((bf16[16,256,512]{2,1,0:T(8,128)(2,1)}, bf16[16,256,512]{2,1,0:T(8,128)(2,1)S(1)}, u32[]{:S(2)}) %copy-start) | copy-done | bytes 4194328
  18.8 1.6 %collective-permute-done.2.refs_0_ = bf16[528,128]{1,0:T(8,128)(2,1)S(1)} collective-permute-done((bf16[528,128]{1,0:T(8,128)(2,1)S(1)}, bf16[528,128]{1,0:T(8,128)(2,1)S(1)}, u32[]{:S(2)}, u32[]{:S(2)}) %collective-permute-start.2) | collective-permute-done | bytes 135200 | tf_op jit(solution)/shard_map/ppermute | solution.py:559
  21.5 5.8 %intra.1.refs_0_ = f32[512,2048]{1,0:T(8,128)S(1)} custom-call(bf16[512,2048]{1,0:T(8,128)(2,1)S(1)} %get-tuple-element.74.q, bf16[512,2048]{1,0:T(8,128)(2,1)S(1)} %get-tuple-element.69.k, bf16[512,2048]{1,0:T(8,128)(2,1)S(1)} %get-tuple-element.70.v, f32[16,512]{1,0:T(8,128)S(1)} %get-tuple-element.71.row, f32[4,512,128]{2,1,0:T(8,128)S(1)} %get-tuple-element.75.col, ...), custom_call_target="tpu_custom_call" | custom-call | flops 2147483648 | bytes 11702272 | tf_op jit(solution)/shard_map/intra/pallas_call | solution.py:125
  28.2 1.6 %collective-permute-start.5 = (bf16[528,128]{1,0:T(8,128)(2,1)S(1)}, bf16[528,128]{1,0:T(8,128)(2,1)S(1)}, u32[]{:S(2)}, u32[]{:S(2)}) collective-permute-start(bf16[528,128]{1,0:T(8,128)(2,1)S(1)} %get-tuple-element.87._), channel_id=1, source_target_pairs={{0,4},{2,6},{4,0},{6,2},{8,12},{10,14},{12,8},{14,10},{16,20},{18,... | collective-permute-start | bytes 405512 | tf_op jit(solution)/shard_map/ppermute | solution.py:554
  29.8 1.9 %own_dscaled.1 = (f32[512,2048]{1,0:T(8,128)S(1)}, bf16[2048,512]{1,0:T(8,128)(2,1)S(1)}) custom-call(bf16[512,2048]{1,0:T(8,128)(2,1)S(1)} %copy-done.2, bf16[256,4096]{1,0:T(8,128)(2,1)} %grad.1, f32[1,2048]{1,0:T(1,128)S(1)} %bitcast.2, bf16[512,2048]{1,0:T(8,128)(2,1)S(1)} %get-tuple-element.74.q, f32[16,512]{1,0:T(8,128)S(1)} %get-tuple-element.71.row, ...), custom_call_target="tpu_custom_call" | custom-call | flops 268435456 | bytes 12759040 | tf_op jit(solution)/shard_map/own_dscaled/pallas_call | solution.py:125
  35.4 1.7 %attention.3 = (f32[512,2048]{1,0:T(8,128)S(1)}, f32[8,512]{1,0:T(8,128)S(1)}) custom-call(bf16[512,2048]{1,0:T(8,128)(2,1)S(1)} %get-tuple-element.74.q, f32[512,2048]{1,0:T(8,128)S(1)} %intra.1.refs_0_, f32[512,2048]{1,0:T(8,128)S(1)} %got_dscaled.1.dscaled, f32[4,512,128]{2,1,0:T(8,128)S(1)} %get-tuple-element.89.growth, ...), custom_call_target="tpu_custom_call", output_to_operand_aliasing={{0}: (5, {})} | custom-call | flops 134217728 | bytes 20733952 | tf_op jit(solution)/shard_map/attention/pallas_call | solution.py:125
  38.0 2.8 %collective-permute-done.7.refs_1_ = f32[8,512]{1,0:T(8,128)S(1)} collective-permute-done((f32[8,512]{1,0:T(8,128)S(1)}, f32[8,512]{1,0:T(8,128)S(1)}, u32[]{:S(2)}, u32[]{:S(2)}) %collective-permute-start.7) | collective-permute-done | bytes 16416 | tf_op jit(solution)/shard_map/ppermute | solution.py:731
  44.4 1.6 %collective-permute-start.9 = (bf16[528,128]{1,0:T(8,128)(2,1)S(1)}, bf16[528,128]{1,0:T(8,128)(2,1)S(1)}, u32[]{:S(2)}, u32[]{:S(2)}) collective-permute-start(bf16[528,128]{1,0:T(8,128)(2,1)S(1)} %get-tuple-element.106._), channel_id=1, source_target_pairs={{0,4},{2,6},{4,0},{6,2},{8,12},{10,14},{12,8},{14,10},{16,20},{18,... | collective-permute-start | bytes 405512 | tf_op jit(solution)/shard_map/ppermute | solution.py:554
  46.0 2.3 %gate.6 = (bf16[512,2048]{1,0:T(8,128)(2,1)}, f32[8,128]{1,0:T(8,128)S(1)}) custom-call(bf16[512,2048]{1,0:T(8,128)(2,1)S(1)} %copy-done.2, f32[512,2048]{1,0:T(8,128)S(1)} %get-tuple-element.97.att, f32[512,2048]{1,0:T(8,128)S(1)} %got_dscaled.1.dscaled, f32[512,128]{1,0:T(8,128)S(1)} %get-tuple-element.99.refs_0_.scale, ...), custom_call_target="tpu_custom_call" | custom-call | flops 268435456 | bytes 12984320 | tf_op jit(solution)/shard_map/gate/pallas_call | solution.py:125
  48.3 1.8 %collective-permute-done.9.got.got_pair = bf16[528,128]{1,0:T(8,128)(2,1)S(1)} collective-permute-done((bf16[528,128]{1,0:T(8,128)(2,1)S(1)}, bf16[528,128]{1,0:T(8,128)(2,1)S(1)}, u32[]{:S(2)}, u32[]{:S(2)}) %collective-permute-start.9) | collective-permute-done | bytes 135200 | tf_op jit(solution)/shard_map/ppermute | solution.py:554
  50.2 2.3 %collective-permute-start.10 = (bf16[528,128]{1,0:T(8,128)(2,1)S(1)}, bf16[528,128]{1,0:T(8,128)(2,1)S(1)}, u32[]{:S(2)}, u32[]{:S(2)}) collective-permute-start(bf16[528,128]{1,0:T(8,128)(2,1)S(1)} %get-tuple-element.109._), channel_id=1, source_target_pairs={{0,24},{2,26},{4,28},{6,30},{8,0},{10,2},{12,4},{14,6},{16,8},{18,... | collective-permute-start | bytes 405512 | tf_op jit(solution)/shard_map/ppermute | solution.py:559
  52.5 4.0 %key_value.2 = (f32[512,2048]{1,0:T(8,128)S(1)}, f32[512,2048]{1,0:T(8,128)S(1)}) custom-call(bf16[512,2048]{1,0:T(8,128)(2,1)S(1)} %get-tuple-element.74.q, bf16[512,2048]{1,0:T(8,128)(2,1)S(1)} %get-tuple-element.70.v, bf16[512,2048]{1,0:T(8,128)(2,1)S(1)} %get-tuple-element.102.dattn, f32[16,256,512]{2,1,0:T(8,128)S(1)} %get-tuple-element.110.table0, ...), custom_call_target="tpu_custom_call" | custom-call | flops 2147483648 | bytes 33689600 | tf_op jit(solution)/shard_map/key_value/pallas_call | solution.py:125
  56.9 6.4 %query.1 = (bf16[512,2048]{1,0:T(8,128)(2,1)}, f32[8,128]{1,0:T(8,128)S(1)}) custom-call(bf16[512,2048]{1,0:T(8,128)(2,1)S(1)} %get-tuple-element.69.k, bf16[512,2048]{1,0:T(8,128)(2,1)S(1)} %get-tuple-element.70.v, bf16[512,2048]{1,0:T(8,128)(2,1)S(1)} %get-tuple-element.102.dattn, f32[16,512]{1,0:T(8,128)S(1)} %get-tuple-element.71.row, ...), custom_call_target="tpu_custom_call" | custom-call | flops 2415919104 | bytes 11198464 | tf_op jit(solution)/shard_map/query/pallas_call | solution.py:125
  64.5 1.6 %collective-permute-start.12 = (bf16[528,128]{1,0:T(8,128)(2,1)S(1)}, bf16[528,128]{1,0:T(8,128)(2,1)S(1)}, u32[]{:S(2)}, u32[]{:S(2)}) collective-permute-start(bf16[528,128]{1,0:T(8,128)(2,1)S(1)} %get-tuple-element.118._), channel_id=1, source_target_pairs={{0,4},{2,6},{4,0},{6,2},{8,12},{10,14},{12,8},{14,10},{16,20},{18,... | collective-permute-start | bytes 405512 | tf_op jit(solution)/shard_map/ppermute | solution.py:554
  66.1 4.2 %key_value.3 = (f32[512,2048]{1,0:T(8,128)S(1)}, f32[512,2048]{1,0:T(8,128)S(1)}) custom-call(bf16[512,2048]{1,0:T(8,128)(2,1)S(1)} %get-tuple-element.74.q, bf16[512,2048]{1,0:T(8,128)(2,1)S(1)} %get-tuple-element.70.v, bf16[512,2048]{1,0:T(8,128)(2,1)S(1)} %get-tuple-element.102.dattn, ...), custom_call_target="tpu_custom_call", output_to_operand_aliasing={{0}: (8, {}), {1}: (9, {})} | custom-call | flops 2147483648 | bytes 42078208 | tf_op jit(solution)/shard_map/key_value/pallas_call | solution.py:125
  70.7 3.2 %final.2 = (bf16[512,2048]{1,0:T(8,128)(2,1)}, bf16[512,2048]{1,0:T(8,128)(2,1)}, f32[1,2048]{1,0:T(1,128)}) custom-call(bf16[512,2048]{1,0:T(8,128)(2,1)S(1)} %get-tuple-element.69.k, bf16[512,2048]{1,0:T(8,128)(2,1)S(1)} %get-tuple-element.70.v, f32[512,2048]{1,0:T(8,128)S(1)} %get-tuple-element.120.refs_0_.dk, f32[512,2048]{1,0:T(8,128)S(1)} %get-tuple-element.121.dv, ...), custom_call_target="tpu_custom_call" | custom-call | flops 268435456 | bytes 18104320 | tf_op jit(solution)/shard_map/final/pallas_call | solution.py:125
  73.9 3.9 %final.3 = (bf16[512,2048]{1,0:T(8,128)(2,1)}, bf16[512,2048]{1,0:T(8,128)(2,1)}, f32[1,2048]{1,0:T(1,128)}) custom-call(bf16[512,2048]{1,0:T(8,128)(2,1)S(1)} %get-tuple-element.69.k, bf16[512,2048]{1,0:T(8,128)(2,1)S(1)} %get-tuple-element.70.v, ...), custom_call_target="tpu_custom_call", output_to_operand_aliasing={{0}: (6, {}), {1}: (7, {}), {2}: (8, {})} | custom-call | flops 268435456 | bytes 22306816 | tf_op jit(solution)/shard_map/final/pallas_call | solution.py:125
  (40 shorter events, 14.6 us)
Async XLA Ops:
  3.5 3.9 %collective-permute-start = (f32[2,520,128]{2,1,0:T(8,128)S(1)}, f32[2,520,128]{2,1,0:T(8,128)S(1)}, u32[]{:S(2)}, u32[]{:S(2)}) collective-permute-start(f32[2,520,128]{2,1,0:T(8,128)S(1)} %get-tuple-element.72), channel_id=1, source_target_pairs={{0,2},{2,0},{4,6},{6,4},{8,10},{10,8},{12,14},{14,12},{16,18},{18,... | collective-permute-start | bytes 1597448 | tf_op jit(solution)/shard_map/ppermute | solution.py:554
  4.0 29.6 %collective-permute-start.3 = (bf16[256,2048]{1,0:T(8,128)(2,1)S(1)}, bf16[256,2048]{1,0:T(8,128)(2,1)S(1)}, u32[]{:S(2)}, u32[]{:S(2)}) collective-permute-start(bf16[256,2048]{1,0:T(8,128)(2,1)S(1)} %get-tuple-element.85), channel_id=1, source_target_pairs={{0,1},{1,0},{2,3},{3,2},{4,5},{5,4},{6,7},{7,6},{8,9},{9,8},{10,11... | collective-permute-start | bytes 3145736 | tf_op jit(solution)/shard_map/ppermute | solution.py:645
  7.5 5.7 %collective-permute-start.1 = (bf16[528,128]{1,0:T(8,128)(2,1)S(1)}, bf16[528,128]{1,0:T(8,128)(2,1)S(1)}, u32[]{:S(2)}, u32[]{:S(2)}) collective-permute-start(bf16[528,128]{1,0:T(8,128)(2,1)S(1)} %get-tuple-element.73._), channel_id=1, source_target_pairs={{0,4},{2,6},{4,0},{6,2},{8,12},{10,14},{12,8},{14,10},{16,20},{18,... | collective-permute-start | bytes 405512 | tf_op jit(solution)/shard_map/ppermute | solution.py:554
  13.3 7.0 %collective-permute-start.2 = (bf16[528,128]{1,0:T(8,128)(2,1)S(1)}, bf16[528,128]{1,0:T(8,128)(2,1)S(1)}, u32[]{:S(2)}, u32[]{:S(2)}) collective-permute-start(bf16[528,128]{1,0:T(8,128)(2,1)S(1)} %get-tuple-element.79._), channel_id=1, source_target_pairs={{0,8},{2,10},{4,12},{6,14},{8,16},{10,18},{12,20},{14,22},{16,24},... | collective-permute-start | bytes 405512 | tf_op jit(solution)/shard_map/ppermute | solution.py:559
  16.8 2.0 %copy-start = (bf16[16,256,512]{2,1,0:T(8,128)(2,1)}, bf16[16,256,512]{2,1,0:T(8,128)(2,1)S(1)}, u32[]{:S(2)}) copy-start(bf16[16,256,512]{2,1,0:T(8,128)(2,1)S(1)} %get-tuple-element.112.probs0) | copy-start | bytes 12582916
  20.5 7.6 %collective-permute-start.4 = (bf16[528,128]{1,0:T(8,128)(2,1)S(1)}, bf16[528,128]{1,0:T(8,128)(2,1)S(1)}, u32[]{:S(2)}, u32[]{:S(2)}) collective-permute-start(bf16[528,128]{1,0:T(8,128)(2,1)S(1)} %get-tuple-element.84._), channel_id=1, source_target_pairs={{0,16},{2,18},{4,20},{6,22},{8,24},{10,26},{12,28},{14,30},{16,0},... | collective-permute-start | bytes 405512 | tf_op jit(solution)/shard_map/ppermute | solution.py:559
  28.1 1.7 %copy-start.2 = (bf16[512,2048]{1,0:T(8,128)(2,1)S(1)}, bf16[512,2048]{1,0:T(8,128)(2,1)}, u32[]{:S(2)}) copy-start(bf16[512,2048]{1,0:T(8,128)(2,1)} %gate.7) | copy-start | bytes 6291460
  28.1 1.7 %copy-start.3 = (f32[2048]{0:T(1024)S(1)}, f32[2048]{0:T(1024)}, u32[]{:S(2)}) copy-start(f32[2048]{0:T(1024)} %param.12) | copy-start | bytes 24580
  28.2 5.1 %collective-permute-start.5 = (bf16[528,128]{1,0:T(8,128)(2,1)S(1)}, bf16[528,128]{1,0:T(8,128)(2,1)S(1)}, u32[]{:S(2)}, u32[]{:S(2)}) collective-permute-start(bf16[528,128]{1,0:T(8,128)(2,1)S(1)} %get-tuple-element.87._), channel_id=1, source_target_pairs={{0,4},{2,6},{4,0},{6,2},{8,12},{10,14},{12,8},{14,10},{16,20},{18,... | collective-permute-start | bytes 405512 | tf_op jit(solution)/shard_map/ppermute | solution.py:554
  33.5 1.9 %collective-permute-start.6 = (bf16[2,528,128]{2,1,0:T(8,128)(2,1)S(1)}, bf16[2,528,128]{2,1,0:T(8,128)(2,1)S(1)}, u32[]{:S(2)}, u32[]{:S(2)}) collective-permute-start(bf16[2,528,128]{2,1,0:T(8,128)(2,1)S(1)} %get-tuple-element.92), channel_id=1, source_target_pairs={{0,2},{2,0},{4,6},{6,4},{8,10},{10,8},{12,14},{14,12},{16,18},{18,... | collective-permute-start | bytes 811016 | tf_op jit(solution)/shard_map/ppermute | solution.py:554
  37.1 3.8 %collective-permute-start.7 = (f32[8,512]{1,0:T(8,128)S(1)}, f32[8,512]{1,0:T(8,128)S(1)}, u32[]{:S(2)}, u32[]{:S(2)}) collective-permute-start(f32[8,512]{1,0:T(8,128)S(1)} %get-tuple-element.98.refs_0_), channel_id=1, source_target_pairs={{0,1},{1,0},{2,3},{3,2},{4,5},{5,4},{6,7},{7,6},{8,9},{9,8},{10,11... | collective-permute-start | bytes 49160 | tf_op jit(solution)/shard_map/ppermute | solution.py:731
  42.3 2.0 %collective-permute-start.8 = (f32[2,520,128]{2,1,0:T(8,128)S(1)}, f32[2,520,128]{2,1,0:T(8,128)S(1)}, u32[]{:S(2)}, u32[]{:S(2)}) collective-permute-start(f32[2,520,128]{2,1,0:T(8,128)S(1)} %get-tuple-element.104), channel_id=1, source_target_pairs={{0,2},{2,0},{4,6},{6,4},{8,10},{10,8},{12,14},{14,12},{16,18},{18,... | collective-permute-start | bytes 1597448 | tf_op jit(solution)/shard_map/ppermute | solution.py:554
  44.4 5.7 %collective-permute-start.9 = (bf16[528,128]{1,0:T(8,128)(2,1)S(1)}, bf16[528,128]{1,0:T(8,128)(2,1)S(1)}, u32[]{:S(2)}, u32[]{:S(2)}) collective-permute-start(bf16[528,128]{1,0:T(8,128)(2,1)S(1)} %get-tuple-element.106._), channel_id=1, source_target_pairs={{0,4},{2,6},{4,0},{6,2},{8,12},{10,14},{12,8},{14,10},{16,20},{18,... | collective-permute-start | bytes 405512 | tf_op jit(solution)/shard_map/ppermute | solution.py:554
  46.0 6.5 %copy-start.1 = (bf16[16,256,512]{2,1,0:T(8,128)(2,1)S(1)}, bf16[16,256,512]{2,1,0:T(8,128)(2,1)}, u32[]{:S(2)}) copy-start(bf16[16,256,512]{2,1,0:T(8,128)(2,1)} %copy-done) | copy-start | bytes 12582916
  50.2 6.3 %collective-permute-start.10 = (bf16[528,128]{1,0:T(8,128)(2,1)S(1)}, bf16[528,128]{1,0:T(8,128)(2,1)S(1)}, u32[]{:S(2)}, u32[]{:S(2)}) collective-permute-start(bf16[528,128]{1,0:T(8,128)(2,1)S(1)} %get-tuple-element.109._), channel_id=1, source_target_pairs={{0,24},{2,26},{4,28},{6,30},{8,0},{10,2},{12,4},{14,6},{16,8},{18,... | collective-permute-start | bytes 405512 | tf_op jit(solution)/shard_map/ppermute | solution.py:559
  56.6 7.8 %collective-permute-start.11 = (bf16[528,128]{1,0:T(8,128)(2,1)S(1)}, bf16[528,128]{1,0:T(8,128)(2,1)S(1)}, u32[]{:S(2)}, u32[]{:S(2)}) collective-permute-start(bf16[528,128]{1,0:T(8,128)(2,1)S(1)} %get-tuple-element.114._), channel_id=1, source_target_pairs={{0,16},{2,18},{4,20},{6,22},{8,24},{10,26},{12,28},{14,30},{16,0},... | collective-permute-start | bytes 405512 | tf_op jit(solution)/shard_map/ppermute | solution.py:559
  64.5 5.8 %collective-permute-start.12 = (bf16[528,128]{1,0:T(8,128)(2,1)S(1)}, bf16[528,128]{1,0:T(8,128)(2,1)S(1)}, u32[]{:S(2)}, u32[]{:S(2)}) collective-permute-start(bf16[528,128]{1,0:T(8,128)(2,1)S(1)} %get-tuple-element.118._), channel_id=1, source_target_pairs={{0,4},{2,6},{4,0},{6,2},{8,12},{10,14},{12,8},{14,10},{16,20},{18,... | collective-permute-start | bytes 405512 | tf_op jit(solution)/shard_map/ppermute | solution.py:554
  70.6 3.3 %collective-permute-start.13 = (bf16[2,528,128]{2,1,0:T(8,128)(2,1)S(1)}, bf16[2,528,128]{2,1,0:T(8,128)(2,1)S(1)}, u32[]{:S(2)}, u32[]{:S(2)}) collective-permute-start(bf16[2,528,128]{2,1,0:T(8,128)(2,1)S(1)} %get-tuple-element.124), channel_id=1, source_target_pairs={{0,2},{2,0},{4,6},{6,4},{8,10},{10,8},{12,14},{14,12},{16,18},{18,... | collective-permute-start | bytes 811016 | tf_op jit(solution)/shard_map/ppermute | solution.py:554

commit v7 on v6

--- a/solution.py
+++ b/solution.py
@@ -395,7 +395,7 @@
     if same:
         att, sq, inn, both = refs
     else:
-        _, sq_before, inn_before, att, sums, sq, inn, both = refs
+        sq_before, inn_before, att, sums, sq, inn, both = refs
         sq[...] = sq_before[...]
         inn[...] = inn_before[...]
     for y in range(2):
@@ -522,25 +522,49 @@
     lax.fori_loop(first, first + TEAM // 2, one, 0)
 
 
-def final_body(heads, same, k, v, dk, dv, shrink, state, *refs):
-    hq = heads // TEAM
-    w = hq * HEAD
-    key_grad, value_grad, gain_grad, key_out, value_out, sems = refs[-6:]
-    if not same:
-        gain_grad[...] = refs[2][...]
-    copies = []
+def final_rows(hq, y, j, same, k, v, dk, dv, shrink, state, key_out, value_out):
+    g = quarter_of(y, same)
+    _, c = head_at(g, hq, j)
+    fade = shrink[g, :, j : j + 1]
+    after = state[y, chunk(j), :]
+    key_out[y, :, chunk(j)] = (dk[:, c] + nt(v[:, c], after) * fade).astype(BF16)
+    value_out[y, :, chunk(j)] = (dv[:, c] + nn(k[:, c], after) * fade).astype(BF16)
+
+
+def own_final_body(heads, k, v, dk, dv, shrink, state, key_out, value_out, gain_grad):
+    hq = heads // TEAM
     for y in range(2):
-        g = quarter_of(y, same)
         items = read_narrow(state.at[y], hq)
         for j in range(hq):
-            _, c = head_at(g, hq, j)
-            fade = shrink[g, :, j : j + 1]
-            after = state[y, chunk(j), :]
-            key_out[y, :, chunk(j)] = (dk[:, c] + nt(v[:, c], after) * fade).astype(BF16)
-            value_out[y, :, chunk(j)] = (dv[:, c] + nn(k[:, c], after) * fade).astype(BF16)
-            gain_grad[:, c] = items[j][2]
-        copies.append(leave(key_out.at[y], key_grad, sems.at[0, y], g, w))
-        copies.append(leave(value_out.at[y], value_grad, sems.at[1, y], g, w))
+            final_rows(hq, y, j, True, k, v, dk, dv, shrink, state, key_out, value_out)
+            gain_grad[:, head_at(quarter_of(y, True), hq, j)[1]] = items[j][2]
+
+
+def final_body(heads, k, v, dk, dv, shrink, state, own_key, own_value, own_gain, *refs):
+    hq = heads // TEAM
+    key_grad, value_grad, gain_grad, key_out, value_out, sems = refs
+    copies = []
+
+    def send(src, dst, cols):
+        copy = pltpu.make_async_copy(src, dst.at[:, cols], sems.at[len(copies)])
+        copy.start()
+        copies.append(copy)
+
+    for y in range(2):
+        for j, _, count, c in several(quarter_of(y, True), hq):
+            place = slice(j * HEAD, (j + count) * HEAD)
+            send(own_key.at[y, :, place], key_grad, c)
+            send(own_value.at[y, :, place], value_grad, c)
+    gain_grad[...] = own_gain[...]
+    for y in range(2):
+        items = read_narrow(state.at[y], hq)
+        for j, _, count, c in several(quarter_of(y, False), hq):
+            for m in range(j, j + count):
+                final_rows(hq, y, m, False, k, v, dk, dv, shrink, state, key_out, value_out)
+                gain_grad[:, head_at(quarter_of(y, False), hq, m)[1]] = items[m][2]
+            place = slice(j * HEAD, (j + count) * HEAD)
+            send(key_out.at[y, :, place], key_grad, c)
+            send(value_out.at[y, :, place], value_grad, c)
     for copy in copies:
         copy.wait()
 
@@ -556,7 +580,8 @@
 
 def across(x, k):
     n = lax.axis_size("ctx")
-    return lax.ppermute(x, "ctx", [(i, (i + TEAM * k) % n) for i in range(n)])
+    moves = [(i, i + TEAM * k) for i in range(n)]
+    return lax.ppermute(x, "ctx", [(i, j % n) for i, j in moves if k < 0 or j < n])
 
 
 def local(queries, keys, values, log_decay, gate, gain, grad_out):
@@ -717,15 +742,16 @@
         "attention",
         [wide_scratch],
         small // 2,
+        alias={1: 0},
     )
     att, sums = call(
         functools.partial(attention_body, heads, False),
-        [queries, intra, dscaled, growth, got, att, squares, inner],
+        [queries, att, dscaled, growth, got, squares, inner],
         [f32(rows, width), f32(8, rows)],
         "attention",
         [pltpu.VMEM((rows, HEAD), F32)] * 2 + [wide_scratch],
         small // 2,
-        alias={5: 0},
+        alias={1: 0},
     )
     if swaps:
         others = lax.ppermute(sums, "tp", [(0, 1), (1, 0)])
@@ -800,18 +826,23 @@
     work = {"pair": gate_beside, "one": key_value_first, "last": query_beside, "pair_back": key_value_last}
     back_mine, back_got = scan(True, keep, give, work)
     gate_grad, query_grad, (dk, dv) = done["gate"], done["query"], done["key_value"]
-    final = lambda same, state, *before: call(
-        functools.partial(final_body, heads, same),
-        [keys, values, dk, dv, shrink, state, *before],
+    both = bf(2, rows, hq * HEAD)
+    own_key, own_value, own_gain = call(
+        functools.partial(own_final_body, heads),
+        [keys, values, dk, dv, shrink, back_mine],
+        [both, both, f32(1, width)],
+        "own_final",
+        flops=small,
+    )
+    key_grad, value_grad, gain_grad = call(
+        functools.partial(final_body, heads),
+        [keys, values, dk, dv, shrink, back_got, own_key, own_value, own_gain],
         [bf(rows, width), bf(rows, width), f32(1, width)],
         "final",
-        [pltpu.VMEM((2, rows, hq * HEAD), BF16)] * 2 + [pltpu.SemaphoreType.DMA((2, 2))],
+        [pltpu.VMEM(both.shape, BF16)] * 2 + [pltpu.SemaphoreType.DMA((8 * hq,))],
         small,
-        [VMEM] * 6 + [HBM, HBM, VMEM][: len(before)],
-        [HBM, HBM, VMEM],
-        {6 + i: i for i in range(len(before))},
-    )
-    key_grad, value_grad, gain_grad = final(False, back_got, *final(True, back_mine))
+        out_specs=[HBM, HBM, VMEM],
+    )
     return query_grad, key_grad, value_grad, gate_grad, gain_grad.reshape(width)
 
 

time: 78.2 us -> 80.1 us (1.024)
  starting transfers between devices: 16 us -> 23 us
  local copies, waits for them, and re-layouts: 1.99 us -> 0.02 us
  waiting for transfers between devices: 11.3 us -> 9.72 us
  Pallas kernels: 47.6 us -> 46.1 us
    ppermute x4, starting transfers between devices: 5.44 us -> 12.4 us  [across(): lax.ppermute(x, 'ctx', [(i, j % n) for i, j in moves if k < 0 or j < n])]
    unnamed x8 -> x10, local copies, waits for them, and re-layouts: 1.99 us -> 0.02 us
    ppermute x4, waiting for transfers between devices: 3.47 us -> 1.64 us  [across(): lax.ppermute(x, 'ctx', [(i, j % n) for i, j in moves if k < 0 or j < n])]
    pallas_call x28, Pallas kernels: 47.6 us -> 46.1 us  [call(): pl.pallas_call(body, in_specs=in_specs or [VMEM] * len(inputs), out_specs...]
  transfers between devices with their start and end apart: 14 -> 14, of which waited for: 8 -> 8; matrix products, arithmetic and copies ran while one was open for 0% -> 0% of each run, Pallas kernels for 48% -> 45%
where the time goes in v7:
time: 80.1 us; the launch traced here: 79.9 us
  Pallas kernels  46.1 us (58%)
  starting transfers between devices  23 us (29%)
  waiting for transfers between devices  9.72 us (12%)
  between operations  1.11 us (1%)
    pallas_call x28, Pallas kernels, call(): pl.pallas_call(body, in_specs=in_specs or [VMEM] * len(inputs), out_specs...  46.1 us
    ppermute x4, starting transfers between devices, across(): lax.ppermute(x, 'ctx', [(i, j % n) for i, j in moves if k < 0 or j < n])  12.4 us
    ppermute x8, starting transfers between devices, swap(): return lax.ppermute(x, 'ctx', [(i, i ^ bit) for i in range(n)])  7.04 us
    ppermute x8, waiting for transfers between devices, swap(): return lax.ppermute(x, 'ctx', [(i, i ^ bit) for i in range(n)])  5.28 us
    ppermute x1, waiting for transfers between devices, local(): others = lax.ppermute(sums, 'tp', [(0, 1), (1, 0)])  2.8 us
    ppermute x1, starting transfers between devices, local(): arrived = lax.ppermute(outs[4], 'tp', [(0, 1), (1, 0)])  2.56 us
    ppermute x4, waiting for transfers between devices, across(): lax.ppermute(x, 'ctx', [(i, j % n) for i, j in moves if k < 0 or j < n])  1.64 us
  transfers between devices with their start and end apart: 14, of which 8 were waited for; matrix products, arithmetic and copies ran while one was open for 0% of the time, Pallas kernels for 45%

profile of v7, /device:TPU:0, one launch (start us, length us, event | category | flops | bytes accessed | tf_op | source)
XLA Modules:
  0.0 79.9 jit_solution(8798776851295569064)
XLA Ops:
  0.6 2.8 %sent_states.1 = (f32[2,520,128]{2,1,0:T(8,128)S(1)}, f32[16,512]{1,0:T(8,128)S(1)}, bf16[512,2048]{1,0:T(8,128)(2,1)S(1)}, bf16[512,2048]{1,0:T(8,128)(2,1)S(1)}, bf16[256,2048]{1,0:T(8,128)(2,1)S(1)}) custom-call(bf16[512,2048]{1,0:T(8,128)(2,1)} %k_hbm.1, bf16[512,2048]{1,0:T(8,128)(2,1)} %v_hbm.1, f32[16,512]{1,0:T(8,128)} %ld_hbm.1, bf16[256,4096]{1,0:T(8,128)(2,1)} %grad.1), custom_call_target="tpu_custom_call" | custom-call | flops 134217728 | bytes 12132352 | tf_op jit(solution)/shard_map/sent_states/pallas_call | solution.py:125
  4.0 2.6 %collective-permute-start.3 = (bf16[256,2048]{1,0:T(8,128)(2,1)S(1)}, bf16[256,2048]{1,0:T(8,128)(2,1)S(1)}, u32[]{:S(2)}, u32[]{:S(2)}) collective-permute-start(bf16[256,2048]{1,0:T(8,128)(2,1)S(1)} %get-tuple-element.85), channel_id=1, source_target_pairs={{0,1},{1,0},{2,3},{3,2},{4,5},{5,4},{6,7},{7,6},{8,9},{9,8},{10,11... | collective-permute-start | bytes 3145736 | tf_op jit(solution)/shard_map/ppermute | solution.py:670
  7.5 1.6 %collective-permute-start.1 = (bf16[528,128]{1,0:T(8,128)(2,1)S(1)}, bf16[528,128]{1,0:T(8,128)(2,1)S(1)}, u32[]{:S(2)}, u32[]{:S(2)}) collective-permute-start(bf16[528,128]{1,0:T(8,128)(2,1)S(1)} %get-tuple-element.73._), channel_id=1, source_target_pairs={{0,4},{2,6},{4,0},{6,2},{8,12},{10,14},{12,8},{14,10},{16,20},{18,... | collective-permute-start | bytes 405512 | tf_op jit(solution)/shard_map/ppermute | solution.py:578
  9.1 1.6 %decays.1 = (f32[4,512,128]{2,1,0:T(8,128)S(1)}, f32[4,512,128]{2,1,0:T(8,128)S(1)}, f32[4,512,128]{2,1,0:T(8,128)S(1)}, bf16[512,2048]{1,0:T(8,128)(2,1)S(1)}) custom-call(f32[16,512]{1,0:T(8,128)S(1)} %get-tuple-element.71.row, bf16[512,2048]{1,0:T(8,128)(2,1)} %q_hbm.1, bf16[528,128]{1,0:T(8,128)(2,1)S(1)} %get-tuple-element.73._), custom_call_target="tpu_custom_call" | custom-call | bytes 7507968 | tf_op jit(solution)/shard_map/decays/pallas_call | solution.py:125
  10.7 1.6 %turned_probs.2 = (f32[16,256,512]{2,1,0:T(8,128)S(1)}, f32[16,256,256]{2,1,0:T(8,128)S(1)}, bf16[16,256,512]{2,1,0:T(8,128)(2,1)S(1)}, bf16[16,256,256]{2,1,0:T(8,128)(2,1)S(1)}) custom-call(bf16[512,2048]{1,0:T(8,128)(2,1)S(1)} %get-tuple-element.74.q, bf16[512,2048]{1,0:T(8,128)(2,1)S(1)} %get-tuple-element.69.k, f32[16,512]{1,0:T(8,128)S(1)} %get-tuple-element.71.row, ...), custom_call_target="tpu_custom_call" | custom-call | flops 536870912 | bytes 24285184 | tf_op jit(solution)/shard_map/turned_probs/pallas_call | solution.py:125
  13.3 3.5 %collective-permute-start.2 = (bf16[528,128]{1,0:T(8,128)(2,1)S(1)}, bf16[528,128]{1,0:T(8,128)(2,1)S(1)}, u32[]{:S(2)}, u32[]{:S(2)}) collective-permute-start(bf16[528,128]{1,0:T(8,128)(2,1)S(1)} %get-tuple-element.79._), channel_id=1, source_target_pairs={{0,8},{2,10},{4,12},{6,14},{8,16},{10,18},{12,20},{14,22},{16,24},... | collective-permute-start | bytes 405512 | tf_op jit(solution)/shard_map/ppermute | solution.py:584
  16.8 1.6 %turned_probs.3 = (f32[16,256,512]{2,1,0:T(8,128)S(1)}, f32[16,256,256]{2,1,0:T(8,128)S(1)}, bf16[16,256,512]{2,1,0:T(8,128)(2,1)S(1)}, bf16[16,256,256]{2,1,0:T(8,128)(2,1)S(1)}) custom-call(bf16[512,2048]{1,0:T(8,128)(2,1)S(1)} %get-tuple-element.74.q, ...), custom_call_target="tpu_custom_call", output_to_operand_aliasing={{0}: (5, {}), {1}: (6, {}), {2}: (7, {}), {3}: (8, {})} | custom-call | flops 536870912 | bytes 43159552 | tf_op jit(solution)/shard_map/turned_probs/pallas_call | solution.py:125
  19.4 5.6 %collective-permute-start.4 = (bf16[528,128]{1,0:T(8,128)(2,1)S(1)}, bf16[528,128]{1,0:T(8,128)(2,1)S(1)}, u32[]{:S(2)}, u32[]{:S(2)}) collective-permute-start(bf16[528,128]{1,0:T(8,128)(2,1)S(1)} %get-tuple-element.84._), channel_id=1, source_target_pairs={{0,16},{2,18},{4,20},{6,22},{8,24},{10,26},{12,28},{14,30},{1,17},... | collective-permute-start | bytes 405512 | tf_op jit(solution)/shard_map/ppermute | solution.py:584
  25.0 5.8 %intra.1.refs_0_ = f32[512,2048]{1,0:T(8,128)S(1)} custom-call(bf16[512,2048]{1,0:T(8,128)(2,1)S(1)} %get-tuple-element.74.q, bf16[512,2048]{1,0:T(8,128)(2,1)S(1)} %get-tuple-element.69.k, bf16[512,2048]{1,0:T(8,128)(2,1)S(1)} %get-tuple-element.70.v, f32[16,512]{1,0:T(8,128)S(1)} %get-tuple-element.71.row, f32[4,512,128]{2,1,0:T(8,128)S(1)} %get-tuple-element.75.col, ...), custom_call_target="tpu_custom_call" | custom-call | flops 2147483648 | bytes 11702272 | tf_op jit(solution)/shard_map/intra/pallas_call | solution.py:125
  31.0 1.6 %collective-permute-start.5 = (bf16[528,128]{1,0:T(8,128)(2,1)S(1)}, bf16[528,128]{1,0:T(8,128)(2,1)S(1)}, u32[]{:S(2)}, u32[]{:S(2)}) collective-permute-start(bf16[528,128]{1,0:T(8,128)(2,1)S(1)} %get-tuple-element.87._), channel_id=1, source_target_pairs={{0,4},{2,6},{4,0},{6,2},{8,12},{10,14},{12,8},{14,10},{16,20},{18,... | collective-permute-start | bytes 405512 | tf_op jit(solution)/shard_map/ppermute | solution.py:578
  32.6 1.9 %own_dscaled.1 = (f32[512,2048]{1,0:T(8,128)S(1)}, bf16[2048,512]{1,0:T(8,128)(2,1)S(1)}) custom-call(bf16[512,2048]{1,0:T(8,128)(2,1)S(1)} %copy-done.3, bf16[256,4096]{1,0:T(8,128)(2,1)} %grad.1, f32[1,2048]{1,0:T(1,128)S(1)} %bitcast.2, bf16[512,2048]{1,0:T(8,128)(2,1)S(1)} %get-tuple-element.74.q, f32[16,512]{1,0:T(8,128)S(1)} %get-tuple-element.71.row, ...), custom_call_target="tpu_custom_call" | custom-call | flops 268435456 | bytes 12759040 | tf_op jit(solution)/shard_map/own_dscaled/pallas_call | solution.py:125
  34.5 1.6 %collective-permute-done.5.other = bf16[528,128]{1,0:T(8,128)(2,1)S(1)} collective-permute-done((bf16[528,128]{1,0:T(8,128)(2,1)S(1)}, bf16[528,128]{1,0:T(8,128)(2,1)S(1)}, u32[]{:S(2)}, u32[]{:S(2)}) %collective-permute-start.5) | collective-permute-done | bytes 135200 | tf_op jit(solution)/shard_map/ppermute | solution.py:578
  37.0 1.7 %attention.2 = (f32[512,2048]{1,0:T(8,128)S(1)}, f32[512,128]{1,0:T(8,128)S(1)}, f32[512,128]{1,0:T(8,128)S(1)}) custom-call(bf16[512,2048]{1,0:T(8,128)(2,1)S(1)} %get-tuple-element.74.q, f32[512,2048]{1,0:T(8,128)S(1)} %intra.1.refs_0_, f32[512,2048]{1,0:T(8,128)S(1)} %got_dscaled.1.dscaled, ...), custom_call_target="tpu_custom_call", output_to_operand_aliasing={{0}: (1, {})} | custom-call | flops 134217728 | bytes 16523264 | tf_op jit(solution)/shard_map/attention/pallas_call | solution.py:125
  38.7 2.2 %attention.3 = (f32[512,2048]{1,0:T(8,128)S(1)}, f32[8,512]{1,0:T(8,128)S(1)}) custom-call(bf16[512,2048]{1,0:T(8,128)(2,1)S(1)} %get-tuple-element.74.q, f32[512,2048]{1,0:T(8,128)S(1)} %get-tuple-element.93.intra, f32[512,2048]{1,0:T(8,128)S(1)} %got_dscaled.1.dscaled, ...), custom_call_target="tpu_custom_call", output_to_operand_aliasing={{0}: (1, {})} | custom-call | flops 134217728 | bytes 16539648 | tf_op jit(solution)/shard_map/attention/pallas_call | solution.py:125
  41.9 2.8 %collective-permute-done.7.refs_1_ = f32[8,512]{1,0:T(8,128)S(1)} collective-permute-done((f32[8,512]{1,0:T(8,128)S(1)}, f32[8,512]{1,0:T(8,128)S(1)}, u32[]{:S(2)}, u32[]{:S(2)}) %collective-permute-start.7) | collective-permute-done | bytes 16416 | tf_op jit(solution)/shard_map/ppermute | solution.py:757
  48.3 1.6 %collective-permute-start.9 = (bf16[528,128]{1,0:T(8,128)(2,1)S(1)}, bf16[528,128]{1,0:T(8,128)(2,1)S(1)}, u32[]{:S(2)}, u32[]{:S(2)}) collective-permute-start(bf16[528,128]{1,0:T(8,128)(2,1)S(1)} %get-tuple-element.106._), channel_id=1, source_target_pairs={{0,4},{2,6},{4,0},{6,2},{8,12},{10,14},{12,8},{14,10},{16,20},{18,... | collective-permute-start | bytes 405512 | tf_op jit(solution)/shard_map/ppermute | solution.py:578
  49.8 2.2 %gate.6 = (bf16[512,2048]{1,0:T(8,128)(2,1)}, f32[8,128]{1,0:T(8,128)S(1)}) custom-call(bf16[512,2048]{1,0:T(8,128)(2,1)S(1)} %copy-done.3, f32[512,2048]{1,0:T(8,128)S(1)} %get-tuple-element.97.att, f32[512,2048]{1,0:T(8,128)S(1)} %got_dscaled.1.dscaled, f32[512,128]{1,0:T(8,128)S(1)} %get-tuple-element.99.refs_0_.scale, ...), custom_call_target="tpu_custom_call" | custom-call | flops 268435456 | bytes 12984320 | tf_op jit(solution)/shard_map/gate/pallas_call | solution.py:125
  52.0 2.0 %collective-permute-done.9.got.got_pair = bf16[528,128]{1,0:T(8,128)(2,1)S(1)} collective-permute-done((bf16[528,128]{1,0:T(8,128)(2,1)S(1)}, bf16[528,128]{1,0:T(8,128)(2,1)S(1)}, u32[]{:S(2)}, u32[]{:S(2)}) %collective-permute-start.9) | collective-permute-done | bytes 135200 | tf_op jit(solution)/shard_map/ppermute | solution.py:578
  54.0 2.9 %collective-permute-start.10 = (bf16[528,128]{1,0:T(8,128)(2,1)S(1)}, bf16[528,128]{1,0:T(8,128)(2,1)S(1)}, u32[]{:S(2)}, u32[]{:S(2)}) collective-permute-start(bf16[528,128]{1,0:T(8,128)(2,1)S(1)} %get-tuple-element.109._), channel_id=1, source_target_pairs={{0,24},{2,26},{4,28},{6,30},{8,0},{10,2},{12,4},{14,6},{16,8},{18,... | collective-permute-start | bytes 405512 | tf_op jit(solution)/shard_map/ppermute | solution.py:584
  56.9 4.0 %key_value.2 = (f32[512,2048]{1,0:T(8,128)S(1)}, f32[512,2048]{1,0:T(8,128)S(1)}) custom-call(bf16[512,2048]{1,0:T(8,128)(2,1)S(1)} %get-tuple-element.74.q, bf16[512,2048]{1,0:T(8,128)(2,1)S(1)} %get-tuple-element.70.v, bf16[512,2048]{1,0:T(8,128)(2,1)S(1)} %get-tuple-element.102.dattn, f32[16,256,512]{2,1,0:T(8,128)S(1)} %get-tuple-element.110.table0, ...), custom_call_target="tpu_custom_call" | custom-call | flops 2147483648 | bytes 33689600 | tf_op jit(solution)/shard_map/key_value/pallas_call | solution.py:125
  61.5 6.4 %query.1 = (bf16[512,2048]{1,0:T(8,128)(2,1)}, f32[8,128]{1,0:T(8,128)S(1)}) custom-call(bf16[512,2048]{1,0:T(8,128)(2,1)S(1)} %get-tuple-element.69.k, bf16[512,2048]{1,0:T(8,128)(2,1)S(1)} %get-tuple-element.70.v, bf16[512,2048]{1,0:T(8,128)(2,1)S(1)} %get-tuple-element.102.dattn, f32[16,512]{1,0:T(8,128)S(1)} %get-tuple-element.71.row, ...), custom_call_target="tpu_custom_call" | custom-call | flops 2415919104 | bytes 11198464 | tf_op jit(solution)/shard_map/query/pallas_call | solution.py:125
  68.8 1.6 %collective-permute-start.12 = (bf16[528,128]{1,0:T(8,128)(2,1)S(1)}, bf16[528,128]{1,0:T(8,128)(2,1)S(1)}, u32[]{:S(2)}, u32[]{:S(2)}) collective-permute-start(bf16[528,128]{1,0:T(8,128)(2,1)S(1)} %get-tuple-element.118._), channel_id=1, source_target_pairs={{0,4},{2,6},{4,0},{6,2},{8,12},{10,14},{12,8},{14,10},{16,20},{18,... | collective-permute-start | bytes 405512 | tf_op jit(solution)/shard_map/ppermute | solution.py:578
  70.4 4.2 %key_value.3 = (f32[512,2048]{1,0:T(8,128)S(1)}, f32[512,2048]{1,0:T(8,128)S(1)}) custom-call(bf16[512,2048]{1,0:T(8,128)(2,1)S(1)} %get-tuple-element.74.q, bf16[512,2048]{1,0:T(8,128)(2,1)S(1)} %get-tuple-element.70.v, bf16[512,2048]{1,0:T(8,128)(2,1)S(1)} %get-tuple-element.102.dattn, ...), custom_call_target="tpu_custom_call", output_to_operand_aliasing={{0}: (8, {}), {1}: (9, {})} | custom-call | flops 2147483648 | bytes 42078208 | tf_op jit(solution)/shard_map/key_value/pallas_call | solution.py:125
  76.5 3.3 %final.1 = (bf16[512,2048]{1,0:T(8,128)(2,1)}, bf16[512,2048]{1,0:T(8,128)(2,1)}, f32[1,2048]{1,0:T(1,128)}) custom-call(bf16[512,2048]{1,0:T(8,128)(2,1)S(1)} %get-tuple-element.69.k, bf16[512,2048]{1,0:T(8,128)(2,1)S(1)} %get-tuple-element.70.v, f32[512,2048]{1,0:T(8,128)S(1)} %get-tuple-element.120.refs_0_.dk, f32[512,2048]{1,0:T(8,128)S(1)} %get-tuple-element.121.dv, ...), custom_call_target="tpu_custom_call" | custom-call | flops 268435456 | bytes 20209664 | tf_op jit(solution)/shard_map/final/pallas_call | solution.py:125
  (42 shorter events, 12.4 us)
Async XLA Ops:
  3.5 3.9 %collective-permute-start = (f32[2,520,128]{2,1,0:T(8,128)S(1)}, f32[2,520,128]{2,1,0:T(8,128)S(1)}, u32[]{:S(2)}, u32[]{:S(2)}) collective-permute-start(f32[2,520,128]{2,1,0:T(8,128)S(1)} %get-tuple-element.72), channel_id=1, source_target_pairs={{0,2},{2,0},{4,6},{6,4},{8,10},{10,8},{12,14},{14,12},{16,18},{18,... | collective-permute-start | bytes 1597448 | tf_op jit(solution)/shard_map/ppermute | solution.py:578
  4.0 32.4 %collective-permute-start.3 = (bf16[256,2048]{1,0:T(8,128)(2,1)S(1)}, bf16[256,2048]{1,0:T(8,128)(2,1)S(1)}, u32[]{:S(2)}, u32[]{:S(2)}) collective-permute-start(bf16[256,2048]{1,0:T(8,128)(2,1)S(1)} %get-tuple-element.85), channel_id=1, source_target_pairs={{0,1},{1,0},{2,3},{3,2},{4,5},{5,4},{6,7},{7,6},{8,9},{9,8},{10,11... | collective-permute-start | bytes 3145736 | tf_op jit(solution)/shard_map/ppermute | solution.py:670
  7.5 5.7 %collective-permute-start.1 = (bf16[528,128]{1,0:T(8,128)(2,1)S(1)}, bf16[528,128]{1,0:T(8,128)(2,1)S(1)}, u32[]{:S(2)}, u32[]{:S(2)}) collective-permute-start(bf16[528,128]{1,0:T(8,128)(2,1)S(1)} %get-tuple-element.73._), channel_id=1, source_target_pairs={{0,4},{2,6},{4,0},{6,2},{8,12},{10,14},{12,8},{14,10},{16,20},{18,... | collective-permute-start | bytes 405512 | tf_op jit(solution)/shard_map/ppermute | solution.py:578
  13.3 6.0 %collective-permute-start.2 = (bf16[528,128]{1,0:T(8,128)(2,1)S(1)}, bf16[528,128]{1,0:T(8,128)(2,1)S(1)}, u32[]{:S(2)}, u32[]{:S(2)}) collective-permute-start(bf16[528,128]{1,0:T(8,128)(2,1)S(1)} %get-tuple-element.79._), channel_id=1, source_target_pairs={{0,8},{2,10},{4,12},{6,14},{8,16},{10,18},{12,20},{14,22},{16,24},... | collective-permute-start | bytes 405512 | tf_op jit(solution)/shard_map/ppermute | solution.py:584
  18.5 12.4 %copy-start = (bf16[16,256,512]{2,1,0:T(8,128)(2,1)}, bf16[16,256,512]{2,1,0:T(8,128)(2,1)S(1)}, u32[]{:S(2)}) copy-start(bf16[16,256,512]{2,1,0:T(8,128)(2,1)S(1)} %get-tuple-element.112.probs0) | copy-start | bytes 12582916
  19.4 11.4 %collective-permute-start.4 = (bf16[528,128]{1,0:T(8,128)(2,1)S(1)}, bf16[528,128]{1,0:T(8,128)(2,1)S(1)}, u32[]{:S(2)}, u32[]{:S(2)}) collective-permute-start(bf16[528,128]{1,0:T(8,128)(2,1)S(1)} %get-tuple-element.84._), channel_id=1, source_target_pairs={{0,16},{2,18},{4,20},{6,22},{8,24},{10,26},{12,28},{14,30},{1,17},... | collective-permute-start | bytes 405512 | tf_op jit(solution)/shard_map/ppermute | solution.py:584
  30.8 1.7 %copy-start.3 = (bf16[512,2048]{1,0:T(8,128)(2,1)S(1)}, bf16[512,2048]{1,0:T(8,128)(2,1)}, u32[]{:S(2)}) copy-start(bf16[512,2048]{1,0:T(8,128)(2,1)} %gate.7) | copy-start | bytes 6291460
  30.9 1.7 %copy-start.4 = (f32[2048]{0:T(1024)S(1)}, f32[2048]{0:T(1024)}, u32[]{:S(2)}) copy-start(f32[2048]{0:T(1024)} %param.12) | copy-start | bytes 24580
  31.0 5.1 %collective-permute-start.5 = (bf16[528,128]{1,0:T(8,128)(2,1)S(1)}, bf16[528,128]{1,0:T(8,128)(2,1)S(1)}, u32[]{:S(2)}, u32[]{:S(2)}) collective-permute-start(bf16[528,128]{1,0:T(8,128)(2,1)S(1)} %get-tuple-element.87._), channel_id=1, source_target_pairs={{0,4},{2,6},{4,0},{6,2},{8,12},{10,14},{12,8},{14,10},{16,20},{18,... | collective-permute-start | bytes 405512 | tf_op jit(solution)/shard_map/ppermute | solution.py:578
  36.3 2.4 %collective-permute-start.6 = (bf16[2,528,128]{2,1,0:T(8,128)(2,1)S(1)}, bf16[2,528,128]{2,1,0:T(8,128)(2,1)S(1)}, u32[]{:S(2)}, u32[]{:S(2)}) collective-permute-start(bf16[2,528,128]{2,1,0:T(8,128)(2,1)S(1)} %get-tuple-element.94), channel_id=1, source_target_pairs={{0,2},{2,0},{4,6},{6,4},{8,10},{10,8},{12,14},{14,12},{16,18},{18,... | collective-permute-start | bytes 811016 | tf_op jit(solution)/shard_map/ppermute | solution.py:578
  40.9 3.8 %collective-permute-start.7 = (f32[8,512]{1,0:T(8,128)S(1)}, f32[8,512]{1,0:T(8,128)S(1)}, u32[]{:S(2)}, u32[]{:S(2)}) collective-permute-start(f32[8,512]{1,0:T(8,128)S(1)} %get-tuple-element.98.refs_0_), channel_id=1, source_target_pairs={{0,1},{1,0},{2,3},{3,2},{4,5},{5,4},{6,7},{7,6},{8,9},{9,8},{10,11... | collective-permute-start | bytes 49160 | tf_op jit(solution)/shard_map/ppermute | solution.py:757
  46.2 2.0 %collective-permute-start.8 = (f32[2,520,128]{2,1,0:T(8,128)S(1)}, f32[2,520,128]{2,1,0:T(8,128)S(1)}, u32[]{:S(2)}, u32[]{:S(2)}) collective-permute-start(f32[2,520,128]{2,1,0:T(8,128)S(1)} %get-tuple-element.104), channel_id=1, source_target_pairs={{0,2},{2,0},{4,6},{6,4},{8,10},{10,8},{12,14},{14,12},{16,18},{18,... | collective-permute-start | bytes 1597448 | tf_op jit(solution)/shard_map/ppermute | solution.py:578
  48.3 5.7 %collective-permute-start.9 = (bf16[528,128]{1,0:T(8,128)(2,1)S(1)}, bf16[528,128]{1,0:T(8,128)(2,1)S(1)}, u32[]{:S(2)}, u32[]{:S(2)}) collective-permute-start(bf16[528,128]{1,0:T(8,128)(2,1)S(1)} %get-tuple-element.106._), channel_id=1, source_target_pairs={{0,4},{2,6},{4,0},{6,2},{8,12},{10,14},{12,8},{14,10},{16,20},{18,... | collective-permute-start | bytes 405512 | tf_op jit(solution)/shard_map/ppermute | solution.py:578
  49.8 7.1 %copy-start.1 = (bf16[16,256,512]{2,1,0:T(8,128)(2,1)S(1)}, bf16[16,256,512]{2,1,0:T(8,128)(2,1)}, u32[]{:S(2)}) copy-start(bf16[16,256,512]{2,1,0:T(8,128)(2,1)} %copy-done) | copy-start | bytes 12582916
  54.0 6.9 %collective-permute-start.10 = (bf16[528,128]{1,0:T(8,128)(2,1)S(1)}, bf16[528,128]{1,0:T(8,128)(2,1)S(1)}, u32[]{:S(2)}, u32[]{:S(2)}) collective-permute-start(bf16[528,128]{1,0:T(8,128)(2,1)S(1)} %get-tuple-element.109._), channel_id=1, source_target_pairs={{0,24},{2,26},{4,28},{6,30},{8,0},{10,2},{12,4},{14,6},{16,8},{18,... | collective-permute-start | bytes 405512 | tf_op jit(solution)/shard_map/ppermute | solution.py:584
  61.0 7.7 %collective-permute-start.11 = (bf16[528,128]{1,0:T(8,128)(2,1)S(1)}, bf16[528,128]{1,0:T(8,128)(2,1)S(1)}, u32[]{:S(2)}, u32[]{:S(2)}) collective-permute-start(bf16[528,128]{1,0:T(8,128)(2,1)S(1)} %get-tuple-element.114._), channel_id=1, source_target_pairs={{0,16},{2,18},{4,20},{6,22},{8,24},{10,26},{12,28},{14,30},{16,0},... | collective-permute-start | bytes 405512 | tf_op jit(solution)/shard_map/ppermute | solution.py:584
  61.5 8.9 %copy-start.2 = (bf16[16,256,512]{2,1,0:T(8,128)(2,1)S(1)}, bf16[16,256,512]{2,1,0:T(8,128)(2,1)}, u32[]{:S(2)}) copy-start(bf16[16,256,512]{2,1,0:T(8,128)(2,1)} %copy-done) | copy-start | bytes 12582916
  68.8 5.8 %collective-permute-start.12 = (bf16[528,128]{1,0:T(8,128)(2,1)S(1)}, bf16[528,128]{1,0:T(8,128)(2,1)S(1)}, u32[]{:S(2)}, u32[]{:S(2)}) collective-permute-start(bf16[528,128]{1,0:T(8,128)(2,1)S(1)} %get-tuple-element.118._), channel_id=1, source_target_pairs={{0,4},{2,6},{4,0},{6,2},{8,12},{10,14},{12,8},{14,10},{16,20},{18,... | collective-permute-start | bytes 405512 | tf_op jit(solution)/shard_map/ppermute | solution.py:578
  74.9 1.6 %collective-permute-start.13 = (bf16[2,528,128]{2,1,0:T(8,128)(2,1)S(1)}, bf16[2,528,128]{2,1,0:T(8,128)(2,1)S(1)}, u32[]{:S(2)}, u32[]{:S(2)}) collective-permute-start(bf16[2,528,128]{2,1,0:T(8,128)(2,1)S(1)} %get-tuple-element.124), channel_id=1, source_target_pairs={{0,2},{2,0},{4,6},{6,4},{8,10},{10,8},{12,14},{14,12},{16,18},{18,... | collective-permute-start | bytes 811016 | tf_op jit(solution)/shard_map/ppermute | solution.py:578

commit v8 on v7

--- a/solution.py
+++ b/solution.py
@@ -16,7 +16,7 @@
 EPSILON = 1e-06
 F32 = jnp.float32
 BF16 = jnp.bfloat16
-GRANT = 6 * 1024 * 1024
+GRANT = 5 * 1024 * 1024
 VMEM = pl.BlockSpec(memory_space=pltpu.VMEM)
 HBM = pl.BlockSpec(memory_space=pltpu.HBM)
 ANY = pl.BlockSpec(memory_space=pl.ANY)
@@ -395,7 +395,7 @@
     if same:
         att, sq, inn, both = refs
     else:
-        sq_before, inn_before, att, sums, sq, inn, both = refs
+        _, sq_before, inn_before, att, sums, sq, inn, both = refs
         sq[...] = sq_before[...]
         inn[...] = inn_before[...]
     for y in range(2):
@@ -505,13 +505,15 @@
         copy.wait()
 
 
-def key_value_body(heads, first, q, v, dattn, table0, table1, probs0, probs1, _, *refs):
-    hq = heads // TEAM
+def key_value_body(heads, first, last, q, v, dattn, table0, table1, probs0, probs1, _, *refs):
+    hq = heads // TEAM
+    count = min(hq, 2)
     dk, dv = refs[-2:]
 
-    def one(g, _):
-        for j in range(hq):
-            h, c = head_at(g, hq, j)
+    def one(step, _):
+        for m in range(count):
+            h = step * count + m
+            _, c = head_at(h, 1, 0)
             for i, (table, probs) in enumerate(((table0, probs0), (table1, probs1))):
                 t = slice(i * HALF, BLOCK)
                 dscores = (nt(v[half(i), c], dattn[t, c]) * table[h]).astype(BF16)
@@ -519,7 +521,7 @@
                 dv[half(i), c] = nn(probs[h], dattn[t, c])
         return 0
 
-    lax.fori_loop(first, first + TEAM // 2, one, 0)
+    lax.fori_loop(first, last, one, 0)
 
 
 def final_rows(hq, y, j, same, k, v, dk, dv, shrink, state, key_out, value_out):
@@ -580,8 +582,7 @@
 
 def across(x, k):
     n = lax.axis_size("ctx")
-    moves = [(i, i + TEAM * k) for i in range(n)]
-    return lax.ppermute(x, "ctx", [(i, j % n) for i, j in moves if k < 0 or j < n])
+    return lax.ppermute(x, "ctx", [(i, (i + TEAM * k) % n) for i in range(n)])
 
 
 def local(queries, keys, values, log_decay, gate, gain, grad_out):
@@ -742,16 +743,15 @@
         "attention",
         [wide_scratch],
         small // 2,
-        alias={1: 0},
     )
     att, sums = call(
         functools.partial(attention_body, heads, False),
-        [queries, att, dscaled, growth, got, squares, inner],
+        [queries, intra, dscaled, growth, got, att, squares, inner],
         [f32(rows, width), f32(8, rows)],
         "attention",
         [pltpu.VMEM((rows, HEAD), F32)] * 2 + [wide_scratch],
         small // 2,
-        alias={1: 0},
+        alias={5: 0},
     )
     if swaps:
         others = lax.ppermute(sums, "tp", [(0, 1), (1, 0)])
@@ -787,16 +787,26 @@
         )
         return token
 
-    def key_value_first(after):
+    units = heads // min(hq, 2)
+    cuts = [0, units // 8, units // 8 + units // 2, units]
+
+    def key_value_beside(after):
+        before = done.get("key_value", [])
+        piece = done.get("piece", 0)
+        done["piece"] = piece + 1
         done["key_value"] = call(
-            functools.partial(key_value_body, heads, 0),
-            [queries, values, dattn, *done["probs"], after],
+            functools.partial(key_value_body, heads, cuts[piece], cuts[piece + 1]),
+            [queries, values, dattn, *done["probs"], after, *before],
             [f32(rows, width)] * 2,
             "key_value",
-            flops=2 * large,
-            in_specs=[VMEM] * 7 + [ANY],
+            flops=4 * large * (cuts[piece + 1] - cuts[piece]) // units,
+            in_specs=[VMEM] * 7 + [ANY] + [VMEM] * len(before),
+            alias={8 + i: i for i in range(len(before))},
         )
         return done["key_value"][0]
+
+    def gate_and_key_value(after):
+        return key_value_beside(gate_beside(after))
 
     def query_beside(after):
         done["query"], token = call(
@@ -811,19 +821,7 @@
         )
         return token
 
-    def key_value_last(after):
-        done["key_value"] = call(
-            functools.partial(key_value_body, heads, TEAM // 2),
-            [queries, values, dattn, *done["probs"], after, *done["key_value"]],
-            [f32(rows, width)] * 2,
-            "key_value",
-            flops=2 * large,
-            in_specs=[VMEM] * 7 + [ANY, VMEM, VMEM],
-            alias={8: 0, 9: 1},
-        )
-        return done["key_value"][0]
-
-    work = {"pair": gate_beside, "one": key_value_first, "last": query_beside, "pair_back": key_value_last}
+    work = {"pair": gate_and_key_value, "one": key_value_beside, "last": query_beside, "pair_back": key_value_beside}
     back_mine, back_got = scan(True, keep, give, work)
     gate_grad, query_grad, (dk, dv) = done["gate"], done["query"], done["key_value"]
     both = bf(2, rows, hq * HEAD)

time: 80.1 us -> 76 us (0.949)
  starting transfers between devices: 23 us -> 13 us
  waiting for transfers between devices: 9.72 us -> 14.1 us
  local copies, waits for them, and re-layouts: 0.02 us -> 2.03 us
    ppermute x4, starting transfers between devices: 12.4 us -> 5.44 us  [across(): return lax.ppermute(x, 'ctx', [(i, (i + TEAM * k) % n) for i in range(n)])]
    ppermute x4, waiting for transfers between devices: 1.64 us -> 4.91 us  [across(): return lax.ppermute(x, 'ctx', [(i, (i + TEAM * k) % n) for i in range(n)])]
    ppermute x8, starting transfers between devices: 7.04 us -> 4.08 us  [swap(): return lax.ppermute(x, 'ctx', [(i, i ^ bit) for i in range(n)])]
    unnamed x10 -> x12, local copies, waits for them, and re-layouts: 0.02 us -> 2.03 us
    ppermute x8, waiting for transfers between devices: 5.28 us -> 6.37 us  [swap(): return lax.ppermute(x, 'ctx', [(i, i ^ bit) for i in range(n)])]
    pallas_call x28 -> x29, Pallas kernels: 46.1 us -> 45.5 us  [call(): pl.pallas_call(body, in_specs=in_specs or [VMEM] * len(inputs), out_specs...]
  transfers between devices with their start and end apart: 14 -> 14, of which waited for: 8 -> 8; matrix products, arithmetic and copies ran while one was open for 0% -> 0% of each run, Pallas kernels for 45% -> 47%
where the time goes in v8:
time: 76 us; the launch traced here: 75.8 us
  Pallas kernels  45.5 us (60%)
  waiting for transfers between devices  14.1 us (19%)
  starting transfers between devices  13 us (17%)
  local copies, waits for them, and re-layouts  2.03 us (3%)
  between operations  1.12 us (1%)
    pallas_call x29, Pallas kernels, call(): pl.pallas_call(body, in_specs=in_specs or [VMEM] * len(inputs), out_specs...  45.5 us
    ppermute x8, waiting for transfers between devices, swap(): return lax.ppermute(x, 'ctx', [(i, i ^ bit) for i in range(n)])  6.37 us
    ppermute x4, starting transfers between devices, across(): return lax.ppermute(x, 'ctx', [(i, (i + TEAM * k) % n) for i in range(n)])  5.44 us
    ppermute x4, waiting for transfers between devices, across(): return lax.ppermute(x, 'ctx', [(i, (i + TEAM * k) % n) for i in range(n)])  4.91 us
    ppermute x8, starting transfers between devices, swap(): return lax.ppermute(x, 'ctx', [(i, i ^ bit) for i in range(n)])  4.08 us
    ppermute x1, waiting for transfers between devices, local(): others = lax.ppermute(sums, 'tp', [(0, 1), (1, 0)])  2.84 us
    ppermute x1, starting transfers between devices, local(): arrived = lax.ppermute(outs[4], 'tp', [(0, 1), (1, 0)])  2.56 us
    unnamed x12, local copies, waits for them, and re-layouts  2.03 us
  transfers between devices with their start and end apart: 14, of which 8 were waited for; matrix products, arithmetic and copies ran while one was open for 0% of the time, Pallas kernels for 47%

profile of v8, /device:TPU:0, one launch (start us, length us, event | category | flops | bytes accessed | tf_op | source)
XLA Modules:
  0.0 75.8 jit_solution(2824549302380145214)
XLA Ops:
  0.6 2.8 %sent_states.1 = (f32[2,520,128]{2,1,0:T(8,128)S(1)}, f32[16,512]{1,0:T(8,128)S(1)}, bf16[512,2048]{1,0:T(8,128)(2,1)S(1)}, bf16[512,2048]{1,0:T(8,128)(2,1)S(1)}, bf16[256,2048]{1,0:T(8,128)(2,1)S(1)}) custom-call(bf16[512,2048]{1,0:T(8,128)(2,1)} %k_hbm.1, bf16[512,2048]{1,0:T(8,128)(2,1)} %v_hbm.1, f32[16,512]{1,0:T(8,128)} %ld_hbm.1, bf16[256,4096]{1,0:T(8,128)(2,1)} %grad.1), custom_call_target="tpu_custom_call" | custom-call | flops 134217728 | bytes 12132352 | tf_op jit(solution)/shard_map/sent_states/pallas_call | solution.py:125
  4.0 2.6 %collective-permute-start.3 = (bf16[256,2048]{1,0:T(8,128)(2,1)S(1)}, bf16[256,2048]{1,0:T(8,128)(2,1)S(1)}, u32[]{:S(2)}, u32[]{:S(2)}) collective-permute-start(bf16[256,2048]{1,0:T(8,128)(2,1)S(1)} %get-tuple-element.87), channel_id=1, source_target_pairs={{0,1},{1,0},{2,3},{3,2},{4,5},{5,4},{6,7},{7,6},{8,9},{9,8},{10,11... | collective-permute-start | bytes 3145736 | tf_op jit(solution)/shard_map/ppermute | solution.py:671
  7.5 1.6 %collective-permute-start.1 = (bf16[528,128]{1,0:T(8,128)(2,1)S(1)}, bf16[528,128]{1,0:T(8,128)(2,1)S(1)}, u32[]{:S(2)}, u32[]{:S(2)}) collective-permute-start(bf16[528,128]{1,0:T(8,128)(2,1)S(1)} %get-tuple-element.75._), channel_id=1, source_target_pairs={{0,4},{2,6},{4,0},{6,2},{8,12},{10,14},{12,8},{14,10},{16,20},{18,... | collective-permute-start | bytes 405512 | tf_op jit(solution)/shard_map/ppermute | solution.py:580
  9.1 1.6 %decays.1 = (f32[4,512,128]{2,1,0:T(8,128)S(1)}, f32[4,512,128]{2,1,0:T(8,128)S(1)}, f32[4,512,128]{2,1,0:T(8,128)S(1)}, bf16[512,2048]{1,0:T(8,128)(2,1)S(1)}) custom-call(f32[16,512]{1,0:T(8,128)S(1)} %get-tuple-element.73.row, bf16[512,2048]{1,0:T(8,128)(2,1)} %q_hbm.1, bf16[528,128]{1,0:T(8,128)(2,1)S(1)} %get-tuple-element.75._), custom_call_target="tpu_custom_call" | custom-call | bytes 7507968 | tf_op jit(solution)/shard_map/decays/pallas_call | solution.py:125
  11.7 1.6 %turned_probs.2 = (f32[16,256,512]{2,1,0:T(8,128)S(1)}, f32[16,256,256]{2,1,0:T(8,128)S(1)}, bf16[16,256,512]{2,1,0:T(8,128)(2,1)S(1)}, bf16[16,256,256]{2,1,0:T(8,128)(2,1)S(1)}) custom-call(bf16[512,2048]{1,0:T(8,128)(2,1)S(1)} %get-tuple-element.76.q, bf16[512,2048]{1,0:T(8,128)(2,1)S(1)} %get-tuple-element.71.k, f32[16,512]{1,0:T(8,128)S(1)} %get-tuple-element.73.row, ...), custom_call_target="tpu_custom_call" | custom-call | flops 536870912 | bytes 24285184 | tf_op jit(solution)/shard_map/turned_probs/pallas_call | solution.py:125
  13.4 1.8 %collective-permute-start.2 = (bf16[528,128]{1,0:T(8,128)(2,1)S(1)}, bf16[528,128]{1,0:T(8,128)(2,1)S(1)}, u32[]{:S(2)}, u32[]{:S(2)}) collective-permute-start(bf16[528,128]{1,0:T(8,128)(2,1)S(1)} %get-tuple-element.81._), channel_id=1, source_target_pairs={{0,8},{2,10},{4,12},{6,14},{8,16},{10,18},{12,20},{14,22},{16,24},... | collective-permute-start | bytes 405512 | tf_op jit(solution)/shard_map/ppermute | solution.py:585
  15.2 1.6 %turned_probs.3 = (f32[16,256,512]{2,1,0:T(8,128)S(1)}, f32[16,256,256]{2,1,0:T(8,128)S(1)}, bf16[16,256,512]{2,1,0:T(8,128)(2,1)S(1)}, bf16[16,256,256]{2,1,0:T(8,128)(2,1)S(1)}) custom-call(bf16[512,2048]{1,0:T(8,128)(2,1)S(1)} %get-tuple-element.76.q, ...), custom_call_target="tpu_custom_call", output_to_operand_aliasing={{0}: (5, {}), {1}: (6, {}), {2}: (7, {}), {3}: (8, {})} | custom-call | flops 536870912 | bytes 43159552 | tf_op jit(solution)/shard_map/turned_probs/pallas_call | solution.py:125
  16.9 4.0 %collective-permute-done.2.refs_0_ = bf16[528,128]{1,0:T(8,128)(2,1)S(1)} collective-permute-done((bf16[528,128]{1,0:T(8,128)(2,1)S(1)}, bf16[528,128]{1,0:T(8,128)(2,1)S(1)}, u32[]{:S(2)}, u32[]{:S(2)}) %collective-permute-start.2) | collective-permute-done | bytes 135200 | tf_op jit(solution)/shard_map/ppermute | solution.py:585
  21.8 5.8 %intra.1.refs_0_ = f32[512,2048]{1,0:T(8,128)S(1)} custom-call(bf16[512,2048]{1,0:T(8,128)(2,1)S(1)} %get-tuple-element.76.q, bf16[512,2048]{1,0:T(8,128)(2,1)S(1)} %get-tuple-element.71.k, bf16[512,2048]{1,0:T(8,128)(2,1)S(1)} %get-tuple-element.72.v, f32[16,512]{1,0:T(8,128)S(1)} %get-tuple-element.73.row, f32[4,512,128]{2,1,0:T(8,128)S(1)} %get-tuple-element.77.col, ...), custom_call_target="tpu_custom_call" | custom-call | flops 2147483648 | bytes 11702272 | tf_op jit(solution)/shard_map/intra/pallas_call | solution.py:125
  29.2 1.9 %own_dscaled.1 = (f32[512,2048]{1,0:T(8,128)S(1)}, bf16[2048,512]{1,0:T(8,128)(2,1)S(1)}) custom-call(bf16[512,2048]{1,0:T(8,128)(2,1)S(1)} %copy-done, bf16[256,4096]{1,0:T(8,128)(2,1)} %grad.1, f32[1,2048]{1,0:T(1,128)S(1)} %bitcast.2, bf16[512,2048]{1,0:T(8,128)(2,1)S(1)} %get-tuple-element.76.q, f32[16,512]{1,0:T(8,128)S(1)} %get-tuple-element.73.row, ...), custom_call_target="tpu_custom_call" | custom-call | flops 268435456 | bytes 12759040 | tf_op jit(solution)/shard_map/own_dscaled/pallas_call | solution.py:125
  31.2 2.5 %collective-permute-done.5.other = bf16[528,128]{1,0:T(8,128)(2,1)S(1)} collective-permute-done((bf16[528,128]{1,0:T(8,128)(2,1)S(1)}, bf16[528,128]{1,0:T(8,128)(2,1)S(1)}, u32[]{:S(2)}, u32[]{:S(2)}) %collective-permute-start.5) | collective-permute-done | bytes 135200 | tf_op jit(solution)/shard_map/ppermute | solution.py:580
  34.6 1.2 %attention.2 = (f32[512,2048]{1,0:T(8,128)S(1)}, f32[512,128]{1,0:T(8,128)S(1)}, f32[512,128]{1,0:T(8,128)S(1)}) custom-call(bf16[512,2048]{1,0:T(8,128)(2,1)S(1)} %get-tuple-element.76.q, f32[512,2048]{1,0:T(8,128)S(1)} %intra.1.refs_0_, f32[512,2048]{1,0:T(8,128)S(1)} %got_dscaled.1.dscaled, f32[4,512,128]{2,1,0:T(8,128)S(1)} %get-tuple-element.91.growth, ...), custom_call_target="tpu_custom_call" | custom-call | flops 134217728 | bytes 16523264 | tf_op jit(solution)/shard_map/attention/pallas_call | solution.py:125
  35.8 1.7 %attention.3 = (f32[512,2048]{1,0:T(8,128)S(1)}, f32[8,512]{1,0:T(8,128)S(1)}) custom-call(bf16[512,2048]{1,0:T(8,128)(2,1)S(1)} %get-tuple-element.76.q, f32[512,2048]{1,0:T(8,128)S(1)} %intra.1.refs_0_, f32[512,2048]{1,0:T(8,128)S(1)} %got_dscaled.1.dscaled, f32[4,512,128]{2,1,0:T(8,128)S(1)} %get-tuple-element.91.growth, ...), custom_call_target="tpu_custom_call", output_to_operand_aliasing={{0}: (5, {})} | custom-call | flops 134217728 | bytes 20733952 | tf_op jit(solution)/shard_map/attention/pallas_call | solution.py:125
  38.4 2.8 %collective-permute-done.7.refs_1_ = f32[8,512]{1,0:T(8,128)S(1)} collective-permute-done((f32[8,512]{1,0:T(8,128)S(1)}, f32[8,512]{1,0:T(8,128)S(1)}, u32[]{:S(2)}, u32[]{:S(2)}) %collective-permute-start.7) | collective-permute-done | bytes 16416 | tf_op jit(solution)/shard_map/ppermute | solution.py:757
  41.3 1.5 %sent_dattn.1 = (bf16[512,2048]{1,0:T(8,128)(2,1)S(1)}, f32[2,520,128]{2,1,0:T(8,128)S(1)}, f32[512,128]{1,0:T(8,128)S(1)}, f32[512,128]{1,0:T(8,128)S(1)}) custom-call(f32[512,2048]{1,0:T(8,128)S(1)} %get-tuple-element.99.att, f32[512,2048]{1,0:T(8,128)S(1)} %got_dscaled.1.dscaled, bf16[2048,512]{1,0:T(8,128)(2,1)S(1)} %get-tuple-element.93.refs_0_.turned, ...), custom_call_target="tpu_custom_call" | custom-call | flops 134217728 | bytes 13713408 | tf_op jit(solution)/shard_map/sent_dattn/pallas_call | solution.py:125
  45.5 2.2 %gate.6 = (bf16[512,2048]{1,0:T(8,128)(2,1)}, f32[8,128]{1,0:T(8,128)S(1)}) custom-call(bf16[512,2048]{1,0:T(8,128)(2,1)S(1)} %copy-done, f32[512,2048]{1,0:T(8,128)S(1)} %get-tuple-element.99.att, f32[512,2048]{1,0:T(8,128)S(1)} %got_dscaled.1.dscaled, f32[512,128]{1,0:T(8,128)S(1)} %get-tuple-element.101.refs_0_.scale, ...), custom_call_target="tpu_custom_call" | custom-call | flops 268435456 | bytes 12984320 | tf_op jit(solution)/shard_map/gate/pallas_call | solution.py:125
  48.8 1.7 %collective-permute-done.9.got.got_pair = bf16[528,128]{1,0:T(8,128)(2,1)S(1)} collective-permute-done((bf16[528,128]{1,0:T(8,128)(2,1)S(1)}, bf16[528,128]{1,0:T(8,128)(2,1)S(1)}, u32[]{:S(2)}, u32[]{:S(2)}) %collective-permute-start.9) | collective-permute-done | bytes 135200 | tf_op jit(solution)/shard_map/ppermute | solution.py:580
  50.6 2.8 %collective-permute-start.10 = (bf16[528,128]{1,0:T(8,128)(2,1)S(1)}, bf16[528,128]{1,0:T(8,128)(2,1)S(1)}, u32[]{:S(2)}, u32[]{:S(2)}) collective-permute-start(bf16[528,128]{1,0:T(8,128)(2,1)S(1)} %get-tuple-element.115._), channel_id=1, source_target_pairs={{0,24},{2,26},{4,28},{6,30},{8,0},{10,2},{12,4},{14,6},{16,8},{18,... | collective-permute-start | bytes 405512 | tf_op jit(solution)/shard_map/ppermute | solution.py:585
  53.4 4.3 %key_value.4 = (f32[512,2048]{1,0:T(8,128)S(1)}, f32[512,2048]{1,0:T(8,128)S(1)}) custom-call(bf16[512,2048]{1,0:T(8,128)(2,1)S(1)} %get-tuple-element.76.q, bf16[512,2048]{1,0:T(8,128)(2,1)S(1)} %get-tuple-element.72.v, bf16[512,2048]{1,0:T(8,128)(2,1)S(1)} %get-tuple-element.104.dattn, ...), custom_call_target="tpu_custom_call", output_to_operand_aliasing={{0}: (8, {}), {1}: (9, {})} | custom-call | flops 2147483648 | bytes 42078208 | tf_op jit(solution)/shard_map/key_value/pallas_call | solution.py:125
  59.0 6.3 %query.1 = (bf16[512,2048]{1,0:T(8,128)(2,1)}, f32[8,128]{1,0:T(8,128)S(1)}) custom-call(bf16[512,2048]{1,0:T(8,128)(2,1)S(1)} %get-tuple-element.71.k, bf16[512,2048]{1,0:T(8,128)(2,1)S(1)} %get-tuple-element.72.v, bf16[512,2048]{1,0:T(8,128)(2,1)S(1)} %get-tuple-element.104.dattn, f32[16,512]{1,0:T(8,128)S(1)} %get-tuple-element.73.row, ...), custom_call_target="tpu_custom_call" | custom-call | flops 2415919104 | bytes 11198464 | tf_op jit(solution)/shard_map/query/pallas_call | solution.py:125
  66.0 3.3 %key_value.5 = (f32[512,2048]{1,0:T(8,128)S(1)}, f32[512,2048]{1,0:T(8,128)S(1)}) custom-call(bf16[512,2048]{1,0:T(8,128)(2,1)S(1)} %get-tuple-element.76.q, bf16[512,2048]{1,0:T(8,128)(2,1)S(1)} %get-tuple-element.72.v, bf16[512,2048]{1,0:T(8,128)(2,1)S(1)} %get-tuple-element.104.dattn, ...), custom_call_target="tpu_custom_call", output_to_operand_aliasing={{0}: (8, {}), {1}: (9, {})} | custom-call | flops 1610612736 | bytes 42078208 | tf_op jit(solution)/shard_map/key_value/pallas_call | solution.py:125
  69.3 1.2 %collective-permute-done.12.other = bf16[528,128]{1,0:T(8,128)(2,1)S(1)} collective-permute-done((bf16[528,128]{1,0:T(8,128)(2,1)S(1)}, bf16[528,128]{1,0:T(8,128)(2,1)S(1)}, u32[]{:S(2)}, u32[]{:S(2)}) %collective-permute-start.12) | collective-permute-done | bytes 135200 | tf_op jit(solution)/shard_map/ppermute | solution.py:580
  70.8 1.4 %own_final.1 = (bf16[2,512,512]{2,1,0:T(8,128)(2,1)S(1)}, bf16[2,512,512]{2,1,0:T(8,128)(2,1)S(1)}, f32[1,2048]{1,0:T(1,128)S(1)}) custom-call(bf16[512,2048]{1,0:T(8,128)(2,1)S(1)} %get-tuple-element.71.k, bf16[512,2048]{1,0:T(8,128)(2,1)S(1)} %get-tuple-element.72.v, f32[512,2048]{1,0:T(8,128)S(1)} %get-tuple-element.124.refs_0_.dk, ...), custom_call_target="tpu_custom_call" | custom-call | flops 268435456 | bytes 16007168 | tf_op jit(solution)/shard_map/own_final/pallas_call | solution.py:125
  72.3 3.3 %final.1 = (bf16[512,2048]{1,0:T(8,128)(2,1)}, bf16[512,2048]{1,0:T(8,128)(2,1)}, f32[1,2048]{1,0:T(1,128)}) custom-call(bf16[512,2048]{1,0:T(8,128)(2,1)S(1)} %get-tuple-element.71.k, bf16[512,2048]{1,0:T(8,128)(2,1)S(1)} %get-tuple-element.72.v, f32[512,2048]{1,0:T(8,128)S(1)} %get-tuple-element.124.refs_0_.dk, f32[512,2048]{1,0:T(8,128)S(1)} %get-tuple-element.125.dv, ...), custom_call_target="tpu_custom_call" | custom-call | flops 268435456 | bytes 20209664 | tf_op jit(solution)/shard_map/final/pallas_call | solution.py:125
  (45 shorter events, 13.0 us)
Async XLA Ops:
  3.5 3.9 %collective-permute-start = (f32[2,520,128]{2,1,0:T(8,128)S(1)}, f32[2,520,128]{2,1,0:T(8,128)S(1)}, u32[]{:S(2)}, u32[]{:S(2)}) collective-permute-start(f32[2,520,128]{2,1,0:T(8,128)S(1)} %get-tuple-element.74), channel_id=1, source_target_pairs={{0,2},{2,0},{4,6},{6,4},{8,10},{10,8},{12,14},{14,12},{16,18},{18,... | collective-permute-start | bytes 1597448 | tf_op jit(solution)/shard_map/ppermute | solution.py:580
  4.0 30.0 %collective-permute-start.3 = (bf16[256,2048]{1,0:T(8,128)(2,1)S(1)}, bf16[256,2048]{1,0:T(8,128)(2,1)S(1)}, u32[]{:S(2)}, u32[]{:S(2)}) collective-permute-start(bf16[256,2048]{1,0:T(8,128)(2,1)S(1)} %get-tuple-element.87), channel_id=1, source_target_pairs={{0,1},{1,0},{2,3},{3,2},{4,5},{5,4},{6,7},{7,6},{8,9},{9,8},{10,11... | collective-permute-start | bytes 3145736 | tf_op jit(solution)/shard_map/ppermute | solution.py:671
  7.5 5.8 %collective-permute-start.1 = (bf16[528,128]{1,0:T(8,128)(2,1)S(1)}, bf16[528,128]{1,0:T(8,128)(2,1)S(1)}, u32[]{:S(2)}, u32[]{:S(2)}) collective-permute-start(bf16[528,128]{1,0:T(8,128)(2,1)S(1)} %get-tuple-element.75._), channel_id=1, source_target_pairs={{0,4},{2,6},{4,0},{6,2},{8,12},{10,14},{12,8},{14,10},{16,20},{18,... | collective-permute-start | bytes 405512 | tf_op jit(solution)/shard_map/ppermute | solution.py:580
  10.7 1.0 %copy-start.3 = (f32[4,512,128]{2,1,0:T(8,128)}, f32[4,512,128]{2,1,0:T(8,128)S(1)}, u32[]{:S(2)}) copy-start(f32[4,512,128]{2,1,0:T(8,128)S(1)} %get-tuple-element.126.shrink) | copy-start | bytes 3145732
  11.7 24.1 %copy-start.1 = (f32[4,512,128]{2,1,0:T(8,128)}, f32[4,512,128]{2,1,0:T(8,128)S(1)}, u32[]{:S(2)}) copy-start(f32[4,512,128]{2,1,0:T(8,128)S(1)} %get-tuple-element.91.growth) | copy-start | bytes 3145732
  13.4 7.5 %collective-permute-start.2 = (bf16[528,128]{1,0:T(8,128)(2,1)S(1)}, bf16[528,128]{1,0:T(8,128)(2,1)S(1)}, u32[]{:S(2)}, u32[]{:S(2)}) collective-permute-start(bf16[528,128]{1,0:T(8,128)(2,1)S(1)} %get-tuple-element.81._), channel_id=1, source_target_pairs={{0,8},{2,10},{4,12},{6,14},{8,16},{10,18},{12,20},{14,22},{16,24},... | collective-permute-start | bytes 405512 | tf_op jit(solution)/shard_map/ppermute | solution.py:585
  21.0 7.5 %collective-permute-start.4 = (bf16[528,128]{1,0:T(8,128)(2,1)S(1)}, bf16[528,128]{1,0:T(8,128)(2,1)S(1)}, u32[]{:S(2)}, u32[]{:S(2)}) collective-permute-start(bf16[528,128]{1,0:T(8,128)(2,1)S(1)} %get-tuple-element.86._), channel_id=1, source_target_pairs={{0,16},{2,18},{4,20},{6,22},{8,24},{10,26},{12,28},{14,30},{16,0},... | collective-permute-start | bytes 405512 | tf_op jit(solution)/shard_map/ppermute | solution.py:585
  27.6 1.6 %copy-start = (bf16[512,2048]{1,0:T(8,128)(2,1)S(1)}, bf16[512,2048]{1,0:T(8,128)(2,1)}, u32[]{:S(2)}) copy-start(bf16[512,2048]{1,0:T(8,128)(2,1)} %gate.7) | copy-start | bytes 6291460
  27.6 1.6 %copy-start.5 = (f32[2048]{0:T(1024)S(1)}, f32[2048]{0:T(1024)}, u32[]{:S(2)}) copy-start(f32[2048]{0:T(1024)} %param.12) | copy-start | bytes 24580
  28.6 5.1 %collective-permute-start.5 = (bf16[528,128]{1,0:T(8,128)(2,1)S(1)}, bf16[528,128]{1,0:T(8,128)(2,1)S(1)}, u32[]{:S(2)}, u32[]{:S(2)}) collective-permute-start(bf16[528,128]{1,0:T(8,128)(2,1)S(1)} %get-tuple-element.89._), channel_id=1, source_target_pairs={{0,4},{2,6},{4,0},{6,2},{8,12},{10,14},{12,8},{14,10},{16,20},{18,... | collective-permute-start | bytes 405512 | tf_op jit(solution)/shard_map/ppermute | solution.py:580
  33.9 1.9 %collective-permute-start.6 = (bf16[2,528,128]{2,1,0:T(8,128)(2,1)S(1)}, bf16[2,528,128]{2,1,0:T(8,128)(2,1)S(1)}, u32[]{:S(2)}, u32[]{:S(2)}) collective-permute-start(bf16[2,528,128]{2,1,0:T(8,128)(2,1)S(1)} %get-tuple-element.94), channel_id=1, source_target_pairs={{0,2},{2,0},{4,6},{6,4},{8,10},{10,8},{12,14},{14,12},{16,18},{18,... | collective-permute-start | bytes 811016 | tf_op jit(solution)/shard_map/ppermute | solution.py:580
  37.5 3.8 %collective-permute-start.7 = (f32[8,512]{1,0:T(8,128)S(1)}, f32[8,512]{1,0:T(8,128)S(1)}, u32[]{:S(2)}, u32[]{:S(2)}) collective-permute-start(f32[8,512]{1,0:T(8,128)S(1)} %get-tuple-element.100.refs_0_), channel_id=1, source_target_pairs={{0,1},{1,0},{2,3},{3,2},{4,5},{5,4},{6,7},{7,6},{8,9},{9,8},{10,11... | collective-permute-start | bytes 49160 | tf_op jit(solution)/shard_map/ppermute | solution.py:757
  42.8 2.0 %collective-permute-start.8 = (f32[2,520,128]{2,1,0:T(8,128)S(1)}, f32[2,520,128]{2,1,0:T(8,128)S(1)}, u32[]{:S(2)}, u32[]{:S(2)}) collective-permute-start(f32[2,520,128]{2,1,0:T(8,128)S(1)} %get-tuple-element.106), channel_id=1, source_target_pairs={{0,2},{2,0},{4,6},{6,4},{8,10},{10,8},{12,14},{14,12},{16,18},{18,... | collective-permute-start | bytes 1597448 | tf_op jit(solution)/shard_map/ppermute | solution.py:580
  44.9 5.7 %collective-permute-start.9 = (bf16[528,128]{1,0:T(8,128)(2,1)S(1)}, bf16[528,128]{1,0:T(8,128)(2,1)S(1)}, u32[]{:S(2)}, u32[]{:S(2)}) collective-permute-start(bf16[528,128]{1,0:T(8,128)(2,1)S(1)} %get-tuple-element.108._), channel_id=1, source_target_pairs={{0,4},{2,6},{4,0},{6,2},{8,12},{10,14},{12,8},{14,10},{16,20},{18,... | collective-permute-start | bytes 405512 | tf_op jit(solution)/shard_map/ppermute | solution.py:580
  50.6 7.1 %collective-permute-start.10 = (bf16[528,128]{1,0:T(8,128)(2,1)S(1)}, bf16[528,128]{1,0:T(8,128)(2,1)S(1)}, u32[]{:S(2)}, u32[]{:S(2)}) collective-permute-start(bf16[528,128]{1,0:T(8,128)(2,1)S(1)} %get-tuple-element.115._), channel_id=1, source_target_pairs={{0,24},{2,26},{4,28},{6,30},{8,0},{10,2},{12,4},{14,6},{16,8},{18,... | collective-permute-start | bytes 405512 | tf_op jit(solution)/shard_map/ppermute | solution.py:585
  57.8 1.2 %copy-start.2 = (f32[4,512,128]{2,1,0:T(8,128)S(1)}, f32[4,512,128]{2,1,0:T(8,128)}, u32[]{:S(2)}) copy-start(f32[4,512,128]{2,1,0:T(8,128)} %copy-done.1) | copy-start | bytes 3145732
  57.9 7.4 %collective-permute-start.11 = (bf16[528,128]{1,0:T(8,128)(2,1)S(1)}, bf16[528,128]{1,0:T(8,128)(2,1)S(1)}, u32[]{:S(2)}, u32[]{:S(2)}) collective-permute-start(bf16[528,128]{1,0:T(8,128)(2,1)S(1)} %get-tuple-element.118._), channel_id=1, source_target_pairs={{0,16},{2,18},{4,20},{6,22},{8,24},{10,26},{12,28},{14,30},{16,0},... | collective-permute-start | bytes 405512 | tf_op jit(solution)/shard_map/ppermute | solution.py:585
  65.4 5.1 %collective-permute-start.12 = (bf16[528,128]{1,0:T(8,128)(2,1)S(1)}, bf16[528,128]{1,0:T(8,128)(2,1)S(1)}, u32[]{:S(2)}, u32[]{:S(2)}) collective-permute-start(bf16[528,128]{1,0:T(8,128)(2,1)S(1)} %get-tuple-element.122._), channel_id=1, source_target_pairs={{0,4},{2,6},{4,0},{6,2},{8,12},{10,14},{12,8},{14,10},{16,20},{18,... | collective-permute-start | bytes 405512 | tf_op jit(solution)/shard_map/ppermute | solution.py:580
  69.3 1.5 %copy-start.4 = (f32[4,512,128]{2,1,0:T(8,128)S(1)}, f32[4,512,128]{2,1,0:T(8,128)}, u32[]{:S(2)}) copy-start(f32[4,512,128]{2,1,0:T(8,128)} %copy-done.3) | copy-start | bytes 3145732
  70.7 1.6 %collective-permute-start.13 = (bf16[2,528,128]{2,1,0:T(8,128)(2,1)S(1)}, bf16[2,528,128]{2,1,0:T(8,128)(2,1)S(1)}, u32[]{:S(2)}, u32[]{:S(2)}) collective-permute-start(bf16[2,528,128]{2,1,0:T(8,128)(2,1)S(1)} %get-tuple-element.128), channel_id=1, source_target_pairs={{0,2},{2,0},{4,6},{6,4},{8,10},{10,8},{12,14},{14,12},{16,18},{18,... | collective-permute-start | bytes 811016 | tf_op jit(solution)/shard_map/ppermute | solution.py:580

commit v9 on v8

--- a/solution.py
+++ b/solution.py
@@ -161,39 +161,38 @@
     write_narrow(send, hq, items)
 
 
-def doubled(reverse, hq, step, groups, before, got):
-    there = group() + step < groups if reverse else group() - step >= 0
+def met(reverse, step, before, other):
+    near = lax.rem(group() // step, 2) == (0 if reverse else 1)
     out = []
-    for old, (term, edge, gain) in zip(before, read_narrow(got, hq)):
-        term = jnp.where(there, term, 0.0)
-        edge = jnp.where(there, edge, 0.0)
+    for old, (term, edge, gain) in zip(before, other):
+        term = jnp.where(near, term, 0.0)
+        edge = jnp.where(near, edge, 0.0)
         if old is None:
             out.append((term, edge, gain))
         else:
-            out.append((old[0] + jnp.exp(old[1]) * term, old[1] + edge, old[2] + gain))
+            out.append((old[0] + jnp.exp(old[1]) * term, old[1] + edge, gain))
     return out
 
 
-def doubling_body(reverse, hq, step, groups, total, *refs):
-    so_far, send = refs[-2:]
+def window_body(reverse, hq, step, total, *refs):
+    so_far, whole, send = refs[-3:]
     if step == 1:
         got = refs[0]
         before = [None] * hq
     else:
         got = refs[1]
         before = read_wide(refs[0], hq)
-    items = doubled(reverse, hq, step, groups, before, got)
-    write_wide(so_far, hq, items)
-    whole = []
-    for (t, e, g), (s, es, gs) in zip(read_wide(total, hq), items):
-        whole.append((t + jnp.exp(e) * s, e + es, g + gs))
-    write_narrow(send, hq, whole)
-
-
-def into_chips_body(reverse, hq, step, groups, own, got_pair, total, so_far, got, *refs):
+    other = read_narrow(got, hq)
+    write_wide(so_far, hq, met(reverse, step, before, other))
+    items = joined(read_wide(total, hq), other, lax.rem(group() // step, 2) == 0, reverse)
+    write_wide(whole, hq, items)
+    write_narrow(send, hq, items)
+
+
+def into_chips_body(reverse, hq, step, own, got_pair, total, so_far, got, *refs):
     keep, send = refs[-2:]
     before = read_wide(so_far, hq) if step > 1 else [None] * hq
-    entering = doubled(reverse, hq, step, groups, before, got)
+    entering = met(reverse, step, before, read_narrow(got, hq))
     mine_near = pair() == (1 if reverse else 0)
     kept, sent = [], []
     for (r, _, gr), (c, ec, _), (o, eo, _), (_, _, gt) in zip(
@@ -286,7 +285,7 @@
         block_states(heads // TEAM, y, True, k, v, row, keep)
 
 
-def decays_body(heads, row, q_hbm, _, col, growth, shrink, q, sem):
+def decays_body(heads, row, q_hbm, _, col, growth, q, sem):
     hq = heads // TEAM
     copy = pltpu.make_async_copy(q_hbm, q, sem)
     copy.start()
@@ -295,7 +294,6 @@
         across = jnp.concatenate([rows, jnp.zeros((HEAD - hq, BLOCK), F32)], axis=0).T
         col[g] = across
         growth[g] = jnp.exp(across)
-        shrink[g] = jnp.exp(across[BLOCK - 1 : BLOCK, :] - across)
     copy.wait()
 
 
@@ -524,25 +522,31 @@
     lax.fori_loop(first, last, one, 0)
 
 
+def fades(col, y, same):
+    sums = col[quarter_of(y, same)]
+    return jnp.exp(sums[BLOCK - 1 : BLOCK, :] - sums)
+
+
 def final_rows(hq, y, j, same, k, v, dk, dv, shrink, state, key_out, value_out):
     g = quarter_of(y, same)
     _, c = head_at(g, hq, j)
-    fade = shrink[g, :, j : j + 1]
+    fade = shrink[:, j : j + 1]
     after = state[y, chunk(j), :]
     key_out[y, :, chunk(j)] = (dk[:, c] + nt(v[:, c], after) * fade).astype(BF16)
     value_out[y, :, chunk(j)] = (dv[:, c] + nn(k[:, c], after) * fade).astype(BF16)
 
 
-def own_final_body(heads, k, v, dk, dv, shrink, state, key_out, value_out, gain_grad):
+def own_final_body(heads, k, v, dk, dv, col, state, key_out, value_out, gain_grad):
     hq = heads // TEAM
     for y in range(2):
         items = read_narrow(state.at[y], hq)
+        shrink = fades(col, y, True)
         for j in range(hq):
             final_rows(hq, y, j, True, k, v, dk, dv, shrink, state, key_out, value_out)
             gain_grad[:, head_at(quarter_of(y, True), hq, j)[1]] = items[j][2]
 
 
-def final_body(heads, k, v, dk, dv, shrink, state, own_key, own_value, own_gain, *refs):
+def final_body(heads, k, v, dk, dv, col, state, own_key, own_value, own_gain, *refs):
     hq = heads // TEAM
     key_grad, value_grad, gain_grad, key_out, value_out, sems = refs
     copies = []
@@ -560,6 +564,7 @@
     gain_grad[...] = own_gain[...]
     for y in range(2):
         items = read_narrow(state.at[y], hq)
+        shrink = fades(col, y, False)
         for j, _, count, c in several(quarter_of(y, False), hq):
             for m in range(j, j + count):
                 final_rows(hq, y, m, False, k, v, dk, dv, shrink, state, key_out, value_out)
@@ -578,11 +583,6 @@
 def swap(x, bit):
     n = lax.axis_size("ctx")
     return lax.ppermute(x, "ctx", [(i, i ^ bit) for i in range(n)])
-
-
-def across(x, k):
-    n = lax.axis_size("ctx")
-    return lax.ppermute(x, "ctx", [(i, (i + TEAM * k) % n) for i in range(n)])
 
 
 def local(queries, keys, values, log_decay, gate, gain, grad_out):
@@ -626,24 +626,17 @@
         total, send = step_call(group_total_body, reverse, [own, got_pair], unread, [wide, narrow], "group_total")
         so_far, step = total, 1
         while 2 * step < groups:
-            far = across(send, -step if reverse else step)
+            far = swap(send, TEAM * step)
             unread = beside(work, send, "one") if step == 1 else []
             before = [] if step == 1 else [so_far]
-            so_far, send = step_call(
-                doubling_body, reverse, [total, *before, far], unread, [wide, narrow], "doubling", step, groups
+            so_far, total, send = step_call(
+                window_body, reverse, [total, *before, far], unread, [wide, wide, narrow], "window", step
             )
             step *= 2
-        far = across(send, -step if reverse else step)
+        far = swap(send, TEAM * step)
         unread = beside(work, send, "last")
         kept, send = step_call(
-            into_chips_body,
-            reverse,
-            [own, got_pair, total, so_far, far],
-            unread,
-            [wide, narrow],
-            "into_chips",
-            step,
-            groups,
+            into_chips_body, reverse, [own, got_pair, total, so_far, far], unread, [wide, narrow], "into_chips", step
         )
         other = swap(send, 2)
         unread = beside(work, send, "pair_back")
@@ -683,7 +676,7 @@
             *done["decays"], done["queries"] = call(
                 functools.partial(decays_body, heads),
                 [row, in_hbm(queries), after],
-                [table] * 3 + [bf(rows, width)],
+                [table] * 2 + [bf(rows, width)],
                 "decays",
                 [pltpu.SemaphoreType.DMA(())],
                 in_specs=[VMEM, HBM, ANY],
@@ -726,7 +719,7 @@
     work = {"pair": probs_beside, "one": probs_beside, "last": intra_beside, "pair_back": dscaled_beside}
     mine, got = scan(False, keep, give, work)
     queries = done["queries"]
-    (col, growth, shrink), intra, (dscaled, turned) = done["decays"], done["intra"], done["dscaled"]
+    (col, growth), intra, (dscaled, turned) = done["decays"], done["intra"], done["dscaled"]
     (dscaled,) = call(
         functools.partial(got_dscaled_body, heads, swaps),
         [gate, arrived, gain_row, dscaled],
@@ -788,7 +781,7 @@
         return token
 
     units = heads // min(hq, 2)
-    cuts = [0, units // 8, units // 8 + units // 2, units]
+    cuts = [0, units // 4, (5 * units) // 8, units]
 
     def key_value_beside(after):
         before = done.get("key_value", [])
@@ -827,14 +820,14 @@
     both = bf(2, rows, hq * HEAD)
     own_key, own_value, own_gain = call(
         functools.partial(own_final_body, heads),
-        [keys, values, dk, dv, shrink, back_mine],
+        [keys, values, dk, dv, col, back_mine],
         [both, both, f32(1, width)],
         "own_final",
         flops=small,
     )
     key_grad, value_grad, gain_grad = call(
         functools.partial(final_body, heads),
-        [keys, values, dk, dv, shrink, back_got, own_key, own_value, own_gain],
+        [keys, values, dk, dv, col, back_got, own_key, own_value, own_gain],
         [bf(rows, width), bf(rows, width), f32(1, width)],
         "final",
         [pltpu.VMEM(both.shape, BF16)] * 2 + [pltpu.SemaphoreType.DMA((8 * hq,))],

time: 76 us -> 74.2 us (0.976)
  waiting for transfers between devices: 14.1 us -> 9.81 us
  starting transfers between devices: 13 us -> 17.2 us
  local copies, waits for them, and re-layouts: 2.03 us -> 0.01 us
    ppermute x8 -> x12, starting transfers between devices: 4.08 us -> 13.7 us  [swap(): return lax.ppermute(x, 'ctx', [(i, i ^ bit) for i in range(n)])]
    ppermute x4 -> x0, starting transfers between devices: 5.44 us -> none  [across(): return lax.ppermute(x, 'ctx', [(i, (i + TEAM * k) % n) for i in range(n)])]
    ppermute x4 -> x0, waiting for transfers between devices: 4.91 us -> none  [across(): return lax.ppermute(x, 'ctx', [(i, (i + TEAM * k) % n) for i in range(n)])]
    unnamed x12 -> x4, local copies, waits for them, and re-layouts: 2.03 us -> 0.01 us
    ppermute x8 -> x12, waiting for transfers between devices: 6.37 us -> 7 us  [swap(): return lax.ppermute(x, 'ctx', [(i, i ^ bit) for i in range(n)])]
  transfers between devices with their start and end apart: 14 -> 14, of which waited for: 8 -> 9; matrix products, arithmetic and copies ran while one was open for 0% -> 0% of each run, Pallas kernels for 47% -> 49%
where the time goes in v9:
time: 74.2 us; the launch traced here: 74.1 us
  Pallas kernels  46 us (62%)
  starting transfers between devices  17.2 us (23%)
  waiting for transfers between devices  9.81 us (13%)
  between operations  1.06 us (1%)
    pallas_call x29, Pallas kernels, call(): pl.pallas_call(body, in_specs=in_specs or [VMEM] * len(inputs), out_specs...  46 us
    ppermute x12, starting transfers between devices, swap(): return lax.ppermute(x, 'ctx', [(i, i ^ bit) for i in range(n)])  13.7 us
    ppermute x12, waiting for transfers between devices, swap(): return lax.ppermute(x, 'ctx', [(i, i ^ bit) for i in range(n)])  7 us
    ppermute x1, waiting for transfers between devices, local(): others = lax.ppermute(sums, 'tp', [(0, 1), (1, 0)])  2.81 us
    ppermute x1, starting transfers between devices, local(): arrived = lax.ppermute(outs[4], 'tp', [(0, 1), (1, 0)])  2.56 us
  transfers between devices with their start and end apart: 14, of which 9 were waited for; matrix products, arithmetic and copies ran while one was open for 0% of the time, Pallas kernels for 49%

profile of v9, /device:TPU:0, one launch (start us, length us, event | category | flops | bytes accessed | tf_op | source)
XLA Modules:
  0.0 74.1 jit_solution(11054130729712657532)
XLA Ops:
  0.6 2.8 %sent_states.1 = (f32[2,520,128]{2,1,0:T(8,128)S(1)}, f32[16,512]{1,0:T(8,128)S(1)}, bf16[512,2048]{1,0:T(8,128)(2,1)S(1)}, bf16[512,2048]{1,0:T(8,128)(2,1)S(1)}, bf16[256,2048]{1,0:T(8,128)(2,1)S(1)}) custom-call(bf16[512,2048]{1,0:T(8,128)(2,1)} %k_hbm.1, bf16[512,2048]{1,0:T(8,128)(2,1)} %v_hbm.1, f32[16,512]{1,0:T(8,128)} %ld_hbm.1, bf16[256,4096]{1,0:T(8,128)(2,1)} %grad.1), custom_call_target="tpu_custom_call" | custom-call | flops 134217728 | bytes 12132352 | tf_op jit(solution)/shard_map/sent_states/pallas_call | solution.py:125
  4.0 2.6 %collective-permute-start.3 = (bf16[256,2048]{1,0:T(8,128)(2,1)S(1)}, bf16[256,2048]{1,0:T(8,128)(2,1)S(1)}, u32[]{:S(2)}, u32[]{:S(2)}) collective-permute-start(bf16[256,2048]{1,0:T(8,128)(2,1)S(1)} %get-tuple-element.88), channel_id=1, source_target_pairs={{0,1},{1,0},{2,3},{3,2},{4,5},{5,4},{6,7},{7,6},{8,9},{9,8},{10,11... | collective-permute-start | bytes 3145736 | tf_op jit(solution)/shard_map/ppermute | solution.py:664
  7.5 1.6 %collective-permute-start.1 = (bf16[528,128]{1,0:T(8,128)(2,1)S(1)}, bf16[528,128]{1,0:T(8,128)(2,1)S(1)}, u32[]{:S(2)}, u32[]{:S(2)}) collective-permute-start(bf16[528,128]{1,0:T(8,128)(2,1)S(1)} %get-tuple-element.76._), channel_id=1, source_target_pairs={{0,4},{2,6},{4,0},{6,2},{8,12},{10,14},{12,8},{14,10},{16,20},{18,... | collective-permute-start | bytes 405512 | tf_op jit(solution)/shard_map/ppermute | solution.py:585
  9.1 1.6 %decays.1 = (f32[4,512,128]{2,1,0:T(8,128)S(1)}, f32[4,512,128]{2,1,0:T(8,128)S(1)}, bf16[512,2048]{1,0:T(8,128)(2,1)S(1)}) custom-call(f32[16,512]{1,0:T(8,128)S(1)} %get-tuple-element.74.row, bf16[512,2048]{1,0:T(8,128)(2,1)} %q_hbm.1, bf16[528,128]{1,0:T(8,128)(2,1)S(1)} %get-tuple-element.76._), custom_call_target="tpu_custom_call" | custom-call | bytes 6459392 | tf_op jit(solution)/shard_map/decays/pallas_call | solution.py:125
  10.7 1.8 %turned_probs.2 = (f32[16,256,512]{2,1,0:T(8,128)S(1)}, f32[16,256,256]{2,1,0:T(8,128)S(1)}, bf16[16,256,512]{2,1,0:T(8,128)(2,1)S(1)}, bf16[16,256,256]{2,1,0:T(8,128)(2,1)S(1)}) custom-call(bf16[512,2048]{1,0:T(8,128)(2,1)S(1)} %get-tuple-element.77.q, bf16[512,2048]{1,0:T(8,128)(2,1)S(1)} %get-tuple-element.72.k, f32[16,512]{1,0:T(8,128)S(1)} %get-tuple-element.74.row, ...), custom_call_target="tpu_custom_call" | custom-call | flops 536870912 | bytes 24285184 | tf_op jit(solution)/shard_map/turned_probs/pallas_call | solution.py:125
  13.3 1.6 %collective-permute-start.2 = (bf16[528,128]{1,0:T(8,128)(2,1)S(1)}, bf16[528,128]{1,0:T(8,128)(2,1)S(1)}, u32[]{:S(2)}, u32[]{:S(2)}) collective-permute-start(bf16[528,128]{1,0:T(8,128)(2,1)S(1)} %get-tuple-element.82._), channel_id=1, source_target_pairs={{0,8},{2,10},{4,12},{6,14},{8,0},{10,2},{12,4},{14,6},{16,24},{18,... | collective-permute-start | bytes 405512 | tf_op jit(solution)/shard_map/ppermute | solution.py:585
  15.0 1.6 %turned_probs.3 = (f32[16,256,512]{2,1,0:T(8,128)S(1)}, f32[16,256,256]{2,1,0:T(8,128)S(1)}, bf16[16,256,512]{2,1,0:T(8,128)(2,1)S(1)}, bf16[16,256,256]{2,1,0:T(8,128)(2,1)S(1)}) custom-call(bf16[512,2048]{1,0:T(8,128)(2,1)S(1)} %get-tuple-element.77.q, ...), custom_call_target="tpu_custom_call", output_to_operand_aliasing={{0}: (5, {}), {1}: (6, {}), {2}: (7, {}), {3}: (8, {})} | custom-call | flops 536870912 | bytes 43159552 | tf_op jit(solution)/shard_map/turned_probs/pallas_call | solution.py:125
  16.6 1.8 %collective-permute-done.2.refs_0_ = bf16[528,128]{1,0:T(8,128)(2,1)S(1)} collective-permute-done((bf16[528,128]{1,0:T(8,128)(2,1)S(1)}, bf16[528,128]{1,0:T(8,128)(2,1)S(1)}, u32[]{:S(2)}, u32[]{:S(2)}) %collective-permute-start.2) | collective-permute-done | bytes 135200 | tf_op jit(solution)/shard_map/ppermute | solution.py:585
  18.5 2.7 %collective-permute-start.4 = (bf16[528,128]{1,0:T(8,128)(2,1)S(1)}, bf16[528,128]{1,0:T(8,128)(2,1)S(1)}, u32[]{:S(2)}, u32[]{:S(2)}) collective-permute-start(bf16[528,128]{1,0:T(8,128)(2,1)S(1)} %get-tuple-element.87._), channel_id=1, source_target_pairs={{0,16},{2,18},{4,20},{6,22},{8,24},{10,26},{12,28},{14,30},{16,0},... | collective-permute-start | bytes 405512 | tf_op jit(solution)/shard_map/ppermute | solution.py:585
  21.2 5.8 %intra.1.refs_0_ = f32[512,2048]{1,0:T(8,128)S(1)} custom-call(bf16[512,2048]{1,0:T(8,128)(2,1)S(1)} %get-tuple-element.77.q, bf16[512,2048]{1,0:T(8,128)(2,1)S(1)} %get-tuple-element.72.k, bf16[512,2048]{1,0:T(8,128)(2,1)S(1)} %get-tuple-element.73.v, f32[16,512]{1,0:T(8,128)S(1)} %get-tuple-element.74.row, f32[4,512,128]{2,1,0:T(8,128)S(1)} %get-tuple-element.78.col, ...), custom_call_target="tpu_custom_call" | custom-call | flops 2147483648 | bytes 11702272 | tf_op jit(solution)/shard_map/intra/pallas_call | solution.py:125
  27.2 1.6 %collective-permute-start.5 = (bf16[528,128]{1,0:T(8,128)(2,1)S(1)}, bf16[528,128]{1,0:T(8,128)(2,1)S(1)}, u32[]{:S(2)}, u32[]{:S(2)}) collective-permute-start(bf16[528,128]{1,0:T(8,128)(2,1)S(1)} %get-tuple-element.91._), channel_id=1, source_target_pairs={{0,4},{2,6},{4,0},{6,2},{8,12},{10,14},{12,8},{14,10},{16,20},{18,... | collective-permute-start | bytes 405512 | tf_op jit(solution)/shard_map/ppermute | solution.py:585
  28.8 1.9 %own_dscaled.1 = (f32[512,2048]{1,0:T(8,128)S(1)}, bf16[2048,512]{1,0:T(8,128)(2,1)S(1)}) custom-call(bf16[512,2048]{1,0:T(8,128)(2,1)S(1)} %copy-done, bf16[256,4096]{1,0:T(8,128)(2,1)} %grad.1, f32[1,2048]{1,0:T(1,128)S(1)} %bitcast.2, bf16[512,2048]{1,0:T(8,128)(2,1)S(1)} %get-tuple-element.77.q, f32[16,512]{1,0:T(8,128)S(1)} %get-tuple-element.74.row, ...), custom_call_target="tpu_custom_call" | custom-call | flops 268435456 | bytes 12759040 | tf_op jit(solution)/shard_map/own_dscaled/pallas_call | solution.py:125
  30.7 1.5 %collective-permute-done.5.other = bf16[528,128]{1,0:T(8,128)(2,1)S(1)} collective-permute-done((bf16[528,128]{1,0:T(8,128)(2,1)S(1)}, bf16[528,128]{1,0:T(8,128)(2,1)S(1)}, u32[]{:S(2)}, u32[]{:S(2)}) %collective-permute-start.5) | collective-permute-done | bytes 135200 | tf_op jit(solution)/shard_map/ppermute | solution.py:585
  34.4 1.7 %attention.3 = (f32[512,2048]{1,0:T(8,128)S(1)}, f32[8,512]{1,0:T(8,128)S(1)}) custom-call(bf16[512,2048]{1,0:T(8,128)(2,1)S(1)} %get-tuple-element.77.q, f32[512,2048]{1,0:T(8,128)S(1)} %intra.1.refs_0_, f32[512,2048]{1,0:T(8,128)S(1)} %got_dscaled.1.dscaled, f32[4,512,128]{2,1,0:T(8,128)S(1)} %get-tuple-element.93.growth, ...), custom_call_target="tpu_custom_call", output_to_operand_aliasing={{0}: (5, {})} | custom-call | flops 134217728 | bytes 20733952 | tf_op jit(solution)/shard_map/attention/pallas_call | solution.py:125
  37.0 2.8 %collective-permute-done.7.refs_1_ = f32[8,512]{1,0:T(8,128)S(1)} collective-permute-done((f32[8,512]{1,0:T(8,128)S(1)}, f32[8,512]{1,0:T(8,128)S(1)}, u32[]{:S(2)}, u32[]{:S(2)}) %collective-permute-start.7) | collective-permute-done | bytes 16416 | tf_op jit(solution)/shard_map/ppermute | solution.py:750
  43.4 1.6 %collective-permute-start.9 = (bf16[528,128]{1,0:T(8,128)(2,1)S(1)}, bf16[528,128]{1,0:T(8,128)(2,1)S(1)}, u32[]{:S(2)}, u32[]{:S(2)}) collective-permute-start(bf16[528,128]{1,0:T(8,128)(2,1)S(1)} %get-tuple-element.110._), channel_id=1, source_target_pairs={{0,4},{2,6},{4,0},{6,2},{8,12},{10,14},{12,8},{14,10},{16,20},{18,... | collective-permute-start | bytes 405512 | tf_op jit(solution)/shard_map/ppermute | solution.py:585
  45.0 2.3 %gate.6 = (bf16[512,2048]{1,0:T(8,128)(2,1)}, f32[8,128]{1,0:T(8,128)S(1)}) custom-call(bf16[512,2048]{1,0:T(8,128)(2,1)S(1)} %copy-done, f32[512,2048]{1,0:T(8,128)S(1)} %get-tuple-element.101.att, f32[512,2048]{1,0:T(8,128)S(1)} %got_dscaled.1.dscaled, f32[512,128]{1,0:T(8,128)S(1)} %get-tuple-element.103.refs_0_.scale, ...), custom_call_target="tpu_custom_call" | custom-call | flops 268435456 | bytes 12984320 | tf_op jit(solution)/shard_map/gate/pallas_call | solution.py:125
  47.3 2.2 %key_value.3 = (f32[512,2048]{1,0:T(8,128)S(1)}, f32[512,2048]{1,0:T(8,128)S(1)}) custom-call(bf16[512,2048]{1,0:T(8,128)(2,1)S(1)} %get-tuple-element.77.q, bf16[512,2048]{1,0:T(8,128)(2,1)S(1)} %get-tuple-element.73.v, bf16[512,2048]{1,0:T(8,128)(2,1)S(1)} %get-tuple-element.106.dattn, f32[16,256,512]{2,1,0:T(8,128)S(1)} %get-tuple-element.111.table0, ...), custom_call_target="tpu_custom_call" | custom-call | flops 1073741824 | bytes 33558528 | tf_op jit(solution)/shard_map/key_value/pallas_call | solution.py:125
  49.6 1.7 %collective-permute-start.10 = (bf16[528,128]{1,0:T(8,128)(2,1)S(1)}, bf16[528,128]{1,0:T(8,128)(2,1)S(1)}, u32[]{:S(2)}, u32[]{:S(2)}) collective-permute-start(bf16[528,128]{1,0:T(8,128)(2,1)S(1)} %get-tuple-element.117._), channel_id=1, source_target_pairs={{0,8},{2,10},{4,12},{6,14},{8,0},{10,2},{12,4},{14,6},{16,24},{18,... | collective-permute-start | bytes 405512 | tf_op jit(solution)/shard_map/ppermute | solution.py:585
  51.2 3.3 %key_value.4 = (f32[512,2048]{1,0:T(8,128)S(1)}, f32[512,2048]{1,0:T(8,128)S(1)}) custom-call(bf16[512,2048]{1,0:T(8,128)(2,1)S(1)} %get-tuple-element.77.q, bf16[512,2048]{1,0:T(8,128)(2,1)S(1)} %get-tuple-element.73.v, bf16[512,2048]{1,0:T(8,128)(2,1)S(1)} %get-tuple-element.106.dattn, ...), custom_call_target="tpu_custom_call", output_to_operand_aliasing={{0}: (8, {}), {1}: (9, {})} | custom-call | flops 1610612736 | bytes 42078208 | tf_op jit(solution)/shard_map/key_value/pallas_call | solution.py:125
  55.1 1.7 %collective-permute-start.11 = (bf16[528,128]{1,0:T(8,128)(2,1)S(1)}, bf16[528,128]{1,0:T(8,128)(2,1)S(1)}, u32[]{:S(2)}, u32[]{:S(2)}) collective-permute-start(bf16[528,128]{1,0:T(8,128)(2,1)S(1)} %get-tuple-element.120._), channel_id=1, source_target_pairs={{0,16},{2,18},{4,20},{6,22},{8,24},{10,26},{12,28},{14,30},{16,0},... | collective-permute-start | bytes 405512 | tf_op jit(solution)/shard_map/ppermute | solution.py:585
  56.8 6.4 %query.1 = (bf16[512,2048]{1,0:T(8,128)(2,1)}, f32[8,128]{1,0:T(8,128)S(1)}) custom-call(bf16[512,2048]{1,0:T(8,128)(2,1)S(1)} %get-tuple-element.72.k, bf16[512,2048]{1,0:T(8,128)(2,1)S(1)} %get-tuple-element.73.v, bf16[512,2048]{1,0:T(8,128)(2,1)S(1)} %get-tuple-element.106.dattn, f32[16,512]{1,0:T(8,128)S(1)} %get-tuple-element.74.row, ...), custom_call_target="tpu_custom_call" | custom-call | flops 2415919104 | bytes 11198464 | tf_op jit(solution)/shard_map/query/pallas_call | solution.py:125
  64.3 3.3 %key_value.5 = (f32[512,2048]{1,0:T(8,128)S(1)}, f32[512,2048]{1,0:T(8,128)S(1)}) custom-call(bf16[512,2048]{1,0:T(8,128)(2,1)S(1)} %get-tuple-element.77.q, bf16[512,2048]{1,0:T(8,128)(2,1)S(1)} %get-tuple-element.73.v, bf16[512,2048]{1,0:T(8,128)(2,1)S(1)} %get-tuple-element.106.dattn, ...), custom_call_target="tpu_custom_call", output_to_operand_aliasing={{0}: (8, {}), {1}: (9, {})} | custom-call | flops 1610612736 | bytes 42078208 | tf_op jit(solution)/shard_map/key_value/pallas_call | solution.py:125
  70.6 3.3 %final.1 = (bf16[512,2048]{1,0:T(8,128)(2,1)}, bf16[512,2048]{1,0:T(8,128)(2,1)}, f32[1,2048]{1,0:T(1,128)}) custom-call(bf16[512,2048]{1,0:T(8,128)(2,1)S(1)} %get-tuple-element.72.k, bf16[512,2048]{1,0:T(8,128)(2,1)S(1)} %get-tuple-element.73.v, f32[512,2048]{1,0:T(8,128)S(1)} %get-tuple-element.127.refs_0_.dk, f32[512,2048]{1,0:T(8,128)S(1)} %get-tuple-element.128.dv, ...), custom_call_target="tpu_custom_call" | custom-call | flops 268435456 | bytes 20209664 | tf_op jit(solution)/shard_map/final/pallas_call | solution.py:125
  (37 shorter events, 13.9 us)
Async XLA Ops:
  3.5 3.9 %collective-permute-start = (f32[2,520,128]{2,1,0:T(8,128)S(1)}, f32[2,520,128]{2,1,0:T(8,128)S(1)}, u32[]{:S(2)}, u32[]{:S(2)}) collective-permute-start(f32[2,520,128]{2,1,0:T(8,128)S(1)} %get-tuple-element.75), channel_id=1, source_target_pairs={{0,2},{2,0},{4,6},{6,4},{8,10},{10,8},{12,14},{14,12},{16,18},{18,... | collective-permute-start | bytes 1597448 | tf_op jit(solution)/shard_map/ppermute | solution.py:585
  4.0 28.6 %collective-permute-start.3 = (bf16[256,2048]{1,0:T(8,128)(2,1)S(1)}, bf16[256,2048]{1,0:T(8,128)(2,1)S(1)}, u32[]{:S(2)}, u32[]{:S(2)}) collective-permute-start(bf16[256,2048]{1,0:T(8,128)(2,1)S(1)} %get-tuple-element.88), channel_id=1, source_target_pairs={{0,1},{1,0},{2,3},{3,2},{4,5},{5,4},{6,7},{7,6},{8,9},{9,8},{10,11... | collective-permute-start | bytes 3145736 | tf_op jit(solution)/shard_map/ppermute | solution.py:664
  7.5 5.7 %collective-permute-start.1 = (bf16[528,128]{1,0:T(8,128)(2,1)S(1)}, bf16[528,128]{1,0:T(8,128)(2,1)S(1)}, u32[]{:S(2)}, u32[]{:S(2)}) collective-permute-start(bf16[528,128]{1,0:T(8,128)(2,1)S(1)} %get-tuple-element.76._), channel_id=1, source_target_pairs={{0,4},{2,6},{4,0},{6,2},{8,12},{10,14},{12,8},{14,10},{16,20},{18,... | collective-permute-start | bytes 405512 | tf_op jit(solution)/shard_map/ppermute | solution.py:585
  13.3 5.1 %collective-permute-start.2 = (bf16[528,128]{1,0:T(8,128)(2,1)S(1)}, bf16[528,128]{1,0:T(8,128)(2,1)S(1)}, u32[]{:S(2)}, u32[]{:S(2)}) collective-permute-start(bf16[528,128]{1,0:T(8,128)(2,1)S(1)} %get-tuple-element.82._), channel_id=1, source_target_pairs={{0,8},{2,10},{4,12},{6,14},{8,0},{10,2},{12,4},{14,6},{16,24},{18,... | collective-permute-start | bytes 405512 | tf_op jit(solution)/shard_map/ppermute | solution.py:585
  18.5 8.5 %collective-permute-start.4 = (bf16[528,128]{1,0:T(8,128)(2,1)S(1)}, bf16[528,128]{1,0:T(8,128)(2,1)S(1)}, u32[]{:S(2)}, u32[]{:S(2)}) collective-permute-start(bf16[528,128]{1,0:T(8,128)(2,1)S(1)} %get-tuple-element.87._), channel_id=1, source_target_pairs={{0,16},{2,18},{4,20},{6,22},{8,24},{10,26},{12,28},{14,30},{16,0},... | collective-permute-start | bytes 405512 | tf_op jit(solution)/shard_map/ppermute | solution.py:585
  27.0 1.8 %copy-start = (bf16[512,2048]{1,0:T(8,128)(2,1)S(1)}, bf16[512,2048]{1,0:T(8,128)(2,1)}, u32[]{:S(2)}) copy-start(bf16[512,2048]{1,0:T(8,128)(2,1)} %gate.7) | copy-start | bytes 6291460
  27.0 1.8 %copy-start.1 = (f32[2048]{0:T(1024)S(1)}, f32[2048]{0:T(1024)}, u32[]{:S(2)}) copy-start(f32[2048]{0:T(1024)} %param.12) | copy-start | bytes 24580
  27.2 5.1 %collective-permute-start.5 = (bf16[528,128]{1,0:T(8,128)(2,1)S(1)}, bf16[528,128]{1,0:T(8,128)(2,1)S(1)}, u32[]{:S(2)}, u32[]{:S(2)}) collective-permute-start(bf16[528,128]{1,0:T(8,128)(2,1)S(1)} %get-tuple-element.91._), channel_id=1, source_target_pairs={{0,4},{2,6},{4,0},{6,2},{8,12},{10,14},{12,8},{14,10},{16,20},{18,... | collective-permute-start | bytes 405512 | tf_op jit(solution)/shard_map/ppermute | solution.py:585
  32.5 1.9 %collective-permute-start.6 = (bf16[2,528,128]{2,1,0:T(8,128)(2,1)S(1)}, bf16[2,528,128]{2,1,0:T(8,128)(2,1)S(1)}, u32[]{:S(2)}, u32[]{:S(2)}) collective-permute-start(bf16[2,528,128]{2,1,0:T(8,128)(2,1)S(1)} %get-tuple-element.96), channel_id=1, source_target_pairs={{0,2},{2,0},{4,6},{6,4},{8,10},{10,8},{12,14},{14,12},{16,18},{18,... | collective-permute-start | bytes 811016 | tf_op jit(solution)/shard_map/ppermute | solution.py:585
  36.0 3.8 %collective-permute-start.7 = (f32[8,512]{1,0:T(8,128)S(1)}, f32[8,512]{1,0:T(8,128)S(1)}, u32[]{:S(2)}, u32[]{:S(2)}) collective-permute-start(f32[8,512]{1,0:T(8,128)S(1)} %get-tuple-element.102.refs_0_), channel_id=1, source_target_pairs={{0,1},{1,0},{2,3},{3,2},{4,5},{5,4},{6,7},{7,6},{8,9},{9,8},{10,11... | collective-permute-start | bytes 49160 | tf_op jit(solution)/shard_map/ppermute | solution.py:750
  41.3 2.0 %collective-permute-start.8 = (f32[2,520,128]{2,1,0:T(8,128)S(1)}, f32[2,520,128]{2,1,0:T(8,128)S(1)}, u32[]{:S(2)}, u32[]{:S(2)}) collective-permute-start(f32[2,520,128]{2,1,0:T(8,128)S(1)} %get-tuple-element.108), channel_id=1, source_target_pairs={{0,2},{2,0},{4,6},{6,4},{8,10},{10,8},{12,14},{14,12},{16,18},{18,... | collective-permute-start | bytes 1597448 | tf_op jit(solution)/shard_map/ppermute | solution.py:585
  43.4 6.1 %collective-permute-start.9 = (bf16[528,128]{1,0:T(8,128)(2,1)S(1)}, bf16[528,128]{1,0:T(8,128)(2,1)S(1)}, u32[]{:S(2)}, u32[]{:S(2)}) collective-permute-start(bf16[528,128]{1,0:T(8,128)(2,1)S(1)} %get-tuple-element.110._), channel_id=1, source_target_pairs={{0,4},{2,6},{4,0},{6,2},{8,12},{10,14},{12,8},{14,10},{16,20},{18,... | collective-permute-start | bytes 405512 | tf_op jit(solution)/shard_map/ppermute | solution.py:585
  49.6 5.4 %collective-permute-start.10 = (bf16[528,128]{1,0:T(8,128)(2,1)S(1)}, bf16[528,128]{1,0:T(8,128)(2,1)S(1)}, u32[]{:S(2)}, u32[]{:S(2)}) collective-permute-start(bf16[528,128]{1,0:T(8,128)(2,1)S(1)} %get-tuple-element.117._), channel_id=1, source_target_pairs={{0,8},{2,10},{4,12},{6,14},{8,0},{10,2},{12,4},{14,6},{16,24},{18,... | collective-permute-start | bytes 405512 | tf_op jit(solution)/shard_map/ppermute | solution.py:585
  55.1 8.5 %collective-permute-start.11 = (bf16[528,128]{1,0:T(8,128)(2,1)S(1)}, bf16[528,128]{1,0:T(8,128)(2,1)S(1)}, u32[]{:S(2)}, u32[]{:S(2)}) collective-permute-start(bf16[528,128]{1,0:T(8,128)(2,1)S(1)} %get-tuple-element.120._), channel_id=1, source_target_pairs={{0,16},{2,18},{4,20},{6,22},{8,24},{10,26},{12,28},{14,30},{16,0},... | collective-permute-start | bytes 405512 | tf_op jit(solution)/shard_map/ppermute | solution.py:585
  63.7 5.1 %collective-permute-start.12 = (bf16[528,128]{1,0:T(8,128)(2,1)S(1)}, bf16[528,128]{1,0:T(8,128)(2,1)S(1)}, u32[]{:S(2)}, u32[]{:S(2)}) collective-permute-start(bf16[528,128]{1,0:T(8,128)(2,1)S(1)} %get-tuple-element.125._), channel_id=1, source_target_pairs={{0,4},{2,6},{4,0},{6,2},{8,12},{10,14},{12,8},{14,10},{16,20},{18,... | collective-permute-start | bytes 405512 | tf_op jit(solution)/shard_map/ppermute | solution.py:585
  69.0 1.6 %collective-permute-start.13 = (bf16[2,528,128]{2,1,0:T(8,128)(2,1)S(1)}, bf16[2,528,128]{2,1,0:T(8,128)(2,1)S(1)}, u32[]{:S(2)}, u32[]{:S(2)}) collective-permute-start(bf16[2,528,128]{2,1,0:T(8,128)(2,1)S(1)} %get-tuple-element.130), channel_id=1, source_target_pairs={{0,2},{2,0},{4,6},{6,4},{8,10},{10,8},{12,14},{14,12},{16,18},{18,... | collective-permute-start | bytes 811016 | tf_op jit(solution)/shard_map/ppermute | solution.py:585

commit v10 on v9

--- a/solution.py
+++ b/solution.py
@@ -147,10 +147,11 @@
 
 def chip_total_body(reverse, hq, keep, got, own, send):
     first = core() == 0
+    read_got = read_narrow if reverse else read_wide
     here, there = pair(), 1 - pair()
-    own_items = joined(read_wide(keep.at[here], hq), read_wide(got.at[here], hq), first, reverse)
+    own_items = joined(read_wide(keep.at[here], hq), read_got(got.at[here], hq), first, reverse)
     write_wide(own, hq, own_items)
-    send_items = joined(read_wide(keep.at[there], hq), read_wide(got.at[there], hq), first, reverse)
+    send_items = joined(read_wide(keep.at[there], hq), read_got(got.at[there], hq), first, reverse)
     write_narrow(send, hq, send_items)
 
 
@@ -209,11 +210,12 @@
 def into_cores_body(reverse, hq, keep, got, own, other, *refs):
     mine, send = refs[-2:]
     mine_near = core() == (1 if reverse else 0)
+    read_got = read_narrow if reverse else read_wide
     for y in range(2):
         a, b = read_wide(own, hq), read_narrow(other, hq)
         here = pair() == y
         items_mine, items_send = [], []
-        for p, q, (k, ek, _), (g, eg, _) in zip(a, b, read_wide(keep.at[y], hq), read_wide(got.at[y], hq)):
+        for p, q, (k, ek, _), (g, eg, _) in zip(a, b, read_wide(keep.at[y], hq), read_got(got.at[y], hq)):
             r = jnp.where(here, p[0], q[0])
             gain = jnp.where(here, p[2], q[2])
             zero = jnp.zeros_like(ek)
@@ -326,8 +328,9 @@
     lax.fori_loop(first, first + TEAM // 2, one, 0)
 
 
-def intra_body(heads, q, k, v, row, col, _, intra):
-    hq = heads // TEAM
+def intra_body(heads, first, last, q, k, v, row, col, *refs):
+    hq = heads // TEAM
+    intra = refs[-1]
 
     def one(g, _):
         for j in range(hq):
@@ -340,7 +343,7 @@
                 intra[half(i), c] = nn(probs, v[u, c])
         return 0
 
-    lax.fori_loop(0, TEAM, one, 0)
+    lax.fori_loop(first, last, one, 0)
 
 
 def dscaled_rows(heads, where, gate, ref, gain, dscaled):
@@ -455,7 +458,7 @@
             for m in range(count):
                 edge = jnp.broadcast_to(row[pl.ds(h + m, 1), :][:, BLOCK - 1 : BLOCK], (1, HEAD))
                 items.append((both[chunk(m), chunk(m)], edge, parts[m]))
-        write_wide(out.at[y], hq, items)
+        (write_wide if same else write_narrow)(out.at[y], hq, items)
 
 
 def leave(out, ref, sems, g, w):
@@ -694,15 +697,21 @@
         return done["probs"][3]
 
     def intra_beside(after):
+        before = [done["intra"]] if "intra" in done else []
+        first, last = (1, TEAM) if before else (0, 1)
         (done["intra"],) = call(
-            functools.partial(intra_body, heads),
-            [done["queries"], keys, values, row, done["decays"][0], after],
+            functools.partial(intra_body, heads, first, last),
+            [done["queries"], keys, values, row, done["decays"][0], after, *before],
             [f32(rows, width)],
             "intra",
-            flops=2 * large,
-            in_specs=[VMEM] * 5 + [ANY],
+            flops=2 * large * (last - first) // TEAM,
+            in_specs=[VMEM] * 5 + [ANY] + [VMEM] * len(before),
+            alias={6: 0} if before else None,
         )
         return done["intra"]
+
+    def probs_and_intra(after):
+        return intra_beside(probs_beside(after))
 
     def dscaled_beside(after):
         done["dscaled"] = call(
@@ -714,19 +723,20 @@
             small,
             [VMEM, HBM, VMEM, VMEM, VMEM, ANY],
         )
-        return done["dscaled"][1]
-
-    work = {"pair": probs_beside, "one": probs_beside, "last": intra_beside, "pair_back": dscaled_beside}
+        (dscaled,) = call(
+            functools.partial(got_dscaled_body, heads, swaps),
+            [gate, arrived, gain_row, done["dscaled"][0]],
+            [f32(rows, width)],
+            "got_dscaled",
+            alias={3: 0},
+        )
+        done["dscaled"] = dscaled, done["dscaled"][1]
+        return dscaled
+
+    work = {"pair": probs_beside, "one": probs_and_intra, "last": intra_beside, "pair_back": dscaled_beside}
     mine, got = scan(False, keep, give, work)
     queries = done["queries"]
     (col, growth), intra, (dscaled, turned) = done["decays"], done["intra"], done["dscaled"]
-    (dscaled,) = call(
-        functools.partial(got_dscaled_body, heads, swaps),
-        [gate, arrived, gain_row, dscaled],
-        [f32(rows, width)],
-        "got_dscaled",
-        alias={3: 0},
-    )
     tall = f32(rows, HEAD)
     wide_scratch = pltpu.VMEM((rows, 2 * HEAD), F32)
     att, squares, inner = call(
@@ -753,7 +763,7 @@
     dattn, give, scale, coef = call(
         functools.partial(dattn_body, heads, channels, False),
         [att, dscaled, turned, gain_row, row, sums, others],
-        [bf(rows, width), wide2, tall, tall],
+        [bf(rows, width), narrow2, tall, tall],
         "sent_dattn",
         flops=small // 2,
     )
@@ -781,7 +791,7 @@
         return token
 
     units = heads // min(hq, 2)
-    cuts = [0, units // 4, (5 * units) // 8, units]
+    cuts = [0, units // 8, units // 2, units]
 
     def key_value_beside(after):
         before = done.get("key_value", [])

time: 74.2 us -> 73.5 us (level)
  waiting for transfers between devices: 9.81 us -> 7.73 us
  starting transfers between devices: 17.2 us -> 18.7 us
    ppermute x12, waiting for transfers between devices: 7 us -> 4.99 us  [swap(): return lax.ppermute(x, 'ctx', [(i, i ^ bit) for i in range(n)])]
    ppermute x12, starting transfers between devices: 13.7 us -> 15 us  [swap(): return lax.ppermute(x, 'ctx', [(i, i ^ bit) for i in range(n)])]
    pallas_call x29 -> x30, Pallas kernels: 46 us -> 45.9 us  [call(): pl.pallas_call(body, in_specs=in_specs or [VMEM] * len(inputs), out_specs...]
  transfers between devices with their start and end apart: 14 -> 14, of which waited for: 9 -> 10; matrix products, arithmetic and copies ran while one was open for 0% -> 0% of each run, Pallas kernels for 49% -> 49%
where the time goes in v10:
time: 73.5 us; the launch traced here: 73.4 us
  Pallas kernels  45.9 us (62%)
  starting transfers between devices  18.7 us (25%)
  waiting for transfers between devices  7.73 us (11%)
  between operations  1.05 us (1%)
    pallas_call x30, Pallas kernels, call(): pl.pallas_call(body, in_specs=in_specs or [VMEM] * len(inputs), out_specs...  45.9 us
    ppermute x12, starting transfers between devices, swap(): return lax.ppermute(x, 'ctx', [(i, i ^ bit) for i in range(n)])  15 us
    ppermute x12, waiting for transfers between devices, swap(): return lax.ppermute(x, 'ctx', [(i, i ^ bit) for i in range(n)])  4.99 us
    ppermute x1, waiting for transfers between devices, local(): others = lax.ppermute(sums, 'tp', [(0, 1), (1, 0)])  2.69 us
    ppermute x1, starting transfers between devices, local(): arrived = lax.ppermute(outs[4], 'tp', [(0, 1), (1, 0)])  2.56 us
  transfers between devices with their start and end apart: 14, of which 10 were waited for; matrix products, arithmetic and copies ran while one was open for 0% of the time, Pallas kernels for 49%

profile of v10, /device:TPU:0, one launch (start us, length us, event | category | flops | bytes accessed | tf_op | source)
XLA Modules:
  0.0 73.4 jit_solution(14200903104007496952)
XLA Ops:
  0.6 2.8 %sent_states.1 = (f32[2,520,128]{2,1,0:T(8,128)S(1)}, f32[16,512]{1,0:T(8,128)S(1)}, bf16[512,2048]{1,0:T(8,128)(2,1)S(1)}, bf16[512,2048]{1,0:T(8,128)(2,1)S(1)}, bf16[256,2048]{1,0:T(8,128)(2,1)S(1)}) custom-call(bf16[512,2048]{1,0:T(8,128)(2,1)} %k_hbm.1, bf16[512,2048]{1,0:T(8,128)(2,1)} %v_hbm.1, f32[16,512]{1,0:T(8,128)} %ld_hbm.1, bf16[256,4096]{1,0:T(8,128)(2,1)} %grad.1), custom_call_target="tpu_custom_call" | custom-call | flops 134217728 | bytes 12132352 | tf_op jit(solution)/shard_map/sent_states/pallas_call | solution.py:125
  4.0 2.6 %collective-permute-start.3 = (bf16[256,2048]{1,0:T(8,128)(2,1)S(1)}, bf16[256,2048]{1,0:T(8,128)(2,1)S(1)}, u32[]{:S(2)}, u32[]{:S(2)}) collective-permute-start(bf16[256,2048]{1,0:T(8,128)(2,1)S(1)} %get-tuple-element.88), channel_id=1, source_target_pairs={{0,1},{1,0},{2,3},{3,2},{4,5},{5,4},{6,7},{7,6},{8,9},{9,8},{10,11... | collective-permute-start | bytes 3145736 | tf_op jit(solution)/shard_map/ppermute | solution.py:667
  7.5 1.6 %collective-permute-start.1 = (bf16[528,128]{1,0:T(8,128)(2,1)S(1)}, bf16[528,128]{1,0:T(8,128)(2,1)S(1)}, u32[]{:S(2)}, u32[]{:S(2)}) collective-permute-start(bf16[528,128]{1,0:T(8,128)(2,1)S(1)} %get-tuple-element.76._), channel_id=1, source_target_pairs={{0,4},{2,6},{4,0},{6,2},{8,12},{10,14},{12,8},{14,10},{16,20},{18,... | collective-permute-start | bytes 405512 | tf_op jit(solution)/shard_map/ppermute | solution.py:588
  9.1 1.6 %decays.1 = (f32[4,512,128]{2,1,0:T(8,128)S(1)}, f32[4,512,128]{2,1,0:T(8,128)S(1)}, bf16[512,2048]{1,0:T(8,128)(2,1)S(1)}) custom-call(f32[16,512]{1,0:T(8,128)S(1)} %get-tuple-element.74.row, bf16[512,2048]{1,0:T(8,128)(2,1)} %q_hbm.1, bf16[528,128]{1,0:T(8,128)(2,1)S(1)} %get-tuple-element.76._), custom_call_target="tpu_custom_call" | custom-call | bytes 6459392 | tf_op jit(solution)/shard_map/decays/pallas_call | solution.py:125
  10.7 1.6 %turned_probs.2 = (f32[16,256,512]{2,1,0:T(8,128)S(1)}, f32[16,256,256]{2,1,0:T(8,128)S(1)}, bf16[16,256,512]{2,1,0:T(8,128)(2,1)S(1)}, bf16[16,256,256]{2,1,0:T(8,128)(2,1)S(1)}) custom-call(bf16[512,2048]{1,0:T(8,128)(2,1)S(1)} %get-tuple-element.77.q, bf16[512,2048]{1,0:T(8,128)(2,1)S(1)} %get-tuple-element.72.k, f32[16,512]{1,0:T(8,128)S(1)} %get-tuple-element.74.row, ...), custom_call_target="tpu_custom_call" | custom-call | flops 536870912 | bytes 24285184 | tf_op jit(solution)/shard_map/turned_probs/pallas_call | solution.py:125
  13.3 1.6 %collective-permute-start.2 = (bf16[528,128]{1,0:T(8,128)(2,1)S(1)}, bf16[528,128]{1,0:T(8,128)(2,1)S(1)}, u32[]{:S(2)}, u32[]{:S(2)}) collective-permute-start(bf16[528,128]{1,0:T(8,128)(2,1)S(1)} %get-tuple-element.82._), channel_id=1, source_target_pairs={{0,8},{2,10},{4,12},{6,14},{8,0},{10,2},{12,4},{14,6},{16,24},{18,... | collective-permute-start | bytes 405512 | tf_op jit(solution)/shard_map/ppermute | solution.py:588
  15.0 1.6 %turned_probs.3 = (f32[16,256,512]{2,1,0:T(8,128)S(1)}, f32[16,256,256]{2,1,0:T(8,128)S(1)}, bf16[16,256,512]{2,1,0:T(8,128)(2,1)S(1)}, bf16[16,256,256]{2,1,0:T(8,128)(2,1)S(1)}) custom-call(bf16[512,2048]{1,0:T(8,128)(2,1)S(1)} %get-tuple-element.77.q, ...), custom_call_target="tpu_custom_call", output_to_operand_aliasing={{0}: (5, {}), {1}: (6, {}), {2}: (7, {}), {3}: (8, {})} | custom-call | flops 536870912 | bytes 43159552 | tf_op jit(solution)/shard_map/turned_probs/pallas_call | solution.py:125
  16.6 1.4 %intra.2.refs_1_ = f32[512,2048]{1,0:T(8,128)S(1)} custom-call(bf16[512,2048]{1,0:T(8,128)(2,1)S(1)} %get-tuple-element.77.q, bf16[512,2048]{1,0:T(8,128)(2,1)S(1)} %get-tuple-element.72.k, bf16[512,2048]{1,0:T(8,128)(2,1)S(1)} %get-tuple-element.73.v, f32[16,512]{1,0:T(8,128)S(1)} %get-tuple-element.74.row, f32[4,512,128]{2,1,0:T(8,128)S(1)} %get-tuple-element.78.col, ...), custom_call_target="tpu_custom_call" | custom-call | flops 536870912 | bytes 13664256 | tf_op jit(solution)/shard_map/intra/pallas_call | solution.py:125
  18.5 2.7 %collective-permute-start.4 = (bf16[528,128]{1,0:T(8,128)(2,1)S(1)}, bf16[528,128]{1,0:T(8,128)(2,1)S(1)}, u32[]{:S(2)}, u32[]{:S(2)}) collective-permute-start(bf16[528,128]{1,0:T(8,128)(2,1)S(1)} %get-tuple-element.87.refs_0_), channel_id=1, source_target_pairs={{0,16},{2,18},{4,20},{6,22},{8,24},{10,26},{12,28},{14,30},{16,0},... | collective-permute-start | bytes 405512 | tf_op jit(solution)/shard_map/ppermute | solution.py:588
  21.1 4.4 %intra.3.refs_0_ = f32[512,2048]{1,0:T(8,128)S(1)} custom-call(bf16[512,2048]{1,0:T(8,128)(2,1)S(1)} %get-tuple-element.77.q, bf16[512,2048]{1,0:T(8,128)(2,1)S(1)} %get-tuple-element.72.k, bf16[512,2048]{1,0:T(8,128)(2,1)S(1)} %get-tuple-element.73.v, f32[16,512]{1,0:T(8,128)S(1)} %get-tuple-element.74.row, ...), custom_call_target="tpu_custom_call", output_to_operand_aliasing={{}: (6, {})} | custom-call | flops 1610612736 | bytes 15896576 | tf_op jit(solution)/shard_map/intra/pallas_call | solution.py:125
  26.7 1.6 %collective-permute-start.5 = (bf16[528,128]{1,0:T(8,128)(2,1)S(1)}, bf16[528,128]{1,0:T(8,128)(2,1)S(1)}, u32[]{:S(2)}, u32[]{:S(2)}) collective-permute-start(bf16[528,128]{1,0:T(8,128)(2,1)S(1)} %get-tuple-element.91._), channel_id=1, source_target_pairs={{0,4},{2,6},{4,0},{6,2},{8,12},{10,14},{12,8},{14,10},{16,20},{18,... | collective-permute-start | bytes 405512 | tf_op jit(solution)/shard_map/ppermute | solution.py:588
  28.3 1.9 %own_dscaled.1 = (f32[512,2048]{1,0:T(8,128)S(1)}, bf16[2048,512]{1,0:T(8,128)(2,1)S(1)}) custom-call(bf16[512,2048]{1,0:T(8,128)(2,1)S(1)} %copy-done, bf16[256,4096]{1,0:T(8,128)(2,1)} %grad.1, f32[1,2048]{1,0:T(1,128)S(1)} %bitcast.2, bf16[512,2048]{1,0:T(8,128)(2,1)S(1)} %get-tuple-element.77.q, f32[16,512]{1,0:T(8,128)S(1)} %get-tuple-element.74.row, ...), custom_call_target="tpu_custom_call" | custom-call | flops 268435456 | bytes 12759040 | tf_op jit(solution)/shard_map/own_dscaled/pallas_call | solution.py:125
  33.6 1.6 %attention.3 = (f32[512,2048]{1,0:T(8,128)S(1)}, f32[8,512]{1,0:T(8,128)S(1)}) custom-call(bf16[512,2048]{1,0:T(8,128)(2,1)S(1)} %get-tuple-element.77.q, f32[512,2048]{1,0:T(8,128)S(1)} %intra.3.refs_0_, f32[512,2048]{1,0:T(8,128)S(1)} %got_dscaled.1.refs_0_.dscaled, f32[4,512,128]{2,1,0:T(8,128)S(1)} %get-tuple-element.93.growth, ...), custom_call_target="tpu_custom_call", output_to_operand_aliasing={{0}: (5, {})} | custom-call | flops 134217728 | bytes 20733952 | tf_op jit(solution)/shard_map/attention/pallas_call | solution.py:125
  36.3 2.7 %collective-permute-done.7.refs_1_ = f32[8,512]{1,0:T(8,128)S(1)} collective-permute-done((f32[8,512]{1,0:T(8,128)S(1)}, f32[8,512]{1,0:T(8,128)S(1)}, u32[]{:S(2)}, u32[]{:S(2)}) %collective-permute-start.7) | collective-permute-done | bytes 16416 | tf_op jit(solution)/shard_map/ppermute | solution.py:760
  39.0 1.5 %sent_dattn.1 = (bf16[512,2048]{1,0:T(8,128)(2,1)S(1)}, bf16[2,528,128]{2,1,0:T(8,128)(2,1)S(1)}, f32[512,128]{1,0:T(8,128)S(1)}, f32[512,128]{1,0:T(8,128)S(1)}) custom-call(f32[512,2048]{1,0:T(8,128)S(1)} %get-tuple-element.100.att, f32[512,2048]{1,0:T(8,128)S(1)} %got_dscaled.1.refs_0_.dscaled, bf16[2048,512]{1,0:T(8,128)(2,1)S(1)} %get-tuple-element.101.turned, ...), custom_call_target="tpu_custom_call" | custom-call | flops 134217728 | bytes 13451264 | tf_op jit(solution)/shard_map/sent_dattn/pallas_call | solution.py:125
  42.2 1.6 %collective-permute-start.9 = (bf16[528,128]{1,0:T(8,128)(2,1)S(1)}, bf16[528,128]{1,0:T(8,128)(2,1)S(1)}, u32[]{:S(2)}, u32[]{:S(2)}) collective-permute-start(bf16[528,128]{1,0:T(8,128)(2,1)S(1)} %get-tuple-element.110._), channel_id=1, source_target_pairs={{0,4},{2,6},{4,0},{6,2},{8,12},{10,14},{12,8},{14,10},{16,20},{18,... | collective-permute-start | bytes 405512 | tf_op jit(solution)/shard_map/ppermute | solution.py:588
  43.8 2.3 %gate.6 = (bf16[512,2048]{1,0:T(8,128)(2,1)}, f32[8,128]{1,0:T(8,128)S(1)}) custom-call(bf16[512,2048]{1,0:T(8,128)(2,1)S(1)} %copy-done, f32[512,2048]{1,0:T(8,128)S(1)} %get-tuple-element.100.att, f32[512,2048]{1,0:T(8,128)S(1)} %got_dscaled.1.refs_0_.dscaled, f32[512,128]{1,0:T(8,128)S(1)} %get-tuple-element.103.refs_0_.scale, ...), custom_call_target="tpu_custom_call" | custom-call | flops 268435456 | bytes 12984320 | tf_op jit(solution)/shard_map/gate/pallas_call | solution.py:125
  49.2 3.5 %key_value.4 = (f32[512,2048]{1,0:T(8,128)S(1)}, f32[512,2048]{1,0:T(8,128)S(1)}) custom-call(bf16[512,2048]{1,0:T(8,128)(2,1)S(1)} %get-tuple-element.77.q, bf16[512,2048]{1,0:T(8,128)(2,1)S(1)} %get-tuple-element.73.v, bf16[512,2048]{1,0:T(8,128)(2,1)S(1)} %get-tuple-element.106.dattn, ...), custom_call_target="tpu_custom_call", output_to_operand_aliasing={{0}: (8, {}), {1}: (9, {})} | custom-call | flops 1610612736 | bytes 42078208 | tf_op jit(solution)/shard_map/key_value/pallas_call | solution.py:125
  53.2 2.5 %collective-permute-start.11 = (bf16[528,128]{1,0:T(8,128)(2,1)S(1)}, bf16[528,128]{1,0:T(8,128)(2,1)S(1)}, u32[]{:S(2)}, u32[]{:S(2)}) collective-permute-start(bf16[528,128]{1,0:T(8,128)(2,1)S(1)} %get-tuple-element.120._), channel_id=1, source_target_pairs={{0,16},{2,18},{4,20},{6,22},{8,24},{10,26},{12,28},{14,30},{16,0},... | collective-permute-start | bytes 405512 | tf_op jit(solution)/shard_map/ppermute | solution.py:588
  55.6 6.4 %query.1 = (bf16[512,2048]{1,0:T(8,128)(2,1)}, f32[8,128]{1,0:T(8,128)S(1)}) custom-call(bf16[512,2048]{1,0:T(8,128)(2,1)S(1)} %get-tuple-element.72.k, bf16[512,2048]{1,0:T(8,128)(2,1)S(1)} %get-tuple-element.73.v, bf16[512,2048]{1,0:T(8,128)(2,1)S(1)} %get-tuple-element.106.dattn, f32[16,512]{1,0:T(8,128)S(1)} %get-tuple-element.74.row, ...), custom_call_target="tpu_custom_call" | custom-call | flops 2415919104 | bytes 11198464 | tf_op jit(solution)/shard_map/query/pallas_call | solution.py:125
  62.2 1.6 %collective-permute-start.12 = (bf16[528,128]{1,0:T(8,128)(2,1)S(1)}, bf16[528,128]{1,0:T(8,128)(2,1)S(1)}, u32[]{:S(2)}, u32[]{:S(2)}) collective-permute-start(bf16[528,128]{1,0:T(8,128)(2,1)S(1)} %get-tuple-element.125._), channel_id=1, source_target_pairs={{0,4},{2,6},{4,0},{6,2},{8,12},{10,14},{12,8},{14,10},{16,20},{18,... | collective-permute-start | bytes 405512 | tf_op jit(solution)/shard_map/ppermute | solution.py:588
  63.7 4.3 %key_value.5 = (f32[512,2048]{1,0:T(8,128)S(1)}, f32[512,2048]{1,0:T(8,128)S(1)}) custom-call(bf16[512,2048]{1,0:T(8,128)(2,1)S(1)} %get-tuple-element.77.q, bf16[512,2048]{1,0:T(8,128)(2,1)S(1)} %get-tuple-element.73.v, bf16[512,2048]{1,0:T(8,128)(2,1)S(1)} %get-tuple-element.106.dattn, ...), custom_call_target="tpu_custom_call", output_to_operand_aliasing={{0}: (8, {}), {1}: (9, {})} | custom-call | flops 2147483648 | bytes 42078208 | tf_op jit(solution)/shard_map/key_value/pallas_call | solution.py:125
  68.4 1.4 %own_final.1 = (bf16[2,512,512]{2,1,0:T(8,128)(2,1)S(1)}, bf16[2,512,512]{2,1,0:T(8,128)(2,1)S(1)}, f32[1,2048]{1,0:T(1,128)S(1)}) custom-call(bf16[512,2048]{1,0:T(8,128)(2,1)S(1)} %get-tuple-element.72.k, bf16[512,2048]{1,0:T(8,128)(2,1)S(1)} %get-tuple-element.73.v, f32[512,2048]{1,0:T(8,128)S(1)} %get-tuple-element.127.refs_0_.dk, ...), custom_call_target="tpu_custom_call" | custom-call | flops 268435456 | bytes 16007168 | tf_op jit(solution)/shard_map/own_final/pallas_call | solution.py:125
  70.0 3.3 %final.1 = (bf16[512,2048]{1,0:T(8,128)(2,1)}, bf16[512,2048]{1,0:T(8,128)(2,1)}, f32[1,2048]{1,0:T(1,128)}) custom-call(bf16[512,2048]{1,0:T(8,128)(2,1)S(1)} %get-tuple-element.72.k, bf16[512,2048]{1,0:T(8,128)(2,1)S(1)} %get-tuple-element.73.v, f32[512,2048]{1,0:T(8,128)S(1)} %get-tuple-element.127.refs_0_.dk, f32[512,2048]{1,0:T(8,128)S(1)} %get-tuple-element.128.dv, ...), custom_call_target="tpu_custom_call" | custom-call | flops 268435456 | bytes 20209664 | tf_op jit(solution)/shard_map/final/pallas_call | solution.py:125
  (38 shorter events, 14.4 us)
Async XLA Ops:
  3.5 3.9 %collective-permute-start = (f32[2,520,128]{2,1,0:T(8,128)S(1)}, f32[2,520,128]{2,1,0:T(8,128)S(1)}, u32[]{:S(2)}, u32[]{:S(2)}) collective-permute-start(f32[2,520,128]{2,1,0:T(8,128)S(1)} %get-tuple-element.75), channel_id=1, source_target_pairs={{0,2},{2,0},{4,6},{6,4},{8,10},{10,8},{12,14},{14,12},{16,18},{18,... | collective-permute-start | bytes 1597448 | tf_op jit(solution)/shard_map/ppermute | solution.py:588
  4.0 26.3 %collective-permute-start.3 = (bf16[256,2048]{1,0:T(8,128)(2,1)S(1)}, bf16[256,2048]{1,0:T(8,128)(2,1)S(1)}, u32[]{:S(2)}, u32[]{:S(2)}) collective-permute-start(bf16[256,2048]{1,0:T(8,128)(2,1)S(1)} %get-tuple-element.88), channel_id=1, source_target_pairs={{0,1},{1,0},{2,3},{3,2},{4,5},{5,4},{6,7},{7,6},{8,9},{9,8},{10,11... | collective-permute-start | bytes 3145736 | tf_op jit(solution)/shard_map/ppermute | solution.py:667
  7.5 5.7 %collective-permute-start.1 = (bf16[528,128]{1,0:T(8,128)(2,1)S(1)}, bf16[528,128]{1,0:T(8,128)(2,1)S(1)}, u32[]{:S(2)}, u32[]{:S(2)}) collective-permute-start(bf16[528,128]{1,0:T(8,128)(2,1)S(1)} %get-tuple-element.76._), channel_id=1, source_target_pairs={{0,4},{2,6},{4,0},{6,2},{8,12},{10,14},{12,8},{14,10},{16,20},{18,... | collective-permute-start | bytes 405512 | tf_op jit(solution)/shard_map/ppermute | solution.py:588
  13.3 5.1 %collective-permute-start.2 = (bf16[528,128]{1,0:T(8,128)(2,1)S(1)}, bf16[528,128]{1,0:T(8,128)(2,1)S(1)}, u32[]{:S(2)}, u32[]{:S(2)}) collective-permute-start(bf16[528,128]{1,0:T(8,128)(2,1)S(1)} %get-tuple-element.82._), channel_id=1, source_target_pairs={{0,8},{2,10},{4,12},{6,14},{8,0},{10,2},{12,4},{14,6},{16,24},{18,... | collective-permute-start | bytes 405512 | tf_op jit(solution)/shard_map/ppermute | solution.py:588
  18.5 8.1 %collective-permute-start.4 = (bf16[528,128]{1,0:T(8,128)(2,1)S(1)}, bf16[528,128]{1,0:T(8,128)(2,1)S(1)}, u32[]{:S(2)}, u32[]{:S(2)}) collective-permute-start(bf16[528,128]{1,0:T(8,128)(2,1)S(1)} %get-tuple-element.87.refs_0_), channel_id=1, source_target_pairs={{0,16},{2,18},{4,20},{6,22},{8,24},{10,26},{12,28},{14,30},{16,0},... | collective-permute-start | bytes 405512 | tf_op jit(solution)/shard_map/ppermute | solution.py:588
  25.5 2.8 %copy-start = (bf16[512,2048]{1,0:T(8,128)(2,1)S(1)}, bf16[512,2048]{1,0:T(8,128)(2,1)}, u32[]{:S(2)}) copy-start(bf16[512,2048]{1,0:T(8,128)(2,1)} %gate.7) | copy-start | bytes 6291460
  25.5 2.8 %copy-start.1 = (f32[2048]{0:T(1024)S(1)}, f32[2048]{0:T(1024)}, u32[]{:S(2)}) copy-start(f32[2048]{0:T(1024)} %param.12) | copy-start | bytes 24580
  26.7 5.1 %collective-permute-start.5 = (bf16[528,128]{1,0:T(8,128)(2,1)S(1)}, bf16[528,128]{1,0:T(8,128)(2,1)S(1)}, u32[]{:S(2)}, u32[]{:S(2)}) collective-permute-start(bf16[528,128]{1,0:T(8,128)(2,1)S(1)} %get-tuple-element.91._), channel_id=1, source_target_pairs={{0,4},{2,6},{4,0},{6,2},{8,12},{10,14},{12,8},{14,10},{16,20},{18,... | collective-permute-start | bytes 405512 | tf_op jit(solution)/shard_map/ppermute | solution.py:588
  32.0 1.6 %collective-permute-start.6 = (bf16[2,528,128]{2,1,0:T(8,128)(2,1)S(1)}, bf16[2,528,128]{2,1,0:T(8,128)(2,1)S(1)}, u32[]{:S(2)}, u32[]{:S(2)}) collective-permute-start(bf16[2,528,128]{2,1,0:T(8,128)(2,1)S(1)} %get-tuple-element.95), channel_id=1, source_target_pairs={{0,2},{2,0},{4,6},{6,4},{8,10},{10,8},{12,14},{14,12},{16,18},{18,... | collective-permute-start | bytes 811016 | tf_op jit(solution)/shard_map/ppermute | solution.py:588
  35.3 3.8 %collective-permute-start.7 = (f32[8,512]{1,0:T(8,128)S(1)}, f32[8,512]{1,0:T(8,128)S(1)}, u32[]{:S(2)}, u32[]{:S(2)}) collective-permute-start(f32[8,512]{1,0:T(8,128)S(1)} %get-tuple-element.102.refs_0_), channel_id=1, source_target_pairs={{0,1},{1,0},{2,3},{3,2},{4,5},{5,4},{6,7},{7,6},{8,9},{9,8},{10,11... | collective-permute-start | bytes 49160 | tf_op jit(solution)/shard_map/ppermute | solution.py:760
  40.5 1.6 %collective-permute-start.8 = (bf16[2,528,128]{2,1,0:T(8,128)(2,1)S(1)}, bf16[2,528,128]{2,1,0:T(8,128)(2,1)S(1)}, u32[]{:S(2)}, u32[]{:S(2)}) collective-permute-start(bf16[2,528,128]{2,1,0:T(8,128)(2,1)S(1)} %get-tuple-element.108), channel_id=1, source_target_pairs={{0,2},{2,0},{4,6},{6,4},{8,10},{10,8},{12,14},{14,12},{16,18},{18,... | collective-permute-start | bytes 811016 | tf_op jit(solution)/shard_map/ppermute | solution.py:588
  42.2 5.7 %collective-permute-start.9 = (bf16[528,128]{1,0:T(8,128)(2,1)S(1)}, bf16[528,128]{1,0:T(8,128)(2,1)S(1)}, u32[]{:S(2)}, u32[]{:S(2)}) collective-permute-start(bf16[528,128]{1,0:T(8,128)(2,1)S(1)} %get-tuple-element.110._), channel_id=1, source_target_pairs={{0,4},{2,6},{4,0},{6,2},{8,12},{10,14},{12,8},{14,10},{16,20},{18,... | collective-permute-start | bytes 405512 | tf_op jit(solution)/shard_map/ppermute | solution.py:588
  48.0 5.1 %collective-permute-start.10 = (bf16[528,128]{1,0:T(8,128)(2,1)S(1)}, bf16[528,128]{1,0:T(8,128)(2,1)S(1)}, u32[]{:S(2)}, u32[]{:S(2)}) collective-permute-start(bf16[528,128]{1,0:T(8,128)(2,1)S(1)} %get-tuple-element.117._), channel_id=1, source_target_pairs={{0,8},{2,10},{4,12},{6,14},{8,0},{10,2},{12,4},{14,6},{16,24},{18,... | collective-permute-start | bytes 405512 | tf_op jit(solution)/shard_map/ppermute | solution.py:588
  53.2 8.8 %collective-permute-start.11 = (bf16[528,128]{1,0:T(8,128)(2,1)S(1)}, bf16[528,128]{1,0:T(8,128)(2,1)S(1)}, u32[]{:S(2)}, u32[]{:S(2)}) collective-permute-start(bf16[528,128]{1,0:T(8,128)(2,1)S(1)} %get-tuple-element.120._), channel_id=1, source_target_pairs={{0,16},{2,18},{4,20},{6,22},{8,24},{10,26},{12,28},{14,30},{16,0},... | collective-permute-start | bytes 405512 | tf_op jit(solution)/shard_map/ppermute | solution.py:588
  62.2 5.9 %collective-permute-start.12 = (bf16[528,128]{1,0:T(8,128)(2,1)S(1)}, bf16[528,128]{1,0:T(8,128)(2,1)S(1)}, u32[]{:S(2)}, u32[]{:S(2)}) collective-permute-start(bf16[528,128]{1,0:T(8,128)(2,1)S(1)} %get-tuple-element.125._), channel_id=1, source_target_pairs={{0,4},{2,6},{4,0},{6,2},{8,12},{10,14},{12,8},{14,10},{16,20},{18,... | collective-permute-start | bytes 405512 | tf_op jit(solution)/shard_map/ppermute | solution.py:588
  68.3 1.6 %collective-permute-start.13 = (bf16[2,528,128]{2,1,0:T(8,128)(2,1)S(1)}, bf16[2,528,128]{2,1,0:T(8,128)(2,1)S(1)}, u32[]{:S(2)}, u32[]{:S(2)}) collective-permute-start(bf16[2,528,128]{2,1,0:T(8,128)(2,1)S(1)} %get-tuple-element.130), channel_id=1, source_target_pairs={{0,2},{2,0},{4,6},{6,4},{8,10},{10,8},{12,14},{14,12},{16,18},{18,... | collective-permute-start | bytes 811016 | tf_op jit(solution)/shard_map/ppermute | solution.py:588

commit v11 on v10

--- a/solution.py
+++ b/solution.py
@@ -384,11 +384,13 @@
     dscaled_rows(heads, 1 - lax.axis_index("tp") if swaps else 1, gate, got, gain, dscaled)
 
 
-def diagonal(a, b):
+def states_of(state, j, count):
+    if count == 1:
+        return state[chunk(j), :]
     zero = jnp.zeros((HEAD, HEAD), BF16)
-    return jnp.concatenate(
-        [jnp.concatenate([a, zero], axis=1), jnp.concatenate([zero, b], axis=1)], axis=0
-    )
+    upper = jnp.concatenate([state[chunk(j), :], zero], axis=1)
+    lower = jnp.concatenate([zero, state[chunk(j + 1), :]], axis=1)
+    return jnp.concatenate([upper, lower], axis=0)
 
 
 def attention_body(heads, same, q, intra, dscaled, growth, state, *refs):
@@ -402,10 +404,7 @@
     for y in range(2):
         g = quarter_of(y, same)
         for j, h, count, c in several(g, hq):
-            if count == 2:
-                both[...] = nn(q[:, c], diagonal(state[y, chunk(j), :], state[y, chunk(j + 1), :]))
-            else:
-                both[:, 0:HEAD] = nn(q[:, c], state[y, chunk(j), :])
+            both[:, 0 : count * HEAD] = nn(q[:, c], states_of(state.at[y], j, count))
             for i in range(BLOCK // HEAD):
                 r = chunk(i)
                 a_sq = a_in = 0.0
@@ -433,7 +432,7 @@
     if same:
         rsb, coefb, _, dattn, out = refs
     else:
-        sum_a, sum_b, dattn, out, rsb, coefb = refs
+        sum_a, sum_b, _, dattn, out, rsb, coefb = refs
         total = sum_a[...] + sum_b[...]
         rs = lax.rsqrt(total[0:1, :] / channels + EPSILON)
         coef = total[1:2, :] * (rs * rs * rs) / channels
@@ -468,15 +467,23 @@
     return copy
 
 
-def gate_body(heads, gate, att, dscaled, scale, _, gate_grad, token, out, sems):
+def unscaled_gate_body(heads, gate, att, dscaled, out):
+    hq = heads // TEAM
+    for g in range(TEAM):
+        for j in range(hq):
+            _, c = head_at(g, hq, j)
+            closed = jax.nn.sigmoid(-gate[:, c].astype(F32))
+            out[:, c] = dscaled[:, c] * att[:, c] * closed
+
+
+def gate_body(heads, unscaled, scale, _, gate_grad, token, out, sems):
     hq = heads // TEAM
     token[...] = jnp.zeros_like(token)
     copies = []
     for g in range(TEAM):
         for j in range(hq):
             _, c = head_at(g, hq, j)
-            opened = jax.nn.sigmoid(gate[:, c].astype(F32))
-            out[g, :, chunk(j)] = (dscaled[:, c] * att[:, c] * scale[...] * (1.0 - opened)).astype(BF16)
+            out[g, :, chunk(j)] = (unscaled[:, c] * scale[...]).astype(BF16)
         copies.append(leave(out.at[g], gate_grad, sems.at[g], g, hq * HEAD))
     for copy in copies:
         copy.wait()
@@ -491,16 +498,18 @@
     token[...] = jnp.zeros_like(token)
     copies = []
     for slot, (state, g) in enumerate(by_quarter(mine, got)):
-        for j in range(hq):
-            h, c = head_at(g, hq, j)
-            line = row[pl.ds(h, 1), :]
-            for i in range(2):
-                d = dattn[half(i), c]
-                u = slice(0, (i + 1) * HALF)
-                table = decay_table(col[g, half(i), j : j + 1], line[:, u], True)
-                dscores = (nt(d, v[u, c]) * table).astype(BF16)
-                inter = nt(d, state[chunk(j), :]) * growth[g, half(i), j : j + 1]
-                out[slot, half(i), chunk(j)] = (inter + nn(dscores, k[u, c])).astype(BF16)
+        for j, first, count, cols in several(g, hq):
+            both = nt(dattn[:, cols], states_of(state, j, count))
+            for m in range(count):
+                h, c = head_at(g, hq, j + m)
+                line = row[pl.ds(h, 1), :]
+                for i in range(2):
+                    d = dattn[half(i), c]
+                    u = slice(0, (i + 1) * HALF)
+                    table = decay_table(col[g, half(i), j + m : j + m + 1], line[:, u], True)
+                    dscores = (nt(d, v[u, c]) * table).astype(BF16)
+                    inter = both[half(i), chunk(m)] * growth[g, half(i), j + m : j + m + 1]
+                    out[slot, half(i), chunk(j + m)] = (inter + nn(dscores, k[u, c])).astype(BF16)
         copies.append(leave(out.at[slot], query_grad, sems.at[slot], g, hq * HEAD))
     for copy in copies:
         copy.wait()
@@ -530,13 +539,14 @@
     return jnp.exp(sums[BLOCK - 1 : BLOCK, :] - sums)
 
 
-def final_rows(hq, y, j, same, k, v, dk, dv, shrink, state, key_out, value_out):
-    g = quarter_of(y, same)
-    _, c = head_at(g, hq, j)
-    fade = shrink[:, j : j + 1]
-    after = state[y, chunk(j), :]
-    key_out[y, :, chunk(j)] = (dk[:, c] + nt(v[:, c], after) * fade).astype(BF16)
-    value_out[y, :, chunk(j)] = (dv[:, c] + nn(k[:, c], after) * fade).astype(BF16)
+def final_rows(hq, y, j, count, c, k, v, dk, dv, shrink, state, key_out, value_out):
+    after = states_of(state.at[y], j, count)
+    key_side, value_side = nt(v[:, c], after), nn(k[:, c], after)
+    for m in range(count):
+        fade = shrink[:, j + m : j + m + 1]
+        own = pl.ds(pl.multiple_of(c.start + m * HEAD, HEAD), HEAD)
+        key_out[y, :, chunk(j + m)] = (dk[:, own] + key_side[:, chunk(m)] * fade).astype(BF16)
+        value_out[y, :, chunk(j + m)] = (dv[:, own] + value_side[:, chunk(m)] * fade).astype(BF16)
 
 
 def own_final_body(heads, k, v, dk, dv, col, state, key_out, value_out, gain_grad):
@@ -544,9 +554,10 @@
     for y in range(2):
         items = read_narrow(state.at[y], hq)
         shrink = fades(col, y, True)
-        for j in range(hq):
-            final_rows(hq, y, j, True, k, v, dk, dv, shrink, state, key_out, value_out)
-            gain_grad[:, head_at(quarter_of(y, True), hq, j)[1]] = items[j][2]
+        for j, _, count, c in several(quarter_of(y, True), hq):
+            final_rows(hq, y, j, count, c, k, v, dk, dv, shrink, state, key_out, value_out)
+            for m in range(j, j + count):
+                gain_grad[:, head_at(quarter_of(y, True), hq, m)[1]] = items[m][2]
 
 
 def final_body(heads, k, v, dk, dv, col, state, own_key, own_value, own_gain, *refs):
@@ -569,8 +580,8 @@
         items = read_narrow(state.at[y], hq)
         shrink = fades(col, y, False)
         for j, _, count, c in several(quarter_of(y, False), hq):
+            final_rows(hq, y, j, count, c, k, v, dk, dv, shrink, state, key_out, value_out)
             for m in range(j, j + count):
-                final_rows(hq, y, m, False, k, v, dk, dv, shrink, state, key_out, value_out)
                 gain_grad[:, head_at(quarter_of(y, False), hq, m)[1]] = items[m][2]
             place = slice(j * HEAD, (j + count) * HEAD)
             send(key_out.at[y, :, place], key_grad, c)
@@ -756,16 +767,20 @@
         small // 2,
         alias={5: 0},
     )
+    (unscaled_gate,) = call(
+        functools.partial(unscaled_gate_body, heads), [gate, att, dscaled], [f32(rows, width)], "unscaled_gate"
+    )
     if swaps:
         others = lax.ppermute(sums, "tp", [(0, 1), (1, 0)])
     else:
         others = lax.psum(sums, "tp") - sums
     dattn, give, scale, coef = call(
         functools.partial(dattn_body, heads, channels, False),
-        [att, dscaled, turned, gain_row, row, sums, others],
+        [att, dscaled, turned, gain_row, row, sums, others, unscaled_gate],
         [bf(rows, width), narrow2, tall, tall],
         "sent_dattn",
         flops=small // 2,
+        in_specs=[VMEM] * 7 + [ANY],
     )
     dattn, keep = call(
         functools.partial(dattn_body, heads, channels, True),
@@ -780,18 +795,18 @@
     def gate_beside(after):
         done["gate"], token = call(
             functools.partial(gate_body, heads),
-            [gate, att, dscaled, scale, after],
+            [unscaled_gate, scale, after],
             [bf(rows, width), f32(SIDE, HEAD)],
             "gate",
             out_scratch,
             small,
-            [VMEM] * 4 + [ANY],
+            [VMEM] * 2 + [ANY],
             [HBM, VMEM],
         )
         return token
 
     units = heads // min(hq, 2)
-    cuts = [0, units // 8, units // 2, units]
+    cuts = [0, units // 4, (5 * units) // 8, units]
 
     def key_value_beside(after):
         before = done.get("key_value", [])

time: 73.5 us -> 73 us (level)
  starting transfers between devices: 18.7 us -> 17.4 us
    ppermute x12, starting transfers between devices: 15 us -> 14 us  [swap(): return lax.ppermute(x, 'ctx', [(i, i ^ bit) for i in range(n)])]
    ppermute x1, waiting for transfers between devices: 2.69 us -> 1.68 us  [local(): others = lax.ppermute(sums, 'tp', [(0, 1), (1, 0)])]
    pallas_call x30 -> x31, Pallas kernels: 45.9 us -> 46.4 us  [call(): pl.pallas_call(body, in_specs=in_specs or [VMEM] * len(inputs), out_specs...]
  transfers between devices with their start and end apart: 14 -> 14, of which waited for: 10 -> 10; matrix products, arithmetic and copies ran while one was open for 0% -> 0% of each run, Pallas kernels for 49% -> 50%
where the time goes in v11:
time: 73 us; the launch traced here: 72.8 us
  Pallas kernels  46.4 us (64%)
  starting transfers between devices  17.4 us (24%)
  waiting for transfers between devices  7.35 us (10%)
  between operations  1.08 us (1%)
    pallas_call x31, Pallas kernels, call(): pl.pallas_call(body, in_specs=in_specs or [VMEM] * len(inputs), out_specs...  46.4 us
    ppermute x12, starting transfers between devices, swap(): return lax.ppermute(x, 'ctx', [(i, i ^ bit) for i in range(n)])  14 us
    ppermute x12, waiting for transfers between devices, swap(): return lax.ppermute(x, 'ctx', [(i, i ^ bit) for i in range(n)])  5.67 us
    ppermute x1, starting transfers between devices, local(): arrived = lax.ppermute(outs[4], 'tp', [(0, 1), (1, 0)])  2.56 us
    ppermute x1, waiting for transfers between devices, local(): others = lax.ppermute(sums, 'tp', [(0, 1), (1, 0)])  1.68 us
  transfers between devices with their start and end apart: 14, of which 10 were waited for; matrix products, arithmetic and copies ran while one was open for 0% of the time, Pallas kernels for 50%

profile of v11, /device:TPU:0, one launch (start us, length us, event | category | flops | bytes accessed | tf_op | source)
XLA Modules:
  0.0 72.8 jit_solution(7299161539644157585)
XLA Ops:
  0.6 2.8 %sent_states.1 = (f32[2,520,128]{2,1,0:T(8,128)S(1)}, f32[16,512]{1,0:T(8,128)S(1)}, bf16[512,2048]{1,0:T(8,128)(2,1)S(1)}, bf16[512,2048]{1,0:T(8,128)(2,1)S(1)}, bf16[256,2048]{1,0:T(8,128)(2,1)S(1)}) custom-call(bf16[512,2048]{1,0:T(8,128)(2,1)} %k_hbm.1, bf16[512,2048]{1,0:T(8,128)(2,1)} %v_hbm.1, f32[16,512]{1,0:T(8,128)} %ld_hbm.1, bf16[256,4096]{1,0:T(8,128)(2,1)} %grad.1), custom_call_target="tpu_custom_call" | custom-call | flops 134217728 | bytes 12132352 | tf_op jit(solution)/shard_map/sent_states/pallas_call | solution.py:125
  4.0 2.6 %collective-permute-start.3 = (bf16[256,2048]{1,0:T(8,128)(2,1)S(1)}, bf16[256,2048]{1,0:T(8,128)(2,1)S(1)}, u32[]{:S(2)}, u32[]{:S(2)}) collective-permute-start(bf16[256,2048]{1,0:T(8,128)(2,1)S(1)} %get-tuple-element.88), channel_id=1, source_target_pairs={{0,1},{1,0},{2,3},{3,2},{4,5},{5,4},{6,7},{7,6},{8,9},{9,8},{10,11... | collective-permute-start | bytes 3145736 | tf_op jit(solution)/shard_map/ppermute | solution.py:678
  7.5 1.6 %collective-permute-start.1 = (bf16[528,128]{1,0:T(8,128)(2,1)S(1)}, bf16[528,128]{1,0:T(8,128)(2,1)S(1)}, u32[]{:S(2)}, u32[]{:S(2)}) collective-permute-start(bf16[528,128]{1,0:T(8,128)(2,1)S(1)} %get-tuple-element.76._), channel_id=1, source_target_pairs={{0,4},{2,6},{4,0},{6,2},{8,12},{10,14},{12,8},{14,10},{16,20},{18,... | collective-permute-start | bytes 405512 | tf_op jit(solution)/shard_map/ppermute | solution.py:599
  9.1 1.6 %decays.1 = (f32[4,512,128]{2,1,0:T(8,128)S(1)}, f32[4,512,128]{2,1,0:T(8,128)S(1)}, bf16[512,2048]{1,0:T(8,128)(2,1)S(1)}) custom-call(f32[16,512]{1,0:T(8,128)S(1)} %get-tuple-element.74.row, bf16[512,2048]{1,0:T(8,128)(2,1)} %q_hbm.1, bf16[528,128]{1,0:T(8,128)(2,1)S(1)} %get-tuple-element.76._), custom_call_target="tpu_custom_call" | custom-call | bytes 6459392 | tf_op jit(solution)/shard_map/decays/pallas_call | solution.py:125
  10.7 1.6 %turned_probs.2 = (f32[16,256,512]{2,1,0:T(8,128)S(1)}, f32[16,256,256]{2,1,0:T(8,128)S(1)}, bf16[16,256,512]{2,1,0:T(8,128)(2,1)S(1)}, bf16[16,256,256]{2,1,0:T(8,128)(2,1)S(1)}) custom-call(bf16[512,2048]{1,0:T(8,128)(2,1)S(1)} %get-tuple-element.77.q, bf16[512,2048]{1,0:T(8,128)(2,1)S(1)} %get-tuple-element.72.k, f32[16,512]{1,0:T(8,128)S(1)} %get-tuple-element.74.row, ...), custom_call_target="tpu_custom_call" | custom-call | flops 536870912 | bytes 24285184 | tf_op jit(solution)/shard_map/turned_probs/pallas_call | solution.py:125
  13.3 1.6 %collective-permute-start.2 = (bf16[528,128]{1,0:T(8,128)(2,1)S(1)}, bf16[528,128]{1,0:T(8,128)(2,1)S(1)}, u32[]{:S(2)}, u32[]{:S(2)}) collective-permute-start(bf16[528,128]{1,0:T(8,128)(2,1)S(1)} %get-tuple-element.82._), channel_id=1, source_target_pairs={{0,8},{2,10},{4,12},{6,14},{8,0},{10,2},{12,4},{14,6},{16,24},{18,... | collective-permute-start | bytes 405512 | tf_op jit(solution)/shard_map/ppermute | solution.py:599
  15.0 1.6 %turned_probs.3 = (f32[16,256,512]{2,1,0:T(8,128)S(1)}, f32[16,256,256]{2,1,0:T(8,128)S(1)}, bf16[16,256,512]{2,1,0:T(8,128)(2,1)S(1)}, bf16[16,256,256]{2,1,0:T(8,128)(2,1)S(1)}) custom-call(bf16[512,2048]{1,0:T(8,128)(2,1)S(1)} %get-tuple-element.77.q, ...), custom_call_target="tpu_custom_call", output_to_operand_aliasing={{0}: (5, {}), {1}: (6, {}), {2}: (7, {}), {3}: (8, {})} | custom-call | flops 536870912 | bytes 43159552 | tf_op jit(solution)/shard_map/turned_probs/pallas_call | solution.py:125
  16.6 1.4 %intra.2.refs_1_ = f32[512,2048]{1,0:T(8,128)S(1)} custom-call(bf16[512,2048]{1,0:T(8,128)(2,1)S(1)} %get-tuple-element.77.q, bf16[512,2048]{1,0:T(8,128)(2,1)S(1)} %get-tuple-element.72.k, bf16[512,2048]{1,0:T(8,128)(2,1)S(1)} %get-tuple-element.73.v, f32[16,512]{1,0:T(8,128)S(1)} %get-tuple-element.74.row, f32[4,512,128]{2,1,0:T(8,128)S(1)} %get-tuple-element.78.col, ...), custom_call_target="tpu_custom_call" | custom-call | flops 536870912 | bytes 13664256 | tf_op jit(solution)/shard_map/intra/pallas_call | solution.py:125
  18.7 2.7 %collective-permute-start.4 = (bf16[528,128]{1,0:T(8,128)(2,1)S(1)}, bf16[528,128]{1,0:T(8,128)(2,1)S(1)}, u32[]{:S(2)}, u32[]{:S(2)}) collective-permute-start(bf16[528,128]{1,0:T(8,128)(2,1)S(1)} %get-tuple-element.87.refs_0_), channel_id=1, source_target_pairs={{0,16},{2,18},{4,20},{6,22},{8,24},{10,26},{12,28},{14,30},{16,0},... | collective-permute-start | bytes 405512 | tf_op jit(solution)/shard_map/ppermute | solution.py:599
  21.3 4.4 %intra.3.refs_0_ = f32[512,2048]{1,0:T(8,128)S(1)} custom-call(bf16[512,2048]{1,0:T(8,128)(2,1)S(1)} %get-tuple-element.77.q, bf16[512,2048]{1,0:T(8,128)(2,1)S(1)} %get-tuple-element.72.k, bf16[512,2048]{1,0:T(8,128)(2,1)S(1)} %get-tuple-element.73.v, f32[16,512]{1,0:T(8,128)S(1)} %get-tuple-element.74.row, ...), custom_call_target="tpu_custom_call", output_to_operand_aliasing={{}: (6, {})} | custom-call | flops 1610612736 | bytes 15896576 | tf_op jit(solution)/shard_map/intra/pallas_call | solution.py:125
  27.2 1.6 %collective-permute-start.5 = (bf16[528,128]{1,0:T(8,128)(2,1)S(1)}, bf16[528,128]{1,0:T(8,128)(2,1)S(1)}, u32[]{:S(2)}, u32[]{:S(2)}) collective-permute-start(bf16[528,128]{1,0:T(8,128)(2,1)S(1)} %get-tuple-element.91._), channel_id=1, source_target_pairs={{0,4},{2,6},{4,0},{6,2},{8,12},{10,14},{12,8},{14,10},{16,20},{18,... | collective-permute-start | bytes 405512 | tf_op jit(solution)/shard_map/ppermute | solution.py:599
  28.8 1.9 %own_dscaled.1 = (f32[512,2048]{1,0:T(8,128)S(1)}, bf16[2048,512]{1,0:T(8,128)(2,1)S(1)}) custom-call(bf16[512,2048]{1,0:T(8,128)(2,1)S(1)} %copy-done.2, bf16[256,4096]{1,0:T(8,128)(2,1)} %grad.1, f32[1,2048]{1,0:T(1,128)S(1)} %bitcast.2, bf16[512,2048]{1,0:T(8,128)(2,1)S(1)} %get-tuple-element.77.q, f32[16,512]{1,0:T(8,128)S(1)} %get-tuple-element.74.row, ...), custom_call_target="tpu_custom_call" | custom-call | flops 268435456 | bytes 12759040 | tf_op jit(solution)/shard_map/own_dscaled/pallas_call | solution.py:125
  34.2 1.6 %attention.3 = (f32[512,2048]{1,0:T(8,128)S(1)}, f32[8,512]{1,0:T(8,128)S(1)}) custom-call(bf16[512,2048]{1,0:T(8,128)(2,1)S(1)} %get-tuple-element.77.q, f32[512,2048]{1,0:T(8,128)S(1)} %intra.3.refs_0_, f32[512,2048]{1,0:T(8,128)S(1)} %got_dscaled.1.refs_0_.dscaled, f32[4,512,128]{2,1,0:T(8,128)S(1)} %get-tuple-element.93.growth, ...), custom_call_target="tpu_custom_call", output_to_operand_aliasing={{0}: (5, {})} | custom-call | flops 134217728 | bytes 20733952 | tf_op jit(solution)/shard_map/attention/pallas_call | solution.py:125
  37.9 1.7 %collective-permute-done.7.refs_1_ = f32[8,512]{1,0:T(8,128)S(1)} collective-permute-done((f32[8,512]{1,0:T(8,128)S(1)}, f32[8,512]{1,0:T(8,128)S(1)}, u32[]{:S(2)}, u32[]{:S(2)}) %collective-permute-start.7) | collective-permute-done | bytes 16416 | tf_op jit(solution)/shard_map/ppermute | solution.py:774
  39.6 1.4 %sent_dattn.1 = (bf16[512,2048]{1,0:T(8,128)(2,1)S(1)}, bf16[2,528,128]{2,1,0:T(8,128)(2,1)S(1)}, f32[512,128]{1,0:T(8,128)S(1)}, f32[512,128]{1,0:T(8,128)S(1)}) custom-call(f32[512,2048]{1,0:T(8,128)S(1)} %get-tuple-element.100.att, f32[512,2048]{1,0:T(8,128)S(1)} %got_dscaled.1.refs_0_.dscaled, bf16[2048,512]{1,0:T(8,128)(2,1)S(1)} %get-tuple-element.101.turned, ...), custom_call_target="tpu_custom_call" | custom-call | flops 134217728 | bytes 17645568 | tf_op jit(solution)/shard_map/sent_dattn/pallas_call | solution.py:125
  42.8 1.6 %collective-permute-start.9 = (bf16[528,128]{1,0:T(8,128)(2,1)S(1)}, bf16[528,128]{1,0:T(8,128)(2,1)S(1)}, u32[]{:S(2)}, u32[]{:S(2)}) collective-permute-start(bf16[528,128]{1,0:T(8,128)(2,1)S(1)} %get-tuple-element.110._), channel_id=1, source_target_pairs={{0,4},{2,6},{4,0},{6,2},{8,12},{10,14},{12,8},{14,10},{16,20},{18,... | collective-permute-start | bytes 405512 | tf_op jit(solution)/shard_map/ppermute | solution.py:599
  44.4 1.5 %gate.7 = (bf16[512,2048]{1,0:T(8,128)(2,1)}, f32[8,128]{1,0:T(8,128)S(1)}) custom-call(f32[512,2048]{1,0:T(8,128)S(1)} %unscaled_gate.1.refs_2_.unscaled, f32[512,128]{1,0:T(8,128)S(1)} %get-tuple-element.103.refs_0_.scale, bf16[528,128]{1,0:T(8,128)(2,1)S(1)} %get-tuple-element.110._), custom_call_target="tpu_custom_call" | custom-call | flops 268435456 | bytes 6692864 | tf_op jit(solution)/shard_map/gate/pallas_call | solution.py:125
  45.9 2.2 %key_value.3 = (f32[512,2048]{1,0:T(8,128)S(1)}, f32[512,2048]{1,0:T(8,128)S(1)}) custom-call(bf16[512,2048]{1,0:T(8,128)(2,1)S(1)} %get-tuple-element.77.q, bf16[512,2048]{1,0:T(8,128)(2,1)S(1)} %get-tuple-element.73.v, bf16[512,2048]{1,0:T(8,128)(2,1)S(1)} %get-tuple-element.106.dattn, f32[16,256,512]{2,1,0:T(8,128)S(1)} %get-tuple-element.111.table0, ...), custom_call_target="tpu_custom_call" | custom-call | flops 1073741824 | bytes 33558528 | tf_op jit(solution)/shard_map/key_value/pallas_call | solution.py:125
  49.2 3.5 %key_value.4 = (f32[512,2048]{1,0:T(8,128)S(1)}, f32[512,2048]{1,0:T(8,128)S(1)}) custom-call(bf16[512,2048]{1,0:T(8,128)(2,1)S(1)} %get-tuple-element.77.q, bf16[512,2048]{1,0:T(8,128)(2,1)S(1)} %get-tuple-element.73.v, bf16[512,2048]{1,0:T(8,128)(2,1)S(1)} %get-tuple-element.106.dattn, ...), custom_call_target="tpu_custom_call", output_to_operand_aliasing={{0}: (8, {}), {1}: (9, {})} | custom-call | flops 1610612736 | bytes 42078208 | tf_op jit(solution)/shard_map/key_value/pallas_call | solution.py:125
  53.7 1.9 %collective-permute-start.11 = (bf16[528,128]{1,0:T(8,128)(2,1)S(1)}, bf16[528,128]{1,0:T(8,128)(2,1)S(1)}, u32[]{:S(2)}, u32[]{:S(2)}) collective-permute-start(bf16[528,128]{1,0:T(8,128)(2,1)S(1)} %get-tuple-element.120._), channel_id=1, source_target_pairs={{0,16},{2,18},{4,20},{6,22},{8,24},{10,26},{12,28},{14,30},{16,0},... | collective-permute-start | bytes 405512 | tf_op jit(solution)/shard_map/ppermute | solution.py:599
  55.7 6.8 %query.1 = (bf16[512,2048]{1,0:T(8,128)(2,1)}, f32[8,128]{1,0:T(8,128)S(1)}) custom-call(bf16[512,2048]{1,0:T(8,128)(2,1)S(1)} %get-tuple-element.72.k, bf16[512,2048]{1,0:T(8,128)(2,1)S(1)} %get-tuple-element.73.v, bf16[512,2048]{1,0:T(8,128)(2,1)S(1)} %get-tuple-element.106.dattn, f32[16,512]{1,0:T(8,128)S(1)} %get-tuple-element.74.row, ...), custom_call_target="tpu_custom_call" | custom-call | flops 2415919104 | bytes 11198464 | tf_op jit(solution)/shard_map/query/pallas_call | solution.py:125
  62.6 1.6 %collective-permute-start.12 = (bf16[528,128]{1,0:T(8,128)(2,1)S(1)}, bf16[528,128]{1,0:T(8,128)(2,1)S(1)}, u32[]{:S(2)}, u32[]{:S(2)}) collective-permute-start(bf16[528,128]{1,0:T(8,128)(2,1)S(1)} %get-tuple-element.125._), channel_id=1, source_target_pairs={{0,4},{2,6},{4,0},{6,2},{8,12},{10,14},{12,8},{14,10},{16,20},{18,... | collective-permute-start | bytes 405512 | tf_op jit(solution)/shard_map/ppermute | solution.py:599
  64.2 3.3 %key_value.5 = (f32[512,2048]{1,0:T(8,128)S(1)}, f32[512,2048]{1,0:T(8,128)S(1)}) custom-call(bf16[512,2048]{1,0:T(8,128)(2,1)S(1)} %get-tuple-element.77.q, bf16[512,2048]{1,0:T(8,128)(2,1)S(1)} %get-tuple-element.73.v, bf16[512,2048]{1,0:T(8,128)(2,1)S(1)} %get-tuple-element.106.dattn, ...), custom_call_target="tpu_custom_call", output_to_operand_aliasing={{0}: (8, {}), {1}: (9, {})} | custom-call | flops 1610612736 | bytes 42078208 | tf_op jit(solution)/shard_map/key_value/pallas_call | solution.py:125
  69.5 3.1 %final.1 = (bf16[512,2048]{1,0:T(8,128)(2,1)}, bf16[512,2048]{1,0:T(8,128)(2,1)}, f32[1,2048]{1,0:T(1,128)}) custom-call(bf16[512,2048]{1,0:T(8,128)(2,1)S(1)} %get-tuple-element.72.k, bf16[512,2048]{1,0:T(8,128)(2,1)S(1)} %get-tuple-element.73.v, f32[512,2048]{1,0:T(8,128)S(1)} %get-tuple-element.127.refs_0_.dk, f32[512,2048]{1,0:T(8,128)S(1)} %get-tuple-element.128.dv, ...), custom_call_target="tpu_custom_call" | custom-call | flops 268435456 | bytes 20209664 | tf_op jit(solution)/shard_map/final/pallas_call | solution.py:125
  (43 shorter events, 16.1 us)
Async XLA Ops:
  3.5 3.9 %collective-permute-start = (f32[2,520,128]{2,1,0:T(8,128)S(1)}, f32[2,520,128]{2,1,0:T(8,128)S(1)}, u32[]{:S(2)}, u32[]{:S(2)}) collective-permute-start(f32[2,520,128]{2,1,0:T(8,128)S(1)} %get-tuple-element.75), channel_id=1, source_target_pairs={{0,2},{2,0},{4,6},{6,4},{8,10},{10,8},{12,14},{14,12},{16,18},{18,... | collective-permute-start | bytes 1597448 | tf_op jit(solution)/shard_map/ppermute | solution.py:599
  4.0 26.8 %collective-permute-start.3 = (bf16[256,2048]{1,0:T(8,128)(2,1)S(1)}, bf16[256,2048]{1,0:T(8,128)(2,1)S(1)}, u32[]{:S(2)}, u32[]{:S(2)}) collective-permute-start(bf16[256,2048]{1,0:T(8,128)(2,1)S(1)} %get-tuple-element.88), channel_id=1, source_target_pairs={{0,1},{1,0},{2,3},{3,2},{4,5},{5,4},{6,7},{7,6},{8,9},{9,8},{10,11... | collective-permute-start | bytes 3145736 | tf_op jit(solution)/shard_map/ppermute | solution.py:678
  7.5 5.7 %collective-permute-start.1 = (bf16[528,128]{1,0:T(8,128)(2,1)S(1)}, bf16[528,128]{1,0:T(8,128)(2,1)S(1)}, u32[]{:S(2)}, u32[]{:S(2)}) collective-permute-start(bf16[528,128]{1,0:T(8,128)(2,1)S(1)} %get-tuple-element.76._), channel_id=1, source_target_pairs={{0,4},{2,6},{4,0},{6,2},{8,12},{10,14},{12,8},{14,10},{16,20},{18,... | collective-permute-start | bytes 405512 | tf_op jit(solution)/shard_map/ppermute | solution.py:599
  13.3 5.3 %collective-permute-start.2 = (bf16[528,128]{1,0:T(8,128)(2,1)S(1)}, bf16[528,128]{1,0:T(8,128)(2,1)S(1)}, u32[]{:S(2)}, u32[]{:S(2)}) collective-permute-start(bf16[528,128]{1,0:T(8,128)(2,1)S(1)} %get-tuple-element.82._), channel_id=1, source_target_pairs={{0,8},{2,10},{4,12},{6,14},{8,0},{10,2},{12,4},{14,6},{16,24},{18,... | collective-permute-start | bytes 405512 | tf_op jit(solution)/shard_map/ppermute | solution.py:599
  16.6 2.0 %copy-start = (bf16[16,256,512]{2,1,0:T(8,128)(2,1)}, bf16[16,256,512]{2,1,0:T(8,128)(2,1)S(1)}, u32[]{:S(2)}) copy-start(bf16[16,256,512]{2,1,0:T(8,128)(2,1)S(1)} %get-tuple-element.113.probs0) | copy-start | bytes 12582916
  18.7 8.4 %collective-permute-start.4 = (bf16[528,128]{1,0:T(8,128)(2,1)S(1)}, bf16[528,128]{1,0:T(8,128)(2,1)S(1)}, u32[]{:S(2)}, u32[]{:S(2)}) collective-permute-start(bf16[528,128]{1,0:T(8,128)(2,1)S(1)} %get-tuple-element.87.refs_0_), channel_id=1, source_target_pairs={{0,16},{2,18},{4,20},{6,22},{8,24},{10,26},{12,28},{14,30},{16,0},... | collective-permute-start | bytes 405512 | tf_op jit(solution)/shard_map/ppermute | solution.py:599
  25.7 3.1 %copy-start.2 = (bf16[512,2048]{1,0:T(8,128)(2,1)S(1)}, bf16[512,2048]{1,0:T(8,128)(2,1)}, u32[]{:S(2)}) copy-start(bf16[512,2048]{1,0:T(8,128)(2,1)} %gate.6) | copy-start | bytes 6291460
  25.7 3.1 %copy-start.3 = (f32[2048]{0:T(1024)S(1)}, f32[2048]{0:T(1024)}, u32[]{:S(2)}) copy-start(f32[2048]{0:T(1024)} %param.12) | copy-start | bytes 24580
  27.2 5.1 %collective-permute-start.5 = (bf16[528,128]{1,0:T(8,128)(2,1)S(1)}, bf16[528,128]{1,0:T(8,128)(2,1)S(1)}, u32[]{:S(2)}, u32[]{:S(2)}) collective-permute-start(bf16[528,128]{1,0:T(8,128)(2,1)S(1)} %get-tuple-element.91._), channel_id=1, source_target_pairs={{0,4},{2,6},{4,0},{6,2},{8,12},{10,14},{12,8},{14,10},{16,20},{18,... | collective-permute-start | bytes 405512 | tf_op jit(solution)/shard_map/ppermute | solution.py:599
  32.6 1.6 %collective-permute-start.6 = (bf16[2,528,128]{2,1,0:T(8,128)(2,1)S(1)}, bf16[2,528,128]{2,1,0:T(8,128)(2,1)S(1)}, u32[]{:S(2)}, u32[]{:S(2)}) collective-permute-start(bf16[2,528,128]{2,1,0:T(8,128)(2,1)S(1)} %get-tuple-element.95), channel_id=1, source_target_pairs={{0,2},{2,0},{4,6},{6,4},{8,10},{10,8},{12,14},{14,12},{16,18},{18,... | collective-permute-start | bytes 811016 | tf_op jit(solution)/shard_map/ppermute | solution.py:599
  35.8 3.8 %collective-permute-start.7 = (f32[8,512]{1,0:T(8,128)S(1)}, f32[8,512]{1,0:T(8,128)S(1)}, u32[]{:S(2)}, u32[]{:S(2)}) collective-permute-start(f32[8,512]{1,0:T(8,128)S(1)} %get-tuple-element.102.refs_0_), channel_id=1, source_target_pairs={{0,1},{1,0},{2,3},{3,2},{4,5},{5,4},{6,7},{7,6},{8,9},{9,8},{10,11... | collective-permute-start | bytes 49160 | tf_op jit(solution)/shard_map/ppermute | solution.py:774
  41.1 1.6 %collective-permute-start.8 = (bf16[2,528,128]{2,1,0:T(8,128)(2,1)S(1)}, bf16[2,528,128]{2,1,0:T(8,128)(2,1)S(1)}, u32[]{:S(2)}, u32[]{:S(2)}) collective-permute-start(bf16[2,528,128]{2,1,0:T(8,128)(2,1)S(1)} %get-tuple-element.108), channel_id=1, source_target_pairs={{0,2},{2,0},{4,6},{6,4},{8,10},{10,8},{12,14},{14,12},{16,18},{18,... | collective-permute-start | bytes 811016 | tf_op jit(solution)/shard_map/ppermute | solution.py:599
  42.3 3.6 %copy-start.1 = (bf16[16,256,512]{2,1,0:T(8,128)(2,1)S(1)}, bf16[16,256,512]{2,1,0:T(8,128)(2,1)}, u32[]{:S(2)}) copy-start(bf16[16,256,512]{2,1,0:T(8,128)(2,1)} %copy-done) | copy-start | bytes 12582916
  42.8 5.7 %collective-permute-start.9 = (bf16[528,128]{1,0:T(8,128)(2,1)S(1)}, bf16[528,128]{1,0:T(8,128)(2,1)S(1)}, u32[]{:S(2)}, u32[]{:S(2)}) collective-permute-start(bf16[528,128]{1,0:T(8,128)(2,1)S(1)} %get-tuple-element.110._), channel_id=1, source_target_pairs={{0,4},{2,6},{4,0},{6,2},{8,12},{10,14},{12,8},{14,10},{16,20},{18,... | collective-permute-start | bytes 405512 | tf_op jit(solution)/shard_map/ppermute | solution.py:599
  48.6 5.1 %collective-permute-start.10 = (bf16[528,128]{1,0:T(8,128)(2,1)S(1)}, bf16[528,128]{1,0:T(8,128)(2,1)S(1)}, u32[]{:S(2)}, u32[]{:S(2)}) collective-permute-start(bf16[528,128]{1,0:T(8,128)(2,1)S(1)} %get-tuple-element.117._), channel_id=1, source_target_pairs={{0,8},{2,10},{4,12},{6,14},{8,0},{10,2},{12,4},{14,6},{16,24},{18,... | collective-permute-start | bytes 405512 | tf_op jit(solution)/shard_map/ppermute | solution.py:599
  53.7 8.7 %collective-permute-start.11 = (bf16[528,128]{1,0:T(8,128)(2,1)S(1)}, bf16[528,128]{1,0:T(8,128)(2,1)S(1)}, u32[]{:S(2)}, u32[]{:S(2)}) collective-permute-start(bf16[528,128]{1,0:T(8,128)(2,1)S(1)} %get-tuple-element.120._), channel_id=1, source_target_pairs={{0,16},{2,18},{4,20},{6,22},{8,24},{10,26},{12,28},{14,30},{16,0},... | collective-permute-start | bytes 405512 | tf_op jit(solution)/shard_map/ppermute | solution.py:599
  62.6 5.1 %collective-permute-start.12 = (bf16[528,128]{1,0:T(8,128)(2,1)S(1)}, bf16[528,128]{1,0:T(8,128)(2,1)S(1)}, u32[]{:S(2)}, u32[]{:S(2)}) collective-permute-start(bf16[528,128]{1,0:T(8,128)(2,1)S(1)} %get-tuple-element.125._), channel_id=1, source_target_pairs={{0,4},{2,6},{4,0},{6,2},{8,12},{10,14},{12,8},{14,10},{16,20},{18,... | collective-permute-start | bytes 405512 | tf_op jit(solution)/shard_map/ppermute | solution.py:599
  67.9 1.6 %collective-permute-start.13 = (bf16[2,528,128]{2,1,0:T(8,128)(2,1)S(1)}, bf16[2,528,128]{2,1,0:T(8,128)(2,1)S(1)}, u32[]{:S(2)}, u32[]{:S(2)}) collective-permute-start(bf16[2,528,128]{2,1,0:T(8,128)(2,1)S(1)} %get-tuple-element.130), channel_id=1, source_target_pairs={{0,2},{2,0},{4,6},{6,4},{8,10},{10,8},{12,14},{14,12},{16,18},{18,... | collective-permute-start | bytes 811016 | tf_op jit(solution)/shard_map/ppermute | solution.py:599

commit v12 on v11

--- a/solution.py
+++ b/solution.py
@@ -467,7 +467,7 @@
     return copy
 
 
-def unscaled_gate_body(heads, gate, att, dscaled, out):
+def unscaled_gate_body(heads, gate, att, dscaled, _, out):
     hq = heads // TEAM
     for g in range(TEAM):
         for j in range(hq):
@@ -493,24 +493,26 @@
     return [(ref.at[y], quarter_of(y, same)) for ref, same in ((mine, True), (got, False)) for y in range(2)]
 
 
-def query_body(heads, k, v, dattn, row, col, growth, mine, got, _, query_grad, token, out, sems):
-    hq = heads // TEAM
+def query_body(heads, first, last, k, v, dattn, row, col, growth, mine, got, _, *refs):
+    hq = heads // TEAM
+    query_grad, token, out, sems = refs[-4:]
     token[...] = jnp.zeros_like(token)
+    pairs = [(state, g, *pair) for state, g in by_quarter(mine, got) for pair in several(g, hq)]
     copies = []
-    for slot, (state, g) in enumerate(by_quarter(mine, got)):
-        for j, first, count, cols in several(g, hq):
-            both = nt(dattn[:, cols], states_of(state, j, count))
-            for m in range(count):
-                h, c = head_at(g, hq, j + m)
-                line = row[pl.ds(h, 1), :]
-                for i in range(2):
-                    d = dattn[half(i), c]
-                    u = slice(0, (i + 1) * HALF)
-                    table = decay_table(col[g, half(i), j + m : j + m + 1], line[:, u], True)
-                    dscores = (nt(d, v[u, c]) * table).astype(BF16)
-                    inter = both[half(i), chunk(m)] * growth[g, half(i), j + m : j + m + 1]
-                    out[slot, half(i), chunk(j + m)] = (inter + nn(dscores, k[u, c])).astype(BF16)
-        copies.append(leave(out.at[slot], query_grad, sems.at[slot], g, hq * HEAD))
+    for n, (state, g, j, _, count, cols) in enumerate(pairs[first:last]):
+        for m in range(count):
+            h, c = head_at(g, hq, j + m)
+            line = row[pl.ds(h, 1), :]
+            for i in range(2):
+                d = dattn[half(i), c]
+                u = slice(0, (i + 1) * HALF)
+                table = decay_table(col[g, half(i), j + m : j + m + 1], line[:, u], True)
+                dscores = (nt(d, v[u, c]) * table).astype(BF16)
+                inter = nt(d, state[chunk(j + m), :]) * growth[g, half(i), j + m : j + m + 1]
+                out[n, half(i), chunk(m)] = (inter + nn(dscores, k[u, c])).astype(BF16)
+        copy = pltpu.make_async_copy(out.at[n, :, 0 : count * HEAD], query_grad.at[:, cols], sems.at[n])
+        copy.start()
+        copies.append(copy)
     for copy in copies:
         copy.wait()
 
@@ -545,22 +547,32 @@
     for m in range(count):
         fade = shrink[:, j + m : j + m + 1]
         own = pl.ds(pl.multiple_of(c.start + m * HEAD, HEAD), HEAD)
-        key_out[y, :, chunk(j + m)] = (dk[:, own] + key_side[:, chunk(m)] * fade).astype(BF16)
-        value_out[y, :, chunk(j + m)] = (dv[:, own] + value_side[:, chunk(m)] * fade).astype(BF16)
-
-
-def own_final_body(heads, k, v, dk, dv, col, state, key_out, value_out, gain_grad):
-    hq = heads // TEAM
+        key_out[:, chunk(j + m)] = (dk[:, own] + key_side[:, chunk(m)] * fade).astype(BF16)
+        value_out[:, chunk(j + m)] = (dv[:, own] + value_side[:, chunk(m)] * fade).astype(BF16)
+
+
+def own_final_body(heads, k, v, dk, dv, col, state, key_grad, value_grad, own_key, own_value, gain_grad, key_out, value_out, sems):
+    hq = heads // TEAM
+    copies = []
     for y in range(2):
         items = read_narrow(state.at[y], hq)
         shrink = fades(col, y, True)
         for j, _, count, c in several(quarter_of(y, True), hq):
-            final_rows(hq, y, j, count, c, k, v, dk, dv, shrink, state, key_out, value_out)
+            outs = (key_out, value_out) if y == 0 else (own_key, own_value)
+            final_rows(hq, y, j, count, c, k, v, dk, dv, shrink, state, *outs)
             for m in range(j, j + count):
                 gain_grad[:, head_at(quarter_of(y, True), hq, m)[1]] = items[m][2]
-
-
-def final_body(heads, k, v, dk, dv, col, state, own_key, own_value, own_gain, *refs):
+            if y == 0:
+                place = slice(j * HEAD, (j + count) * HEAD)
+                for out, dst in ((key_out, key_grad), (value_out, value_grad)):
+                    copy = pltpu.make_async_copy(out.at[:, place], dst.at[:, c], sems.at[len(copies)])
+                    copy.start()
+                    copies.append(copy)
+    for copy in copies:
+        copy.wait()
+
+
+def final_body(heads, k, v, dk, dv, col, state, own_key, own_value, own_gain, _key, _value, *refs):
     hq = heads // TEAM
     key_grad, value_grad, gain_grad, key_out, value_out, sems = refs
     copies = []
@@ -570,17 +582,16 @@
         copy.start()
         copies.append(copy)
 
-    for y in range(2):
-        for j, _, count, c in several(quarter_of(y, True), hq):
-            place = slice(j * HEAD, (j + count) * HEAD)
-            send(own_key.at[y, :, place], key_grad, c)
-            send(own_value.at[y, :, place], value_grad, c)
+    for j, _, count, c in several(quarter_of(1, True), hq):
+        place = slice(j * HEAD, (j + count) * HEAD)
+        send(own_key.at[:, place], key_grad, c)
+        send(own_value.at[:, place], value_grad, c)
     gain_grad[...] = own_gain[...]
     for y in range(2):
         items = read_narrow(state.at[y], hq)
         shrink = fades(col, y, False)
         for j, _, count, c in several(quarter_of(y, False), hq):
-            final_rows(hq, y, j, count, c, k, v, dk, dv, shrink, state, key_out, value_out)
+            final_rows(hq, y, j, count, c, k, v, dk, dv, shrink, state, key_out.at[y], value_out.at[y])
             for m in range(j, j + count):
                 gain_grad[:, head_at(quarter_of(y, False), hq, m)[1]] = items[m][2]
             place = slice(j * HEAD, (j + count) * HEAD)
@@ -768,7 +779,12 @@
         alias={5: 0},
     )
     (unscaled_gate,) = call(
-        functools.partial(unscaled_gate_body, heads), [gate, att, dscaled], [f32(rows, width)], "unscaled_gate"
+        functools.partial(unscaled_gate_body, heads),
+        [gate, att, dscaled, intra],
+        [f32(rows, width)],
+        "unscaled_gate",
+        in_specs=[VMEM] * 3 + [ANY],
+        alias={3: 0},
     )
     if swaps:
         others = lax.ppermute(sums, "tp", [(0, 1), (1, 0)])
@@ -826,38 +842,52 @@
     def gate_and_key_value(after):
         return key_value_beside(gate_beside(after))
 
+    pairs = TEAM * hq // min(hq, 2)
+
     def query_beside(after):
+        before = [done["query"]] if "query" in done else []
+        first, last = (pairs // 8, pairs) if before else (0, pairs // 8)
         done["query"], token = call(
-            functools.partial(query_body, heads),
-            [keys, values, dattn, row, col, growth, mine, got, after],
+            functools.partial(query_body, heads, first, last),
+            [keys, values, dattn, row, col, growth, mine, got, after, *before],
             [bf(rows, width), f32(SIDE, HEAD)],
             "query",
-            out_scratch,
-            2 * large + small,
-            [VMEM] * 8 + [ANY],
+            [pltpu.VMEM((pairs, rows, 2 * HEAD), BF16), pltpu.SemaphoreType.DMA((pairs,))],
+            (2 * large + small) * (last - first) // pairs,
+            [VMEM] * 8 + [ANY] + [HBM] * len(before),
             [HBM, VMEM],
+            {9: 0} if before else None,
         )
         return token
 
-    work = {"pair": gate_and_key_value, "one": key_value_beside, "last": query_beside, "pair_back": key_value_beside}
+    def key_value_and_query(after):
+        return query_beside(key_value_beside(after))
+
+    work = {"pair": gate_and_key_value, "one": key_value_and_query, "last": query_beside, "pair_back": key_value_beside}
     back_mine, back_got = scan(True, keep, give, work)
     gate_grad, query_grad, (dk, dv) = done["gate"], done["query"], done["key_value"]
-    both = bf(2, rows, hq * HEAD)
-    own_key, own_value, own_gain = call(
+    quarter = bf(rows, hq * HEAD)
+    scratch = pltpu.VMEM(quarter.shape, BF16)
+    key_grad, value_grad, own_key, own_value, own_gain = call(
         functools.partial(own_final_body, heads),
         [keys, values, dk, dv, col, back_mine],
-        [both, both, f32(1, width)],
+        [bf(rows, width), bf(rows, width), quarter, quarter, f32(1, width)],
         "own_final",
-        flops=small,
+        [scratch, scratch, pltpu.SemaphoreType.DMA((2 * hq,))],
+        small,
+        out_specs=[HBM, HBM, VMEM, VMEM, VMEM],
     )
+    scratch = pltpu.VMEM((2, *quarter.shape), BF16)
     key_grad, value_grad, gain_grad = call(
         functools.partial(final_body, heads),
-        [keys, values, dk, dv, col, back_got, own_key, own_value, own_gain],
+        [keys, values, dk, dv, col, back_got, own_key, own_value, own_gain, key_grad, value_grad],
         [bf(rows, width), bf(rows, width), f32(1, width)],
         "final",
-        [pltpu.VMEM(both.shape, BF16)] * 2 + [pltpu.SemaphoreType.DMA((8 * hq,))],
+        [scratch, scratch, pltpu.SemaphoreType.DMA((8 * hq,))],
         small,
-        out_specs=[HBM, HBM, VMEM],
+        [VMEM] * 9 + [HBM] * 2,
+        [HBM, HBM, VMEM],
+        {9: 0, 10: 1},
     )
     return query_grad, key_grad, value_grad, gate_grad, gain_grad.reshape(width)
 

time: 73 us -> 74.3 us (1.018)
  starting transfers between devices: 17.4 us -> 18.9 us
  Pallas kernels: 46.4 us -> 47.6 us
    ppermute x12, starting transfers between devices: 14 us -> 15.3 us  [swap(): return lax.ppermute(x, 'ctx', [(i, i ^ bit) for i in range(n)])]
    pallas_call x31 -> x32, Pallas kernels: 46.4 us -> 47.6 us  [call(): pl.pallas_call(body, in_specs=in_specs or [VMEM] * len(inputs), out_specs...]
  transfers between devices with their start and end apart: 14 -> 14, of which waited for: 10 -> 10; matrix products, arithmetic and copies ran while one was open for 0% -> 0% of each run, Pallas kernels for 50% -> 51%
where the time goes in v12:
time: 74.3 us; the launch traced here: 74.1 us
  Pallas kernels  47.6 us (64%)
  starting transfers between devices  18.9 us (25%)
  waiting for transfers between devices  6.61 us (9%)
  between operations  1.06 us (1%)
    pallas_call x32, Pallas kernels, call(): pl.pallas_call(body, in_specs=in_specs or [VMEM] * len(inputs), out_specs...  47.6 us
    ppermute x12, starting transfers between devices, swap(): return lax.ppermute(x, 'ctx', [(i, i ^ bit) for i in range(n)])  15.3 us
    ppermute x12, waiting for transfers between devices, swap(): return lax.ppermute(x, 'ctx', [(i, i ^ bit) for i in range(n)])  5.11 us
    ppermute x1, starting transfers between devices, local(): arrived = lax.ppermute(outs[4], 'tp', [(0, 1), (1, 0)])  2.56 us
  transfers between devices with their start and end apart: 14, of which 10 were waited for; matrix products, arithmetic and copies ran while one was open for 0% of the time, Pallas kernels for 51%

profile of v12, /device:TPU:0, one launch (start us, length us, event | category | flops | bytes accessed | tf_op | source)
XLA Modules:
  0.0 74.1 jit_solution(14950675359527863643)
XLA Ops:
  0.6 2.8 %sent_states.1 = (f32[2,520,128]{2,1,0:T(8,128)S(1)}, f32[16,512]{1,0:T(8,128)S(1)}, bf16[512,2048]{1,0:T(8,128)(2,1)S(1)}, bf16[512,2048]{1,0:T(8,128)(2,1)S(1)}, bf16[256,2048]{1,0:T(8,128)(2,1)S(1)}) custom-call(bf16[512,2048]{1,0:T(8,128)(2,1)} %k_hbm.1, bf16[512,2048]{1,0:T(8,128)(2,1)} %v_hbm.1, f32[16,512]{1,0:T(8,128)} %ld_hbm.1, bf16[256,4096]{1,0:T(8,128)(2,1)} %grad.1), custom_call_target="tpu_custom_call" | custom-call | flops 134217728 | bytes 12132352 | tf_op jit(solution)/shard_map/sent_states/pallas_call | solution.py:125
  4.0 2.6 %collective-permute-start.3 = (bf16[256,2048]{1,0:T(8,128)(2,1)S(1)}, bf16[256,2048]{1,0:T(8,128)(2,1)S(1)}, u32[]{:S(2)}, u32[]{:S(2)}) collective-permute-start(bf16[256,2048]{1,0:T(8,128)(2,1)S(1)} %get-tuple-element.92), channel_id=1, source_target_pairs={{0,1},{1,0},{2,3},{3,2},{4,5},{5,4},{6,7},{7,6},{8,9},{9,8},{10,11... | collective-permute-start | bytes 3145736 | tf_op jit(solution)/shard_map/ppermute | solution.py:689
  7.5 1.6 %collective-permute-start.1 = (bf16[528,128]{1,0:T(8,128)(2,1)S(1)}, bf16[528,128]{1,0:T(8,128)(2,1)S(1)}, u32[]{:S(2)}, u32[]{:S(2)}) collective-permute-start(bf16[528,128]{1,0:T(8,128)(2,1)S(1)} %get-tuple-element.80._), channel_id=1, source_target_pairs={{0,4},{2,6},{4,0},{6,2},{8,12},{10,14},{12,8},{14,10},{16,20},{18,... | collective-permute-start | bytes 405512 | tf_op jit(solution)/shard_map/ppermute | solution.py:610
  9.1 1.6 %decays.1 = (f32[4,512,128]{2,1,0:T(8,128)S(1)}, f32[4,512,128]{2,1,0:T(8,128)S(1)}, bf16[512,2048]{1,0:T(8,128)(2,1)S(1)}) custom-call(f32[16,512]{1,0:T(8,128)S(1)} %get-tuple-element.78.row, bf16[512,2048]{1,0:T(8,128)(2,1)} %q_hbm.1, bf16[528,128]{1,0:T(8,128)(2,1)S(1)} %get-tuple-element.80._), custom_call_target="tpu_custom_call" | custom-call | bytes 6459392 | tf_op jit(solution)/shard_map/decays/pallas_call | solution.py:125
  10.7 1.6 %turned_probs.2 = (f32[16,256,512]{2,1,0:T(8,128)S(1)}, f32[16,256,256]{2,1,0:T(8,128)S(1)}, bf16[16,256,512]{2,1,0:T(8,128)(2,1)S(1)}, bf16[16,256,256]{2,1,0:T(8,128)(2,1)S(1)}) custom-call(bf16[512,2048]{1,0:T(8,128)(2,1)S(1)} %get-tuple-element.81.q, bf16[512,2048]{1,0:T(8,128)(2,1)S(1)} %get-tuple-element.76.k, f32[16,512]{1,0:T(8,128)S(1)} %get-tuple-element.78.row, ...), custom_call_target="tpu_custom_call" | custom-call | flops 536870912 | bytes 24285184 | tf_op jit(solution)/shard_map/turned_probs/pallas_call | solution.py:125
  13.3 1.6 %collective-permute-start.2 = (bf16[528,128]{1,0:T(8,128)(2,1)S(1)}, bf16[528,128]{1,0:T(8,128)(2,1)S(1)}, u32[]{:S(2)}, u32[]{:S(2)}) collective-permute-start(bf16[528,128]{1,0:T(8,128)(2,1)S(1)} %get-tuple-element.86._), channel_id=1, source_target_pairs={{0,8},{2,10},{4,12},{6,14},{8,0},{10,2},{12,4},{14,6},{16,24},{18,... | collective-permute-start | bytes 405512 | tf_op jit(solution)/shard_map/ppermute | solution.py:610
  15.0 1.6 %turned_probs.3 = (f32[16,256,512]{2,1,0:T(8,128)S(1)}, f32[16,256,256]{2,1,0:T(8,128)S(1)}, bf16[16,256,512]{2,1,0:T(8,128)(2,1)S(1)}, bf16[16,256,256]{2,1,0:T(8,128)(2,1)S(1)}) custom-call(bf16[512,2048]{1,0:T(8,128)(2,1)S(1)} %get-tuple-element.81.q, ...), custom_call_target="tpu_custom_call", output_to_operand_aliasing={{0}: (5, {}), {1}: (6, {}), {2}: (7, {}), {3}: (8, {})} | custom-call | flops 536870912 | bytes 43159552 | tf_op jit(solution)/shard_map/turned_probs/pallas_call | solution.py:125
  18.5 2.7 %collective-permute-start.4 = (bf16[528,128]{1,0:T(8,128)(2,1)S(1)}, bf16[528,128]{1,0:T(8,128)(2,1)S(1)}, u32[]{:S(2)}, u32[]{:S(2)}) collective-permute-start(bf16[528,128]{1,0:T(8,128)(2,1)S(1)} %get-tuple-element.91.refs_0_), channel_id=1, source_target_pairs={{0,16},{2,18},{4,20},{6,22},{8,24},{10,26},{12,28},{14,30},{16,0},... | collective-permute-start | bytes 405512 | tf_op jit(solution)/shard_map/ppermute | solution.py:610
  21.1 4.4 %intra.3.refs_0_._ = f32[512,2048]{1,0:T(8,128)S(1)} custom-call(bf16[512,2048]{1,0:T(8,128)(2,1)S(1)} %get-tuple-element.81.q, bf16[512,2048]{1,0:T(8,128)(2,1)S(1)} %get-tuple-element.76.k, bf16[512,2048]{1,0:T(8,128)(2,1)S(1)} %get-tuple-element.77.v, f32[16,512]{1,0:T(8,128)S(1)} %get-tuple-element.78.row, ...), custom_call_target="tpu_custom_call", output_to_operand_aliasing={{}: (6, {})} | custom-call | flops 1610612736 | bytes 15896576 | tf_op jit(solution)/shard_map/intra/pallas_call | solution.py:125
  26.7 1.6 %collective-permute-start.5 = (bf16[528,128]{1,0:T(8,128)(2,1)S(1)}, bf16[528,128]{1,0:T(8,128)(2,1)S(1)}, u32[]{:S(2)}, u32[]{:S(2)}) collective-permute-start(bf16[528,128]{1,0:T(8,128)(2,1)S(1)} %get-tuple-element.95._), channel_id=1, source_target_pairs={{0,4},{2,6},{4,0},{6,2},{8,12},{10,14},{12,8},{14,10},{16,20},{18,... | collective-permute-start | bytes 405512 | tf_op jit(solution)/shard_map/ppermute | solution.py:610
  28.3 1.9 %own_dscaled.1 = (f32[512,2048]{1,0:T(8,128)S(1)}, bf16[2048,512]{1,0:T(8,128)(2,1)S(1)}) custom-call(bf16[512,2048]{1,0:T(8,128)(2,1)S(1)} %copy-done, bf16[256,4096]{1,0:T(8,128)(2,1)} %grad.1, f32[1,2048]{1,0:T(1,128)S(1)} %bitcast.2, bf16[512,2048]{1,0:T(8,128)(2,1)S(1)} %get-tuple-element.81.q, f32[16,512]{1,0:T(8,128)S(1)} %get-tuple-element.78.row, ...), custom_call_target="tpu_custom_call" | custom-call | flops 268435456 | bytes 12759040 | tf_op jit(solution)/shard_map/own_dscaled/pallas_call | solution.py:125
  33.6 1.6 %attention.3 = (f32[512,2048]{1,0:T(8,128)S(1)}, f32[8,512]{1,0:T(8,128)S(1)}) custom-call(bf16[512,2048]{1,0:T(8,128)(2,1)S(1)} %get-tuple-element.81.q, f32[512,2048]{1,0:T(8,128)S(1)} %intra.3.refs_0_._, f32[512,2048]{1,0:T(8,128)S(1)} %got_dscaled.1.refs_0_.dscaled, ...), custom_call_target="tpu_custom_call", output_to_operand_aliasing={{0}: (5, {})} | custom-call | flops 134217728 | bytes 20733952 | tf_op jit(solution)/shard_map/attention/pallas_call | solution.py:125
  37.6 1.5 %collective-permute-done.7.refs_1_ = f32[8,512]{1,0:T(8,128)S(1)} collective-permute-done((f32[8,512]{1,0:T(8,128)S(1)}, f32[8,512]{1,0:T(8,128)S(1)}, u32[]{:S(2)}, u32[]{:S(2)}) %collective-permute-start.7) | collective-permute-done | bytes 16416 | tf_op jit(solution)/shard_map/ppermute | solution.py:790
  39.1 1.5 %sent_dattn.1 = (bf16[512,2048]{1,0:T(8,128)(2,1)S(1)}, bf16[2,528,128]{2,1,0:T(8,128)(2,1)S(1)}, f32[512,128]{1,0:T(8,128)S(1)}, f32[512,128]{1,0:T(8,128)S(1)}) custom-call(f32[512,2048]{1,0:T(8,128)S(1)} %get-tuple-element.104.att, f32[512,2048]{1,0:T(8,128)S(1)} %got_dscaled.1.refs_0_.dscaled, bf16[2048,512]{1,0:T(8,128)(2,1)S(1)} %get-tuple-element.105.turned, ...), custom_call_target="tpu_custom_call" | custom-call | flops 134217728 | bytes 17645568 | tf_op jit(solution)/shard_map/sent_dattn/pallas_call | solution.py:125
  42.2 1.6 %collective-permute-start.9 = (bf16[528,128]{1,0:T(8,128)(2,1)S(1)}, bf16[528,128]{1,0:T(8,128)(2,1)S(1)}, u32[]{:S(2)}, u32[]{:S(2)}) collective-permute-start(bf16[528,128]{1,0:T(8,128)(2,1)S(1)} %get-tuple-element.114._), channel_id=1, source_target_pairs={{0,4},{2,6},{4,0},{6,2},{8,12},{10,14},{12,8},{14,10},{16,20},{18,... | collective-permute-start | bytes 405512 | tf_op jit(solution)/shard_map/ppermute | solution.py:610
  43.8 1.5 %gate.7 = (bf16[512,2048]{1,0:T(8,128)(2,1)}, f32[8,128]{1,0:T(8,128)S(1)}) custom-call(f32[512,2048]{1,0:T(8,128)S(1)} %unscaled_gate.1.refs_2_.unscaled, f32[512,128]{1,0:T(8,128)S(1)} %get-tuple-element.107.refs_0_.scale, bf16[528,128]{1,0:T(8,128)(2,1)S(1)} %get-tuple-element.114._), custom_call_target="tpu_custom_call" | custom-call | flops 268435456 | bytes 6692864 | tf_op jit(solution)/shard_map/gate/pallas_call | solution.py:125
  45.3 2.2 %key_value.3 = (f32[512,2048]{1,0:T(8,128)S(1)}, f32[512,2048]{1,0:T(8,128)S(1)}) custom-call(bf16[512,2048]{1,0:T(8,128)(2,1)S(1)} %get-tuple-element.81.q, bf16[512,2048]{1,0:T(8,128)(2,1)S(1)} %get-tuple-element.77.v, bf16[512,2048]{1,0:T(8,128)(2,1)S(1)} %get-tuple-element.110.dattn, f32[16,256,512]{2,1,0:T(8,128)S(1)} %get-tuple-element.115.table0, ...), custom_call_target="tpu_custom_call" | custom-call | flops 1073741824 | bytes 33558528 | tf_op jit(solution)/shard_map/key_value/pallas_call | solution.py:125
  49.2 3.5 %key_value.4 = (f32[512,2048]{1,0:T(8,128)S(1)}, f32[512,2048]{1,0:T(8,128)S(1)}) custom-call(bf16[512,2048]{1,0:T(8,128)(2,1)S(1)} %get-tuple-element.81.q, bf16[512,2048]{1,0:T(8,128)(2,1)S(1)} %get-tuple-element.77.v, bf16[512,2048]{1,0:T(8,128)(2,1)S(1)} %get-tuple-element.110.dattn, ...), custom_call_target="tpu_custom_call", output_to_operand_aliasing={{0}: (8, {}), {1}: (9, {})} | custom-call | flops 1610612736 | bytes 42078208 | tf_op jit(solution)/shard_map/key_value/pallas_call | solution.py:125
  52.7 1.6 %query.2 = (bf16[512,2048]{1,0:T(8,128)(2,1)}, f32[8,128]{1,0:T(8,128)S(1)}) custom-call(bf16[512,2048]{1,0:T(8,128)(2,1)S(1)} %get-tuple-element.76.k, bf16[512,2048]{1,0:T(8,128)(2,1)S(1)} %get-tuple-element.77.v, bf16[512,2048]{1,0:T(8,128)(2,1)S(1)} %get-tuple-element.110.dattn, f32[16,512]{1,0:T(8,128)S(1)} %get-tuple-element.78.row, ...), custom_call_target="tpu_custom_call" | custom-call | flops 301989888 | bytes 15257600 | tf_op jit(solution)/shard_map/query/pallas_call | solution.py:125
  54.5 2.9 %collective-permute-start.11 = (bf16[528,128]{1,0:T(8,128)(2,1)S(1)}, bf16[528,128]{1,0:T(8,128)(2,1)S(1)}, u32[]{:S(2)}, u32[]{:S(2)}) collective-permute-start(bf16[528,128]{1,0:T(8,128)(2,1)S(1)} %get-tuple-element.125._), channel_id=1, source_target_pairs={{0,16},{2,18},{4,20},{6,22},{8,24},{10,26},{12,28},{14,30},{16,0},... | collective-permute-start | bytes 405512 | tf_op jit(solution)/shard_map/ppermute | solution.py:610
  57.3 5.6 %query.3 = (bf16[512,2048]{1,0:T(8,128)(2,1)}, f32[8,128]{1,0:T(8,128)S(1)}) custom-call(bf16[512,2048]{1,0:T(8,128)(2,1)S(1)} %get-tuple-element.76.k, bf16[512,2048]{1,0:T(8,128)(2,1)S(1)} %get-tuple-element.77.v, bf16[512,2048]{1,0:T(8,128)(2,1)S(1)} %get-tuple-element.110.dattn, ...), custom_call_target="tpu_custom_call", output_to_operand_aliasing={{0}: (9, {})} | custom-call | flops 2113929216 | bytes 13295616 | tf_op jit(solution)/shard_map/query/pallas_call | solution.py:125
  64.7 3.3 %key_value.5 = (f32[512,2048]{1,0:T(8,128)S(1)}, f32[512,2048]{1,0:T(8,128)S(1)}) custom-call(bf16[512,2048]{1,0:T(8,128)(2,1)S(1)} %get-tuple-element.81.q, bf16[512,2048]{1,0:T(8,128)(2,1)S(1)} %get-tuple-element.77.v, bf16[512,2048]{1,0:T(8,128)(2,1)S(1)} %get-tuple-element.110.dattn, ...), custom_call_target="tpu_custom_call", output_to_operand_aliasing={{0}: (8, {}), {1}: (9, {})} | custom-call | flops 1610612736 | bytes 42078208 | tf_op jit(solution)/shard_map/key_value/pallas_call | solution.py:125
  69.0 1.9 %own_final.1 = (bf16[512,2048]{1,0:T(8,128)(2,1)}, bf16[512,2048]{1,0:T(8,128)(2,1)}, bf16[512,512]{1,0:T(8,128)(2,1)S(1)}, bf16[512,512]{1,0:T(8,128)(2,1)S(1)}, f32[1,2048]{1,0:T(1,128)S(1)}) custom-call(bf16[512,2048]{1,0:T(8,128)(2,1)S(1)} %get-tuple-element.76.k, bf16[512,2048]{1,0:T(8,128)(2,1)S(1)} %get-tuple-element.77.v, ...), custom_call_target="tpu_custom_call" | custom-call | flops 268435456 | bytes 19152896 | tf_op jit(solution)/shard_map/own_final/pallas_call | solution.py:125
  70.9 3.0 %final.1 = (bf16[512,2048]{1,0:T(8,128)(2,1)}, bf16[512,2048]{1,0:T(8,128)(2,1)}, f32[1,2048]{1,0:T(1,128)}) custom-call(bf16[512,2048]{1,0:T(8,128)(2,1)S(1)} %get-tuple-element.76.k, bf16[512,2048]{1,0:T(8,128)(2,1)S(1)} %get-tuple-element.77.v, f32[512,2048]{1,0:T(8,128)S(1)} %get-tuple-element.133.refs_0_.dk, ...), custom_call_target="tpu_custom_call", output_to_operand_aliasing={{0}: (9, {}), {1}: (10, {})} | custom-call | flops 268435456 | bytes 23355392 | tf_op jit(solution)/shard_map/final/pallas_call | solution.py:125
  (40 shorter events, 17.5 us)
Async XLA Ops:
  3.5 3.9 %collective-permute-start = (f32[2,520,128]{2,1,0:T(8,128)S(1)}, f32[2,520,128]{2,1,0:T(8,128)S(1)}, u32[]{:S(2)}, u32[]{:S(2)}) collective-permute-start(f32[2,520,128]{2,1,0:T(8,128)S(1)} %get-tuple-element.79), channel_id=1, source_target_pairs={{0,2},{2,0},{4,6},{6,4},{8,10},{10,8},{12,14},{14,12},{16,18},{18,... | collective-permute-start | bytes 1597448 | tf_op jit(solution)/shard_map/ppermute | solution.py:610
  4.0 26.3 %collective-permute-start.3 = (bf16[256,2048]{1,0:T(8,128)(2,1)S(1)}, bf16[256,2048]{1,0:T(8,128)(2,1)S(1)}, u32[]{:S(2)}, u32[]{:S(2)}) collective-permute-start(bf16[256,2048]{1,0:T(8,128)(2,1)S(1)} %get-tuple-element.92), channel_id=1, source_target_pairs={{0,1},{1,0},{2,3},{3,2},{4,5},{5,4},{6,7},{7,6},{8,9},{9,8},{10,11... | collective-permute-start | bytes 3145736 | tf_op jit(solution)/shard_map/ppermute | solution.py:689
  7.5 5.7 %collective-permute-start.1 = (bf16[528,128]{1,0:T(8,128)(2,1)S(1)}, bf16[528,128]{1,0:T(8,128)(2,1)S(1)}, u32[]{:S(2)}, u32[]{:S(2)}) collective-permute-start(bf16[528,128]{1,0:T(8,128)(2,1)S(1)} %get-tuple-element.80._), channel_id=1, source_target_pairs={{0,4},{2,6},{4,0},{6,2},{8,12},{10,14},{12,8},{14,10},{16,20},{18,... | collective-permute-start | bytes 405512 | tf_op jit(solution)/shard_map/ppermute | solution.py:610
  13.3 5.1 %collective-permute-start.2 = (bf16[528,128]{1,0:T(8,128)(2,1)S(1)}, bf16[528,128]{1,0:T(8,128)(2,1)S(1)}, u32[]{:S(2)}, u32[]{:S(2)}) collective-permute-start(bf16[528,128]{1,0:T(8,128)(2,1)S(1)} %get-tuple-element.86._), channel_id=1, source_target_pairs={{0,8},{2,10},{4,12},{6,14},{8,0},{10,2},{12,4},{14,6},{16,24},{18,... | collective-permute-start | bytes 405512 | tf_op jit(solution)/shard_map/ppermute | solution.py:610
  18.5 8.1 %collective-permute-start.4 = (bf16[528,128]{1,0:T(8,128)(2,1)S(1)}, bf16[528,128]{1,0:T(8,128)(2,1)S(1)}, u32[]{:S(2)}, u32[]{:S(2)}) collective-permute-start(bf16[528,128]{1,0:T(8,128)(2,1)S(1)} %get-tuple-element.91.refs_0_), channel_id=1, source_target_pairs={{0,16},{2,18},{4,20},{6,22},{8,24},{10,26},{12,28},{14,30},{16,0},... | collective-permute-start | bytes 405512 | tf_op jit(solution)/shard_map/ppermute | solution.py:610
  26.6 1.7 %copy-start = (bf16[512,2048]{1,0:T(8,128)(2,1)S(1)}, bf16[512,2048]{1,0:T(8,128)(2,1)}, u32[]{:S(2)}) copy-start(bf16[512,2048]{1,0:T(8,128)(2,1)} %gate.6) | copy-start | bytes 6291460
  26.6 1.7 %copy-start.1 = (f32[2048]{0:T(1024)S(1)}, f32[2048]{0:T(1024)}, u32[]{:S(2)}) copy-start(f32[2048]{0:T(1024)} %param.12) | copy-start | bytes 24580
  26.7 5.1 %collective-permute-start.5 = (bf16[528,128]{1,0:T(8,128)(2,1)S(1)}, bf16[528,128]{1,0:T(8,128)(2,1)S(1)}, u32[]{:S(2)}, u32[]{:S(2)}) collective-permute-start(bf16[528,128]{1,0:T(8,128)(2,1)S(1)} %get-tuple-element.95._), channel_id=1, source_target_pairs={{0,4},{2,6},{4,0},{6,2},{8,12},{10,14},{12,8},{14,10},{16,20},{18,... | collective-permute-start | bytes 405512 | tf_op jit(solution)/shard_map/ppermute | solution.py:610
  32.0 1.6 %collective-permute-start.6 = (bf16[2,528,128]{2,1,0:T(8,128)(2,1)S(1)}, bf16[2,528,128]{2,1,0:T(8,128)(2,1)S(1)}, u32[]{:S(2)}, u32[]{:S(2)}) collective-permute-start(bf16[2,528,128]{2,1,0:T(8,128)(2,1)S(1)} %get-tuple-element.99), channel_id=1, source_target_pairs={{0,2},{2,0},{4,6},{6,4},{8,10},{10,8},{12,14},{14,12},{16,18},{18,... | collective-permute-start | bytes 811016 | tf_op jit(solution)/shard_map/ppermute | solution.py:610
  35.3 3.8 %collective-permute-start.7 = (f32[8,512]{1,0:T(8,128)S(1)}, f32[8,512]{1,0:T(8,128)S(1)}, u32[]{:S(2)}, u32[]{:S(2)}) collective-permute-start(f32[8,512]{1,0:T(8,128)S(1)} %get-tuple-element.106.refs_0_), channel_id=1, source_target_pairs={{0,1},{1,0},{2,3},{3,2},{4,5},{5,4},{6,7},{7,6},{8,9},{9,8},{10,11... | collective-permute-start | bytes 49160 | tf_op jit(solution)/shard_map/ppermute | solution.py:790
  40.5 1.6 %collective-permute-start.8 = (bf16[2,528,128]{2,1,0:T(8,128)(2,1)S(1)}, bf16[2,528,128]{2,1,0:T(8,128)(2,1)S(1)}, u32[]{:S(2)}, u32[]{:S(2)}) collective-permute-start(bf16[2,528,128]{2,1,0:T(8,128)(2,1)S(1)} %get-tuple-element.112), channel_id=1, source_target_pairs={{0,2},{2,0},{4,6},{6,4},{8,10},{10,8},{12,14},{14,12},{16,18},{18,... | collective-permute-start | bytes 811016 | tf_op jit(solution)/shard_map/ppermute | solution.py:610
  42.2 5.7 %collective-permute-start.9 = (bf16[528,128]{1,0:T(8,128)(2,1)S(1)}, bf16[528,128]{1,0:T(8,128)(2,1)S(1)}, u32[]{:S(2)}, u32[]{:S(2)}) collective-permute-start(bf16[528,128]{1,0:T(8,128)(2,1)S(1)} %get-tuple-element.114._), channel_id=1, source_target_pairs={{0,4},{2,6},{4,0},{6,2},{8,12},{10,14},{12,8},{14,10},{16,20},{18,... | collective-permute-start | bytes 405512 | tf_op jit(solution)/shard_map/ppermute | solution.py:610
  48.0 6.3 %collective-permute-start.10 = (bf16[528,128]{1,0:T(8,128)(2,1)S(1)}, bf16[528,128]{1,0:T(8,128)(2,1)S(1)}, u32[]{:S(2)}, u32[]{:S(2)}) collective-permute-start(bf16[528,128]{1,0:T(8,128)(2,1)S(1)} %get-tuple-element.121._), channel_id=1, source_target_pairs={{0,8},{2,10},{4,12},{6,14},{8,0},{10,2},{12,4},{14,6},{16,24},{18,... | collective-permute-start | bytes 405512 | tf_op jit(solution)/shard_map/ppermute | solution.py:610
  54.5 8.7 %collective-permute-start.11 = (bf16[528,128]{1,0:T(8,128)(2,1)S(1)}, bf16[528,128]{1,0:T(8,128)(2,1)S(1)}, u32[]{:S(2)}, u32[]{:S(2)}) collective-permute-start(bf16[528,128]{1,0:T(8,128)(2,1)S(1)} %get-tuple-element.125._), channel_id=1, source_target_pairs={{0,16},{2,18},{4,20},{6,22},{8,24},{10,26},{12,28},{14,30},{16,0},... | collective-permute-start | bytes 405512 | tf_op jit(solution)/shard_map/ppermute | solution.py:610
  63.3 5.4 %collective-permute-start.12 = (bf16[528,128]{1,0:T(8,128)(2,1)S(1)}, bf16[528,128]{1,0:T(8,128)(2,1)S(1)}, u32[]{:S(2)}, u32[]{:S(2)}) collective-permute-start(bf16[528,128]{1,0:T(8,128)(2,1)S(1)} %get-tuple-element.131._), channel_id=1, source_target_pairs={{0,4},{2,6},{4,0},{6,2},{8,12},{10,14},{12,8},{14,10},{16,20},{18,... | collective-permute-start | bytes 405512 | tf_op jit(solution)/shard_map/ppermute | solution.py:610
  68.9 2.0 %collective-permute-start.13 = (bf16[2,528,128]{2,1,0:T(8,128)(2,1)S(1)}, bf16[2,528,128]{2,1,0:T(8,128)(2,1)S(1)}, u32[]{:S(2)}, u32[]{:S(2)}) collective-permute-start(bf16[2,528,128]{2,1,0:T(8,128)(2,1)S(1)} %get-tuple-element.136), channel_id=1, source_target_pairs={{0,2},{2,0},{4,6},{6,4},{8,10},{10,8},{12,14},{14,12},{16,18},{18,... | collective-permute-start | bytes 811016 | tf_op jit(solution)/shard_map/ppermute | solution.py:610

commit v13 on v11

--- a/solution.py
+++ b/solution.py
@@ -467,7 +467,7 @@
     return copy
 
 
-def unscaled_gate_body(heads, gate, att, dscaled, out):
+def unscaled_gate_body(heads, gate, att, dscaled, _, out):
     hq = heads // TEAM
     for g in range(TEAM):
         for j in range(hq):
@@ -493,24 +493,26 @@
     return [(ref.at[y], quarter_of(y, same)) for ref, same in ((mine, True), (got, False)) for y in range(2)]
 
 
-def query_body(heads, k, v, dattn, row, col, growth, mine, got, _, query_grad, token, out, sems):
-    hq = heads // TEAM
+def query_body(heads, k, v, dattn, row, col, growth, mine, got, _, *refs):
+    hq = heads // TEAM
+    query_grad, token, out, sems = refs[-4:]
     token[...] = jnp.zeros_like(token)
+    pairs = [(state, g, *pair) for state, g in by_quarter(mine, got) for pair in several(g, hq)]
     copies = []
-    for slot, (state, g) in enumerate(by_quarter(mine, got)):
-        for j, first, count, cols in several(g, hq):
-            both = nt(dattn[:, cols], states_of(state, j, count))
-            for m in range(count):
-                h, c = head_at(g, hq, j + m)
-                line = row[pl.ds(h, 1), :]
-                for i in range(2):
-                    d = dattn[half(i), c]
-                    u = slice(0, (i + 1) * HALF)
-                    table = decay_table(col[g, half(i), j + m : j + m + 1], line[:, u], True)
-                    dscores = (nt(d, v[u, c]) * table).astype(BF16)
-                    inter = both[half(i), chunk(m)] * growth[g, half(i), j + m : j + m + 1]
-                    out[slot, half(i), chunk(j + m)] = (inter + nn(dscores, k[u, c])).astype(BF16)
-        copies.append(leave(out.at[slot], query_grad, sems.at[slot], g, hq * HEAD))
+    for n, (state, g, j, _, count, cols) in enumerate(pairs):
+        for m in range(count):
+            h, c = head_at(g, hq, j + m)
+            line = row[pl.ds(h, 1), :]
+            for i in range(2):
+                d = dattn[half(i), c]
+                u = slice(0, (i + 1) * HALF)
+                table = decay_table(col[g, half(i), j + m : j + m + 1], line[:, u], True)
+                dscores = (nt(d, v[u, c]) * table).astype(BF16)
+                inter = nt(d, state[chunk(j + m), :]) * growth[g, half(i), j + m : j + m + 1]
+                out[n, half(i), chunk(m)] = (inter + nn(dscores, k[u, c])).astype(BF16)
+        copy = pltpu.make_async_copy(out.at[n, :, 0 : count * HEAD], query_grad.at[:, cols], sems.at[n])
+        copy.start()
+        copies.append(copy)
     for copy in copies:
         copy.wait()
 
@@ -562,7 +564,7 @@
 
 def final_body(heads, k, v, dk, dv, col, state, own_key, own_value, own_gain, *refs):
     hq = heads // TEAM
-    key_grad, value_grad, gain_grad, key_out, value_out, sems = refs
+    key_grad, value_grad, gain_grad, gains, key_out, value_out, sems = refs
     copies = []
 
     def send(src, dst, cols):
@@ -570,19 +572,20 @@
         copy.start()
         copies.append(copy)
 
+    gains[...] = own_gain[...]
+    for y in range(2):
+        for j, (_, _, total) in enumerate(read_narrow(state.at[y], hq)):
+            gains[:, head_at(quarter_of(y, False), hq, j)[1]] = total
+    send(gains, gain_grad, slice(None))
     for y in range(2):
         for j, _, count, c in several(quarter_of(y, True), hq):
             place = slice(j * HEAD, (j + count) * HEAD)
             send(own_key.at[y, :, place], key_grad, c)
             send(own_value.at[y, :, place], value_grad, c)
-    gain_grad[...] = own_gain[...]
     for y in range(2):
-        items = read_narrow(state.at[y], hq)
         shrink = fades(col, y, False)
         for j, _, count, c in several(quarter_of(y, False), hq):
             final_rows(hq, y, j, count, c, k, v, dk, dv, shrink, state, key_out, value_out)
-            for m in range(j, j + count):
-                gain_grad[:, head_at(quarter_of(y, False), hq, m)[1]] = items[m][2]
             place = slice(j * HEAD, (j + count) * HEAD)
             send(key_out.at[y, :, place], key_grad, c)
             send(value_out.at[y, :, place], value_grad, c)
@@ -768,7 +771,12 @@
         alias={5: 0},
     )
     (unscaled_gate,) = call(
-        functools.partial(unscaled_gate_body, heads), [gate, att, dscaled], [f32(rows, width)], "unscaled_gate"
+        functools.partial(unscaled_gate_body, heads),
+        [gate, att, dscaled, intra],
+        [f32(rows, width)],
+        "unscaled_gate",
+        in_specs=[VMEM] * 3 + [ANY],
+        alias={3: 0},
     )
     if swaps:
         others = lax.ppermute(sums, "tp", [(0, 1), (1, 0)])
@@ -826,13 +834,15 @@
     def gate_and_key_value(after):
         return key_value_beside(gate_beside(after))
 
+    pairs = TEAM * hq // min(hq, 2)
+
     def query_beside(after):
         done["query"], token = call(
             functools.partial(query_body, heads),
             [keys, values, dattn, row, col, growth, mine, got, after],
             [bf(rows, width), f32(SIDE, HEAD)],
             "query",
-            out_scratch,
+            [pltpu.VMEM((pairs, rows, 2 * HEAD), BF16), pltpu.SemaphoreType.DMA((pairs,))],
             2 * large + small,
             [VMEM] * 8 + [ANY],
             [HBM, VMEM],
@@ -855,9 +865,11 @@
         [keys, values, dk, dv, col, back_got, own_key, own_value, own_gain],
         [bf(rows, width), bf(rows, width), f32(1, width)],
         "final",
-        [pltpu.VMEM(both.shape, BF16)] * 2 + [pltpu.SemaphoreType.DMA((8 * hq,))],
+        [pltpu.VMEM((1, width), F32)]
+        + [pltpu.VMEM(both.shape, BF16)] * 2
+        + [pltpu.SemaphoreType.DMA((8 * hq + 1,))],
         small,
-        out_specs=[HBM, HBM, VMEM],
+        out_specs=[HBM, HBM, HBM],
     )
     return query_grad, key_grad, value_grad, gate_grad, gain_grad.reshape(width)
 

time: 73 us -> 72.2 us (0.989)
  starting transfers between devices: 17.4 us -> 18.7 us
    ppermute x12, starting transfers between devices: 14 us -> 15 us  [swap(): return lax.ppermute(x, 'ctx', [(i, i ^ bit) for i in range(n)])]
    pallas_call x31, Pallas kernels: 46.4 us -> 45.7 us  [call(): pl.pallas_call(body, in_specs=in_specs or [VMEM] * len(inputs), out_specs...]
  transfers between devices with their start and end apart: 14 -> 14, of which waited for: 10 -> 11; matrix products, arithmetic and copies ran while one was open for 0% -> 0% of each run, Pallas kernels for 50% -> 50%
where the time goes in v13:
time: 72.2 us; the launch traced here: 72 us
  Pallas kernels  45.7 us (63%)
  starting transfers between devices  18.7 us (26%)
  waiting for transfers between devices  6.62 us (9%)
  between operations  1.05 us (1%)
    pallas_call x31, Pallas kernels, call(): pl.pallas_call(body, in_specs=in_specs or [VMEM] * len(inputs), out_specs...  45.7 us
    ppermute x12, starting transfers between devices, swap(): return lax.ppermute(x, 'ctx', [(i, i ^ bit) for i in range(n)])  15 us
    ppermute x12, waiting for transfers between devices, swap(): return lax.ppermute(x, 'ctx', [(i, i ^ bit) for i in range(n)])  5.11 us
    ppermute x1, starting transfers between devices, local(): arrived = lax.ppermute(outs[4], 'tp', [(0, 1), (1, 0)])  2.56 us
    ppermute x1, waiting for transfers between devices, local(): others = lax.ppermute(sums, 'tp', [(0, 1), (1, 0)])  1.46 us
  transfers between devices with their start and end apart: 14, of which 11 were waited for; matrix products, arithmetic and copies ran while one was open for 0% of the time, Pallas kernels for 50%

profile of v13, /device:TPU:0, one launch (start us, length us, event | category | flops | bytes accessed | tf_op | source)
XLA Modules:
  0.0 72.0 jit_solution(2889600788470125786)
XLA Ops:
  0.6 2.8 %sent_states.1 = (f32[2,520,128]{2,1,0:T(8,128)S(1)}, f32[16,512]{1,0:T(8,128)S(1)}, bf16[512,2048]{1,0:T(8,128)(2,1)S(1)}, bf16[512,2048]{1,0:T(8,128)(2,1)S(1)}, bf16[256,2048]{1,0:T(8,128)(2,1)S(1)}) custom-call(bf16[512,2048]{1,0:T(8,128)(2,1)} %k_hbm.1, bf16[512,2048]{1,0:T(8,128)(2,1)} %v_hbm.1, f32[16,512]{1,0:T(8,128)} %ld_hbm.1, bf16[256,4096]{1,0:T(8,128)(2,1)} %grad.1), custom_call_target="tpu_custom_call" | custom-call | flops 134217728 | bytes 12132352 | tf_op jit(solution)/shard_map/sent_states/pallas_call | solution.py:125
  4.0 2.6 %collective-permute-start.3 = (bf16[256,2048]{1,0:T(8,128)(2,1)S(1)}, bf16[256,2048]{1,0:T(8,128)(2,1)S(1)}, u32[]{:S(2)}, u32[]{:S(2)}) collective-permute-start(bf16[256,2048]{1,0:T(8,128)(2,1)S(1)} %get-tuple-element.88), channel_id=1, source_target_pairs={{0,1},{1,0},{2,3},{3,2},{4,5},{5,4},{6,7},{7,6},{8,9},{9,8},{10,11... | collective-permute-start | bytes 3145736 | tf_op jit(solution)/shard_map/ppermute | solution.py:681
  7.5 1.6 %collective-permute-start.1 = (bf16[528,128]{1,0:T(8,128)(2,1)S(1)}, bf16[528,128]{1,0:T(8,128)(2,1)S(1)}, u32[]{:S(2)}, u32[]{:S(2)}) collective-permute-start(bf16[528,128]{1,0:T(8,128)(2,1)S(1)} %get-tuple-element.76._), channel_id=1, source_target_pairs={{0,4},{2,6},{4,0},{6,2},{8,12},{10,14},{12,8},{14,10},{16,20},{18,... | collective-permute-start | bytes 405512 | tf_op jit(solution)/shard_map/ppermute | solution.py:602
  9.1 1.6 %decays.1 = (f32[4,512,128]{2,1,0:T(8,128)S(1)}, f32[4,512,128]{2,1,0:T(8,128)S(1)}, bf16[512,2048]{1,0:T(8,128)(2,1)S(1)}) custom-call(f32[16,512]{1,0:T(8,128)S(1)} %get-tuple-element.74.row, bf16[512,2048]{1,0:T(8,128)(2,1)} %q_hbm.1, bf16[528,128]{1,0:T(8,128)(2,1)S(1)} %get-tuple-element.76._), custom_call_target="tpu_custom_call" | custom-call | bytes 6459392 | tf_op jit(solution)/shard_map/decays/pallas_call | solution.py:125
  10.7 1.6 %turned_probs.2 = (f32[16,256,512]{2,1,0:T(8,128)S(1)}, f32[16,256,256]{2,1,0:T(8,128)S(1)}, bf16[16,256,512]{2,1,0:T(8,128)(2,1)S(1)}, bf16[16,256,256]{2,1,0:T(8,128)(2,1)S(1)}) custom-call(bf16[512,2048]{1,0:T(8,128)(2,1)S(1)} %get-tuple-element.77.q, bf16[512,2048]{1,0:T(8,128)(2,1)S(1)} %get-tuple-element.72.k, f32[16,512]{1,0:T(8,128)S(1)} %get-tuple-element.74.row, ...), custom_call_target="tpu_custom_call" | custom-call | flops 536870912 | bytes 24285184 | tf_op jit(solution)/shard_map/turned_probs/pallas_call | solution.py:125
  13.3 1.6 %collective-permute-start.2 = (bf16[528,128]{1,0:T(8,128)(2,1)S(1)}, bf16[528,128]{1,0:T(8,128)(2,1)S(1)}, u32[]{:S(2)}, u32[]{:S(2)}) collective-permute-start(bf16[528,128]{1,0:T(8,128)(2,1)S(1)} %get-tuple-element.82._), channel_id=1, source_target_pairs={{0,8},{2,10},{4,12},{6,14},{8,0},{10,2},{12,4},{14,6},{16,24},{18,... | collective-permute-start | bytes 405512 | tf_op jit(solution)/shard_map/ppermute | solution.py:602
  15.0 1.6 %turned_probs.3 = (f32[16,256,512]{2,1,0:T(8,128)S(1)}, f32[16,256,256]{2,1,0:T(8,128)S(1)}, bf16[16,256,512]{2,1,0:T(8,128)(2,1)S(1)}, bf16[16,256,256]{2,1,0:T(8,128)(2,1)S(1)}) custom-call(bf16[512,2048]{1,0:T(8,128)(2,1)S(1)} %get-tuple-element.77.q, ...), custom_call_target="tpu_custom_call", output_to_operand_aliasing={{0}: (5, {}), {1}: (6, {}), {2}: (7, {}), {3}: (8, {})} | custom-call | flops 536870912 | bytes 43159552 | tf_op jit(solution)/shard_map/turned_probs/pallas_call | solution.py:125
  16.6 1.4 %intra.2.refs_1_ = f32[512,2048]{1,0:T(8,128)S(1)} custom-call(bf16[512,2048]{1,0:T(8,128)(2,1)S(1)} %get-tuple-element.77.q, bf16[512,2048]{1,0:T(8,128)(2,1)S(1)} %get-tuple-element.72.k, bf16[512,2048]{1,0:T(8,128)(2,1)S(1)} %get-tuple-element.73.v, f32[16,512]{1,0:T(8,128)S(1)} %get-tuple-element.74.row, f32[4,512,128]{2,1,0:T(8,128)S(1)} %get-tuple-element.78.col, ...), custom_call_target="tpu_custom_call" | custom-call | flops 536870912 | bytes 13664256 | tf_op jit(solution)/shard_map/intra/pallas_call | solution.py:125
  18.5 2.7 %collective-permute-start.4 = (bf16[528,128]{1,0:T(8,128)(2,1)S(1)}, bf16[528,128]{1,0:T(8,128)(2,1)S(1)}, u32[]{:S(2)}, u32[]{:S(2)}) collective-permute-start(bf16[528,128]{1,0:T(8,128)(2,1)S(1)} %get-tuple-element.87.refs_0_), channel_id=1, source_target_pairs={{0,16},{2,18},{4,20},{6,22},{8,24},{10,26},{12,28},{14,30},{16,0},... | collective-permute-start | bytes 405512 | tf_op jit(solution)/shard_map/ppermute | solution.py:602
  21.1 4.4 %intra.3.refs_0_._ = f32[512,2048]{1,0:T(8,128)S(1)} custom-call(bf16[512,2048]{1,0:T(8,128)(2,1)S(1)} %get-tuple-element.77.q, bf16[512,2048]{1,0:T(8,128)(2,1)S(1)} %get-tuple-element.72.k, bf16[512,2048]{1,0:T(8,128)(2,1)S(1)} %get-tuple-element.73.v, f32[16,512]{1,0:T(8,128)S(1)} %get-tuple-element.74.row, ...), custom_call_target="tpu_custom_call", output_to_operand_aliasing={{}: (6, {})} | custom-call | flops 1610612736 | bytes 15896576 | tf_op jit(solution)/shard_map/intra/pallas_call | solution.py:125
  26.7 1.6 %collective-permute-start.5 = (bf16[528,128]{1,0:T(8,128)(2,1)S(1)}, bf16[528,128]{1,0:T(8,128)(2,1)S(1)}, u32[]{:S(2)}, u32[]{:S(2)}) collective-permute-start(bf16[528,128]{1,0:T(8,128)(2,1)S(1)} %get-tuple-element.91._), channel_id=1, source_target_pairs={{0,4},{2,6},{4,0},{6,2},{8,12},{10,14},{12,8},{14,10},{16,20},{18,... | collective-permute-start | bytes 405512 | tf_op jit(solution)/shard_map/ppermute | solution.py:602
  28.3 1.9 %own_dscaled.1 = (f32[512,2048]{1,0:T(8,128)S(1)}, bf16[2048,512]{1,0:T(8,128)(2,1)S(1)}) custom-call(bf16[512,2048]{1,0:T(8,128)(2,1)S(1)} %copy-done, bf16[256,4096]{1,0:T(8,128)(2,1)} %grad.1, f32[1,2048]{1,0:T(1,128)S(1)} %bitcast.2, bf16[512,2048]{1,0:T(8,128)(2,1)S(1)} %get-tuple-element.77.q, f32[16,512]{1,0:T(8,128)S(1)} %get-tuple-element.74.row, ...), custom_call_target="tpu_custom_call" | custom-call | flops 268435456 | bytes 12759040 | tf_op jit(solution)/shard_map/own_dscaled/pallas_call | solution.py:125
  33.6 1.7 %attention.3 = (f32[512,2048]{1,0:T(8,128)S(1)}, f32[8,512]{1,0:T(8,128)S(1)}) custom-call(bf16[512,2048]{1,0:T(8,128)(2,1)S(1)} %get-tuple-element.77.q, f32[512,2048]{1,0:T(8,128)S(1)} %intra.3.refs_0_._, f32[512,2048]{1,0:T(8,128)S(1)} %got_dscaled.1.refs_0_.dscaled, ...), custom_call_target="tpu_custom_call", output_to_operand_aliasing={{0}: (5, {})} | custom-call | flops 134217728 | bytes 20733952 | tf_op jit(solution)/shard_map/attention/pallas_call | solution.py:125
  37.6 1.5 %collective-permute-done.7.refs_1_ = f32[8,512]{1,0:T(8,128)S(1)} collective-permute-done((f32[8,512]{1,0:T(8,128)S(1)}, f32[8,512]{1,0:T(8,128)S(1)}, u32[]{:S(2)}, u32[]{:S(2)}) %collective-permute-start.7) | collective-permute-done | bytes 16416 | tf_op jit(solution)/shard_map/ppermute | solution.py:782
  39.0 1.5 %sent_dattn.1 = (bf16[512,2048]{1,0:T(8,128)(2,1)S(1)}, bf16[2,528,128]{2,1,0:T(8,128)(2,1)S(1)}, f32[512,128]{1,0:T(8,128)S(1)}, f32[512,128]{1,0:T(8,128)S(1)}) custom-call(f32[512,2048]{1,0:T(8,128)S(1)} %get-tuple-element.100.att, f32[512,2048]{1,0:T(8,128)S(1)} %got_dscaled.1.refs_0_.dscaled, bf16[2048,512]{1,0:T(8,128)(2,1)S(1)} %get-tuple-element.101.turned, ...), custom_call_target="tpu_custom_call" | custom-call | flops 134217728 | bytes 17645568 | tf_op jit(solution)/shard_map/sent_dattn/pallas_call | solution.py:125
  42.2 1.6 %collective-permute-start.9 = (bf16[528,128]{1,0:T(8,128)(2,1)S(1)}, bf16[528,128]{1,0:T(8,128)(2,1)S(1)}, u32[]{:S(2)}, u32[]{:S(2)}) collective-permute-start(bf16[528,128]{1,0:T(8,128)(2,1)S(1)} %get-tuple-element.110._), channel_id=1, source_target_pairs={{0,4},{2,6},{4,0},{6,2},{8,12},{10,14},{12,8},{14,10},{16,20},{18,... | collective-permute-start | bytes 405512 | tf_op jit(solution)/shard_map/ppermute | solution.py:602
  43.8 1.5 %gate.7 = (bf16[512,2048]{1,0:T(8,128)(2,1)}, f32[8,128]{1,0:T(8,128)S(1)}) custom-call(f32[512,2048]{1,0:T(8,128)S(1)} %unscaled_gate.1.refs_2_.unscaled, f32[512,128]{1,0:T(8,128)S(1)} %get-tuple-element.103.refs_0_.scale, bf16[528,128]{1,0:T(8,128)(2,1)S(1)} %get-tuple-element.110._), custom_call_target="tpu_custom_call" | custom-call | flops 268435456 | bytes 6692864 | tf_op jit(solution)/shard_map/gate/pallas_call | solution.py:125
  45.3 2.2 %key_value.3 = (f32[512,2048]{1,0:T(8,128)S(1)}, f32[512,2048]{1,0:T(8,128)S(1)}) custom-call(bf16[512,2048]{1,0:T(8,128)(2,1)S(1)} %get-tuple-element.77.q, bf16[512,2048]{1,0:T(8,128)(2,1)S(1)} %get-tuple-element.73.v, bf16[512,2048]{1,0:T(8,128)(2,1)S(1)} %get-tuple-element.106.dattn, f32[16,256,512]{2,1,0:T(8,128)S(1)} %get-tuple-element.111.table0, ...), custom_call_target="tpu_custom_call" | custom-call | flops 1073741824 | bytes 33558528 | tf_op jit(solution)/shard_map/key_value/pallas_call | solution.py:125
  49.2 3.5 %key_value.4 = (f32[512,2048]{1,0:T(8,128)S(1)}, f32[512,2048]{1,0:T(8,128)S(1)}) custom-call(bf16[512,2048]{1,0:T(8,128)(2,1)S(1)} %get-tuple-element.77.q, bf16[512,2048]{1,0:T(8,128)(2,1)S(1)} %get-tuple-element.73.v, bf16[512,2048]{1,0:T(8,128)(2,1)S(1)} %get-tuple-element.106.dattn, ...), custom_call_target="tpu_custom_call", output_to_operand_aliasing={{0}: (8, {}), {1}: (9, {})} | custom-call | flops 1610612736 | bytes 42078208 | tf_op jit(solution)/shard_map/key_value/pallas_call | solution.py:125
  53.2 2.5 %collective-permute-start.11 = (bf16[528,128]{1,0:T(8,128)(2,1)S(1)}, bf16[528,128]{1,0:T(8,128)(2,1)S(1)}, u32[]{:S(2)}, u32[]{:S(2)}) collective-permute-start(bf16[528,128]{1,0:T(8,128)(2,1)S(1)} %get-tuple-element.120._), channel_id=1, source_target_pairs={{0,16},{2,18},{4,20},{6,22},{8,24},{10,26},{12,28},{14,30},{16,0},... | collective-permute-start | bytes 405512 | tf_op jit(solution)/shard_map/ppermute | solution.py:602
  55.7 6.4 %query.1 = (bf16[512,2048]{1,0:T(8,128)(2,1)}, f32[8,128]{1,0:T(8,128)S(1)}) custom-call(bf16[512,2048]{1,0:T(8,128)(2,1)S(1)} %get-tuple-element.72.k, bf16[512,2048]{1,0:T(8,128)(2,1)S(1)} %get-tuple-element.73.v, bf16[512,2048]{1,0:T(8,128)(2,1)S(1)} %get-tuple-element.106.dattn, f32[16,512]{1,0:T(8,128)S(1)} %get-tuple-element.74.row, ...), custom_call_target="tpu_custom_call" | custom-call | flops 2415919104 | bytes 11198464 | tf_op jit(solution)/shard_map/query/pallas_call | solution.py:125
  62.2 1.6 %collective-permute-start.12 = (bf16[528,128]{1,0:T(8,128)(2,1)S(1)}, bf16[528,128]{1,0:T(8,128)(2,1)S(1)}, u32[]{:S(2)}, u32[]{:S(2)}) collective-permute-start(bf16[528,128]{1,0:T(8,128)(2,1)S(1)} %get-tuple-element.125._), channel_id=1, source_target_pairs={{0,4},{2,6},{4,0},{6,2},{8,12},{10,14},{12,8},{14,10},{16,20},{18,... | collective-permute-start | bytes 405512 | tf_op jit(solution)/shard_map/ppermute | solution.py:602
  63.8 3.3 %key_value.5 = (f32[512,2048]{1,0:T(8,128)S(1)}, f32[512,2048]{1,0:T(8,128)S(1)}) custom-call(bf16[512,2048]{1,0:T(8,128)(2,1)S(1)} %get-tuple-element.77.q, bf16[512,2048]{1,0:T(8,128)(2,1)S(1)} %get-tuple-element.73.v, bf16[512,2048]{1,0:T(8,128)(2,1)S(1)} %get-tuple-element.106.dattn, ...), custom_call_target="tpu_custom_call", output_to_operand_aliasing={{0}: (8, {}), {1}: (9, {})} | custom-call | flops 1610612736 | bytes 42078208 | tf_op jit(solution)/shard_map/key_value/pallas_call | solution.py:125
  69.1 2.7 %final.1 = (bf16[512,2048]{1,0:T(8,128)(2,1)}, bf16[512,2048]{1,0:T(8,128)(2,1)}, f32[1,2048]{1,0:T(1,128)}) custom-call(bf16[512,2048]{1,0:T(8,128)(2,1)S(1)} %get-tuple-element.72.k, bf16[512,2048]{1,0:T(8,128)(2,1)S(1)} %get-tuple-element.73.v, f32[512,2048]{1,0:T(8,128)S(1)} %get-tuple-element.127.refs_0_.dk, f32[512,2048]{1,0:T(8,128)S(1)} %get-tuple-element.128.dv, ...), custom_call_target="tpu_custom_call" | custom-call | flops 268435456 | bytes 20209664 | tf_op jit(solution)/shard_map/final/pallas_call | solution.py:125
  (39 shorter events, 15.8 us)
Async XLA Ops:
  3.5 3.9 %collective-permute-start = (f32[2,520,128]{2,1,0:T(8,128)S(1)}, f32[2,520,128]{2,1,0:T(8,128)S(1)}, u32[]{:S(2)}, u32[]{:S(2)}) collective-permute-start(f32[2,520,128]{2,1,0:T(8,128)S(1)} %get-tuple-element.75), channel_id=1, source_target_pairs={{0,2},{2,0},{4,6},{6,4},{8,10},{10,8},{12,14},{14,12},{16,18},{18,... | collective-permute-start | bytes 1597448 | tf_op jit(solution)/shard_map/ppermute | solution.py:602
  4.0 26.3 %collective-permute-start.3 = (bf16[256,2048]{1,0:T(8,128)(2,1)S(1)}, bf16[256,2048]{1,0:T(8,128)(2,1)S(1)}, u32[]{:S(2)}, u32[]{:S(2)}) collective-permute-start(bf16[256,2048]{1,0:T(8,128)(2,1)S(1)} %get-tuple-element.88), channel_id=1, source_target_pairs={{0,1},{1,0},{2,3},{3,2},{4,5},{5,4},{6,7},{7,6},{8,9},{9,8},{10,11... | collective-permute-start | bytes 3145736 | tf_op jit(solution)/shard_map/ppermute | solution.py:681
  7.5 5.7 %collective-permute-start.1 = (bf16[528,128]{1,0:T(8,128)(2,1)S(1)}, bf16[528,128]{1,0:T(8,128)(2,1)S(1)}, u32[]{:S(2)}, u32[]{:S(2)}) collective-permute-start(bf16[528,128]{1,0:T(8,128)(2,1)S(1)} %get-tuple-element.76._), channel_id=1, source_target_pairs={{0,4},{2,6},{4,0},{6,2},{8,12},{10,14},{12,8},{14,10},{16,20},{18,... | collective-permute-start | bytes 405512 | tf_op jit(solution)/shard_map/ppermute | solution.py:602
  13.3 5.1 %collective-permute-start.2 = (bf16[528,128]{1,0:T(8,128)(2,1)S(1)}, bf16[528,128]{1,0:T(8,128)(2,1)S(1)}, u32[]{:S(2)}, u32[]{:S(2)}) collective-permute-start(bf16[528,128]{1,0:T(8,128)(2,1)S(1)} %get-tuple-element.82._), channel_id=1, source_target_pairs={{0,8},{2,10},{4,12},{6,14},{8,0},{10,2},{12,4},{14,6},{16,24},{18,... | collective-permute-start | bytes 405512 | tf_op jit(solution)/shard_map/ppermute | solution.py:602
  18.5 8.1 %collective-permute-start.4 = (bf16[528,128]{1,0:T(8,128)(2,1)S(1)}, bf16[528,128]{1,0:T(8,128)(2,1)S(1)}, u32[]{:S(2)}, u32[]{:S(2)}) collective-permute-start(bf16[528,128]{1,0:T(8,128)(2,1)S(1)} %get-tuple-element.87.refs_0_), channel_id=1, source_target_pairs={{0,16},{2,18},{4,20},{6,22},{8,24},{10,26},{12,28},{14,30},{16,0},... | collective-permute-start | bytes 405512 | tf_op jit(solution)/shard_map/ppermute | solution.py:602
  25.5 2.8 %copy-start = (bf16[512,2048]{1,0:T(8,128)(2,1)S(1)}, bf16[512,2048]{1,0:T(8,128)(2,1)}, u32[]{:S(2)}) copy-start(bf16[512,2048]{1,0:T(8,128)(2,1)} %gate.6) | copy-start | bytes 6291460
  25.5 2.8 %copy-start.1 = (f32[2048]{0:T(1024)S(1)}, f32[2048]{0:T(1024)}, u32[]{:S(2)}) copy-start(f32[2048]{0:T(1024)} %param.12) | copy-start | bytes 24580
  26.7 5.1 %collective-permute-start.5 = (bf16[528,128]{1,0:T(8,128)(2,1)S(1)}, bf16[528,128]{1,0:T(8,128)(2,1)S(1)}, u32[]{:S(2)}, u32[]{:S(2)}) collective-permute-start(bf16[528,128]{1,0:T(8,128)(2,1)S(1)} %get-tuple-element.91._), channel_id=1, source_target_pairs={{0,4},{2,6},{4,0},{6,2},{8,12},{10,14},{12,8},{14,10},{16,20},{18,... | collective-permute-start | bytes 405512 | tf_op jit(solution)/shard_map/ppermute | solution.py:602
  32.0 1.6 %collective-permute-start.6 = (bf16[2,528,128]{2,1,0:T(8,128)(2,1)S(1)}, bf16[2,528,128]{2,1,0:T(8,128)(2,1)S(1)}, u32[]{:S(2)}, u32[]{:S(2)}) collective-permute-start(bf16[2,528,128]{2,1,0:T(8,128)(2,1)S(1)} %get-tuple-element.95), channel_id=1, source_target_pairs={{0,2},{2,0},{4,6},{6,4},{8,10},{10,8},{12,14},{14,12},{16,18},{18,... | collective-permute-start | bytes 811016 | tf_op jit(solution)/shard_map/ppermute | solution.py:602
  35.3 3.8 %collective-permute-start.7 = (f32[8,512]{1,0:T(8,128)S(1)}, f32[8,512]{1,0:T(8,128)S(1)}, u32[]{:S(2)}, u32[]{:S(2)}) collective-permute-start(f32[8,512]{1,0:T(8,128)S(1)} %get-tuple-element.102.refs_0_), channel_id=1, source_target_pairs={{0,1},{1,0},{2,3},{3,2},{4,5},{5,4},{6,7},{7,6},{8,9},{9,8},{10,11... | collective-permute-start | bytes 49160 | tf_op jit(solution)/shard_map/ppermute | solution.py:782
  40.5 1.6 %collective-permute-start.8 = (bf16[2,528,128]{2,1,0:T(8,128)(2,1)S(1)}, bf16[2,528,128]{2,1,0:T(8,128)(2,1)S(1)}, u32[]{:S(2)}, u32[]{:S(2)}) collective-permute-start(bf16[2,528,128]{2,1,0:T(8,128)(2,1)S(1)} %get-tuple-element.108), channel_id=1, source_target_pairs={{0,2},{2,0},{4,6},{6,4},{8,10},{10,8},{12,14},{14,12},{16,18},{18,... | collective-permute-start | bytes 811016 | tf_op jit(solution)/shard_map/ppermute | solution.py:602
  42.2 5.7 %collective-permute-start.9 = (bf16[528,128]{1,0:T(8,128)(2,1)S(1)}, bf16[528,128]{1,0:T(8,128)(2,1)S(1)}, u32[]{:S(2)}, u32[]{:S(2)}) collective-permute-start(bf16[528,128]{1,0:T(8,128)(2,1)S(1)} %get-tuple-element.110._), channel_id=1, source_target_pairs={{0,4},{2,6},{4,0},{6,2},{8,12},{10,14},{12,8},{14,10},{16,20},{18,... | collective-permute-start | bytes 405512 | tf_op jit(solution)/shard_map/ppermute | solution.py:602
  48.0 5.1 %collective-permute-start.10 = (bf16[528,128]{1,0:T(8,128)(2,1)S(1)}, bf16[528,128]{1,0:T(8,128)(2,1)S(1)}, u32[]{:S(2)}, u32[]{:S(2)}) collective-permute-start(bf16[528,128]{1,0:T(8,128)(2,1)S(1)} %get-tuple-element.117._), channel_id=1, source_target_pairs={{0,8},{2,10},{4,12},{6,14},{8,0},{10,2},{12,4},{14,6},{16,24},{18,... | collective-permute-start | bytes 405512 | tf_op jit(solution)/shard_map/ppermute | solution.py:602
  53.2 8.8 %collective-permute-start.11 = (bf16[528,128]{1,0:T(8,128)(2,1)S(1)}, bf16[528,128]{1,0:T(8,128)(2,1)S(1)}, u32[]{:S(2)}, u32[]{:S(2)}) collective-permute-start(bf16[528,128]{1,0:T(8,128)(2,1)S(1)} %get-tuple-element.120._), channel_id=1, source_target_pairs={{0,16},{2,18},{4,20},{6,22},{8,24},{10,26},{12,28},{14,30},{16,0},... | collective-permute-start | bytes 405512 | tf_op jit(solution)/shard_map/ppermute | solution.py:602
  62.2 5.1 %collective-permute-start.12 = (bf16[528,128]{1,0:T(8,128)(2,1)S(1)}, bf16[528,128]{1,0:T(8,128)(2,1)S(1)}, u32[]{:S(2)}, u32[]{:S(2)}) collective-permute-start(bf16[528,128]{1,0:T(8,128)(2,1)S(1)} %get-tuple-element.125._), channel_id=1, source_target_pairs={{0,4},{2,6},{4,0},{6,2},{8,12},{10,14},{12,8},{14,10},{16,20},{18,... | collective-permute-start | bytes 405512 | tf_op jit(solution)/shard_map/ppermute | solution.py:602
  67.5 1.6 %collective-permute-start.13 = (bf16[2,528,128]{2,1,0:T(8,128)(2,1)S(1)}, bf16[2,528,128]{2,1,0:T(8,128)(2,1)S(1)}, u32[]{:S(2)}, u32[]{:S(2)}) collective-permute-start(bf16[2,528,128]{2,1,0:T(8,128)(2,1)S(1)} %get-tuple-element.130), channel_id=1, source_target_pairs={{0,2},{2,0},{4,6},{6,4},{8,10},{10,8},{12,14},{14,12},{16,18},{18,... | collective-permute-start | bytes 811016 | tf_op jit(solution)/shard_map/ppermute | solution.py:602

commit v14 on v13

--- a/solution.py
+++ b/solution.py
@@ -122,6 +122,9 @@
 def call(body, inputs, out_shape, name, scratch=(), flops=0, in_specs=None, out_specs=None, alias=None):
     nbytes = sum(x.size * x.dtype.itemsize for x in inputs)
     nbytes += sum(x.size * x.dtype.itemsize for x in out_shape)
+    out_shape = list(out_shape)
+    for o in (alias or {}).values():
+        out_shape[o] = pltpu.VMEM(out_shape[o].shape, out_shape[o].dtype)
     return pl.pallas_call(
         body,
         in_specs=in_specs or [VMEM] * len(inputs),
@@ -460,20 +463,20 @@
         (write_wide if same else write_narrow)(out.at[y], hq, items)
 
 
+def unscaled_gate_body(heads, gate, att, dscaled, _, out):
+    hq = heads // TEAM
+    for g in range(TEAM):
+        for j in range(hq):
+            _, c = head_at(g, hq, j)
+            closed = jax.nn.sigmoid(-gate[:, c].astype(F32))
+            out[:, c] = dscaled[:, c] * att[:, c] * closed
+
+
 def leave(out, ref, sems, g, w):
     cols = pl.ds(pl.multiple_of(g * w, HEAD), w)
     copy = pltpu.make_async_copy(out, ref.at[:, cols], sems)
     copy.start()
     return copy
-
-
-def unscaled_gate_body(heads, gate, att, dscaled, _, out):
-    hq = heads // TEAM
-    for g in range(TEAM):
-        for j in range(hq):
-            _, c = head_at(g, hq, j)
-            closed = jax.nn.sigmoid(-gate[:, c].astype(F32))
-            out[:, c] = dscaled[:, c] * att[:, c] * closed
 
 
 def gate_body(heads, unscaled, scale, _, gate_grad, token, out, sems):
@@ -493,13 +496,11 @@
     return [(ref.at[y], quarter_of(y, same)) for ref, same in ((mine, True), (got, False)) for y in range(2)]
 
 
-def query_body(heads, k, v, dattn, row, col, growth, mine, got, _, *refs):
-    hq = heads // TEAM
-    query_grad, token, out, sems = refs[-4:]
-    token[...] = jnp.zeros_like(token)
+def query_body(heads, first, last, k, v, dattn, row, col, growth, mine, got, _, *refs):
+    hq = heads // TEAM
+    query_grad = refs[-1]
     pairs = [(state, g, *pair) for state, g in by_quarter(mine, got) for pair in several(g, hq)]
-    copies = []
-    for n, (state, g, j, _, count, cols) in enumerate(pairs):
+    for state, g, j, _, count, _ in pairs[first:last]:
         for m in range(count):
             h, c = head_at(g, hq, j + m)
             line = row[pl.ds(h, 1), :]
@@ -509,18 +510,21 @@
                 table = decay_table(col[g, half(i), j + m : j + m + 1], line[:, u], True)
                 dscores = (nt(d, v[u, c]) * table).astype(BF16)
                 inter = nt(d, state[chunk(j + m), :]) * growth[g, half(i), j + m : j + m + 1]
-                out[n, half(i), chunk(m)] = (inter + nn(dscores, k[u, c])).astype(BF16)
-        copy = pltpu.make_async_copy(out.at[n, :, 0 : count * HEAD], query_grad.at[:, cols], sems.at[n])
+                query_grad[half(i), c] = (inter + nn(dscores, k[u, c])).astype(BF16)
+
+
+def key_value_body(heads, first, last, carries, q, v, dattn, table0, table1, probs0, probs1, _, *refs):
+    hq = heads // TEAM
+    count = min(hq, 2)
+    if carries:
+        dk, dv, outside, sems = refs[-4:]
+        rows = [slice(i * HEAD, (i + 1) * HEAD) for i in range(BLOCK // HEAD)]
+        copies = [pltpu.make_async_copy(refs[0].at[r], outside.at[r], sems.at[i]) for i, r in enumerate(rows)]
+    else:
+        dk, dv = refs[-2:]
+        copies = []
+    for copy in copies:
         copy.start()
-        copies.append(copy)
-    for copy in copies:
-        copy.wait()
-
-
-def key_value_body(heads, first, last, q, v, dattn, table0, table1, probs0, probs1, _, *refs):
-    hq = heads // TEAM
-    count = min(hq, 2)
-    dk, dv = refs[-2:]
 
     def one(step, _):
         for m in range(count):
@@ -534,6 +538,8 @@
         return 0
 
     lax.fori_loop(first, last, one, 0)
+    for copy in copies:
+        copy.wait()
 
 
 def fades(col, y, same):
@@ -814,42 +820,51 @@
         return token
 
     units = heads // min(hq, 2)
-    cuts = [0, units // 4, (5 * units) // 8, units]
-
-    def key_value_beside(after):
+    cuts = [0, units // 4, 5 * units // 8, units]
+
+    def key_value_beside(after, carried=()):
         before = done.get("key_value", [])
         piece = done.get("piece", 0)
         done["piece"] = piece + 1
-        done["key_value"] = call(
-            functools.partial(key_value_body, heads, cuts[piece], cuts[piece + 1]),
-            [queries, values, dattn, *done["probs"], after, *before],
-            [f32(rows, width)] * 2,
+        inputs = [queries, values, dattn, *done["probs"], after, *carried, *before]
+        results = call(
+            functools.partial(key_value_body, heads, cuts[piece], cuts[piece + 1], len(carried)),
+            inputs,
+            [f32(rows, width)] * 2 + [bf(rows, width)] * len(carried),
             "key_value",
-            flops=4 * large * (cuts[piece + 1] - cuts[piece]) // units,
-            in_specs=[VMEM] * 7 + [ANY] + [VMEM] * len(before),
-            alias={8 + i: i for i in range(len(before))},
+            [pltpu.SemaphoreType.DMA((rows // HEAD,))] * len(carried),
+            4 * large * (cuts[piece + 1] - cuts[piece]) // units,
+            [VMEM] * 7 + [ANY] + [VMEM] * (len(carried) + len(before)),
+            [VMEM] * 2 + [HBM] * len(carried),
+            {8 + len(carried) + i: i for i in range(len(before))},
         )
-        return done["key_value"][0]
+        done["key_value"] = results[:2]
+        return results[0], results[-1]
 
     def gate_and_key_value(after):
-        return key_value_beside(gate_beside(after))
+        return key_value_beside(gate_beside(after))[0]
 
     pairs = TEAM * hq // min(hq, 2)
 
     def query_beside(after):
-        done["query"], token = call(
-            functools.partial(query_body, heads),
-            [keys, values, dattn, row, col, growth, mine, got, after],
-            [bf(rows, width), f32(SIDE, HEAD)],
+        before = [done["query"]] if "query" in done else []
+        first, last = (pairs - pairs // 8, pairs) if before else (0, pairs - pairs // 8)
+        (done["query"],) = call(
+            functools.partial(query_body, heads, first, last),
+            [keys, values, dattn, row, col, growth, mine, got, after, *before],
+            [bf(rows, width)],
             "query",
-            [pltpu.VMEM((pairs, rows, 2 * HEAD), BF16), pltpu.SemaphoreType.DMA((pairs,))],
-            2 * large + small,
-            [VMEM] * 8 + [ANY],
-            [HBM, VMEM],
+            flops=(2 * large + small) * (last - first) // pairs,
+            in_specs=[VMEM] * 8 + [ANY] + [VMEM] * len(before),
+            alias={9: 0} if before else None,
         )
-        return token
-
-    work = {"pair": gate_and_key_value, "one": key_value_beside, "last": query_beside, "pair_back": key_value_beside}
+        return done["query"]
+
+    def query_and_key_value(after):
+        dk, done["query"] = key_value_beside(after, [query_beside(after)])
+        return dk
+
+    work = {"pair": gate_and_key_value, "one": lambda after: key_value_beside(after)[0], "last": query_beside, "pair_back": query_and_key_value}
     back_mine, back_got = scan(True, keep, give, work)
     gate_grad, query_grad, (dk, dv) = done["gate"], done["query"], done["key_value"]
     both = bf(2, rows, hq * HEAD)

time: 72.2 us -> 72.2 us (level)
  waiting for transfers between devices: 6.62 us -> 7.37 us
    pallas_call x31 -> x32, Pallas kernels: 45.7 us -> 45.1 us  [call(): pl.pallas_call(body, in_specs=in_specs or [VMEM] * len(inputs), out_specs...]
  transfers between devices with their start and end apart: 14 -> 14, of which waited for: 11 -> 11; matrix products, arithmetic and copies ran while one was open for 0% -> 0% of each run, Pallas kernels for 50% -> 49%
where the time goes in v14:
time: 72.2 us; the launch traced here: 72 us
  Pallas kernels  45.1 us (62%)
  starting transfers between devices  18.5 us (26%)
  waiting for transfers between devices  7.37 us (10%)
  between operations  1.05 us (1%)
    pallas_call x32, Pallas kernels, call(): pl.pallas_call(body, in_specs=in_specs or [VMEM] * len(inputs), out_specs...  45.1 us
    ppermute x12, starting transfers between devices, swap(): return lax.ppermute(x, 'ctx', [(i, i ^ bit) for i in range(n)])  14.9 us
    ppermute x12, waiting for transfers between devices, swap(): return lax.ppermute(x, 'ctx', [(i, i ^ bit) for i in range(n)])  5.82 us
    ppermute x1, starting transfers between devices, local(): arrived = lax.ppermute(outs[4], 'tp', [(0, 1), (1, 0)])  2.56 us
    ppermute x1, waiting for transfers between devices, local(): others = lax.ppermute(sums, 'tp', [(0, 1), (1, 0)])  1.52 us
  transfers between devices with their start and end apart: 14, of which 11 were waited for; matrix products, arithmetic and copies ran while one was open for 0% of the time, Pallas kernels for 49%

profile of v14, /device:TPU:0, one launch (start us, length us, event | category | flops | bytes accessed | tf_op | source)
XLA Modules:
  0.0 72.0 jit_solution(15660344418917072648)
XLA Ops:
  0.6 2.8 %sent_states.1 = (f32[2,520,128]{2,1,0:T(8,128)S(1)}, f32[16,512]{1,0:T(8,128)S(1)}, bf16[512,2048]{1,0:T(8,128)(2,1)S(1)}, bf16[512,2048]{1,0:T(8,128)(2,1)S(1)}, bf16[256,2048]{1,0:T(8,128)(2,1)S(1)}) custom-call(bf16[512,2048]{1,0:T(8,128)(2,1)} %k_hbm.1, bf16[512,2048]{1,0:T(8,128)(2,1)} %v_hbm.1, f32[16,512]{1,0:T(8,128)} %ld_hbm.1, bf16[256,4096]{1,0:T(8,128)(2,1)} %grad.1), custom_call_target="tpu_custom_call" | custom-call | flops 134217728 | bytes 12132352 | tf_op jit(solution)/shard_map/sent_states/pallas_call | solution.py:128
  4.0 2.6 %collective-permute-start.3 = (bf16[256,2048]{1,0:T(8,128)(2,1)S(1)}, bf16[256,2048]{1,0:T(8,128)(2,1)S(1)}, u32[]{:S(2)}, u32[]{:S(2)}) collective-permute-start(bf16[256,2048]{1,0:T(8,128)(2,1)S(1)} %get-tuple-element.87), channel_id=1, source_target_pairs={{0,1},{1,0},{2,3},{3,2},{4,5},{5,4},{6,7},{7,6},{8,9},{9,8},{10,11... | collective-permute-start | bytes 3145736 | tf_op jit(solution)/shard_map/ppermute | solution.py:687
  7.5 1.6 %collective-permute-start.1 = (bf16[528,128]{1,0:T(8,128)(2,1)S(1)}, bf16[528,128]{1,0:T(8,128)(2,1)S(1)}, u32[]{:S(2)}, u32[]{:S(2)}) collective-permute-start(bf16[528,128]{1,0:T(8,128)(2,1)S(1)} %get-tuple-element.75._), channel_id=1, source_target_pairs={{0,4},{2,6},{4,0},{6,2},{8,12},{10,14},{12,8},{14,10},{16,20},{18,... | collective-permute-start | bytes 405512 | tf_op jit(solution)/shard_map/ppermute | solution.py:608
  9.1 1.6 %decays.1 = (f32[4,512,128]{2,1,0:T(8,128)S(1)}, f32[4,512,128]{2,1,0:T(8,128)S(1)}, bf16[512,2048]{1,0:T(8,128)(2,1)S(1)}) custom-call(f32[16,512]{1,0:T(8,128)S(1)} %get-tuple-element.71.row, bf16[512,2048]{1,0:T(8,128)(2,1)} %q_hbm.1, bf16[528,128]{1,0:T(8,128)(2,1)S(1)} %get-tuple-element.75._), custom_call_target="tpu_custom_call" | custom-call | bytes 6459392 | tf_op jit(solution)/shard_map/decays/pallas_call | solution.py:128
  10.7 1.6 %turned_probs.2 = (f32[16,256,512]{2,1,0:T(8,128)S(1)}, f32[16,256,256]{2,1,0:T(8,128)S(1)}, bf16[16,256,512]{2,1,0:T(8,128)(2,1)S(1)}, bf16[16,256,256]{2,1,0:T(8,128)(2,1)S(1)}) custom-call(bf16[512,2048]{1,0:T(8,128)(2,1)S(1)} %get-tuple-element.76.q, bf16[512,2048]{1,0:T(8,128)(2,1)S(1)} %get-tuple-element.72.k, f32[16,512]{1,0:T(8,128)S(1)} %get-tuple-element.71.row, ...), custom_call_target="tpu_custom_call" | custom-call | flops 536870912 | bytes 24285184 | tf_op jit(solution)/shard_map/turned_probs/pallas_call | solution.py:128
  13.3 1.6 %collective-permute-start.2 = (bf16[528,128]{1,0:T(8,128)(2,1)S(1)}, bf16[528,128]{1,0:T(8,128)(2,1)S(1)}, u32[]{:S(2)}, u32[]{:S(2)}) collective-permute-start(bf16[528,128]{1,0:T(8,128)(2,1)S(1)} %get-tuple-element.81._), channel_id=1, source_target_pairs={{0,8},{2,10},{4,12},{6,14},{8,0},{10,2},{12,4},{14,6},{16,24},{18,... | collective-permute-start | bytes 405512 | tf_op jit(solution)/shard_map/ppermute | solution.py:608
  15.0 1.6 %turned_probs.3 = (f32[16,256,512]{2,1,0:T(8,128)S(1)}, f32[16,256,256]{2,1,0:T(8,128)S(1)}, bf16[16,256,512]{2,1,0:T(8,128)(2,1)S(1)}, bf16[16,256,256]{2,1,0:T(8,128)(2,1)S(1)}) custom-call(bf16[512,2048]{1,0:T(8,128)(2,1)S(1)} %get-tuple-element.76.q, ...), custom_call_target="tpu_custom_call", output_to_operand_aliasing={{0}: (5, {}), {1}: (6, {}), {2}: (7, {}), {3}: (8, {})} | custom-call | flops 536870912 | bytes 43159552 | tf_op jit(solution)/shard_map/turned_probs/pallas_call | solution.py:128
  16.6 1.4 %intra.2.refs_1_ = f32[512,2048]{1,0:T(8,128)S(1)} custom-call(bf16[512,2048]{1,0:T(8,128)(2,1)S(1)} %get-tuple-element.76.q, bf16[512,2048]{1,0:T(8,128)(2,1)S(1)} %get-tuple-element.72.k, bf16[512,2048]{1,0:T(8,128)(2,1)S(1)} %get-tuple-element.73.v, f32[16,512]{1,0:T(8,128)S(1)} %get-tuple-element.71.row, f32[4,512,128]{2,1,0:T(8,128)S(1)} %get-tuple-element.77.col, ...), custom_call_target="tpu_custom_call" | custom-call | flops 536870912 | bytes 13664256 | tf_op jit(solution)/shard_map/intra/pallas_call | solution.py:128
  18.5 2.7 %collective-permute-start.4 = (bf16[528,128]{1,0:T(8,128)(2,1)S(1)}, bf16[528,128]{1,0:T(8,128)(2,1)S(1)}, u32[]{:S(2)}, u32[]{:S(2)}) collective-permute-start(bf16[528,128]{1,0:T(8,128)(2,1)S(1)} %get-tuple-element.86.refs_0_), channel_id=1, source_target_pairs={{0,16},{2,18},{4,20},{6,22},{8,24},{10,26},{12,28},{14,30},{16,0},... | collective-permute-start | bytes 405512 | tf_op jit(solution)/shard_map/ppermute | solution.py:608
  21.2 4.4 %intra.3.refs_0_._ = f32[512,2048]{1,0:T(8,128)S(1)} custom-call(bf16[512,2048]{1,0:T(8,128)(2,1)S(1)} %get-tuple-element.76.q, bf16[512,2048]{1,0:T(8,128)(2,1)S(1)} %get-tuple-element.72.k, bf16[512,2048]{1,0:T(8,128)(2,1)S(1)} %get-tuple-element.73.v, f32[16,512]{1,0:T(8,128)S(1)} %get-tuple-element.71.row, ...), custom_call_target="tpu_custom_call", output_to_operand_aliasing={{}: (6, {})} | custom-call | flops 1610612736 | bytes 15896576 | tf_op jit(solution)/shard_map/intra/pallas_call | solution.py:128
  26.7 1.6 %collective-permute-start.5 = (bf16[528,128]{1,0:T(8,128)(2,1)S(1)}, bf16[528,128]{1,0:T(8,128)(2,1)S(1)}, u32[]{:S(2)}, u32[]{:S(2)}) collective-permute-start(bf16[528,128]{1,0:T(8,128)(2,1)S(1)} %get-tuple-element.90._), channel_id=1, source_target_pairs={{0,4},{2,6},{4,0},{6,2},{8,12},{10,14},{12,8},{14,10},{16,20},{18,... | collective-permute-start | bytes 405512 | tf_op jit(solution)/shard_map/ppermute | solution.py:608
  28.3 1.9 %own_dscaled.1 = (f32[512,2048]{1,0:T(8,128)S(1)}, bf16[2048,512]{1,0:T(8,128)(2,1)S(1)}) custom-call(bf16[512,2048]{1,0:T(8,128)(2,1)S(1)} %copy-done, bf16[256,4096]{1,0:T(8,128)(2,1)} %grad.1, f32[1,2048]{1,0:T(1,128)S(1)} %bitcast.2, bf16[512,2048]{1,0:T(8,128)(2,1)S(1)} %get-tuple-element.76.q, f32[16,512]{1,0:T(8,128)S(1)} %get-tuple-element.71.row, ...), custom_call_target="tpu_custom_call" | custom-call | flops 268435456 | bytes 12759040 | tf_op jit(solution)/shard_map/own_dscaled/pallas_call | solution.py:128
  33.6 1.7 %attention.3 = (f32[512,2048]{1,0:T(8,128)S(1)}, f32[8,512]{1,0:T(8,128)S(1)}) custom-call(bf16[512,2048]{1,0:T(8,128)(2,1)S(1)} %get-tuple-element.76.q, f32[512,2048]{1,0:T(8,128)S(1)} %intra.3.refs_0_._, f32[512,2048]{1,0:T(8,128)S(1)} %got_dscaled.1.refs_0_.dscaled, ...), custom_call_target="tpu_custom_call", output_to_operand_aliasing={{0}: (5, {})} | custom-call | flops 134217728 | bytes 20733952 | tf_op jit(solution)/shard_map/attention/pallas_call | solution.py:128
  37.5 1.5 %collective-permute-done.7.refs_1_ = f32[8,512]{1,0:T(8,128)S(1)} collective-permute-done((f32[8,512]{1,0:T(8,128)S(1)}, f32[8,512]{1,0:T(8,128)S(1)}, u32[]{:S(2)}, u32[]{:S(2)}) %collective-permute-start.7) | collective-permute-done | bytes 16416 | tf_op jit(solution)/shard_map/ppermute | solution.py:788
  39.0 1.5 %sent_dattn.1 = (bf16[512,2048]{1,0:T(8,128)(2,1)S(1)}, bf16[2,528,128]{2,1,0:T(8,128)(2,1)S(1)}, f32[512,128]{1,0:T(8,128)S(1)}, f32[512,128]{1,0:T(8,128)S(1)}) custom-call(f32[512,2048]{1,0:T(8,128)S(1)} %get-tuple-element.99.att, f32[512,2048]{1,0:T(8,128)S(1)} %got_dscaled.1.refs_0_.dscaled, bf16[2048,512]{1,0:T(8,128)(2,1)S(1)} %get-tuple-element.100.turned, ...), custom_call_target="tpu_custom_call" | custom-call | flops 134217728 | bytes 17645568 | tf_op jit(solution)/shard_map/sent_dattn/pallas_call | solution.py:128
  42.2 1.6 %collective-permute-start.9 = (bf16[528,128]{1,0:T(8,128)(2,1)S(1)}, bf16[528,128]{1,0:T(8,128)(2,1)S(1)}, u32[]{:S(2)}, u32[]{:S(2)}) collective-permute-start(bf16[528,128]{1,0:T(8,128)(2,1)S(1)} %get-tuple-element.112._), channel_id=1, source_target_pairs={{0,4},{2,6},{4,0},{6,2},{8,12},{10,14},{12,8},{14,10},{16,20},{18,... | collective-permute-start | bytes 405512 | tf_op jit(solution)/shard_map/ppermute | solution.py:608
  43.8 1.5 %gate.7 = (bf16[512,2048]{1,0:T(8,128)(2,1)}, f32[8,128]{1,0:T(8,128)S(1)}) custom-call(f32[512,2048]{1,0:T(8,128)S(1)} %unscaled_gate.1.refs_2_.unscaled, f32[512,128]{1,0:T(8,128)S(1)} %get-tuple-element.102.refs_0_.scale, bf16[528,128]{1,0:T(8,128)(2,1)S(1)} %get-tuple-element.112._), custom_call_target="tpu_custom_call" | custom-call | flops 268435456 | bytes 6692864 | tf_op jit(solution)/shard_map/gate/pallas_call | solution.py:128
  45.3 2.2 %key_value.3 = (f32[512,2048]{1,0:T(8,128)S(1)}, f32[512,2048]{1,0:T(8,128)S(1)}) custom-call(bf16[512,2048]{1,0:T(8,128)(2,1)S(1)} %get-tuple-element.76.q, bf16[512,2048]{1,0:T(8,128)(2,1)S(1)} %get-tuple-element.73.v, bf16[512,2048]{1,0:T(8,128)(2,1)S(1)} %get-tuple-element.105.dattn, f32[16,256,512]{2,1,0:T(8,128)S(1)} %get-tuple-element.106.table0, ...), custom_call_target="tpu_custom_call" | custom-call | flops 1073741824 | bytes 33558528 | tf_op jit(solution)/shard_map/key_value/pallas_call | solution.py:128
  49.2 3.5 %key_value.4 = (f32[512,2048]{1,0:T(8,128)S(1)}, f32[512,2048]{1,0:T(8,128)S(1)}) custom-call(bf16[512,2048]{1,0:T(8,128)(2,1)S(1)} %get-tuple-element.76.q, bf16[512,2048]{1,0:T(8,128)(2,1)S(1)} %get-tuple-element.73.v, bf16[512,2048]{1,0:T(8,128)(2,1)S(1)} %get-tuple-element.105.dattn, ...), custom_call_target="tpu_custom_call", output_to_operand_aliasing={{0}: (8, {}), {1}: (9, {})} | custom-call | flops 1610612736 | bytes 42078208 | tf_op jit(solution)/shard_map/key_value/pallas_call | solution.py:128
  53.2 2.5 %collective-permute-start.11 = (bf16[528,128]{1,0:T(8,128)(2,1)S(1)}, bf16[528,128]{1,0:T(8,128)(2,1)S(1)}, u32[]{:S(2)}, u32[]{:S(2)}) collective-permute-start(bf16[528,128]{1,0:T(8,128)(2,1)S(1)} %get-tuple-element.121._), channel_id=1, source_target_pairs={{0,16},{2,18},{4,20},{6,22},{8,24},{10,26},{12,28},{14,30},{16,0},... | collective-permute-start | bytes 405512 | tf_op jit(solution)/shard_map/ppermute | solution.py:608
  55.7 4.9 %query.2.refs_0_ = bf16[512,2048]{1,0:T(8,128)(2,1)S(1)} custom-call(bf16[512,2048]{1,0:T(8,128)(2,1)S(1)} %get-tuple-element.72.k, bf16[512,2048]{1,0:T(8,128)(2,1)S(1)} %get-tuple-element.73.v, bf16[512,2048]{1,0:T(8,128)(2,1)S(1)} %get-tuple-element.105.dattn, f32[16,512]{1,0:T(8,128)S(1)} %get-tuple-element.71.row, ...), custom_call_target="tpu_custom_call" | custom-call | flops 2113929216 | bytes 11194368 | tf_op jit(solution)/shard_map/query/pallas_call | solution.py:128
  61.6 1.4 %collective-permute-start.12 = (bf16[528,128]{1,0:T(8,128)(2,1)S(1)}, bf16[528,128]{1,0:T(8,128)(2,1)S(1)}, u32[]{:S(2)}, u32[]{:S(2)}) collective-permute-start(bf16[528,128]{1,0:T(8,128)(2,1)S(1)} %get-tuple-element.122._), channel_id=1, source_target_pairs={{0,4},{2,6},{4,0},{6,2},{8,12},{10,14},{12,8},{14,10},{16,20},{18,... | collective-permute-start | bytes 405512 | tf_op jit(solution)/shard_map/ppermute | solution.py:608
  63.9 3.3 %key_value.5 = (f32[512,2048]{1,0:T(8,128)S(1)}, f32[512,2048]{1,0:T(8,128)S(1)}, bf16[512,2048]{1,0:T(8,128)(2,1)}) custom-call(bf16[512,2048]{1,0:T(8,128)(2,1)S(1)} %get-tuple-element.76.q, bf16[512,2048]{1,0:T(8,128)(2,1)S(1)} %get-tuple-element.73.v, ...), custom_call_target="tpu_custom_call", output_to_operand_aliasing={{0}: (9, {}), {1}: (10, {})} | custom-call | flops 1610612736 | bytes 46272512 | tf_op jit(solution)/shard_map/key_value/pallas_call | solution.py:128
  69.1 2.7 %final.1 = (bf16[512,2048]{1,0:T(8,128)(2,1)}, bf16[512,2048]{1,0:T(8,128)(2,1)}, f32[1,2048]{1,0:T(1,128)}) custom-call(bf16[512,2048]{1,0:T(8,128)(2,1)S(1)} %get-tuple-element.72.k, bf16[512,2048]{1,0:T(8,128)(2,1)S(1)} %get-tuple-element.73.v, f32[512,2048]{1,0:T(8,128)S(1)} %get-tuple-element.125.refs_0_.dk, f32[512,2048]{1,0:T(8,128)S(1)} %get-tuple-element.126.dv, ...), custom_call_target="tpu_custom_call" | custom-call | flops 268435456 | bytes 20209664 | tf_op jit(solution)/shard_map/final/pallas_call | solution.py:128
  (40 shorter events, 17.3 us)
Async XLA Ops:
  3.5 3.9 %collective-permute-start = (f32[2,520,128]{2,1,0:T(8,128)S(1)}, f32[2,520,128]{2,1,0:T(8,128)S(1)}, u32[]{:S(2)}, u32[]{:S(2)}) collective-permute-start(f32[2,520,128]{2,1,0:T(8,128)S(1)} %get-tuple-element.74), channel_id=1, source_target_pairs={{0,2},{2,0},{4,6},{6,4},{8,10},{10,8},{12,14},{14,12},{16,18},{18,... | collective-permute-start | bytes 1597448 | tf_op jit(solution)/shard_map/ppermute | solution.py:608
  4.0 26.3 %collective-permute-start.3 = (bf16[256,2048]{1,0:T(8,128)(2,1)S(1)}, bf16[256,2048]{1,0:T(8,128)(2,1)S(1)}, u32[]{:S(2)}, u32[]{:S(2)}) collective-permute-start(bf16[256,2048]{1,0:T(8,128)(2,1)S(1)} %get-tuple-element.87), channel_id=1, source_target_pairs={{0,1},{1,0},{2,3},{3,2},{4,5},{5,4},{6,7},{7,6},{8,9},{9,8},{10,11... | collective-permute-start | bytes 3145736 | tf_op jit(solution)/shard_map/ppermute | solution.py:687
  7.5 5.7 %collective-permute-start.1 = (bf16[528,128]{1,0:T(8,128)(2,1)S(1)}, bf16[528,128]{1,0:T(8,128)(2,1)S(1)}, u32[]{:S(2)}, u32[]{:S(2)}) collective-permute-start(bf16[528,128]{1,0:T(8,128)(2,1)S(1)} %get-tuple-element.75._), channel_id=1, source_target_pairs={{0,4},{2,6},{4,0},{6,2},{8,12},{10,14},{12,8},{14,10},{16,20},{18,... | collective-permute-start | bytes 405512 | tf_op jit(solution)/shard_map/ppermute | solution.py:608
  13.3 5.1 %collective-permute-start.2 = (bf16[528,128]{1,0:T(8,128)(2,1)S(1)}, bf16[528,128]{1,0:T(8,128)(2,1)S(1)}, u32[]{:S(2)}, u32[]{:S(2)}) collective-permute-start(bf16[528,128]{1,0:T(8,128)(2,1)S(1)} %get-tuple-element.81._), channel_id=1, source_target_pairs={{0,8},{2,10},{4,12},{6,14},{8,0},{10,2},{12,4},{14,6},{16,24},{18,... | collective-permute-start | bytes 405512 | tf_op jit(solution)/shard_map/ppermute | solution.py:608
  18.5 8.1 %collective-permute-start.4 = (bf16[528,128]{1,0:T(8,128)(2,1)S(1)}, bf16[528,128]{1,0:T(8,128)(2,1)S(1)}, u32[]{:S(2)}, u32[]{:S(2)}) collective-permute-start(bf16[528,128]{1,0:T(8,128)(2,1)S(1)} %get-tuple-element.86.refs_0_), channel_id=1, source_target_pairs={{0,16},{2,18},{4,20},{6,22},{8,24},{10,26},{12,28},{14,30},{16,0},... | collective-permute-start | bytes 405512 | tf_op jit(solution)/shard_map/ppermute | solution.py:608
  25.5 2.8 %copy-start = (bf16[512,2048]{1,0:T(8,128)(2,1)S(1)}, bf16[512,2048]{1,0:T(8,128)(2,1)}, u32[]{:S(2)}) copy-start(bf16[512,2048]{1,0:T(8,128)(2,1)} %gate.6) | copy-start | bytes 6291460
  25.5 2.8 %copy-start.1 = (f32[2048]{0:T(1024)S(1)}, f32[2048]{0:T(1024)}, u32[]{:S(2)}) copy-start(f32[2048]{0:T(1024)} %param.12) | copy-start | bytes 24580
  26.7 5.1 %collective-permute-start.5 = (bf16[528,128]{1,0:T(8,128)(2,1)S(1)}, bf16[528,128]{1,0:T(8,128)(2,1)S(1)}, u32[]{:S(2)}, u32[]{:S(2)}) collective-permute-start(bf16[528,128]{1,0:T(8,128)(2,1)S(1)} %get-tuple-element.90._), channel_id=1, source_target_pairs={{0,4},{2,6},{4,0},{6,2},{8,12},{10,14},{12,8},{14,10},{16,20},{18,... | collective-permute-start | bytes 405512 | tf_op jit(solution)/shard_map/ppermute | solution.py:608
  32.0 1.6 %collective-permute-start.6 = (bf16[2,528,128]{2,1,0:T(8,128)(2,1)S(1)}, bf16[2,528,128]{2,1,0:T(8,128)(2,1)S(1)}, u32[]{:S(2)}, u32[]{:S(2)}) collective-permute-start(bf16[2,528,128]{2,1,0:T(8,128)(2,1)S(1)} %get-tuple-element.94), channel_id=1, source_target_pairs={{0,2},{2,0},{4,6},{6,4},{8,10},{10,8},{12,14},{14,12},{16,18},{18,... | collective-permute-start | bytes 811016 | tf_op jit(solution)/shard_map/ppermute | solution.py:608
  35.3 3.8 %collective-permute-start.7 = (f32[8,512]{1,0:T(8,128)S(1)}, f32[8,512]{1,0:T(8,128)S(1)}, u32[]{:S(2)}, u32[]{:S(2)}) collective-permute-start(f32[8,512]{1,0:T(8,128)S(1)} %get-tuple-element.101.refs_0_), channel_id=1, source_target_pairs={{0,1},{1,0},{2,3},{3,2},{4,5},{5,4},{6,7},{7,6},{8,9},{9,8},{10,11... | collective-permute-start | bytes 49160 | tf_op jit(solution)/shard_map/ppermute | solution.py:788
  40.5 1.6 %collective-permute-start.8 = (bf16[2,528,128]{2,1,0:T(8,128)(2,1)S(1)}, bf16[2,528,128]{2,1,0:T(8,128)(2,1)S(1)}, u32[]{:S(2)}, u32[]{:S(2)}) collective-permute-start(bf16[2,528,128]{2,1,0:T(8,128)(2,1)S(1)} %get-tuple-element.110), channel_id=1, source_target_pairs={{0,2},{2,0},{4,6},{6,4},{8,10},{10,8},{12,14},{14,12},{16,18},{18,... | collective-permute-start | bytes 811016 | tf_op jit(solution)/shard_map/ppermute | solution.py:608
  42.2 5.7 %collective-permute-start.9 = (bf16[528,128]{1,0:T(8,128)(2,1)S(1)}, bf16[528,128]{1,0:T(8,128)(2,1)S(1)}, u32[]{:S(2)}, u32[]{:S(2)}) collective-permute-start(bf16[528,128]{1,0:T(8,128)(2,1)S(1)} %get-tuple-element.112._), channel_id=1, source_target_pairs={{0,4},{2,6},{4,0},{6,2},{8,12},{10,14},{12,8},{14,10},{16,20},{18,... | collective-permute-start | bytes 405512 | tf_op jit(solution)/shard_map/ppermute | solution.py:608
  48.0 5.1 %collective-permute-start.10 = (bf16[528,128]{1,0:T(8,128)(2,1)S(1)}, bf16[528,128]{1,0:T(8,128)(2,1)S(1)}, u32[]{:S(2)}, u32[]{:S(2)}) collective-permute-start(bf16[528,128]{1,0:T(8,128)(2,1)S(1)} %get-tuple-element.116._), channel_id=1, source_target_pairs={{0,8},{2,10},{4,12},{6,14},{8,0},{10,2},{12,4},{14,6},{16,24},{18,... | collective-permute-start | bytes 405512 | tf_op jit(solution)/shard_map/ppermute | solution.py:608
  53.2 8.3 %collective-permute-start.11 = (bf16[528,128]{1,0:T(8,128)(2,1)S(1)}, bf16[528,128]{1,0:T(8,128)(2,1)S(1)}, u32[]{:S(2)}, u32[]{:S(2)}) collective-permute-start(bf16[528,128]{1,0:T(8,128)(2,1)S(1)} %get-tuple-element.121._), channel_id=1, source_target_pairs={{0,16},{2,18},{4,20},{6,22},{8,24},{10,26},{12,28},{14,30},{16,0},... | collective-permute-start | bytes 405512 | tf_op jit(solution)/shard_map/ppermute | solution.py:608
  61.6 5.6 %collective-permute-start.12 = (bf16[528,128]{1,0:T(8,128)(2,1)S(1)}, bf16[528,128]{1,0:T(8,128)(2,1)S(1)}, u32[]{:S(2)}, u32[]{:S(2)}) collective-permute-start(bf16[528,128]{1,0:T(8,128)(2,1)S(1)} %get-tuple-element.122._), channel_id=1, source_target_pairs={{0,4},{2,6},{4,0},{6,2},{8,12},{10,14},{12,8},{14,10},{16,20},{18,... | collective-permute-start | bytes 405512 | tf_op jit(solution)/shard_map/ppermute | solution.py:608
  67.5 1.6 %collective-permute-start.13 = (bf16[2,528,128]{2,1,0:T(8,128)(2,1)S(1)}, bf16[2,528,128]{2,1,0:T(8,128)(2,1)S(1)}, u32[]{:S(2)}, u32[]{:S(2)}) collective-permute-start(bf16[2,528,128]{2,1,0:T(8,128)(2,1)S(1)} %get-tuple-element.128), channel_id=1, source_target_pairs={{0,2},{2,0},{4,6},{6,4},{8,10},{10,8},{12,14},{14,12},{16,18},{18,... | collective-permute-start | bytes 811016 | tf_op jit(solution)/shard_map/ppermute | solution.py:608

commit v15 on v14

--- a/solution.py
+++ b/solution.py
@@ -496,20 +496,18 @@
     return [(ref.at[y], quarter_of(y, same)) for ref, same in ((mine, True), (got, False)) for y in range(2)]
 
 
-def query_body(heads, first, last, k, v, dattn, row, col, growth, mine, got, _, *refs):
-    hq = heads // TEAM
-    query_grad = refs[-1]
-    pairs = [(state, g, *pair) for state, g in by_quarter(mine, got) for pair in several(g, hq)]
-    for state, g, j, _, count, _ in pairs[first:last]:
-        for m in range(count):
-            h, c = head_at(g, hq, j + m)
+def query_body(heads, k, v, dattn, row, col, growth, mine, got, _, query_grad):
+    hq = heads // TEAM
+    for state, g in by_quarter(mine, got):
+        for j in range(hq):
+            h, c = head_at(g, hq, j)
             line = row[pl.ds(h, 1), :]
             for i in range(2):
                 d = dattn[half(i), c]
                 u = slice(0, (i + 1) * HALF)
-                table = decay_table(col[g, half(i), j + m : j + m + 1], line[:, u], True)
+                table = decay_table(col[g, half(i), j : j + 1], line[:, u], True)
                 dscores = (nt(d, v[u, c]) * table).astype(BF16)
-                inter = nt(d, state[chunk(j + m), :]) * growth[g, half(i), j + m : j + m + 1]
+                inter = nt(d, state[chunk(j), :]) * growth[g, half(i), j : j + 1]
                 query_grad[half(i), c] = (inter + nn(dscores, k[u, c])).astype(BF16)
 
 
@@ -844,27 +842,22 @@
     def gate_and_key_value(after):
         return key_value_beside(gate_beside(after))[0]
 
-    pairs = TEAM * hq // min(hq, 2)
-
     def query_beside(after):
-        before = [done["query"]] if "query" in done else []
-        first, last = (pairs - pairs // 8, pairs) if before else (0, pairs - pairs // 8)
         (done["query"],) = call(
-            functools.partial(query_body, heads, first, last),
-            [keys, values, dattn, row, col, growth, mine, got, after, *before],
+            functools.partial(query_body, heads),
+            [keys, values, dattn, row, col, growth, mine, got, after],
             [bf(rows, width)],
             "query",
-            flops=(2 * large + small) * (last - first) // pairs,
-            in_specs=[VMEM] * 8 + [ANY] + [VMEM] * len(before),
-            alias={9: 0} if before else None,
+            flops=2 * large + small,
+            in_specs=[VMEM] * 8 + [ANY],
         )
         return done["query"]
 
-    def query_and_key_value(after):
-        dk, done["query"] = key_value_beside(after, [query_beside(after)])
+    def key_value_last(after):
+        dk, done["query"] = key_value_beside(after, [done["query"]])
         return dk
 
-    work = {"pair": gate_and_key_value, "one": lambda after: key_value_beside(after)[0], "last": query_beside, "pair_back": query_and_key_value}
+    work = {"pair": gate_and_key_value, "one": lambda after: key_value_beside(after)[0], "last": query_beside, "pair_back": key_value_last}
     back_mine, back_got = scan(True, keep, give, work)
     gate_grad, query_grad, (dk, dv) = done["gate"], done["query"], done["key_value"]
     both = bf(2, rows, hq * HEAD)

time: 72.2 us -> 71.6 us (level)
  starting transfers between devices: 18.5 us -> 17.4 us
    ppermute x12, starting transfers between devices: 14.9 us -> 13.9 us  [swap(): return lax.ppermute(x, 'ctx', [(i, i ^ bit) for i in range(n)])]
    pallas_call x32 -> x31, Pallas kernels: 45.1 us -> 44.8 us  [call(): pl.pallas_call(body, in_specs=in_specs or [VMEM] * len(inputs), out_specs...]
where the time goes in v15:
time: 71.6 us; the launch traced here: 71.5 us
  Pallas kernels  44.8 us (63%)
  starting transfers between devices  17.4 us (24%)
  waiting for transfers between devices  7.69 us (11%)
  between operations  1.07 us (1%)
    pallas_call x31, Pallas kernels, call(): pl.pallas_call(body, in_specs=in_specs or [VMEM] * len(inputs), out_specs...  44.8 us
    ppermute x12, starting transfers between devices, swap(): return lax.ppermute(x, 'ctx', [(i, i ^ bit) for i in range(n)])  13.9 us
    ppermute x12, waiting for transfers between devices, swap(): return lax.ppermute(x, 'ctx', [(i, i ^ bit) for i in range(n)])  5.99 us
    ppermute x1, starting transfers between devices, local(): arrived = lax.ppermute(outs[4], 'tp', [(0, 1), (1, 0)])  2.56 us
    ppermute x1, waiting for transfers between devices, local(): others = lax.ppermute(sums, 'tp', [(0, 1), (1, 0)])  1.7 us
  transfers between devices with their start and end apart: 14, of which 11 were waited for; matrix products, arithmetic and copies ran while one was open for 0% of the time, Pallas kernels for 49%

profile of v15, /device:TPU:0, one launch (start us, length us, event | category | flops | bytes accessed | tf_op | source)
XLA Modules:
  0.0 71.5 jit_solution(12518351802697004452)
XLA Ops:
  0.6 2.8 %sent_states.1 = (f32[2,520,128]{2,1,0:T(8,128)S(1)}, f32[16,512]{1,0:T(8,128)S(1)}, bf16[512,2048]{1,0:T(8,128)(2,1)S(1)}, bf16[512,2048]{1,0:T(8,128)(2,1)S(1)}, bf16[256,2048]{1,0:T(8,128)(2,1)S(1)}) custom-call(bf16[512,2048]{1,0:T(8,128)(2,1)} %k_hbm.1, bf16[512,2048]{1,0:T(8,128)(2,1)} %v_hbm.1, f32[16,512]{1,0:T(8,128)} %ld_hbm.1, bf16[256,4096]{1,0:T(8,128)(2,1)} %grad.1), custom_call_target="tpu_custom_call" | custom-call | flops 134217728 | bytes 12132352 | tf_op jit(solution)/shard_map/sent_states/pallas_call | solution.py:128
  4.0 2.6 %collective-permute-start.3 = (bf16[256,2048]{1,0:T(8,128)(2,1)S(1)}, bf16[256,2048]{1,0:T(8,128)(2,1)S(1)}, u32[]{:S(2)}, u32[]{:S(2)}) collective-permute-start(bf16[256,2048]{1,0:T(8,128)(2,1)S(1)} %get-tuple-element.87), channel_id=1, source_target_pairs={{0,1},{1,0},{2,3},{3,2},{4,5},{5,4},{6,7},{7,6},{8,9},{9,8},{10,11... | collective-permute-start | bytes 3145736 | tf_op jit(solution)/shard_map/ppermute | solution.py:685
  7.5 1.6 %collective-permute-start.1 = (bf16[528,128]{1,0:T(8,128)(2,1)S(1)}, bf16[528,128]{1,0:T(8,128)(2,1)S(1)}, u32[]{:S(2)}, u32[]{:S(2)}) collective-permute-start(bf16[528,128]{1,0:T(8,128)(2,1)S(1)} %get-tuple-element.75._), channel_id=1, source_target_pairs={{0,4},{2,6},{4,0},{6,2},{8,12},{10,14},{12,8},{14,10},{16,20},{18,... | collective-permute-start | bytes 405512 | tf_op jit(solution)/shard_map/ppermute | solution.py:606
  9.1 1.6 %decays.1 = (f32[4,512,128]{2,1,0:T(8,128)S(1)}, f32[4,512,128]{2,1,0:T(8,128)S(1)}, bf16[512,2048]{1,0:T(8,128)(2,1)S(1)}) custom-call(f32[16,512]{1,0:T(8,128)S(1)} %get-tuple-element.71.row, bf16[512,2048]{1,0:T(8,128)(2,1)} %q_hbm.1, bf16[528,128]{1,0:T(8,128)(2,1)S(1)} %get-tuple-element.75._), custom_call_target="tpu_custom_call" | custom-call | bytes 6459392 | tf_op jit(solution)/shard_map/decays/pallas_call | solution.py:128
  10.7 1.6 %turned_probs.2 = (f32[16,256,512]{2,1,0:T(8,128)S(1)}, f32[16,256,256]{2,1,0:T(8,128)S(1)}, bf16[16,256,512]{2,1,0:T(8,128)(2,1)S(1)}, bf16[16,256,256]{2,1,0:T(8,128)(2,1)S(1)}) custom-call(bf16[512,2048]{1,0:T(8,128)(2,1)S(1)} %get-tuple-element.76.q, bf16[512,2048]{1,0:T(8,128)(2,1)S(1)} %get-tuple-element.72.k, f32[16,512]{1,0:T(8,128)S(1)} %get-tuple-element.71.row, ...), custom_call_target="tpu_custom_call" | custom-call | flops 536870912 | bytes 24285184 | tf_op jit(solution)/shard_map/turned_probs/pallas_call | solution.py:128
  13.3 1.6 %collective-permute-start.2 = (bf16[528,128]{1,0:T(8,128)(2,1)S(1)}, bf16[528,128]{1,0:T(8,128)(2,1)S(1)}, u32[]{:S(2)}, u32[]{:S(2)}) collective-permute-start(bf16[528,128]{1,0:T(8,128)(2,1)S(1)} %get-tuple-element.81._), channel_id=1, source_target_pairs={{0,8},{2,10},{4,12},{6,14},{8,0},{10,2},{12,4},{14,6},{16,24},{18,... | collective-permute-start | bytes 405512 | tf_op jit(solution)/shard_map/ppermute | solution.py:606
  15.0 1.6 %turned_probs.3 = (f32[16,256,512]{2,1,0:T(8,128)S(1)}, f32[16,256,256]{2,1,0:T(8,128)S(1)}, bf16[16,256,512]{2,1,0:T(8,128)(2,1)S(1)}, bf16[16,256,256]{2,1,0:T(8,128)(2,1)S(1)}) custom-call(bf16[512,2048]{1,0:T(8,128)(2,1)S(1)} %get-tuple-element.76.q, ...), custom_call_target="tpu_custom_call", output_to_operand_aliasing={{0}: (5, {}), {1}: (6, {}), {2}: (7, {}), {3}: (8, {})} | custom-call | flops 536870912 | bytes 43159552 | tf_op jit(solution)/shard_map/turned_probs/pallas_call | solution.py:128
  16.6 1.4 %intra.2.refs_1_ = f32[512,2048]{1,0:T(8,128)S(1)} custom-call(bf16[512,2048]{1,0:T(8,128)(2,1)S(1)} %get-tuple-element.76.q, bf16[512,2048]{1,0:T(8,128)(2,1)S(1)} %get-tuple-element.72.k, bf16[512,2048]{1,0:T(8,128)(2,1)S(1)} %get-tuple-element.73.v, f32[16,512]{1,0:T(8,128)S(1)} %get-tuple-element.71.row, f32[4,512,128]{2,1,0:T(8,128)S(1)} %get-tuple-element.77.col, ...), custom_call_target="tpu_custom_call" | custom-call | flops 536870912 | bytes 13664256 | tf_op jit(solution)/shard_map/intra/pallas_call | solution.py:128
  18.7 2.7 %collective-permute-start.4 = (bf16[528,128]{1,0:T(8,128)(2,1)S(1)}, bf16[528,128]{1,0:T(8,128)(2,1)S(1)}, u32[]{:S(2)}, u32[]{:S(2)}) collective-permute-start(bf16[528,128]{1,0:T(8,128)(2,1)S(1)} %get-tuple-element.86.refs_0_), channel_id=1, source_target_pairs={{0,16},{2,18},{4,20},{6,22},{8,24},{10,26},{12,28},{14,30},{16,0},... | collective-permute-start | bytes 405512 | tf_op jit(solution)/shard_map/ppermute | solution.py:606
  21.3 4.4 %intra.3.refs_0_._ = f32[512,2048]{1,0:T(8,128)S(1)} custom-call(bf16[512,2048]{1,0:T(8,128)(2,1)S(1)} %get-tuple-element.76.q, bf16[512,2048]{1,0:T(8,128)(2,1)S(1)} %get-tuple-element.72.k, bf16[512,2048]{1,0:T(8,128)(2,1)S(1)} %get-tuple-element.73.v, f32[16,512]{1,0:T(8,128)S(1)} %get-tuple-element.71.row, ...), custom_call_target="tpu_custom_call", output_to_operand_aliasing={{}: (6, {})} | custom-call | flops 1610612736 | bytes 15896576 | tf_op jit(solution)/shard_map/intra/pallas_call | solution.py:128
  27.2 1.6 %collective-permute-start.5 = (bf16[528,128]{1,0:T(8,128)(2,1)S(1)}, bf16[528,128]{1,0:T(8,128)(2,1)S(1)}, u32[]{:S(2)}, u32[]{:S(2)}) collective-permute-start(bf16[528,128]{1,0:T(8,128)(2,1)S(1)} %get-tuple-element.90._), channel_id=1, source_target_pairs={{0,4},{2,6},{4,0},{6,2},{8,12},{10,14},{12,8},{14,10},{16,20},{18,... | collective-permute-start | bytes 405512 | tf_op jit(solution)/shard_map/ppermute | solution.py:606
  28.8 1.9 %own_dscaled.1 = (f32[512,2048]{1,0:T(8,128)S(1)}, bf16[2048,512]{1,0:T(8,128)(2,1)S(1)}) custom-call(bf16[512,2048]{1,0:T(8,128)(2,1)S(1)} %copy-done.2, bf16[256,4096]{1,0:T(8,128)(2,1)} %grad.1, f32[1,2048]{1,0:T(1,128)S(1)} %bitcast.2, bf16[512,2048]{1,0:T(8,128)(2,1)S(1)} %get-tuple-element.76.q, f32[16,512]{1,0:T(8,128)S(1)} %get-tuple-element.71.row, ...), custom_call_target="tpu_custom_call" | custom-call | flops 268435456 | bytes 12759040 | tf_op jit(solution)/shard_map/own_dscaled/pallas_call | solution.py:128
  34.2 1.6 %attention.3 = (f32[512,2048]{1,0:T(8,128)S(1)}, f32[8,512]{1,0:T(8,128)S(1)}) custom-call(bf16[512,2048]{1,0:T(8,128)(2,1)S(1)} %get-tuple-element.76.q, f32[512,2048]{1,0:T(8,128)S(1)} %intra.3.refs_0_._, f32[512,2048]{1,0:T(8,128)S(1)} %got_dscaled.1.refs_0_.dscaled, ...), custom_call_target="tpu_custom_call", output_to_operand_aliasing={{0}: (5, {})} | custom-call | flops 134217728 | bytes 20733952 | tf_op jit(solution)/shard_map/attention/pallas_call | solution.py:128
  37.9 1.7 %collective-permute-done.7.refs_1_ = f32[8,512]{1,0:T(8,128)S(1)} collective-permute-done((f32[8,512]{1,0:T(8,128)S(1)}, f32[8,512]{1,0:T(8,128)S(1)}, u32[]{:S(2)}, u32[]{:S(2)}) %collective-permute-start.7) | collective-permute-done | bytes 16416 | tf_op jit(solution)/shard_map/ppermute | solution.py:786
  39.6 1.5 %sent_dattn.1 = (bf16[512,2048]{1,0:T(8,128)(2,1)S(1)}, bf16[2,528,128]{2,1,0:T(8,128)(2,1)S(1)}, f32[512,128]{1,0:T(8,128)S(1)}, f32[512,128]{1,0:T(8,128)S(1)}) custom-call(f32[512,2048]{1,0:T(8,128)S(1)} %get-tuple-element.99.att, f32[512,2048]{1,0:T(8,128)S(1)} %got_dscaled.1.refs_0_.dscaled, bf16[2048,512]{1,0:T(8,128)(2,1)S(1)} %get-tuple-element.100.turned, ...), custom_call_target="tpu_custom_call" | custom-call | flops 134217728 | bytes 17645568 | tf_op jit(solution)/shard_map/sent_dattn/pallas_call | solution.py:128
  42.8 1.6 %collective-permute-start.9 = (bf16[528,128]{1,0:T(8,128)(2,1)S(1)}, bf16[528,128]{1,0:T(8,128)(2,1)S(1)}, u32[]{:S(2)}, u32[]{:S(2)}) collective-permute-start(bf16[528,128]{1,0:T(8,128)(2,1)S(1)} %get-tuple-element.112._), channel_id=1, source_target_pairs={{0,4},{2,6},{4,0},{6,2},{8,12},{10,14},{12,8},{14,10},{16,20},{18,... | collective-permute-start | bytes 405512 | tf_op jit(solution)/shard_map/ppermute | solution.py:606
  44.4 1.5 %gate.7 = (bf16[512,2048]{1,0:T(8,128)(2,1)}, f32[8,128]{1,0:T(8,128)S(1)}) custom-call(f32[512,2048]{1,0:T(8,128)S(1)} %unscaled_gate.1.refs_2_.unscaled, f32[512,128]{1,0:T(8,128)S(1)} %get-tuple-element.102.refs_0_.scale, bf16[528,128]{1,0:T(8,128)(2,1)S(1)} %get-tuple-element.112._), custom_call_target="tpu_custom_call" | custom-call | flops 268435456 | bytes 6692864 | tf_op jit(solution)/shard_map/gate/pallas_call | solution.py:128
  45.9 2.2 %key_value.3 = (f32[512,2048]{1,0:T(8,128)S(1)}, f32[512,2048]{1,0:T(8,128)S(1)}) custom-call(bf16[512,2048]{1,0:T(8,128)(2,1)S(1)} %get-tuple-element.76.q, bf16[512,2048]{1,0:T(8,128)(2,1)S(1)} %get-tuple-element.73.v, bf16[512,2048]{1,0:T(8,128)(2,1)S(1)} %get-tuple-element.105.dattn, f32[16,256,512]{2,1,0:T(8,128)S(1)} %get-tuple-element.106.table0, ...), custom_call_target="tpu_custom_call" | custom-call | flops 1073741824 | bytes 33558528 | tf_op jit(solution)/shard_map/key_value/pallas_call | solution.py:128
  49.2 3.5 %key_value.4 = (f32[512,2048]{1,0:T(8,128)S(1)}, f32[512,2048]{1,0:T(8,128)S(1)}) custom-call(bf16[512,2048]{1,0:T(8,128)(2,1)S(1)} %get-tuple-element.76.q, bf16[512,2048]{1,0:T(8,128)(2,1)S(1)} %get-tuple-element.73.v, bf16[512,2048]{1,0:T(8,128)(2,1)S(1)} %get-tuple-element.105.dattn, ...), custom_call_target="tpu_custom_call", output_to_operand_aliasing={{0}: (8, {}), {1}: (9, {})} | custom-call | flops 1610612736 | bytes 42078208 | tf_op jit(solution)/shard_map/key_value/pallas_call | solution.py:128
  53.8 1.9 %collective-permute-start.11 = (bf16[528,128]{1,0:T(8,128)(2,1)S(1)}, bf16[528,128]{1,0:T(8,128)(2,1)S(1)}, u32[]{:S(2)}, u32[]{:S(2)}) collective-permute-start(bf16[528,128]{1,0:T(8,128)(2,1)S(1)} %get-tuple-element.121._), channel_id=1, source_target_pairs={{0,16},{2,18},{4,20},{6,22},{8,24},{10,26},{12,28},{14,30},{16,0},... | collective-permute-start | bytes 405512 | tf_op jit(solution)/shard_map/ppermute | solution.py:606
  55.7 5.5 %query.1.refs_0_ = bf16[512,2048]{1,0:T(8,128)(2,1)S(1)} custom-call(bf16[512,2048]{1,0:T(8,128)(2,1)S(1)} %get-tuple-element.72.k, bf16[512,2048]{1,0:T(8,128)(2,1)S(1)} %get-tuple-element.73.v, bf16[512,2048]{1,0:T(8,128)(2,1)S(1)} %get-tuple-element.105.dattn, f32[16,512]{1,0:T(8,128)S(1)} %get-tuple-element.71.row, ...), custom_call_target="tpu_custom_call" | custom-call | flops 2415919104 | bytes 11194368 | tf_op jit(solution)/shard_map/query/pallas_call | solution.py:128
  61.6 1.6 %collective-permute-start.12 = (bf16[528,128]{1,0:T(8,128)(2,1)S(1)}, bf16[528,128]{1,0:T(8,128)(2,1)S(1)}, u32[]{:S(2)}, u32[]{:S(2)}) collective-permute-start(bf16[528,128]{1,0:T(8,128)(2,1)S(1)} %get-tuple-element.122._), channel_id=1, source_target_pairs={{0,4},{2,6},{4,0},{6,2},{8,12},{10,14},{12,8},{14,10},{16,20},{18,... | collective-permute-start | bytes 405512 | tf_op jit(solution)/shard_map/ppermute | solution.py:606
  63.2 3.3 %key_value.5 = (f32[512,2048]{1,0:T(8,128)S(1)}, f32[512,2048]{1,0:T(8,128)S(1)}, bf16[512,2048]{1,0:T(8,128)(2,1)}) custom-call(bf16[512,2048]{1,0:T(8,128)(2,1)S(1)} %get-tuple-element.76.q, bf16[512,2048]{1,0:T(8,128)(2,1)S(1)} %get-tuple-element.73.v, ...), custom_call_target="tpu_custom_call", output_to_operand_aliasing={{0}: (9, {}), {1}: (10, {})} | custom-call | flops 1610612736 | bytes 46272512 | tf_op jit(solution)/shard_map/key_value/pallas_call | solution.py:128
  68.6 2.7 %final.1 = (bf16[512,2048]{1,0:T(8,128)(2,1)}, bf16[512,2048]{1,0:T(8,128)(2,1)}, f32[1,2048]{1,0:T(1,128)}) custom-call(bf16[512,2048]{1,0:T(8,128)(2,1)S(1)} %get-tuple-element.72.k, bf16[512,2048]{1,0:T(8,128)(2,1)S(1)} %get-tuple-element.73.v, f32[512,2048]{1,0:T(8,128)S(1)} %get-tuple-element.125.refs_0_.dk, f32[512,2048]{1,0:T(8,128)S(1)} %get-tuple-element.126.dv, ...), custom_call_target="tpu_custom_call" | custom-call | flops 268435456 | bytes 20209664 | tf_op jit(solution)/shard_map/final/pallas_call | solution.py:128
  (43 shorter events, 16.4 us)
Async XLA Ops:
  3.5 3.9 %collective-permute-start = (f32[2,520,128]{2,1,0:T(8,128)S(1)}, f32[2,520,128]{2,1,0:T(8,128)S(1)}, u32[]{:S(2)}, u32[]{:S(2)}) collective-permute-start(f32[2,520,128]{2,1,0:T(8,128)S(1)} %get-tuple-element.74), channel_id=1, source_target_pairs={{0,2},{2,0},{4,6},{6,4},{8,10},{10,8},{12,14},{14,12},{16,18},{18,... | collective-permute-start | bytes 1597448 | tf_op jit(solution)/shard_map/ppermute | solution.py:606
  4.0 26.8 %collective-permute-start.3 = (bf16[256,2048]{1,0:T(8,128)(2,1)S(1)}, bf16[256,2048]{1,0:T(8,128)(2,1)S(1)}, u32[]{:S(2)}, u32[]{:S(2)}) collective-permute-start(bf16[256,2048]{1,0:T(8,128)(2,1)S(1)} %get-tuple-element.87), channel_id=1, source_target_pairs={{0,1},{1,0},{2,3},{3,2},{4,5},{5,4},{6,7},{7,6},{8,9},{9,8},{10,11... | collective-permute-start | bytes 3145736 | tf_op jit(solution)/shard_map/ppermute | solution.py:685
  7.5 5.7 %collective-permute-start.1 = (bf16[528,128]{1,0:T(8,128)(2,1)S(1)}, bf16[528,128]{1,0:T(8,128)(2,1)S(1)}, u32[]{:S(2)}, u32[]{:S(2)}) collective-permute-start(bf16[528,128]{1,0:T(8,128)(2,1)S(1)} %get-tuple-element.75._), channel_id=1, source_target_pairs={{0,4},{2,6},{4,0},{6,2},{8,12},{10,14},{12,8},{14,10},{16,20},{18,... | collective-permute-start | bytes 405512 | tf_op jit(solution)/shard_map/ppermute | solution.py:606
  13.3 5.3 %collective-permute-start.2 = (bf16[528,128]{1,0:T(8,128)(2,1)S(1)}, bf16[528,128]{1,0:T(8,128)(2,1)S(1)}, u32[]{:S(2)}, u32[]{:S(2)}) collective-permute-start(bf16[528,128]{1,0:T(8,128)(2,1)S(1)} %get-tuple-element.81._), channel_id=1, source_target_pairs={{0,8},{2,10},{4,12},{6,14},{8,0},{10,2},{12,4},{14,6},{16,24},{18,... | collective-permute-start | bytes 405512 | tf_op jit(solution)/shard_map/ppermute | solution.py:606
  16.6 2.0 %copy-start = (bf16[16,256,512]{2,1,0:T(8,128)(2,1)}, bf16[16,256,512]{2,1,0:T(8,128)(2,1)S(1)}, u32[]{:S(2)}) copy-start(bf16[16,256,512]{2,1,0:T(8,128)(2,1)S(1)} %get-tuple-element.108.probs0) | copy-start | bytes 12582916
  18.7 8.4 %collective-permute-start.4 = (bf16[528,128]{1,0:T(8,128)(2,1)S(1)}, bf16[528,128]{1,0:T(8,128)(2,1)S(1)}, u32[]{:S(2)}, u32[]{:S(2)}) collective-permute-start(bf16[528,128]{1,0:T(8,128)(2,1)S(1)} %get-tuple-element.86.refs_0_), channel_id=1, source_target_pairs={{0,16},{2,18},{4,20},{6,22},{8,24},{10,26},{12,28},{14,30},{16,0},... | collective-permute-start | bytes 405512 | tf_op jit(solution)/shard_map/ppermute | solution.py:606
  25.7 3.1 %copy-start.2 = (bf16[512,2048]{1,0:T(8,128)(2,1)S(1)}, bf16[512,2048]{1,0:T(8,128)(2,1)}, u32[]{:S(2)}) copy-start(bf16[512,2048]{1,0:T(8,128)(2,1)} %gate.6) | copy-start | bytes 6291460
  25.7 3.1 %copy-start.3 = (f32[2048]{0:T(1024)S(1)}, f32[2048]{0:T(1024)}, u32[]{:S(2)}) copy-start(f32[2048]{0:T(1024)} %param.12) | copy-start | bytes 24580
  27.2 5.1 %collective-permute-start.5 = (bf16[528,128]{1,0:T(8,128)(2,1)S(1)}, bf16[528,128]{1,0:T(8,128)(2,1)S(1)}, u32[]{:S(2)}, u32[]{:S(2)}) collective-permute-start(bf16[528,128]{1,0:T(8,128)(2,1)S(1)} %get-tuple-element.90._), channel_id=1, source_target_pairs={{0,4},{2,6},{4,0},{6,2},{8,12},{10,14},{12,8},{14,10},{16,20},{18,... | collective-permute-start | bytes 405512 | tf_op jit(solution)/shard_map/ppermute | solution.py:606
  32.6 1.6 %collective-permute-start.6 = (bf16[2,528,128]{2,1,0:T(8,128)(2,1)S(1)}, bf16[2,528,128]{2,1,0:T(8,128)(2,1)S(1)}, u32[]{:S(2)}, u32[]{:S(2)}) collective-permute-start(bf16[2,528,128]{2,1,0:T(8,128)(2,1)S(1)} %get-tuple-element.94), channel_id=1, source_target_pairs={{0,2},{2,0},{4,6},{6,4},{8,10},{10,8},{12,14},{14,12},{16,18},{18,... | collective-permute-start | bytes 811016 | tf_op jit(solution)/shard_map/ppermute | solution.py:606
  35.8 3.8 %collective-permute-start.7 = (f32[8,512]{1,0:T(8,128)S(1)}, f32[8,512]{1,0:T(8,128)S(1)}, u32[]{:S(2)}, u32[]{:S(2)}) collective-permute-start(f32[8,512]{1,0:T(8,128)S(1)} %get-tuple-element.101.refs_0_), channel_id=1, source_target_pairs={{0,1},{1,0},{2,3},{3,2},{4,5},{5,4},{6,7},{7,6},{8,9},{9,8},{10,11... | collective-permute-start | bytes 49160 | tf_op jit(solution)/shard_map/ppermute | solution.py:786
  41.1 1.6 %collective-permute-start.8 = (bf16[2,528,128]{2,1,0:T(8,128)(2,1)S(1)}, bf16[2,528,128]{2,1,0:T(8,128)(2,1)S(1)}, u32[]{:S(2)}, u32[]{:S(2)}) collective-permute-start(bf16[2,528,128]{2,1,0:T(8,128)(2,1)S(1)} %get-tuple-element.110), channel_id=1, source_target_pairs={{0,2},{2,0},{4,6},{6,4},{8,10},{10,8},{12,14},{14,12},{16,18},{18,... | collective-permute-start | bytes 811016 | tf_op jit(solution)/shard_map/ppermute | solution.py:606
  42.3 3.6 %copy-start.1 = (bf16[16,256,512]{2,1,0:T(8,128)(2,1)S(1)}, bf16[16,256,512]{2,1,0:T(8,128)(2,1)}, u32[]{:S(2)}) copy-start(bf16[16,256,512]{2,1,0:T(8,128)(2,1)} %copy-done) | copy-start | bytes 12582916
  42.8 5.7 %collective-permute-start.9 = (bf16[528,128]{1,0:T(8,128)(2,1)S(1)}, bf16[528,128]{1,0:T(8,128)(2,1)S(1)}, u32[]{:S(2)}, u32[]{:S(2)}) collective-permute-start(bf16[528,128]{1,0:T(8,128)(2,1)S(1)} %get-tuple-element.112._), channel_id=1, source_target_pairs={{0,4},{2,6},{4,0},{6,2},{8,12},{10,14},{12,8},{14,10},{16,20},{18,... | collective-permute-start | bytes 405512 | tf_op jit(solution)/shard_map/ppermute | solution.py:606
  48.6 5.1 %collective-permute-start.10 = (bf16[528,128]{1,0:T(8,128)(2,1)S(1)}, bf16[528,128]{1,0:T(8,128)(2,1)S(1)}, u32[]{:S(2)}, u32[]{:S(2)}) collective-permute-start(bf16[528,128]{1,0:T(8,128)(2,1)S(1)} %get-tuple-element.116._), channel_id=1, source_target_pairs={{0,8},{2,10},{4,12},{6,14},{8,0},{10,2},{12,4},{14,6},{16,24},{18,... | collective-permute-start | bytes 405512 | tf_op jit(solution)/shard_map/ppermute | solution.py:606
  53.8 7.7 %collective-permute-start.11 = (bf16[528,128]{1,0:T(8,128)(2,1)S(1)}, bf16[528,128]{1,0:T(8,128)(2,1)S(1)}, u32[]{:S(2)}, u32[]{:S(2)}) collective-permute-start(bf16[528,128]{1,0:T(8,128)(2,1)S(1)} %get-tuple-element.121._), channel_id=1, source_target_pairs={{0,16},{2,18},{4,20},{6,22},{8,24},{10,26},{12,28},{14,30},{16,0},... | collective-permute-start | bytes 405512 | tf_op jit(solution)/shard_map/ppermute | solution.py:606
  61.6 5.1 %collective-permute-start.12 = (bf16[528,128]{1,0:T(8,128)(2,1)S(1)}, bf16[528,128]{1,0:T(8,128)(2,1)S(1)}, u32[]{:S(2)}, u32[]{:S(2)}) collective-permute-start(bf16[528,128]{1,0:T(8,128)(2,1)S(1)} %get-tuple-element.122._), channel_id=1, source_target_pairs={{0,4},{2,6},{4,0},{6,2},{8,12},{10,14},{12,8},{14,10},{16,20},{18,... | collective-permute-start | bytes 405512 | tf_op jit(solution)/shard_map/ppermute | solution.py:606
  66.9 1.6 %collective-permute-start.13 = (bf16[2,528,128]{2,1,0:T(8,128)(2,1)S(1)}, bf16[2,528,128]{2,1,0:T(8,128)(2,1)S(1)}, u32[]{:S(2)}, u32[]{:S(2)}) collective-permute-start(bf16[2,528,128]{2,1,0:T(8,128)(2,1)S(1)} %get-tuple-element.128), channel_id=1, source_target_pairs={{0,2},{2,0},{4,6},{6,4},{8,10},{10,8},{12,14},{14,12},{16,18},{18,... | collective-permute-start | bytes 811016 | tf_op jit(solution)/shard_map/ppermute | solution.py:606

commit v16 on v15

--- a/solution.py
+++ b/solution.py
@@ -821,7 +821,7 @@
     cuts = [0, units // 4, 5 * units // 8, units]
 
     def key_value_beside(after, carried=()):
-        before = done.get("key_value", [])
+        before = done.get("key_value", [unscaled_gate, dscaled])
         piece = done.get("piece", 0)
         done["piece"] = piece + 1
         inputs = [queries, values, dattn, *done["probs"], after, *carried, *before]

time: 71.6 us -> 71.7 us (level)
  starting transfers between devices: 17.4 us -> 18.5 us
    ppermute x12, starting transfers between devices: 13.9 us -> 14.9 us  [swap(): return lax.ppermute(x, 'ctx', [(i, i ^ bit) for i in range(n)])]
  transfers between devices with their start and end apart: 14 -> 14, of which waited for: 11 -> 12; matrix products, arithmetic and copies ran while one was open for 0% -> 0% of each run, Pallas kernels for 49% -> 50%
where the time goes in v16:
time: 71.7 us; the launch traced here: 71.5 us
  Pallas kernels  45 us (63%)
  starting transfers between devices  18.5 us (26%)
  waiting for transfers between devices  7.04 us (10%)
  between operations  1.04 us (1%)
    pallas_call x31, Pallas kernels, call(): pl.pallas_call(body, in_specs=in_specs or [VMEM] * len(inputs), out_specs...  45 us
    ppermute x12, starting transfers between devices, swap(): return lax.ppermute(x, 'ctx', [(i, i ^ bit) for i in range(n)])  14.9 us
    ppermute x12, waiting for transfers between devices, swap(): return lax.ppermute(x, 'ctx', [(i, i ^ bit) for i in range(n)])  5.54 us
    ppermute x1, starting transfers between devices, local(): arrived = lax.ppermute(outs[4], 'tp', [(0, 1), (1, 0)])  2.56 us
    ppermute x1, waiting for transfers between devices, local(): others = lax.ppermute(sums, 'tp', [(0, 1), (1, 0)])  1.46 us
  transfers between devices with their start and end apart: 14, of which 12 were waited for; matrix products, arithmetic and copies ran while one was open for 0% of the time, Pallas kernels for 50%

profile of v16, /device:TPU:0, one launch (start us, length us, event | category | flops | bytes accessed | tf_op | source)
XLA Modules:
  0.0 71.5 jit_solution(14362969602297639424)
XLA Ops:
  0.6 2.8 %sent_states.1 = (f32[2,520,128]{2,1,0:T(8,128)S(1)}, f32[16,512]{1,0:T(8,128)S(1)}, bf16[512,2048]{1,0:T(8,128)(2,1)S(1)}, bf16[512,2048]{1,0:T(8,128)(2,1)S(1)}, bf16[256,2048]{1,0:T(8,128)(2,1)S(1)}) custom-call(bf16[512,2048]{1,0:T(8,128)(2,1)} %k_hbm.1, bf16[512,2048]{1,0:T(8,128)(2,1)} %v_hbm.1, f32[16,512]{1,0:T(8,128)} %ld_hbm.1, bf16[256,4096]{1,0:T(8,128)(2,1)} %grad.1), custom_call_target="tpu_custom_call" | custom-call | flops 134217728 | bytes 12132352 | tf_op jit(solution)/shard_map/sent_states/pallas_call | solution.py:128
  4.0 2.6 %collective-permute-start.3 = (bf16[256,2048]{1,0:T(8,128)(2,1)S(1)}, bf16[256,2048]{1,0:T(8,128)(2,1)S(1)}, u32[]{:S(2)}, u32[]{:S(2)}) collective-permute-start(bf16[256,2048]{1,0:T(8,128)(2,1)S(1)} %get-tuple-element.87), channel_id=1, source_target_pairs={{0,1},{1,0},{2,3},{3,2},{4,5},{5,4},{6,7},{7,6},{8,9},{9,8},{10,11... | collective-permute-start | bytes 3145736 | tf_op jit(solution)/shard_map/ppermute | solution.py:685
  7.5 1.6 %collective-permute-start.1 = (bf16[528,128]{1,0:T(8,128)(2,1)S(1)}, bf16[528,128]{1,0:T(8,128)(2,1)S(1)}, u32[]{:S(2)}, u32[]{:S(2)}) collective-permute-start(bf16[528,128]{1,0:T(8,128)(2,1)S(1)} %get-tuple-element.75._), channel_id=1, source_target_pairs={{0,4},{2,6},{4,0},{6,2},{8,12},{10,14},{12,8},{14,10},{16,20},{18,... | collective-permute-start | bytes 405512 | tf_op jit(solution)/shard_map/ppermute | solution.py:606
  9.1 1.6 %decays.1 = (f32[4,512,128]{2,1,0:T(8,128)S(1)}, f32[4,512,128]{2,1,0:T(8,128)S(1)}, bf16[512,2048]{1,0:T(8,128)(2,1)S(1)}) custom-call(f32[16,512]{1,0:T(8,128)S(1)} %get-tuple-element.71.row, bf16[512,2048]{1,0:T(8,128)(2,1)} %q_hbm.1, bf16[528,128]{1,0:T(8,128)(2,1)S(1)} %get-tuple-element.75._), custom_call_target="tpu_custom_call" | custom-call | bytes 6459392 | tf_op jit(solution)/shard_map/decays/pallas_call | solution.py:128
  10.7 1.6 %turned_probs.2 = (f32[16,256,512]{2,1,0:T(8,128)S(1)}, f32[16,256,256]{2,1,0:T(8,128)S(1)}, bf16[16,256,512]{2,1,0:T(8,128)(2,1)S(1)}, bf16[16,256,256]{2,1,0:T(8,128)(2,1)S(1)}) custom-call(bf16[512,2048]{1,0:T(8,128)(2,1)S(1)} %get-tuple-element.76.q, bf16[512,2048]{1,0:T(8,128)(2,1)S(1)} %get-tuple-element.72.k, f32[16,512]{1,0:T(8,128)S(1)} %get-tuple-element.71.row, ...), custom_call_target="tpu_custom_call" | custom-call | flops 536870912 | bytes 24285184 | tf_op jit(solution)/shard_map/turned_probs/pallas_call | solution.py:128
  13.3 1.6 %collective-permute-start.2 = (bf16[528,128]{1,0:T(8,128)(2,1)S(1)}, bf16[528,128]{1,0:T(8,128)(2,1)S(1)}, u32[]{:S(2)}, u32[]{:S(2)}) collective-permute-start(bf16[528,128]{1,0:T(8,128)(2,1)S(1)} %get-tuple-element.81._), channel_id=1, source_target_pairs={{0,8},{2,10},{4,12},{6,14},{8,0},{10,2},{12,4},{14,6},{16,24},{18,... | collective-permute-start | bytes 405512 | tf_op jit(solution)/shard_map/ppermute | solution.py:606
  15.0 1.6 %turned_probs.3 = (f32[16,256,512]{2,1,0:T(8,128)S(1)}, f32[16,256,256]{2,1,0:T(8,128)S(1)}, bf16[16,256,512]{2,1,0:T(8,128)(2,1)S(1)}, bf16[16,256,256]{2,1,0:T(8,128)(2,1)S(1)}) custom-call(bf16[512,2048]{1,0:T(8,128)(2,1)S(1)} %get-tuple-element.76.q, ...), custom_call_target="tpu_custom_call", output_to_operand_aliasing={{0}: (5, {}), {1}: (6, {}), {2}: (7, {}), {3}: (8, {})} | custom-call | flops 536870912 | bytes 43159552 | tf_op jit(solution)/shard_map/turned_probs/pallas_call | solution.py:128
  16.6 1.4 %intra.2.refs_1_ = f32[512,2048]{1,0:T(8,128)S(1)} custom-call(bf16[512,2048]{1,0:T(8,128)(2,1)S(1)} %get-tuple-element.76.q, bf16[512,2048]{1,0:T(8,128)(2,1)S(1)} %get-tuple-element.72.k, bf16[512,2048]{1,0:T(8,128)(2,1)S(1)} %get-tuple-element.73.v, f32[16,512]{1,0:T(8,128)S(1)} %get-tuple-element.71.row, f32[4,512,128]{2,1,0:T(8,128)S(1)} %get-tuple-element.77.col, ...), custom_call_target="tpu_custom_call" | custom-call | flops 536870912 | bytes 13664256 | tf_op jit(solution)/shard_map/intra/pallas_call | solution.py:128
  18.5 2.7 %collective-permute-start.4 = (bf16[528,128]{1,0:T(8,128)(2,1)S(1)}, bf16[528,128]{1,0:T(8,128)(2,1)S(1)}, u32[]{:S(2)}, u32[]{:S(2)}) collective-permute-start(bf16[528,128]{1,0:T(8,128)(2,1)S(1)} %get-tuple-element.86.refs_0_), channel_id=1, source_target_pairs={{0,16},{2,18},{4,20},{6,22},{8,24},{10,26},{12,28},{14,30},{16,0},... | collective-permute-start | bytes 405512 | tf_op jit(solution)/shard_map/ppermute | solution.py:606
  21.1 4.4 %intra.3.refs_0_._ = f32[512,2048]{1,0:T(8,128)S(1)} custom-call(bf16[512,2048]{1,0:T(8,128)(2,1)S(1)} %get-tuple-element.76.q, bf16[512,2048]{1,0:T(8,128)(2,1)S(1)} %get-tuple-element.72.k, bf16[512,2048]{1,0:T(8,128)(2,1)S(1)} %get-tuple-element.73.v, f32[16,512]{1,0:T(8,128)S(1)} %get-tuple-element.71.row, ...), custom_call_target="tpu_custom_call", output_to_operand_aliasing={{}: (6, {})} | custom-call | flops 1610612736 | bytes 15896576 | tf_op jit(solution)/shard_map/intra/pallas_call | solution.py:128
  26.7 1.6 %collective-permute-start.5 = (bf16[528,128]{1,0:T(8,128)(2,1)S(1)}, bf16[528,128]{1,0:T(8,128)(2,1)S(1)}, u32[]{:S(2)}, u32[]{:S(2)}) collective-permute-start(bf16[528,128]{1,0:T(8,128)(2,1)S(1)} %get-tuple-element.90._), channel_id=1, source_target_pairs={{0,4},{2,6},{4,0},{6,2},{8,12},{10,14},{12,8},{14,10},{16,20},{18,... | collective-permute-start | bytes 405512 | tf_op jit(solution)/shard_map/ppermute | solution.py:606
  28.3 1.9 %own_dscaled.1 = (f32[512,2048]{1,0:T(8,128)S(1)}, bf16[2048,512]{1,0:T(8,128)(2,1)S(1)}) custom-call(bf16[512,2048]{1,0:T(8,128)(2,1)S(1)} %copy-done, bf16[256,4096]{1,0:T(8,128)(2,1)} %grad.1, f32[1,2048]{1,0:T(1,128)S(1)} %bitcast.2, bf16[512,2048]{1,0:T(8,128)(2,1)S(1)} %get-tuple-element.76.q, f32[16,512]{1,0:T(8,128)S(1)} %get-tuple-element.71.row, ...), custom_call_target="tpu_custom_call" | custom-call | flops 268435456 | bytes 12759040 | tf_op jit(solution)/shard_map/own_dscaled/pallas_call | solution.py:128
  33.6 1.7 %attention.3 = (f32[512,2048]{1,0:T(8,128)S(1)}, f32[8,512]{1,0:T(8,128)S(1)}) custom-call(bf16[512,2048]{1,0:T(8,128)(2,1)S(1)} %get-tuple-element.76.q, f32[512,2048]{1,0:T(8,128)S(1)} %intra.3.refs_0_._, f32[512,2048]{1,0:T(8,128)S(1)} %got_dscaled.1.refs_0_.dscaled.refs_1_, ...), custom_call_target="tpu_custom_call", output_to_operand_aliasing={{0}: (5, {})} | custom-call | flops 134217728 | bytes 20733952 | tf_op jit(solution)/shard_map/attention/pallas_call | solution.py:128
  37.6 1.5 %collective-permute-done.7.refs_1_ = f32[8,512]{1,0:T(8,128)S(1)} collective-permute-done((f32[8,512]{1,0:T(8,128)S(1)}, f32[8,512]{1,0:T(8,128)S(1)}, u32[]{:S(2)}, u32[]{:S(2)}) %collective-permute-start.7) | collective-permute-done | bytes 16416 | tf_op jit(solution)/shard_map/ppermute | solution.py:786
  39.1 1.5 %sent_dattn.1 = (bf16[512,2048]{1,0:T(8,128)(2,1)S(1)}, bf16[2,528,128]{2,1,0:T(8,128)(2,1)S(1)}, f32[512,128]{1,0:T(8,128)S(1)}, f32[512,128]{1,0:T(8,128)S(1)}) custom-call(f32[512,2048]{1,0:T(8,128)S(1)} %get-tuple-element.99.att, f32[512,2048]{1,0:T(8,128)S(1)} %got_dscaled.1.refs_0_.dscaled.refs_1_, bf16[2048,512]{1,0:T(8,128)(2,1)S(1)} %get-tuple-element.100.turned, ...), custom_call_target="tpu_custom_call" | custom-call | flops 134217728 | bytes 17645568 | tf_op jit(solution)/shard_map/sent_dattn/pallas_call | solution.py:128
  42.3 1.6 %collective-permute-start.9 = (bf16[528,128]{1,0:T(8,128)(2,1)S(1)}, bf16[528,128]{1,0:T(8,128)(2,1)S(1)}, u32[]{:S(2)}, u32[]{:S(2)}) collective-permute-start(bf16[528,128]{1,0:T(8,128)(2,1)S(1)} %get-tuple-element.112._), channel_id=1, source_target_pairs={{0,4},{2,6},{4,0},{6,2},{8,12},{10,14},{12,8},{14,10},{16,20},{18,... | collective-permute-start | bytes 405512 | tf_op jit(solution)/shard_map/ppermute | solution.py:606
  43.8 1.5 %gate.7 = (bf16[512,2048]{1,0:T(8,128)(2,1)}, f32[8,128]{1,0:T(8,128)S(1)}) custom-call(f32[512,2048]{1,0:T(8,128)S(1)} %unscaled_gate.1.refs_2_.unscaled.refs_0_, f32[512,128]{1,0:T(8,128)S(1)} %get-tuple-element.102.refs_0_.scale, bf16[528,128]{1,0:T(8,128)(2,1)S(1)} %get-tuple-element.112._), custom_call_target="tpu_custom_call" | custom-call | flops 268435456 | bytes 6692864 | tf_op jit(solution)/shard_map/gate/pallas_call | solution.py:128
  45.4 2.2 %key_value.3 = (f32[512,2048]{1,0:T(8,128)S(1)}, f32[512,2048]{1,0:T(8,128)S(1)}) custom-call(bf16[512,2048]{1,0:T(8,128)(2,1)S(1)} %get-tuple-element.76.q, bf16[512,2048]{1,0:T(8,128)(2,1)S(1)} %get-tuple-element.73.v, bf16[512,2048]{1,0:T(8,128)(2,1)S(1)} %get-tuple-element.105.dattn, ...), custom_call_target="tpu_custom_call", output_to_operand_aliasing={{0}: (8, {}), {1}: (9, {})} | custom-call | flops 1073741824 | bytes 41947136 | tf_op jit(solution)/shard_map/key_value/pallas_call | solution.py:128
  49.2 3.5 %key_value.4 = (f32[512,2048]{1,0:T(8,128)S(1)}, f32[512,2048]{1,0:T(8,128)S(1)}) custom-call(bf16[512,2048]{1,0:T(8,128)(2,1)S(1)} %get-tuple-element.76.q, bf16[512,2048]{1,0:T(8,128)(2,1)S(1)} %get-tuple-element.73.v, bf16[512,2048]{1,0:T(8,128)(2,1)S(1)} %get-tuple-element.105.dattn, ...), custom_call_target="tpu_custom_call", output_to_operand_aliasing={{0}: (8, {}), {1}: (9, {})} | custom-call | flops 1610612736 | bytes 42078208 | tf_op jit(solution)/shard_map/key_value/pallas_call | solution.py:128
  53.2 2.5 %collective-permute-start.11 = (bf16[528,128]{1,0:T(8,128)(2,1)S(1)}, bf16[528,128]{1,0:T(8,128)(2,1)S(1)}, u32[]{:S(2)}, u32[]{:S(2)}) collective-permute-start(bf16[528,128]{1,0:T(8,128)(2,1)S(1)} %get-tuple-element.121._), channel_id=1, source_target_pairs={{0,16},{2,18},{4,20},{6,22},{8,24},{10,26},{12,28},{14,30},{16,0},... | collective-permute-start | bytes 405512 | tf_op jit(solution)/shard_map/ppermute | solution.py:606
  55.7 5.5 %query.1.refs_0_ = bf16[512,2048]{1,0:T(8,128)(2,1)S(1)} custom-call(bf16[512,2048]{1,0:T(8,128)(2,1)S(1)} %get-tuple-element.72.k, bf16[512,2048]{1,0:T(8,128)(2,1)S(1)} %get-tuple-element.73.v, bf16[512,2048]{1,0:T(8,128)(2,1)S(1)} %get-tuple-element.105.dattn, f32[16,512]{1,0:T(8,128)S(1)} %get-tuple-element.71.row, ...), custom_call_target="tpu_custom_call" | custom-call | flops 2415919104 | bytes 11194368 | tf_op jit(solution)/shard_map/query/pallas_call | solution.py:128
  61.7 1.4 %collective-permute-start.12 = (bf16[528,128]{1,0:T(8,128)(2,1)S(1)}, bf16[528,128]{1,0:T(8,128)(2,1)S(1)}, u32[]{:S(2)}, u32[]{:S(2)}) collective-permute-start(bf16[528,128]{1,0:T(8,128)(2,1)S(1)} %get-tuple-element.122._), channel_id=1, source_target_pairs={{0,4},{2,6},{4,0},{6,2},{8,12},{10,14},{12,8},{14,10},{16,20},{18,... | collective-permute-start | bytes 405512 | tf_op jit(solution)/shard_map/ppermute | solution.py:606
  63.1 3.3 %key_value.5 = (f32[512,2048]{1,0:T(8,128)S(1)}, f32[512,2048]{1,0:T(8,128)S(1)}, bf16[512,2048]{1,0:T(8,128)(2,1)}) custom-call(bf16[512,2048]{1,0:T(8,128)(2,1)S(1)} %get-tuple-element.76.q, bf16[512,2048]{1,0:T(8,128)(2,1)S(1)} %get-tuple-element.73.v, ...), custom_call_target="tpu_custom_call", output_to_operand_aliasing={{0}: (9, {}), {1}: (10, {})} | custom-call | flops 1610612736 | bytes 46272512 | tf_op jit(solution)/shard_map/key_value/pallas_call | solution.py:128
  68.6 2.7 %final.1 = (bf16[512,2048]{1,0:T(8,128)(2,1)}, bf16[512,2048]{1,0:T(8,128)(2,1)}, f32[1,2048]{1,0:T(1,128)}) custom-call(bf16[512,2048]{1,0:T(8,128)(2,1)S(1)} %get-tuple-element.72.k, bf16[512,2048]{1,0:T(8,128)(2,1)S(1)} %get-tuple-element.73.v, f32[512,2048]{1,0:T(8,128)S(1)} %get-tuple-element.125.refs_0_.dk, f32[512,2048]{1,0:T(8,128)S(1)} %get-tuple-element.126.dv, ...), custom_call_target="tpu_custom_call" | custom-call | flops 268435456 | bytes 20209664 | tf_op jit(solution)/shard_map/final/pallas_call | solution.py:128
  (39 shorter events, 16.2 us)
Async XLA Ops:
  3.5 3.9 %collective-permute-start = (f32[2,520,128]{2,1,0:T(8,128)S(1)}, f32[2,520,128]{2,1,0:T(8,128)S(1)}, u32[]{:S(2)}, u32[]{:S(2)}) collective-permute-start(f32[2,520,128]{2,1,0:T(8,128)S(1)} %get-tuple-element.74), channel_id=1, source_target_pairs={{0,2},{2,0},{4,6},{6,4},{8,10},{10,8},{12,14},{14,12},{16,18},{18,... | collective-permute-start | bytes 1597448 | tf_op jit(solution)/shard_map/ppermute | solution.py:606
  4.0 26.3 %collective-permute-start.3 = (bf16[256,2048]{1,0:T(8,128)(2,1)S(1)}, bf16[256,2048]{1,0:T(8,128)(2,1)S(1)}, u32[]{:S(2)}, u32[]{:S(2)}) collective-permute-start(bf16[256,2048]{1,0:T(8,128)(2,1)S(1)} %get-tuple-element.87), channel_id=1, source_target_pairs={{0,1},{1,0},{2,3},{3,2},{4,5},{5,4},{6,7},{7,6},{8,9},{9,8},{10,11... | collective-permute-start | bytes 3145736 | tf_op jit(solution)/shard_map/ppermute | solution.py:685
  7.5 5.7 %collective-permute-start.1 = (bf16[528,128]{1,0:T(8,128)(2,1)S(1)}, bf16[528,128]{1,0:T(8,128)(2,1)S(1)}, u32[]{:S(2)}, u32[]{:S(2)}) collective-permute-start(bf16[528,128]{1,0:T(8,128)(2,1)S(1)} %get-tuple-element.75._), channel_id=1, source_target_pairs={{0,4},{2,6},{4,0},{6,2},{8,12},{10,14},{12,8},{14,10},{16,20},{18,... | collective-permute-start | bytes 405512 | tf_op jit(solution)/shard_map/ppermute | solution.py:606
  13.3 5.1 %collective-permute-start.2 = (bf16[528,128]{1,0:T(8,128)(2,1)S(1)}, bf16[528,128]{1,0:T(8,128)(2,1)S(1)}, u32[]{:S(2)}, u32[]{:S(2)}) collective-permute-start(bf16[528,128]{1,0:T(8,128)(2,1)S(1)} %get-tuple-element.81._), channel_id=1, source_target_pairs={{0,8},{2,10},{4,12},{6,14},{8,0},{10,2},{12,4},{14,6},{16,24},{18,... | collective-permute-start | bytes 405512 | tf_op jit(solution)/shard_map/ppermute | solution.py:606
  18.5 8.1 %collective-permute-start.4 = (bf16[528,128]{1,0:T(8,128)(2,1)S(1)}, bf16[528,128]{1,0:T(8,128)(2,1)S(1)}, u32[]{:S(2)}, u32[]{:S(2)}) collective-permute-start(bf16[528,128]{1,0:T(8,128)(2,1)S(1)} %get-tuple-element.86.refs_0_), channel_id=1, source_target_pairs={{0,16},{2,18},{4,20},{6,22},{8,24},{10,26},{12,28},{14,30},{16,0},... | collective-permute-start | bytes 405512 | tf_op jit(solution)/shard_map/ppermute | solution.py:606
  25.5 2.8 %copy-start = (bf16[512,2048]{1,0:T(8,128)(2,1)S(1)}, bf16[512,2048]{1,0:T(8,128)(2,1)}, u32[]{:S(2)}) copy-start(bf16[512,2048]{1,0:T(8,128)(2,1)} %gate.6) | copy-start | bytes 6291460
  25.5 2.8 %copy-start.1 = (f32[2048]{0:T(1024)S(1)}, f32[2048]{0:T(1024)}, u32[]{:S(2)}) copy-start(f32[2048]{0:T(1024)} %param.12) | copy-start | bytes 24580
  26.7 5.1 %collective-permute-start.5 = (bf16[528,128]{1,0:T(8,128)(2,1)S(1)}, bf16[528,128]{1,0:T(8,128)(2,1)S(1)}, u32[]{:S(2)}, u32[]{:S(2)}) collective-permute-start(bf16[528,128]{1,0:T(8,128)(2,1)S(1)} %get-tuple-element.90._), channel_id=1, source_target_pairs={{0,4},{2,6},{4,0},{6,2},{8,12},{10,14},{12,8},{14,10},{16,20},{18,... | collective-permute-start | bytes 405512 | tf_op jit(solution)/shard_map/ppermute | solution.py:606
  32.0 1.6 %collective-permute-start.6 = (bf16[2,528,128]{2,1,0:T(8,128)(2,1)S(1)}, bf16[2,528,128]{2,1,0:T(8,128)(2,1)S(1)}, u32[]{:S(2)}, u32[]{:S(2)}) collective-permute-start(bf16[2,528,128]{2,1,0:T(8,128)(2,1)S(1)} %get-tuple-element.94), channel_id=1, source_target_pairs={{0,2},{2,0},{4,6},{6,4},{8,10},{10,8},{12,14},{14,12},{16,18},{18,... | collective-permute-start | bytes 811016 | tf_op jit(solution)/shard_map/ppermute | solution.py:606
  35.3 3.8 %collective-permute-start.7 = (f32[8,512]{1,0:T(8,128)S(1)}, f32[8,512]{1,0:T(8,128)S(1)}, u32[]{:S(2)}, u32[]{:S(2)}) collective-permute-start(f32[8,512]{1,0:T(8,128)S(1)} %get-tuple-element.101.refs_0_), channel_id=1, source_target_pairs={{0,1},{1,0},{2,3},{3,2},{4,5},{5,4},{6,7},{7,6},{8,9},{9,8},{10,11... | collective-permute-start | bytes 49160 | tf_op jit(solution)/shard_map/ppermute | solution.py:786
  40.5 1.6 %collective-permute-start.8 = (bf16[2,528,128]{2,1,0:T(8,128)(2,1)S(1)}, bf16[2,528,128]{2,1,0:T(8,128)(2,1)S(1)}, u32[]{:S(2)}, u32[]{:S(2)}) collective-permute-start(bf16[2,528,128]{2,1,0:T(8,128)(2,1)S(1)} %get-tuple-element.110), channel_id=1, source_target_pairs={{0,2},{2,0},{4,6},{6,4},{8,10},{10,8},{12,14},{14,12},{16,18},{18,... | collective-permute-start | bytes 811016 | tf_op jit(solution)/shard_map/ppermute | solution.py:606
  42.3 5.7 %collective-permute-start.9 = (bf16[528,128]{1,0:T(8,128)(2,1)S(1)}, bf16[528,128]{1,0:T(8,128)(2,1)S(1)}, u32[]{:S(2)}, u32[]{:S(2)}) collective-permute-start(bf16[528,128]{1,0:T(8,128)(2,1)S(1)} %get-tuple-element.112._), channel_id=1, source_target_pairs={{0,4},{2,6},{4,0},{6,2},{8,12},{10,14},{12,8},{14,10},{16,20},{18,... | collective-permute-start | bytes 405512 | tf_op jit(solution)/shard_map/ppermute | solution.py:606
  48.0 5.1 %collective-permute-start.10 = (bf16[528,128]{1,0:T(8,128)(2,1)S(1)}, bf16[528,128]{1,0:T(8,128)(2,1)S(1)}, u32[]{:S(2)}, u32[]{:S(2)}) collective-permute-start(bf16[528,128]{1,0:T(8,128)(2,1)S(1)} %get-tuple-element.116._), channel_id=1, source_target_pairs={{0,8},{2,10},{4,12},{6,14},{8,0},{10,2},{12,4},{14,6},{16,24},{18,... | collective-permute-start | bytes 405512 | tf_op jit(solution)/shard_map/ppermute | solution.py:606
  53.2 8.3 %collective-permute-start.11 = (bf16[528,128]{1,0:T(8,128)(2,1)S(1)}, bf16[528,128]{1,0:T(8,128)(2,1)S(1)}, u32[]{:S(2)}, u32[]{:S(2)}) collective-permute-start(bf16[528,128]{1,0:T(8,128)(2,1)S(1)} %get-tuple-element.121._), channel_id=1, source_target_pairs={{0,16},{2,18},{4,20},{6,22},{8,24},{10,26},{12,28},{14,30},{16,0},... | collective-permute-start | bytes 405512 | tf_op jit(solution)/shard_map/ppermute | solution.py:606
  61.7 5.1 %collective-permute-start.12 = (bf16[528,128]{1,0:T(8,128)(2,1)S(1)}, bf16[528,128]{1,0:T(8,128)(2,1)S(1)}, u32[]{:S(2)}, u32[]{:S(2)}) collective-permute-start(bf16[528,128]{1,0:T(8,128)(2,1)S(1)} %get-tuple-element.122._), channel_id=1, source_target_pairs={{0,4},{2,6},{4,0},{6,2},{8,12},{10,14},{12,8},{14,10},{16,20},{18,... | collective-permute-start | bytes 405512 | tf_op jit(solution)/shard_map/ppermute | solution.py:606
  67.0 1.6 %collective-permute-start.13 = (bf16[2,528,128]{2,1,0:T(8,128)(2,1)S(1)}, bf16[2,528,128]{2,1,0:T(8,128)(2,1)S(1)}, u32[]{:S(2)}, u32[]{:S(2)}) collective-permute-start(bf16[2,528,128]{2,1,0:T(8,128)(2,1)S(1)} %get-tuple-element.128), channel_id=1, source_target_pairs={{0,2},{2,0},{4,6},{6,4},{8,10},{10,8},{12,14},{14,12},{16,18},{18,... | collective-permute-start | bytes 811016 | tf_op jit(solution)/shard_map/ppermute | solution.py:606

commit v17 on v15

--- a/solution.py
+++ b/solution.py
@@ -576,16 +576,16 @@
         copy.start()
         copies.append(copy)
 
+    for y in range(2):
+        for j, _, count, c in several(quarter_of(y, True), hq):
+            place = slice(j * HEAD, (j + count) * HEAD)
+            send(own_key.at[y, :, place], key_grad, c)
+            send(own_value.at[y, :, place], value_grad, c)
     gains[...] = own_gain[...]
     for y in range(2):
         for j, (_, _, total) in enumerate(read_narrow(state.at[y], hq)):
             gains[:, head_at(quarter_of(y, False), hq, j)[1]] = total
     send(gains, gain_grad, slice(None))
-    for y in range(2):
-        for j, _, count, c in several(quarter_of(y, True), hq):
-            place = slice(j * HEAD, (j + count) * HEAD)
-            send(own_key.at[y, :, place], key_grad, c)
-            send(own_value.at[y, :, place], value_grad, c)
     for y in range(2):
         shrink = fades(col, y, False)
         for j, _, count, c in several(quarter_of(y, False), hq):

time: 71.6 us -> 71.5 us (level)
  no operation moved by 1% of the time
where the time goes in v17:
time: 71.5 us; the launch traced here: 71.3 us
  Pallas kernels  44.6 us (62%)
  starting transfers between devices  17.4 us (24%)
  waiting for transfers between devices  7.69 us (11%)
  between operations  1.07 us (1%)
    pallas_call x31, Pallas kernels, call(): pl.pallas_call(body, in_specs=in_specs or [VMEM] * len(inputs), out_specs...  44.6 us
    ppermute x12, starting transfers between devices, swap(): return lax.ppermute(x, 'ctx', [(i, i ^ bit) for i in range(n)])  13.9 us
    ppermute x12, waiting for transfers between devices, swap(): return lax.ppermute(x, 'ctx', [(i, i ^ bit) for i in range(n)])  5.99 us
    ppermute x1, starting transfers between devices, local(): arrived = lax.ppermute(outs[4], 'tp', [(0, 1), (1, 0)])  2.56 us
    ppermute x1, waiting for transfers between devices, local(): others = lax.ppermute(sums, 'tp', [(0, 1), (1, 0)])  1.7 us
  transfers between devices with their start and end apart: 14, of which 11 were waited for; matrix products, arithmetic and copies ran while one was open for 0% of the time, Pallas kernels for 49%

profile of v17, /device:TPU:0, one launch (start us, length us, event | category | flops | bytes accessed | tf_op | source)
XLA Modules:
  0.0 71.3 jit_solution(8475123013407735058)
XLA Ops:
  0.6 2.8 %sent_states.1 = (f32[2,520,128]{2,1,0:T(8,128)S(1)}, f32[16,512]{1,0:T(8,128)S(1)}, bf16[512,2048]{1,0:T(8,128)(2,1)S(1)}, bf16[512,2048]{1,0:T(8,128)(2,1)S(1)}, bf16[256,2048]{1,0:T(8,128)(2,1)S(1)}) custom-call(bf16[512,2048]{1,0:T(8,128)(2,1)} %k_hbm.1, bf16[512,2048]{1,0:T(8,128)(2,1)} %v_hbm.1, f32[16,512]{1,0:T(8,128)} %ld_hbm.1, bf16[256,4096]{1,0:T(8,128)(2,1)} %grad.1), custom_call_target="tpu_custom_call" | custom-call | flops 134217728 | bytes 12132352 | tf_op jit(solution)/shard_map/sent_states/pallas_call | solution.py:128
  4.0 2.6 %collective-permute-start.3 = (bf16[256,2048]{1,0:T(8,128)(2,1)S(1)}, bf16[256,2048]{1,0:T(8,128)(2,1)S(1)}, u32[]{:S(2)}, u32[]{:S(2)}) collective-permute-start(bf16[256,2048]{1,0:T(8,128)(2,1)S(1)} %get-tuple-element.87), channel_id=1, source_target_pairs={{0,1},{1,0},{2,3},{3,2},{4,5},{5,4},{6,7},{7,6},{8,9},{9,8},{10,11... | collective-permute-start | bytes 3145736 | tf_op jit(solution)/shard_map/ppermute | solution.py:685
  7.5 1.6 %collective-permute-start.1 = (bf16[528,128]{1,0:T(8,128)(2,1)S(1)}, bf16[528,128]{1,0:T(8,128)(2,1)S(1)}, u32[]{:S(2)}, u32[]{:S(2)}) collective-permute-start(bf16[528,128]{1,0:T(8,128)(2,1)S(1)} %get-tuple-element.75._), channel_id=1, source_target_pairs={{0,4},{2,6},{4,0},{6,2},{8,12},{10,14},{12,8},{14,10},{16,20},{18,... | collective-permute-start | bytes 405512 | tf_op jit(solution)/shard_map/ppermute | solution.py:606
  9.1 1.6 %decays.1 = (f32[4,512,128]{2,1,0:T(8,128)S(1)}, f32[4,512,128]{2,1,0:T(8,128)S(1)}, bf16[512,2048]{1,0:T(8,128)(2,1)S(1)}) custom-call(f32[16,512]{1,0:T(8,128)S(1)} %get-tuple-element.71.row, bf16[512,2048]{1,0:T(8,128)(2,1)} %q_hbm.1, bf16[528,128]{1,0:T(8,128)(2,1)S(1)} %get-tuple-element.75._), custom_call_target="tpu_custom_call" | custom-call | bytes 6459392 | tf_op jit(solution)/shard_map/decays/pallas_call | solution.py:128
  10.7 1.6 %turned_probs.2 = (f32[16,256,512]{2,1,0:T(8,128)S(1)}, f32[16,256,256]{2,1,0:T(8,128)S(1)}, bf16[16,256,512]{2,1,0:T(8,128)(2,1)S(1)}, bf16[16,256,256]{2,1,0:T(8,128)(2,1)S(1)}) custom-call(bf16[512,2048]{1,0:T(8,128)(2,1)S(1)} %get-tuple-element.76.q, bf16[512,2048]{1,0:T(8,128)(2,1)S(1)} %get-tuple-element.72.k, f32[16,512]{1,0:T(8,128)S(1)} %get-tuple-element.71.row, ...), custom_call_target="tpu_custom_call" | custom-call | flops 536870912 | bytes 24285184 | tf_op jit(solution)/shard_map/turned_probs/pallas_call | solution.py:128
  13.3 1.6 %collective-permute-start.2 = (bf16[528,128]{1,0:T(8,128)(2,1)S(1)}, bf16[528,128]{1,0:T(8,128)(2,1)S(1)}, u32[]{:S(2)}, u32[]{:S(2)}) collective-permute-start(bf16[528,128]{1,0:T(8,128)(2,1)S(1)} %get-tuple-element.81._), channel_id=1, source_target_pairs={{0,8},{2,10},{4,12},{6,14},{8,0},{10,2},{12,4},{14,6},{16,24},{18,... | collective-permute-start | bytes 405512 | tf_op jit(solution)/shard_map/ppermute | solution.py:606
  15.0 1.6 %turned_probs.3 = (f32[16,256,512]{2,1,0:T(8,128)S(1)}, f32[16,256,256]{2,1,0:T(8,128)S(1)}, bf16[16,256,512]{2,1,0:T(8,128)(2,1)S(1)}, bf16[16,256,256]{2,1,0:T(8,128)(2,1)S(1)}) custom-call(bf16[512,2048]{1,0:T(8,128)(2,1)S(1)} %get-tuple-element.76.q, ...), custom_call_target="tpu_custom_call", output_to_operand_aliasing={{0}: (5, {}), {1}: (6, {}), {2}: (7, {}), {3}: (8, {})} | custom-call | flops 536870912 | bytes 43159552 | tf_op jit(solution)/shard_map/turned_probs/pallas_call | solution.py:128
  16.6 1.4 %intra.2.refs_1_ = f32[512,2048]{1,0:T(8,128)S(1)} custom-call(bf16[512,2048]{1,0:T(8,128)(2,1)S(1)} %get-tuple-element.76.q, bf16[512,2048]{1,0:T(8,128)(2,1)S(1)} %get-tuple-element.72.k, bf16[512,2048]{1,0:T(8,128)(2,1)S(1)} %get-tuple-element.73.v, f32[16,512]{1,0:T(8,128)S(1)} %get-tuple-element.71.row, f32[4,512,128]{2,1,0:T(8,128)S(1)} %get-tuple-element.77.col, ...), custom_call_target="tpu_custom_call" | custom-call | flops 536870912 | bytes 13664256 | tf_op jit(solution)/shard_map/intra/pallas_call | solution.py:128
  18.7 2.7 %collective-permute-start.4 = (bf16[528,128]{1,0:T(8,128)(2,1)S(1)}, bf16[528,128]{1,0:T(8,128)(2,1)S(1)}, u32[]{:S(2)}, u32[]{:S(2)}) collective-permute-start(bf16[528,128]{1,0:T(8,128)(2,1)S(1)} %get-tuple-element.86.refs_0_), channel_id=1, source_target_pairs={{0,16},{2,18},{4,20},{6,22},{8,24},{10,26},{12,28},{14,30},{16,0},... | collective-permute-start | bytes 405512 | tf_op jit(solution)/shard_map/ppermute | solution.py:606
  21.3 4.4 %intra.3.refs_0_._ = f32[512,2048]{1,0:T(8,128)S(1)} custom-call(bf16[512,2048]{1,0:T(8,128)(2,1)S(1)} %get-tuple-element.76.q, bf16[512,2048]{1,0:T(8,128)(2,1)S(1)} %get-tuple-element.72.k, bf16[512,2048]{1,0:T(8,128)(2,1)S(1)} %get-tuple-element.73.v, f32[16,512]{1,0:T(8,128)S(1)} %get-tuple-element.71.row, ...), custom_call_target="tpu_custom_call", output_to_operand_aliasing={{}: (6, {})} | custom-call | flops 1610612736 | bytes 15896576 | tf_op jit(solution)/shard_map/intra/pallas_call | solution.py:128
  27.2 1.6 %collective-permute-start.5 = (bf16[528,128]{1,0:T(8,128)(2,1)S(1)}, bf16[528,128]{1,0:T(8,128)(2,1)S(1)}, u32[]{:S(2)}, u32[]{:S(2)}) collective-permute-start(bf16[528,128]{1,0:T(8,128)(2,1)S(1)} %get-tuple-element.90._), channel_id=1, source_target_pairs={{0,4},{2,6},{4,0},{6,2},{8,12},{10,14},{12,8},{14,10},{16,20},{18,... | collective-permute-start | bytes 405512 | tf_op jit(solution)/shard_map/ppermute | solution.py:606
  28.8 1.9 %own_dscaled.1 = (f32[512,2048]{1,0:T(8,128)S(1)}, bf16[2048,512]{1,0:T(8,128)(2,1)S(1)}) custom-call(bf16[512,2048]{1,0:T(8,128)(2,1)S(1)} %copy-done.2, bf16[256,4096]{1,0:T(8,128)(2,1)} %grad.1, f32[1,2048]{1,0:T(1,128)S(1)} %bitcast.2, bf16[512,2048]{1,0:T(8,128)(2,1)S(1)} %get-tuple-element.76.q, f32[16,512]{1,0:T(8,128)S(1)} %get-tuple-element.71.row, ...), custom_call_target="tpu_custom_call" | custom-call | flops 268435456 | bytes 12759040 | tf_op jit(solution)/shard_map/own_dscaled/pallas_call | solution.py:128
  34.2 1.6 %attention.3 = (f32[512,2048]{1,0:T(8,128)S(1)}, f32[8,512]{1,0:T(8,128)S(1)}) custom-call(bf16[512,2048]{1,0:T(8,128)(2,1)S(1)} %get-tuple-element.76.q, f32[512,2048]{1,0:T(8,128)S(1)} %intra.3.refs_0_._, f32[512,2048]{1,0:T(8,128)S(1)} %got_dscaled.1.refs_0_.dscaled, ...), custom_call_target="tpu_custom_call", output_to_operand_aliasing={{0}: (5, {})} | custom-call | flops 134217728 | bytes 20733952 | tf_op jit(solution)/shard_map/attention/pallas_call | solution.py:128
  37.9 1.7 %collective-permute-done.7.refs_1_ = f32[8,512]{1,0:T(8,128)S(1)} collective-permute-done((f32[8,512]{1,0:T(8,128)S(1)}, f32[8,512]{1,0:T(8,128)S(1)}, u32[]{:S(2)}, u32[]{:S(2)}) %collective-permute-start.7) | collective-permute-done | bytes 16416 | tf_op jit(solution)/shard_map/ppermute | solution.py:786
  39.6 1.5 %sent_dattn.1 = (bf16[512,2048]{1,0:T(8,128)(2,1)S(1)}, bf16[2,528,128]{2,1,0:T(8,128)(2,1)S(1)}, f32[512,128]{1,0:T(8,128)S(1)}, f32[512,128]{1,0:T(8,128)S(1)}) custom-call(f32[512,2048]{1,0:T(8,128)S(1)} %get-tuple-element.99.att, f32[512,2048]{1,0:T(8,128)S(1)} %got_dscaled.1.refs_0_.dscaled, bf16[2048,512]{1,0:T(8,128)(2,1)S(1)} %get-tuple-element.100.turned, ...), custom_call_target="tpu_custom_call" | custom-call | flops 134217728 | bytes 17645568 | tf_op jit(solution)/shard_map/sent_dattn/pallas_call | solution.py:128
  42.8 1.6 %collective-permute-start.9 = (bf16[528,128]{1,0:T(8,128)(2,1)S(1)}, bf16[528,128]{1,0:T(8,128)(2,1)S(1)}, u32[]{:S(2)}, u32[]{:S(2)}) collective-permute-start(bf16[528,128]{1,0:T(8,128)(2,1)S(1)} %get-tuple-element.112._), channel_id=1, source_target_pairs={{0,4},{2,6},{4,0},{6,2},{8,12},{10,14},{12,8},{14,10},{16,20},{18,... | collective-permute-start | bytes 405512 | tf_op jit(solution)/shard_map/ppermute | solution.py:606
  44.4 1.5 %gate.7 = (bf16[512,2048]{1,0:T(8,128)(2,1)}, f32[8,128]{1,0:T(8,128)S(1)}) custom-call(f32[512,2048]{1,0:T(8,128)S(1)} %unscaled_gate.1.refs_2_.unscaled, f32[512,128]{1,0:T(8,128)S(1)} %get-tuple-element.102.refs_0_.scale, bf16[528,128]{1,0:T(8,128)(2,1)S(1)} %get-tuple-element.112._), custom_call_target="tpu_custom_call" | custom-call | flops 268435456 | bytes 6692864 | tf_op jit(solution)/shard_map/gate/pallas_call | solution.py:128
  45.9 2.2 %key_value.3 = (f32[512,2048]{1,0:T(8,128)S(1)}, f32[512,2048]{1,0:T(8,128)S(1)}) custom-call(bf16[512,2048]{1,0:T(8,128)(2,1)S(1)} %get-tuple-element.76.q, bf16[512,2048]{1,0:T(8,128)(2,1)S(1)} %get-tuple-element.73.v, bf16[512,2048]{1,0:T(8,128)(2,1)S(1)} %get-tuple-element.105.dattn, f32[16,256,512]{2,1,0:T(8,128)S(1)} %get-tuple-element.106.table0, ...), custom_call_target="tpu_custom_call" | custom-call | flops 1073741824 | bytes 33558528 | tf_op jit(solution)/shard_map/key_value/pallas_call | solution.py:128
  49.2 3.5 %key_value.4 = (f32[512,2048]{1,0:T(8,128)S(1)}, f32[512,2048]{1,0:T(8,128)S(1)}) custom-call(bf16[512,2048]{1,0:T(8,128)(2,1)S(1)} %get-tuple-element.76.q, bf16[512,2048]{1,0:T(8,128)(2,1)S(1)} %get-tuple-element.73.v, bf16[512,2048]{1,0:T(8,128)(2,1)S(1)} %get-tuple-element.105.dattn, ...), custom_call_target="tpu_custom_call", output_to_operand_aliasing={{0}: (8, {}), {1}: (9, {})} | custom-call | flops 1610612736 | bytes 42078208 | tf_op jit(solution)/shard_map/key_value/pallas_call | solution.py:128
  53.8 1.9 %collective-permute-start.11 = (bf16[528,128]{1,0:T(8,128)(2,1)S(1)}, bf16[528,128]{1,0:T(8,128)(2,1)S(1)}, u32[]{:S(2)}, u32[]{:S(2)}) collective-permute-start(bf16[528,128]{1,0:T(8,128)(2,1)S(1)} %get-tuple-element.121._), channel_id=1, source_target_pairs={{0,16},{2,18},{4,20},{6,22},{8,24},{10,26},{12,28},{14,30},{16,0},... | collective-permute-start | bytes 405512 | tf_op jit(solution)/shard_map/ppermute | solution.py:606
  55.7 5.5 %query.1.refs_0_ = bf16[512,2048]{1,0:T(8,128)(2,1)S(1)} custom-call(bf16[512,2048]{1,0:T(8,128)(2,1)S(1)} %get-tuple-element.72.k, bf16[512,2048]{1,0:T(8,128)(2,1)S(1)} %get-tuple-element.73.v, bf16[512,2048]{1,0:T(8,128)(2,1)S(1)} %get-tuple-element.105.dattn, f32[16,512]{1,0:T(8,128)S(1)} %get-tuple-element.71.row, ...), custom_call_target="tpu_custom_call" | custom-call | flops 2415919104 | bytes 11194368 | tf_op jit(solution)/shard_map/query/pallas_call | solution.py:128
  61.6 1.6 %collective-permute-start.12 = (bf16[528,128]{1,0:T(8,128)(2,1)S(1)}, bf16[528,128]{1,0:T(8,128)(2,1)S(1)}, u32[]{:S(2)}, u32[]{:S(2)}) collective-permute-start(bf16[528,128]{1,0:T(8,128)(2,1)S(1)} %get-tuple-element.122._), channel_id=1, source_target_pairs={{0,4},{2,6},{4,0},{6,2},{8,12},{10,14},{12,8},{14,10},{16,20},{18,... | collective-permute-start | bytes 405512 | tf_op jit(solution)/shard_map/ppermute | solution.py:606
  63.2 3.3 %key_value.5 = (f32[512,2048]{1,0:T(8,128)S(1)}, f32[512,2048]{1,0:T(8,128)S(1)}, bf16[512,2048]{1,0:T(8,128)(2,1)}) custom-call(bf16[512,2048]{1,0:T(8,128)(2,1)S(1)} %get-tuple-element.76.q, bf16[512,2048]{1,0:T(8,128)(2,1)S(1)} %get-tuple-element.73.v, ...), custom_call_target="tpu_custom_call", output_to_operand_aliasing={{0}: (9, {}), {1}: (10, {})} | custom-call | flops 1610612736 | bytes 46272512 | tf_op jit(solution)/shard_map/key_value/pallas_call | solution.py:128
  68.6 2.6 %final.1 = (bf16[512,2048]{1,0:T(8,128)(2,1)}, bf16[512,2048]{1,0:T(8,128)(2,1)}, f32[1,2048]{1,0:T(1,128)}) custom-call(bf16[512,2048]{1,0:T(8,128)(2,1)S(1)} %get-tuple-element.72.k, bf16[512,2048]{1,0:T(8,128)(2,1)S(1)} %get-tuple-element.73.v, f32[512,2048]{1,0:T(8,128)S(1)} %get-tuple-element.125.refs_0_.dk, f32[512,2048]{1,0:T(8,128)S(1)} %get-tuple-element.126.dv, ...), custom_call_target="tpu_custom_call" | custom-call | flops 268435456 | bytes 20209664 | tf_op jit(solution)/shard_map/final/pallas_call | solution.py:128
  (43 shorter events, 16.4 us)
Async XLA Ops:
  3.5 3.9 %collective-permute-start = (f32[2,520,128]{2,1,0:T(8,128)S(1)}, f32[2,520,128]{2,1,0:T(8,128)S(1)}, u32[]{:S(2)}, u32[]{:S(2)}) collective-permute-start(f32[2,520,128]{2,1,0:T(8,128)S(1)} %get-tuple-element.74), channel_id=1, source_target_pairs={{0,2},{2,0},{4,6},{6,4},{8,10},{10,8},{12,14},{14,12},{16,18},{18,... | collective-permute-start | bytes 1597448 | tf_op jit(solution)/shard_map/ppermute | solution.py:606
  4.0 26.8 %collective-permute-start.3 = (bf16[256,2048]{1,0:T(8,128)(2,1)S(1)}, bf16[256,2048]{1,0:T(8,128)(2,1)S(1)}, u32[]{:S(2)}, u32[]{:S(2)}) collective-permute-start(bf16[256,2048]{1,0:T(8,128)(2,1)S(1)} %get-tuple-element.87), channel_id=1, source_target_pairs={{0,1},{1,0},{2,3},{3,2},{4,5},{5,4},{6,7},{7,6},{8,9},{9,8},{10,11... | collective-permute-start | bytes 3145736 | tf_op jit(solution)/shard_map/ppermute | solution.py:685
  7.5 5.7 %collective-permute-start.1 = (bf16[528,128]{1,0:T(8,128)(2,1)S(1)}, bf16[528,128]{1,0:T(8,128)(2,1)S(1)}, u32[]{:S(2)}, u32[]{:S(2)}) collective-permute-start(bf16[528,128]{1,0:T(8,128)(2,1)S(1)} %get-tuple-element.75._), channel_id=1, source_target_pairs={{0,4},{2,6},{4,0},{6,2},{8,12},{10,14},{12,8},{14,10},{16,20},{18,... | collective-permute-start | bytes 405512 | tf_op jit(solution)/shard_map/ppermute | solution.py:606
  13.3 5.3 %collective-permute-start.2 = (bf16[528,128]{1,0:T(8,128)(2,1)S(1)}, bf16[528,128]{1,0:T(8,128)(2,1)S(1)}, u32[]{:S(2)}, u32[]{:S(2)}) collective-permute-start(bf16[528,128]{1,0:T(8,128)(2,1)S(1)} %get-tuple-element.81._), channel_id=1, source_target_pairs={{0,8},{2,10},{4,12},{6,14},{8,0},{10,2},{12,4},{14,6},{16,24},{18,... | collective-permute-start | bytes 405512 | tf_op jit(solution)/shard_map/ppermute | solution.py:606
  16.6 2.0 %copy-start = (bf16[16,256,512]{2,1,0:T(8,128)(2,1)}, bf16[16,256,512]{2,1,0:T(8,128)(2,1)S(1)}, u32[]{:S(2)}) copy-start(bf16[16,256,512]{2,1,0:T(8,128)(2,1)S(1)} %get-tuple-element.108.probs0) | copy-start | bytes 12582916
  18.7 8.4 %collective-permute-start.4 = (bf16[528,128]{1,0:T(8,128)(2,1)S(1)}, bf16[528,128]{1,0:T(8,128)(2,1)S(1)}, u32[]{:S(2)}, u32[]{:S(2)}) collective-permute-start(bf16[528,128]{1,0:T(8,128)(2,1)S(1)} %get-tuple-element.86.refs_0_), channel_id=1, source_target_pairs={{0,16},{2,18},{4,20},{6,22},{8,24},{10,26},{12,28},{14,30},{16,0},... | collective-permute-start | bytes 405512 | tf_op jit(solution)/shard_map/ppermute | solution.py:606
  25.7 3.1 %copy-start.2 = (bf16[512,2048]{1,0:T(8,128)(2,1)S(1)}, bf16[512,2048]{1,0:T(8,128)(2,1)}, u32[]{:S(2)}) copy-start(bf16[512,2048]{1,0:T(8,128)(2,1)} %gate.6) | copy-start | bytes 6291460
  25.7 3.1 %copy-start.3 = (f32[2048]{0:T(1024)S(1)}, f32[2048]{0:T(1024)}, u32[]{:S(2)}) copy-start(f32[2048]{0:T(1024)} %param.12) | copy-start | bytes 24580
  27.2 5.1 %collective-permute-start.5 = (bf16[528,128]{1,0:T(8,128)(2,1)S(1)}, bf16[528,128]{1,0:T(8,128)(2,1)S(1)}, u32[]{:S(2)}, u32[]{:S(2)}) collective-permute-start(bf16[528,128]{1,0:T(8,128)(2,1)S(1)} %get-tuple-element.90._), channel_id=1, source_target_pairs={{0,4},{2,6},{4,0},{6,2},{8,12},{10,14},{12,8},{14,10},{16,20},{18,... | collective-permute-start | bytes 405512 | tf_op jit(solution)/shard_map/ppermute | solution.py:606
  32.6 1.6 %collective-permute-start.6 = (bf16[2,528,128]{2,1,0:T(8,128)(2,1)S(1)}, bf16[2,528,128]{2,1,0:T(8,128)(2,1)S(1)}, u32[]{:S(2)}, u32[]{:S(2)}) collective-permute-start(bf16[2,528,128]{2,1,0:T(8,128)(2,1)S(1)} %get-tuple-element.94), channel_id=1, source_target_pairs={{0,2},{2,0},{4,6},{6,4},{8,10},{10,8},{12,14},{14,12},{16,18},{18,... | collective-permute-start | bytes 811016 | tf_op jit(solution)/shard_map/ppermute | solution.py:606
  35.8 3.8 %collective-permute-start.7 = (f32[8,512]{1,0:T(8,128)S(1)}, f32[8,512]{1,0:T(8,128)S(1)}, u32[]{:S(2)}, u32[]{:S(2)}) collective-permute-start(f32[8,512]{1,0:T(8,128)S(1)} %get-tuple-element.101.refs_0_), channel_id=1, source_target_pairs={{0,1},{1,0},{2,3},{3,2},{4,5},{5,4},{6,7},{7,6},{8,9},{9,8},{10,11... | collective-permute-start | bytes 49160 | tf_op jit(solution)/shard_map/ppermute | solution.py:786
  41.1 1.6 %collective-permute-start.8 = (bf16[2,528,128]{2,1,0:T(8,128)(2,1)S(1)}, bf16[2,528,128]{2,1,0:T(8,128)(2,1)S(1)}, u32[]{:S(2)}, u32[]{:S(2)}) collective-permute-start(bf16[2,528,128]{2,1,0:T(8,128)(2,1)S(1)} %get-tuple-element.110), channel_id=1, source_target_pairs={{0,2},{2,0},{4,6},{6,4},{8,10},{10,8},{12,14},{14,12},{16,18},{18,... | collective-permute-start | bytes 811016 | tf_op jit(solution)/shard_map/ppermute | solution.py:606
  42.3 3.6 %copy-start.1 = (bf16[16,256,512]{2,1,0:T(8,128)(2,1)S(1)}, bf16[16,256,512]{2,1,0:T(8,128)(2,1)}, u32[]{:S(2)}) copy-start(bf16[16,256,512]{2,1,0:T(8,128)(2,1)} %copy-done) | copy-start | bytes 12582916
  42.8 5.7 %collective-permute-start.9 = (bf16[528,128]{1,0:T(8,128)(2,1)S(1)}, bf16[528,128]{1,0:T(8,128)(2,1)S(1)}, u32[]{:S(2)}, u32[]{:S(2)}) collective-permute-start(bf16[528,128]{1,0:T(8,128)(2,1)S(1)} %get-tuple-element.112._), channel_id=1, source_target_pairs={{0,4},{2,6},{4,0},{6,2},{8,12},{10,14},{12,8},{14,10},{16,20},{18,... | collective-permute-start | bytes 405512 | tf_op jit(solution)/shard_map/ppermute | solution.py:606
  48.6 5.1 %collective-permute-start.10 = (bf16[528,128]{1,0:T(8,128)(2,1)S(1)}, bf16[528,128]{1,0:T(8,128)(2,1)S(1)}, u32[]{:S(2)}, u32[]{:S(2)}) collective-permute-start(bf16[528,128]{1,0:T(8,128)(2,1)S(1)} %get-tuple-element.116._), channel_id=1, source_target_pairs={{0,8},{2,10},{4,12},{6,14},{8,0},{10,2},{12,4},{14,6},{16,24},{18,... | collective-permute-start | bytes 405512 | tf_op jit(solution)/shard_map/ppermute | solution.py:606
  53.8 7.7 %collective-permute-start.11 = (bf16[528,128]{1,0:T(8,128)(2,1)S(1)}, bf16[528,128]{1,0:T(8,128)(2,1)S(1)}, u32[]{:S(2)}, u32[]{:S(2)}) collective-permute-start(bf16[528,128]{1,0:T(8,128)(2,1)S(1)} %get-tuple-element.121._), channel_id=1, source_target_pairs={{0,16},{2,18},{4,20},{6,22},{8,24},{10,26},{12,28},{14,30},{16,0},... | collective-permute-start | bytes 405512 | tf_op jit(solution)/shard_map/ppermute | solution.py:606
  61.6 5.1 %collective-permute-start.12 = (bf16[528,128]{1,0:T(8,128)(2,1)S(1)}, bf16[528,128]{1,0:T(8,128)(2,1)S(1)}, u32[]{:S(2)}, u32[]{:S(2)}) collective-permute-start(bf16[528,128]{1,0:T(8,128)(2,1)S(1)} %get-tuple-element.122._), channel_id=1, source_target_pairs={{0,4},{2,6},{4,0},{6,2},{8,12},{10,14},{12,8},{14,10},{16,20},{18,... | collective-permute-start | bytes 405512 | tf_op jit(solution)/shard_map/ppermute | solution.py:606
  66.9 1.6 %collective-permute-start.13 = (bf16[2,528,128]{2,1,0:T(8,128)(2,1)S(1)}, bf16[2,528,128]{2,1,0:T(8,128)(2,1)S(1)}, u32[]{:S(2)}, u32[]{:S(2)}) collective-permute-start(bf16[2,528,128]{2,1,0:T(8,128)(2,1)S(1)} %get-tuple-element.128), channel_id=1, source_target_pairs={{0,2},{2,0},{4,6},{6,4},{8,10},{10,8},{12,14},{14,12},{16,18},{18,... | collective-permute-start | bytes 811016 | tf_op jit(solution)/shard_map/ppermute | solution.py:606
